TPU v7x, 256 devices: a whole 4x4x8 slice. The times are simulated.
256 devices in a mesh: doc: 8 (over x_hi, y), seq: 32 (over x_lo, z, core).
Axes of the slice: x: 4 (x_hi: 2, x_lo: 2; x = x_hi * 2 + x_lo), y: 4, z: 8, core: 2. Of those that a mesh axis runs over, the one named last changes fastest.
Arguments:
- hidden_in: bfloat16 [32768, 2048], P(('doc', 'seq')), parts along dimension 0
- length: int32 [8], P('doc'), parts along dimension 0, may hold values from 2048 to 4096
- attn_gain: float32 [2048], replicated, may hold values from 0.1 to 1.9
- global_gain: float32 [2048], replicated, may hold values from 0.1 to 1.9
- w_query: bfloat16 [2048, 1024], P(None, 'seq')
- w_key: bfloat16 [2048, 1024], P(None, 'seq')
- w_value: bfloat16 [2048, 1024], P(None, 'seq'), may hold values from -0.125 to 0.125
- w_out: bfloat16 [1024, 2048], P(None, 'seq'), may hold values from -0.75 to 0.75
Outputs:
- attended: bfloat16 [32768, 2048], P(('doc', 'seq')), parts along dimension 0
There are 8 independent parts, one for each index of `doc`. A program takes and returns all parts, laid end to end along the dimension named above; an argument that names none is the same for every part. Nothing has to cross between parts.
All inputs are finite; a program needn't handle non-finite values.
Results may differ from a plain program's by a relative error of at most 0.034.
Values may be sent and summed in bfloat16 or wider, within the bound.
No kernel may reach another device: no remote copies, remote signals or barrier semaphores. Data moves between devices by JAX's collectives and lax.ppermute only.
A program may use at most 64 MiB of HBM per device.

v0:
```python
import jax
import jax.numpy as jnp
from jax import lax
from jax.experimental import pallas as pl
from jax.experimental.pallas import tpu as pltpu
from jax.sharding import PartitionSpec as P

HEAD_DIM = 64
BLOCK = 16
RADIUS = 127
NEGATIVE = -1e30
EPSILON = 1e-06

X, Z, C = 2, 8, 2
SEQ_SHARDS = X * Z * C
TOK = 128
HALF = 32
HEADS_LOCAL = 4
WIDE = HEADS_LOCAL * HEAD_DIM


def place(x, z, core):
    return (x * Z + z) * C + core


def pairs(move):
    return [
        (place(x, z, c), place(*move(x, z, c))) for x in range(X) for z in range(Z) for c in range(C)
    ]


OTHER_CORE = pairs(lambda x, z, c: (x, z, 1 - c))
OTHER_X = pairs(lambda x, z, c: (1 - x, z, c))
AHEAD = pairs(lambda x, z, c: (x, (z + (1 if c == 0 else -1)) % Z, c))
BEHIND = pairs(lambda x, z, c: (x, (z - (1 if c == 0 else -1)) % Z, c))
UP = pairs(lambda x, z, c: (x, (z + 1) % Z, c))
DOWN = pairs(lambda x, z, c: (x, (z - 1) % Z, c))


def send(value, route):
    return lax.ppermute(value, "seq", route)


def rms_norm(values, gain_row):
    mean_square = jnp.mean(values * values, axis=-1, keepdims=True)
    return values * lax.rsqrt(mean_square + EPSILON) * gain_row


def dot_nt(left, right):
    return lax.dot_general(
        left, right, (((1,), (1,)), ((), ())), preferred_element_type=jnp.float32
    )


STEPS = ((0, 0), (0, 1), (1, 1), (0, 2), (1, 2), (0, 3), (1, 3), (0, 4))
SHARDS = len(STEPS)
ROWS = 4 * TOK
G_ROWS = Z * 16
VMEM_LIMIT = 48 * 1024 * 1024


def z_of(z, core, way, hops):
    delta = -hops if way == 0 else hops
    return (z + delta * (1 - 2 * core)) & (Z - 1)


def project_kernel(index, *refs):
    blocks, firsts, seconds = refs[:4], refs[4 : 4 + SHARDS], refs[4 + SHARDS : 4 + 2 * SHARDS]
    g_most, g_last, keep_ref, send_ref, rows, g_rows, table = refs[4 + 2 * SHARDS :]
    z, core, x = index[0], index[1], index[2]
    low_core = core == 0
    for ref, bx, bc in zip(blocks, (x, 1 - x, x, 1 - x), (core, core, 1 - core, 1 - core)):
        rows[pl.ds(pl.multiple_of((bx * 2 + bc) * TOK, TOK), TOK), :] = ref[...]
    g_own = pl.multiple_of(core * G_ROWS, G_ROWS)
    g_other = pl.multiple_of((1 - core) * G_ROWS, G_ROWS)
    for j, (way, hops) in enumerate(STEPS):
        at = z_of(z, core, way, hops) * HALF
        for kind in range(3):
            here = pl.multiple_of(kind * 256 + at, 16)
            table[pl.ds(here, 16), :] = firsts[j][kind * 16 : kind * 16 + 16, :]
            there = pl.multiple_of(kind * 256 + at + 16, 16)
            table[pl.ds(there, 16), :] = seconds[j][kind * 16 : kind * 16 + 16, :]
        g_rows[pl.ds(g_own + j * 16, 16), :] = seconds[j][48:64, :]
    g_rows[pl.ds(g_other, 112), :] = g_most[...]
    g_rows[pl.ds(g_other + 112, 16), :] = g_last[...]
    for kind in range(3):
        out = dot_nt(rows[...], table[kind * 256 : kind * 256 + 256, :]).astype(jnp.bfloat16)
        lanes = slice(kind * 128, kind * 128 + 128)
        keep_ref[:, lanes] = jnp.where(low_core, out[:, :128], out[:, 128:])
        send_ref[:, lanes] = jnp.where(low_core, out[:, 128:], out[:, :128])
    for kind in (1, 2):
        out = dot_nt(g_rows[...], table[kind * 256 : kind * 256 + 256, :]).astype(jnp.bfloat16)
        at = slice((kind - 1) * 256, kind * 256)
        keep_ref[at, 384:] = jnp.where(low_core, out[:, :128], out[:, 128:])
        send_ref[at, 384:] = jnp.where(low_core, out[:, 128:], out[:, :128])


def attention_kernel(index, far_pos, keep_ref, got_ref, below_ref, above_ref, out_ref):
    z, x, limit = index[0], index[2], index[3]
    lane_head = (lax.broadcasted_iota(jnp.int32, (TOK, WIDE), 1) % 128) // HALF
    row = lax.broadcasted_iota(jnp.int32, (HEADS_LOCAL * TOK, TOK), 0) % TOK
    col = lax.broadcasted_iota(jnp.int32, (HEADS_LOCAL * TOK, TOK), 1)
    far_ok = far_pos[...] < limit
    far_keys = jnp.concatenate([keep_ref[:256, 384:], got_ref[:256, 384:]], axis=1)
    far_values = jnp.concatenate([keep_ref[256:, 384:], got_ref[256:, 384:]], axis=1)

    def local(kind, at):
        lanes = slice(kind * 128, kind * 128 + 128)
        return jnp.concatenate([keep_ref[at : at + TOK, lanes], got_ref[at : at + TOK, lanes]], axis=1)

    def halo(ref, kind, seg):
        at = pl.ds(pl.multiple_of(seg * TOK, TOK), TOK)
        lanes = kind * 128 - 128
        return jnp.concatenate([ref[at, lanes : lanes + 128], ref[at, lanes + 256 : lanes + 384]], axis=1)

    for seg in range(2):
        below_seg = jnp.where(z == 0, 1 - seg, seg)
        above_seg = jnp.where(z == Z - 1, 1 - seg, seg)
        for part in range(2):
            base = (seg * Z + z) * 2 * TOK + part * TOK
            at = (seg * 2 + part) * TOK
            queries = local(0, at)
            stacked = jnp.concatenate(
                [jnp.where(lane_head == h, queries, jnp.zeros_like(queries)) for h in range(HEADS_LOCAL)],
                axis=0,
            )

            def neighbours(kind):
                if part == 0:
                    return halo(below_ref, kind, below_seg), local(kind, at), local(kind, at + TOK)
                return local(kind, at - TOK), local(kind, at), halo(above_ref, kind, above_seg)

            k_left, k_mid, k_right = neighbours(1)
            v_left, v_mid, v_right = neighbours(2)
            low = base - TOK
            ok_left = (col > row) & (col + low >= 0) & (col + low < limit)
            ok_mid = col + base < limit
            ok_right = (col < row) & (col + (base + TOK) < limit)
            s_left = jnp.where(ok_left, dot_nt(stacked, k_left), NEGATIVE)
            s_mid = jnp.where(ok_mid, dot_nt(stacked, k_mid), NEGATIVE)
            s_right = jnp.where(ok_right, dot_nt(stacked, k_right), NEGATIVE)
            s_far = jnp.where(far_ok, dot_nt(stacked, far_keys), NEGATIVE)
            near_top = jnp.maximum(jnp.maximum(s_left, s_mid), s_right)
            far_top = jnp.maximum(s_far[:, :128], s_far[:, 128:])
            top = jnp.max(jnp.maximum(near_top, far_top), axis=-1, keepdims=True)
            w_left = jnp.exp(s_left - top)
            w_mid = jnp.exp(s_mid - top)
            w_right = jnp.exp(s_right - top)
            w_far = jnp.exp(s_far - top)
            total = jnp.sum(
                w_left + w_mid + w_right + w_far[:, :128] + w_far[:, 128:], axis=-1, keepdims=True
            )

            def mix(weights, values):
                return jnp.dot(
                    weights.astype(jnp.bfloat16), values, preferred_element_type=jnp.float32
                )

            mixed = mix(w_left, v_left) + mix(w_mid, v_mid) + mix(w_right, v_right) + mix(w_far, far_values)
            mixed = mixed / total
            context = jnp.zeros((TOK, WIDE), jnp.float32)
            for h in range(HEADS_LOCAL):
                context = jnp.where(lane_head == h, mixed[h * TOK : (h + 1) * TOK, :], context)
            mine = jnp.where(x == seg, 0, 1)
            out_ref[mine, part * TOK : (part + 1) * TOK, :] = context.astype(jnp.bfloat16)


def output_kernel(index, own_ref, there_ref, *refs):
    blocks, keep_ref, send_ref = refs[:SHARDS], refs[SHARDS], refs[SHARDS + 1]
    z, core, x = index[0], index[1], index[2]
    own, there = own_ref[...], there_ref[...]
    full = jnp.concatenate([jnp.where(x == 0, own, there), jnp.where(x == 0, there, own)], axis=1)
    for j, (way, hops) in enumerate(STEPS):
        zj = z_of(z, core, way, hops)
        out = dot_nt(full, blocks[j][...])
        keep = jnp.where(core == 0, out[:TOK], out[TOK:])
        sent = jnp.where(core == 0, out[TOK:], out[:TOK]).astype(jnp.bfloat16)
        for side in range(X):
            lanes = pl.ds(pl.multiple_of((side * Z + zj) * 128, 128), 128)
            keep_ref[:, lanes] = keep[:, side * 128 : side * 128 + 128]
            send_ref[:, lanes] = sent[:, side * 128 : side * 128 + 128]


def on_chip(kernel, out_shape, flops, exps, args, scratch=()):
    vmem = pl.BlockSpec(memory_space=pltpu.VMEM)
    return pl.pallas_call(
        kernel,
        out_shape=out_shape,
        in_specs=[pl.BlockSpec(memory_space=pltpu.SMEM)] + [vmem] * (len(args) - 1),
        out_specs=jax.tree.map(lambda _: vmem, out_shape),
        scratch_shapes=list(scratch),
        compiler_params=pltpu.CompilerParams(vmem_limit_bytes=VMEM_LIMIT),
        cost_estimate=pl.CostEstimate(flops=flops, bytes_accessed=4 << 20, transcendentals=exps),
    )(*args)


def after(value, *others):
    return lax.optimization_barrier((value, *others))[0]


def per_device(hidden_in, length, attn_gain, global_gain, w_query, w_key, w_value, w_out):
    width = hidden_in.shape[1]
    me = lax.axis_index("seq")
    core = me & 1
    z = (me >> 1) & (Z - 1)
    x = me >> 4
    limit = length[0]
    bf16 = jnp.bfloat16
    index = jnp.stack([z, core, x, limit]).astype(jnp.int32)

    mine = jnp.stack([w_query.T, w_key.T, w_value.T]).reshape(3, 2, 16, width)
    first = mine[:, 0].reshape(48, width)

    normed = rms_norm(hidden_in.astype(jnp.float32), attn_gain).astype(bf16)
    is_valid = (me * TOK + jnp.arange(TOK, dtype=jnp.int32) < limit).astype(jnp.float32)
    block_sums = jnp.sum(
        (normed.astype(jnp.float32) * is_valid[:, None]).reshape(TOK // BLOCK, BLOCK, width), axis=1
    )
    global_mine = rms_norm(block_sums, global_gain).astype(bf16)
    global_there = send(global_mine, OTHER_X)
    second = jnp.concatenate(
        [
            mine[:, 1].reshape(48, width),
            jnp.where(x == 0, global_mine, global_there),
            jnp.where(x == 0, global_there, global_mine),
        ],
        axis=0,
    )

    one, two = {(0, 0): first}, {(0, 0): second}
    a_one, a_two, b_one, b_two = first, second, first, second
    for step in range(1, 5):
        one[0, step] = a_one = send(a_one, AHEAD)
        if step < 4:
            one[1, step] = b_one = send(b_one, BEHIND)
        two[0, step] = a_two = send(a_two, AHEAD)
        if step < 4:
            two[1, step] = b_two = send(b_two, BEHIND)
    firsts = [one[s] for s in STEPS]
    seconds = [two[s] for s in STEPS]

    to_send = after(normed, one[0, 1])
    across = send(to_send, OTHER_X)
    beside = send(to_send, OTHER_CORE)
    beside_across = send(across, OTHER_CORE)

    g_most = send(jnp.concatenate([s[48:] for s in seconds[:-1]], axis=0), OTHER_CORE)
    g_last = send(seconds[-1][48:], OTHER_CORE)

    half = jax.ShapeDtypeStruct((ROWS, 4 * 128), bf16)
    keep, to_swap = on_chip(
        project_kernel,
        (half, half),
        2 * 768 * 768 * width,
        0,
        (index, normed, across, beside, beside_across, *firsts, *seconds, g_most, g_last),
        (pltpu.VMEM((ROWS, width), bf16), pltpu.VMEM((2 * G_ROWS, width), bf16), pltpu.VMEM((768, width), bf16)),
    )
    got = send(to_swap, OTHER_CORE)

    def edge(part):
        tables = [t.reshape(2, 2, TOK, 512)[:, part, :, 128:384].reshape(2 * TOK, 256) for t in (keep, got)]
        return jnp.concatenate(tables, axis=1)

    below = send(edge(1), UP)
    above = send(edge(0), DOWN)

    deltas = jnp.asarray([-h if w == 0 else h for w, h in STEPS], jnp.int32)
    g_core = jnp.arange(C, dtype=jnp.int32)[:, None, None, None]
    g_z = (z + deltas[None, :, None, None] * (1 - 2 * g_core)) & (Z - 1)
    g_x = jnp.arange(X, dtype=jnp.int32)[None, None, :, None]
    g_k = jnp.arange(8, dtype=jnp.int32)[None, None, None, :]
    far_pos = (((g_x * Z + g_z) * C + g_core) * TOK + g_k * BLOCK).reshape(1, 2 * G_ROWS)
    context = on_chip(
        attention_kernel,
        jax.ShapeDtypeStruct((2, 2 * TOK, WIDE), bf16),
        4 * 4 * TOK * 640 * WIDE * 4,
        4 * 4 * TOK * 640,
        (index, far_pos, keep, got, below, above),
    )

    out_t = after(w_out, one[0, 2]).T.reshape(64, X, 2, HEADS_LOCAL, 2, HALF)
    out_t = jnp.transpose(out_t, (0, 2, 1, 4, 3, 5))
    group_0 = out_t[:, 0].reshape(64, 2 * WIDE)
    group_1 = out_t[:, 1, :, ::-1].reshape(64, 2 * WIDE)
    kept = jnp.where(core == 0, group_0, group_1)
    passed = send(jnp.where(core == 0, group_1, group_0), OTHER_CORE)
    chip = jnp.concatenate([jnp.where(core == 0, kept, passed), jnp.where(core == 0, passed, kept)], axis=0)
    chip_there = send(chip, OTHER_X)
    both = jnp.concatenate([jnp.where(x == 0, chip, chip_there), jnp.where(x == 0, chip_there, chip)], axis=0)
    out_blocks = {(0, 0): both}
    ahead = behind = after(both, two[0, 4], two[1, 3])
    for step in range(1, 5):
        out_blocks[0, step] = ahead = send(ahead, AHEAD)
        if step < 4:
            out_blocks[1, step] = behind = send(behind, BEHIND)

    there = send(context[1], OTHER_X)
    kept_part, sent_part = on_chip(
        output_kernel,
        (jax.ShapeDtypeStruct((TOK, width), jnp.float32), jax.ShapeDtypeStruct((TOK, width), bf16)),
        2 * 256 * 512 * width,
        0,
        (index, context[0], there, *[out_blocks[s] for s in STEPS]),
    )
    return (kept_part + send(sent_part, OTHER_CORE).astype(jnp.float32)).astype(bf16)


def solution(mesh):
    placed = (
        P(("doc", "seq"), None),
        P("doc"),
        P(),
        P(),
        P(None, "seq"),
        P(None, "seq"),
        P(None, "seq"),
        P(None, "seq"),
    )
    return jax.shard_map(
        per_device, mesh=mesh, in_specs=placed, out_specs=P(("doc", "seq"), None), check_vma=False
    )
```

profile of v0, /device:TPU:1, one launch (start us, length us, event | category | flops | bytes accessed | tf_op | source)
XLA Modules:
  0.0 114.7 jit_solution(14847973402561026948)
XLA Ops:
  0.7 1.2 %fusion = f32[128]{0:T(128)S(1)} fusion(bf16[128,2048]{1,0:T(8,128)(2,1)} %param.9), kind=kLoop, calls=%fused_computation.2 | loop fusion | flops 786304 | bytes 524800 | tf_op jit(solution)/shard_map/reduce_sum | solution.py:45
  2.9 2.1 %collective-permute-start.10 = (bf16[8,2048]{1,0:T(8,128)(2,1)S(1)}, bf16[8,2048]{1,0:T(8,128)(2,1)S(1)}, u32[]{:S(2)}, u32[]{:S(2)}) collective-permute-start(bf16[8,2048]{1,0:T(8,128)(2,1)S(1)} %multiply_convert_fusion), channel_id=1, source_target_pairs={{0,16},{1,17},{2,18},{3,19},{4,20},{5,21},{6,22},{7,23},{8,24},{9,... | collective-permute-start | bytes 98312 | tf_op jit(solution)/shard_map/ppermute | solution.py:41
  5.1 5.7 %collective-permute-start = (bf16[48,2048]{1,0:T(8,128)(2,1)S(1)}, bf16[48,2048]{1,0:T(8,128)(2,1)S(1)}, u32[]{:S(2)}, u32[]{:S(2)}) collective-permute-start(bf16[48,2048]{1,0:T(8,128)(2,1)S(1)} %bitcast.49), channel_id=1, source_target_pairs={{0,2},{1,15},{2,4},{3,1},{4,6},{5,3},{6,8},{7,5},{8,10},{9,7},{10,... | collective-permute-start | bytes 589832 | tf_op jit(solution)/shard_map/ppermute | solution.py:41
  12.1 2.7 %collective-permute-start.11 = (bf16[64,2048]{1,0:T(8,128)(2,1)S(1)}, bf16[64,2048]{1,0:T(8,128)(2,1)S(1)}, u32[]{:S(2)}, u32[]{:S(2)}) collective-permute-start(bf16[64,2048]{1,0:T(8,128)(2,1)S(1)} %pad_maximum_fusion.1.refs_12_), channel_id=1, source_target_pairs={{0,2},{1,15},{2,4},{3,1},{4,6},{5,3},{6,8},{7,5},{8,10},{9,7},{10,... | collective-permute-start | bytes 786440 | tf_op jit(solution)/shard_map/ppermute | solution.py:41
  15.7 2.1 %collective-permute-start.2 = (bf16[128,2048]{1,0:T(8,128)(2,1)S(1)}, bf16[128,2048]{1,0:T(8,128)(2,1)}, u32[]{:S(2)}, u32[]{:S(2)}) collective-permute-start(bf16[128,2048]{1,0:T(8,128)(2,1)S(1)} %get-tuple-element.12.refs_0_), channel_id=1, source_target_pairs={{0,1},{1,0},{2,3},{3,2},{4,5},{5,4},{6,7},{7,6},{8,9},{9,8},{10,11... | collective-permute-start | bytes 1572872 | tf_op jit(solution)/shard_map/ppermute | solution.py:41
  17.8 2.0 %collective-permute-start.5 = (bf16[48,2048]{1,0:T(8,128)(2,1)S(1)}, bf16[48,2048]{1,0:T(8,128)(2,1)S(1)}, u32[]{:S(2)}, u32[]{:S(2)}) collective-permute-start(bf16[48,2048]{1,0:T(8,128)(2,1)S(1)} %collective-permute-done.refs_5_), channel_id=1, source_target_pairs={{0,2},{1,15},{2,4},{3,1},{4,6},{5,3},{6,8},{7,5},{8,10},{9,7},{10,... | collective-permute-start | bytes 589832 | tf_op jit(solution)/shard_map/ppermute | solution.py:41
  20.4 2.7 %collective-permute-done.5.refs_7_ = bf16[48,2048]{1,0:T(8,128)(2,1)S(1)} collective-permute-done((bf16[48,2048]{1,0:T(8,128)(2,1)S(1)}, bf16[48,2048]{1,0:T(8,128)(2,1)S(1)}, u32[]{:S(2)}, u32[]{:S(2)}) %collective-permute-start.5) | collective-permute-done | bytes 196640 | tf_op jit(solution)/shard_map/ppermute | solution.py:41
  23.2 3.1 %collective-permute-start.13 = (bf16[64,2048]{1,0:T(8,128)(2,1)S(1)}, bf16[64,2048]{1,0:T(8,128)(2,1)S(1)}, u32[]{:S(2)}, u32[]{:S(2)}) collective-permute-start(bf16[64,2048]{1,0:T(8,128)(2,1)S(1)} %collective-permute-done.11.refs_13_), channel_id=1, source_target_pairs={{0,2},{1,15},{2,4},{3,1},{4,6},{5,3},{6,8},{7,5},{8,10},{9,7},{10,... | collective-permute-start | bytes 786440 | tf_op jit(solution)/shard_map/ppermute | solution.py:41
  26.7 1.0 collective-permute-start.24
  28.6 1.3 %collective-permute-start.14 = (bf16[64,2048]{1,0:T(8,128)(2,1)S(1)}, bf16[64,2048]{1,0:T(8,128)(2,1)S(1)}, u32[]{:S(2)}, u32[]{:S(2)}) collective-permute-start(bf16[64,2048]{1,0:T(8,128)(2,1)S(1)} %collective-permute-done.12.refs_14_), channel_id=1, source_target_pairs={{0,14},{1,3},{2,0},{3,5},{4,2},{5,7},{6,4},{7,9},{8,6},{9,11},{10,... | collective-permute-start | bytes 786440 | tf_op jit(solution)/shard_map/ppermute | solution.py:41
  30.5 2.9 %collective-permute-start.7 = (bf16[48,2048]{1,0:T(8,128)(2,1)S(1)}, bf16[48,2048]{1,0:T(8,128)(2,1)S(1)}, u32[]{:S(2)}, u32[]{:S(2)}) collective-permute-start(bf16[48,2048]{1,0:T(8,128)(2,1)S(1)} %collective-permute-done.5.refs_7_), channel_id=1, source_target_pairs={{0,2},{1,15},{2,4},{3,1},{4,6},{5,3},{6,8},{7,5},{8,10},{9,7},{10,... | collective-permute-start | bytes 589832 | tf_op jit(solution)/shard_map/ppermute | solution.py:41
  34.0 2.9 %collective-permute-done.14.refs_16_ = bf16[64,2048]{1,0:T(8,128)(2,1)S(1)} collective-permute-done((bf16[64,2048]{1,0:T(8,128)(2,1)S(1)}, bf16[64,2048]{1,0:T(8,128)(2,1)S(1)}, u32[]{:S(2)}, u32[]{:S(2)}) %collective-permute-start.14) | collective-permute-done | bytes 262176 | tf_op jit(solution)/shard_map/ppermute | solution.py:41
  37.7 4.7 %collective-permute-done.15.refs_17_ = bf16[64,2048]{1,0:T(8,128)(2,1)S(1)} collective-permute-done((bf16[64,2048]{1,0:T(8,128)(2,1)S(1)}, bf16[64,2048]{1,0:T(8,128)(2,1)S(1)}, u32[]{:S(2)}, u32[]{:S(2)}) %collective-permute-start.15) | collective-permute-done | bytes 262176 | tf_op jit(solution)/shard_map/ppermute | solution.py:41
  43.5 6.1 %collective-permute-start.3 = (bf16[128,2048]{1,0:T(8,128)(2,1)}, bf16[128,2048]{1,0:T(8,128)(2,1)S(1)}, u32[]{:S(2)}, u32[]{:S(2)}) collective-permute-start(bf16[128,2048]{1,0:T(8,128)(2,1)} %collective-permute-done.1.refs_1_), channel_id=1, source_target_pairs={{0,1},{1,0},{2,3},{3,2},{4,5},{5,4},{6,7},{7,6},{8,9},{9,8},{10,11... | collective-permute-start | bytes 1572872 | tf_op jit(solution)/shard_map/ppermute | solution.py:41
  50.3 4.6 %collective-permute-start.18 = (bf16[112,2048]{1,0:T(8,128)(2,1)}, bf16[112,2048]{1,0:T(8,128)(2,1)S(1)}, u32[]{:S(2)}, u32[]{:S(2)}) collective-permute-start(bf16[112,2048]{1,0:T(8,128)(2,1)} %slice_dynamic-update-slice_fusion), channel_id=1, source_target_pairs={{0,1},{1,0},{2,3},{3,2},{4,5},{5,4},{6,7},{7,6},{8,9},{9,8},{10,11... | collective-permute-start | bytes 1376264 | tf_op jit(solution)/shard_map/ppermute | solution.py:41
  55.0 2.7 %collective-permute-start.8 = (bf16[48,2048]{1,0:T(8,128)(2,1)S(1)}, bf16[48,2048]{1,0:T(8,128)(2,1)S(1)}, u32[]{:S(2)}, u32[]{:S(2)}) collective-permute-start(bf16[48,2048]{1,0:T(8,128)(2,1)S(1)} %collective-permute-done.6.refs_8_), channel_id=1, source_target_pairs={{0,14},{1,3},{2,0},{3,5},{4,2},{5,7},{6,4},{7,9},{8,6},{9,11},{10,... | collective-permute-start | bytes 589832 | tf_op jit(solution)/shard_map/ppermute | solution.py:41
  58.6 5.2 %collective-permute-done.8.refs_10_ = bf16[48,2048]{1,0:T(8,128)(2,1)S(1)} collective-permute-done((bf16[48,2048]{1,0:T(8,128)(2,1)S(1)}, bf16[48,2048]{1,0:T(8,128)(2,1)S(1)}, u32[]{:S(2)}, u32[]{:S(2)}) %collective-permute-start.8) | collective-permute-done | bytes 196640 | tf_op jit(solution)/shard_map/ppermute | solution.py:41
  64.6 3.0 %collective-permute-start.26 = (bf16[256,512]{1,0:T(8,128)(2,1)S(1)}, bf16[256,512]{1,0:T(8,128)(2,1)S(1)}, u32[]{:S(2)}, u32[]{:S(2)}) collective-permute-start(bf16[256,512]{1,0:T(8,128)(2,1)S(1)} %pad_maximum_fusion.4.refs_0_), channel_id=1, source_target_pairs={{0,2},{1,15},{2,4},{3,1},{4,6},{5,3},{6,8},{7,5},{8,10},{9,7},{10,... | collective-permute-start | bytes 786440 | tf_op jit(solution)/shard_map/ppermute | solution.py:41
  68.5 4.0 %shard_map.91 = (bf16[512,512]{1,0:T(8,128)(2,1)S(1)}, bf16[512,512]{1,0:T(8,128)(2,1)S(1)}) custom-call(s32[4]{0:T(128)S(1)} %pad_add_fusion.index, bf16[128,2048]{1,0:T(8,128)(2,1)S(1)} %get-tuple-element.12.refs_0_, bf16[128,2048]{1,0:T(8,128)(2,1)} %collective-permute-done.1.refs_1_, bf16[128,2048]{1,0:T(8,128)(2,1)} %collective-permute-done.2.refs_2_, ...), custom_call_target="tpu_custom_call" | custom-call | flops 2415919104 | bytes 4194304 | tf_op jit(solution)/shard_map/pallas_call | solution.py:186
  72.5 3.7 %collective-permute-start.20 = (bf16[512,512]{1,0:T(8,128)(2,1)S(1)}, bf16[512,512]{1,0:T(8,128)(2,1)S(1)}, u32[]{:S(2)}, u32[]{:S(2)}) collective-permute-start(bf16[512,512]{1,0:T(8,128)(2,1)S(1)} %get-tuple-element.14), channel_id=1, source_target_pairs={{0,1},{1,0},{2,3},{3,2},{4,5},{5,4},{6,7},{7,6},{8,9},{9,8},{10,11... | collective-permute-start | bytes 1572872 | tf_op jit(solution)/shard_map/ppermute | solution.py:41
  76.2 2.7 %collective-permute-start.28 = (bf16[256,512]{1,0:T(8,128)(2,1)S(1)}, bf16[256,512]{1,0:T(8,128)(2,1)S(1)}, u32[]{:S(2)}, u32[]{:S(2)}) collective-permute-start(bf16[256,512]{1,0:T(8,128)(2,1)S(1)} %collective-permute-done.26.refs_1_), channel_id=1, source_target_pairs={{0,2},{1,15},{2,4},{3,1},{4,6},{5,3},{6,8},{7,5},{8,10},{9,7},{10,... | collective-permute-start | bytes 786440 | tf_op jit(solution)/shard_map/ppermute | solution.py:41
  79.0 5.3 %collective-permute-done.27.refs_2_ = bf16[256,512]{1,0:T(8,128)(2,1)S(1)} collective-permute-done((bf16[256,512]{1,0:T(8,128)(2,1)S(1)}, bf16[256,512]{1,0:T(8,128)(2,1)S(1)}, u32[]{:S(2)}, u32[]{:S(2)}) %collective-permute-start.27) | collective-permute-done | bytes 262176 | tf_op jit(solution)/shard_map/ppermute | solution.py:41
  84.4 2.7 %collective-permute-start.30 = (bf16[256,512]{1,0:T(8,128)(2,1)S(1)}, bf16[256,512]{1,0:T(8,128)(2,1)S(1)}, u32[]{:S(2)}, u32[]{:S(2)}) collective-permute-start(bf16[256,512]{1,0:T(8,128)(2,1)S(1)} %collective-permute-done.28.refs_3_), channel_id=1, source_target_pairs={{0,2},{1,15},{2,4},{3,1},{4,6},{5,3},{6,8},{7,5},{8,10},{9,7},{10,... | collective-permute-start | bytes 786440 | tf_op jit(solution)/shard_map/ppermute | solution.py:41
  88.5 2.7 %collective-permute-start.22 = (bf16[256,512]{1,0:T(8,128)(2,1)}, bf16[256,512]{1,0:T(8,128)(2,1)S(1)}, u32[]{:S(2)}, u32[]{:S(2)}) collective-permute-start(bf16[256,512]{1,0:T(8,128)(2,1)} %pad_maximum_fusion.3), channel_id=1, source_target_pairs={{0,14},{1,15},{2,0},{3,1},{4,2},{5,3},{6,4},{7,5},{8,6},{9,7},{10,... | collective-permute-start | bytes 786440 | tf_op jit(solution)/shard_map/ppermute | solution.py:41
  92.2 3.1 %collective-permute-start.32 = (bf16[256,512]{1,0:T(8,128)(2,1)S(1)}, bf16[256,512]{1,0:T(8,128)(2,1)S(1)}, u32[]{:S(2)}, u32[]{:S(2)}) collective-permute-start(bf16[256,512]{1,0:T(8,128)(2,1)S(1)} %collective-permute-done.30.refs_5_), channel_id=1, source_target_pairs={{0,2},{1,15},{2,4},{3,1},{4,6},{5,3},{6,8},{7,5},{8,10},{9,7},{10,... | collective-permute-start | bytes 786440 | tf_op jit(solution)/shard_map/ppermute | solution.py:41
  95.3 2.3 %collective-permute-done.21.below_ref = bf16[256,512]{1,0:T(8,128)(2,1)S(1)} collective-permute-done((bf16[256,512]{1,0:T(8,128)(2,1)}, bf16[256,512]{1,0:T(8,128)(2,1)S(1)}, u32[]{:S(2)}, u32[]{:S(2)}) %collective-permute-start.21) | collective-permute-done | bytes 262176 | tf_op jit(solution)/shard_map/ppermute | solution.py:41
  97.6 3.9 %shard_map.92 = bf16[2,256,256]{2,1,0:T(8,128)(2,1)S(1)} custom-call(s32[4]{0:T(128)S(1)} %pad_add_fusion.index, s32[1,256]{1,0:T(1,128)S(1)} %add.107.far_pos, bf16[512,512]{1,0:T(8,128)(2,1)S(1)} %get-tuple-element.13.keep_ref, bf16[512,512]{1,0:T(8,128)(2,1)S(1)} %collective-permute-done.20.got_ref, ...), custom_call_target="tpu_custom_call" | custom-call | flops 1342177280 | bytes 4194304 | tf_op jit(solution)/shard_map/pallas_call | solution.py:186
  101.6 1.6 %collective-permute-done.31.refs_6_ = bf16[256,512]{1,0:T(8,128)(2,1)S(1)} collective-permute-done((bf16[256,512]{1,0:T(8,128)(2,1)S(1)}, bf16[256,512]{1,0:T(8,128)(2,1)S(1)}, u32[]{:S(2)}, u32[]{:S(2)}) %collective-permute-start.31) | collective-permute-done | bytes 262176 | tf_op jit(solution)/shard_map/ppermute | solution.py:41
  103.2 2.2 %collective-permute-done.23.there_ref = bf16[256,256]{1,0:T(8,128)(2,1)S(1)} collective-permute-done((bf16[256,256]{1,0:T(8,128)(2,1)S(1)}, bf16[256,256]{1,0:T(8,128)(2,1)S(1)}, u32[]{:S(2)}, u32[]{:S(2)}) %collective-permute-start.23) | collective-permute-done | bytes 131104 | tf_op jit(solution)/shard_map/ppermute | solution.py:41
  105.4 1.3 %shard_map.93 = (f32[128,2048]{1,0:T(8,128)S(1)}, bf16[128,2048]{1,0:T(8,128)(2,1)S(1)}) custom-call(s32[4]{0:T(128)S(1)} %pad_add_fusion.index, bf16[256,256]{1,0:T(8,128)(2,1)S(1)} %get-tuple-element.36.own_ref, bf16[256,256]{1,0:T(8,128)(2,1)S(1)} %collective-permute-done.23.there_ref, bf16[256,512]{1,0:T(8,128)(2,1)S(1)} %pad_maximum_fusion.4.refs_0_, ...), custom_call_target="tpu_custom_call" | custom-call | flops 536870912 | bytes 4194304 | tf_op jit(solution)/shard_map/pallas_call | solution.py:186
  106.8 5.5 %collective-permute-start.33 = (bf16[128,2048]{1,0:T(8,128)(2,1)S(1)}, bf16[128,2048]{1,0:T(8,128)(2,1)S(1)}, u32[]{:S(2)}, u32[]{:S(2)}) collective-permute-start(bf16[128,2048]{1,0:T(8,128)(2,1)S(1)} %get-tuple-element.18), channel_id=1, source_target_pairs={{0,1},{1,0},{2,3},{3,2},{4,5},{5,4},{6,7},{7,6},{8,9},{9,8},{10,11... | collective-permute-start | bytes 1572872 | tf_op jit(solution)/shard_map/ppermute | solution.py:41
  112.2 1.5 %collective-permute-done.33 = bf16[128,2048]{1,0:T(8,128)(2,1)S(1)} collective-permute-done((bf16[128,2048]{1,0:T(8,128)(2,1)S(1)}, bf16[128,2048]{1,0:T(8,128)(2,1)S(1)}, u32[]{:S(2)}, u32[]{:S(2)}) %collective-permute-start.33) | collective-permute-done | bytes 524320 | tf_op jit(solution)/shard_map/ppermute | solution.py:41
  (105 shorter events, 15.1 us)
Async XLA Ops:
  2.9 7.8 %collective-permute-start.10 = (bf16[8,2048]{1,0:T(8,128)(2,1)S(1)}, bf16[8,2048]{1,0:T(8,128)(2,1)S(1)}, u32[]{:S(2)}, u32[]{:S(2)}) collective-permute-start(bf16[8,2048]{1,0:T(8,128)(2,1)S(1)} %multiply_convert_fusion), channel_id=1, source_target_pairs={{0,16},{1,17},{2,18},{3,19},{4,20},{5,21},{6,22},{7,23},{8,24},{9,... | collective-permute-start | bytes 98312 | tf_op jit(solution)/shard_map/ppermute | solution.py:41
  5.1 9.9 %collective-permute-start = (bf16[48,2048]{1,0:T(8,128)(2,1)S(1)}, bf16[48,2048]{1,0:T(8,128)(2,1)S(1)}, u32[]{:S(2)}, u32[]{:S(2)}) collective-permute-start(bf16[48,2048]{1,0:T(8,128)(2,1)S(1)} %bitcast.49), channel_id=1, source_target_pairs={{0,2},{1,15},{2,4},{3,1},{4,6},{5,3},{6,8},{7,5},{8,10},{9,7},{10,... | collective-permute-start | bytes 589832 | tf_op jit(solution)/shard_map/ppermute | solution.py:41
  10.7 7.1 %collective-permute-start.4 = (bf16[48,2048]{1,0:T(8,128)(2,1)S(1)}, bf16[48,2048]{1,0:T(8,128)(2,1)S(1)}, u32[]{:S(2)}, u32[]{:S(2)}) collective-permute-start(bf16[48,2048]{1,0:T(8,128)(2,1)S(1)} %bitcast.50), channel_id=1, source_target_pairs={{0,14},{1,3},{2,0},{3,5},{4,2},{5,7},{6,4},{7,9},{8,6},{9,11},{10,... | collective-permute-start | bytes 589832 | tf_op jit(solution)/shard_map/ppermute | solution.py:41
  12.1 7.6 %collective-permute-start.11 = (bf16[64,2048]{1,0:T(8,128)(2,1)S(1)}, bf16[64,2048]{1,0:T(8,128)(2,1)S(1)}, u32[]{:S(2)}, u32[]{:S(2)}) collective-permute-start(bf16[64,2048]{1,0:T(8,128)(2,1)S(1)} %pad_maximum_fusion.1.refs_12_), channel_id=1, source_target_pairs={{0,2},{1,15},{2,4},{3,1},{4,6},{5,3},{6,8},{7,5},{8,10},{9,7},{10,... | collective-permute-start | bytes 786440 | tf_op jit(solution)/shard_map/ppermute | solution.py:41
  15.0 11.7 %collective-permute-start.12 = (bf16[64,2048]{1,0:T(8,128)(2,1)S(1)}, bf16[64,2048]{1,0:T(8,128)(2,1)S(1)}, u32[]{:S(2)}, u32[]{:S(2)}) collective-permute-start(bf16[64,2048]{1,0:T(8,128)(2,1)S(1)} %pad_maximum_fusion.1.refs_12_), channel_id=1, source_target_pairs={{0,14},{1,3},{2,0},{3,5},{4,2},{5,7},{6,4},{7,9},{8,6},{9,11},{10,... | collective-permute-start | bytes 786440 | tf_op jit(solution)/shard_map/ppermute | solution.py:41
  15.0 28.5 %collective-permute-start.1 = (bf16[128,2048]{1,0:T(8,128)(2,1)S(1)}, bf16[128,2048]{1,0:T(8,128)(2,1)}, u32[]{:S(2)}, u32[]{:S(2)}) collective-permute-start(bf16[128,2048]{1,0:T(8,128)(2,1)S(1)} %get-tuple-element.12.refs_0_), channel_id=1, source_target_pairs={{0,16},{1,17},{2,18},{3,19},{4,20},{5,21},{6,22},{7,23},{8,24},{9,... | collective-permute-start | bytes 1572872 | tf_op jit(solution)/shard_map/ppermute | solution.py:41
  15.7 48.9 %collective-permute-start.2 = (bf16[128,2048]{1,0:T(8,128)(2,1)S(1)}, bf16[128,2048]{1,0:T(8,128)(2,1)}, u32[]{:S(2)}, u32[]{:S(2)}) collective-permute-start(bf16[128,2048]{1,0:T(8,128)(2,1)S(1)} %get-tuple-element.12.refs_0_), channel_id=1, source_target_pairs={{0,1},{1,0},{2,3},{3,2},{4,5},{5,4},{6,7},{7,6},{8,9},{9,8},{10,11... | collective-permute-start | bytes 1572872 | tf_op jit(solution)/shard_map/ppermute | solution.py:41
  17.8 5.4 %collective-permute-start.5 = (bf16[48,2048]{1,0:T(8,128)(2,1)S(1)}, bf16[48,2048]{1,0:T(8,128)(2,1)S(1)}, u32[]{:S(2)}, u32[]{:S(2)}) collective-permute-start(bf16[48,2048]{1,0:T(8,128)(2,1)S(1)} %collective-permute-done.refs_5_), channel_id=1, source_target_pairs={{0,2},{1,15},{2,4},{3,1},{4,6},{5,3},{6,8},{7,5},{8,10},{9,7},{10,... | collective-permute-start | bytes 589832 | tf_op jit(solution)/shard_map/ppermute | solution.py:41
  19.8 23.2 %collective-permute-start.6 = (bf16[48,2048]{1,0:T(8,128)(2,1)S(1)}, bf16[48,2048]{1,0:T(8,128)(2,1)S(1)}, u32[]{:S(2)}, u32[]{:S(2)}) collective-permute-start(bf16[48,2048]{1,0:T(8,128)(2,1)S(1)} %collective-permute-done.4.refs_6_), channel_id=1, source_target_pairs={{0,14},{1,3},{2,0},{3,5},{4,2},{5,7},{6,4},{7,9},{8,6},{9,11},{10,... | collective-permute-start | bytes 589832 | tf_op jit(solution)/shard_map/ppermute | solution.py:41
  23.2 7.3 %collective-permute-start.13 = (bf16[64,2048]{1,0:T(8,128)(2,1)S(1)}, bf16[64,2048]{1,0:T(8,128)(2,1)S(1)}, u32[]{:S(2)}, u32[]{:S(2)}) collective-permute-start(bf16[64,2048]{1,0:T(8,128)(2,1)S(1)} %collective-permute-done.11.refs_13_), channel_id=1, source_target_pairs={{0,2},{1,15},{2,4},{3,1},{4,6},{5,3},{6,8},{7,5},{8,10},{9,7},{10,... | collective-permute-start | bytes 786440 | tf_op jit(solution)/shard_map/ppermute | solution.py:41
  28.6 8.3 %collective-permute-start.14 = (bf16[64,2048]{1,0:T(8,128)(2,1)S(1)}, bf16[64,2048]{1,0:T(8,128)(2,1)S(1)}, u32[]{:S(2)}, u32[]{:S(2)}) collective-permute-start(bf16[64,2048]{1,0:T(8,128)(2,1)S(1)} %collective-permute-done.12.refs_14_), channel_id=1, source_target_pairs={{0,14},{1,3},{2,0},{3,5},{4,2},{5,7},{6,4},{7,9},{8,6},{9,11},{10,... | collective-permute-start | bytes 786440 | tf_op jit(solution)/shard_map/ppermute | solution.py:41
  30.5 19.8 %collective-permute-start.7 = (bf16[48,2048]{1,0:T(8,128)(2,1)S(1)}, bf16[48,2048]{1,0:T(8,128)(2,1)S(1)}, u32[]{:S(2)}, u32[]{:S(2)}) collective-permute-start(bf16[48,2048]{1,0:T(8,128)(2,1)S(1)} %collective-permute-done.5.refs_7_), channel_id=1, source_target_pairs={{0,2},{1,15},{2,4},{3,1},{4,6},{5,3},{6,8},{7,5},{8,10},{9,7},{10,... | collective-permute-start | bytes 589832 | tf_op jit(solution)/shard_map/ppermute | solution.py:41
  36.9 5.5 %collective-permute-start.15 = (bf16[64,2048]{1,0:T(8,128)(2,1)S(1)}, bf16[64,2048]{1,0:T(8,128)(2,1)S(1)}, u32[]{:S(2)}, u32[]{:S(2)}) collective-permute-start(bf16[64,2048]{1,0:T(8,128)(2,1)S(1)} %collective-permute-done.13.refs_15_), channel_id=1, source_target_pairs={{0,2},{1,15},{2,4},{3,1},{4,6},{5,3},{6,8},{7,5},{8,10},{9,7},{10,... | collective-permute-start | bytes 786440 | tf_op jit(solution)/shard_map/ppermute | solution.py:41
  42.4 7.3 %collective-permute-start.16 = (bf16[64,2048]{1,0:T(8,128)(2,1)S(1)}, bf16[64,2048]{1,0:T(8,128)(2,1)S(1)}, u32[]{:S(2)}, u32[]{:S(2)}) collective-permute-start(bf16[64,2048]{1,0:T(8,128)(2,1)S(1)} %collective-permute-done.14.refs_16_), channel_id=1, source_target_pairs={{0,14},{1,3},{2,0},{3,5},{4,2},{5,7},{6,4},{7,9},{8,6},{9,11},{10,... | collective-permute-start | bytes 786440 | tf_op jit(solution)/shard_map/ppermute | solution.py:41
  43.0 12.0 %collective-permute-start.25 = (bf16[128,512]{1,0:T(8,128)(2,1)S(1)}, bf16[128,512]{1,0:T(8,128)(2,1)S(1)}, u32[]{:S(2)}, u32[]{:S(2)}) collective-permute-start(bf16[128,512]{1,0:T(8,128)(2,1)S(1)} %pad_maximum_fusion.5), channel_id=1, source_target_pairs={{0,16},{1,17},{2,18},{3,19},{4,20},{5,21},{6,22},{7,23},{8,24},{9,... | collective-permute-start | bytes 393224 | tf_op jit(solution)/shard_map/ppermute | solution.py:41
  43.5 24.1 %collective-permute-start.3 = (bf16[128,2048]{1,0:T(8,128)(2,1)}, bf16[128,2048]{1,0:T(8,128)(2,1)S(1)}, u32[]{:S(2)}, u32[]{:S(2)}) collective-permute-start(bf16[128,2048]{1,0:T(8,128)(2,1)} %collective-permute-done.1.refs_1_), channel_id=1, source_target_pairs={{0,1},{1,0},{2,3},{3,2},{4,5},{5,4},{6,7},{7,6},{8,9},{9,8},{10,11... | collective-permute-start | bytes 1572872 | tf_op jit(solution)/shard_map/ppermute | solution.py:41
  49.7 8.0 %collective-permute-start.17 = (bf16[64,2048]{1,0:T(8,128)(2,1)S(1)}, bf16[64,2048]{1,0:T(8,128)(2,1)S(1)}, u32[]{:S(2)}, u32[]{:S(2)}) collective-permute-start(bf16[64,2048]{1,0:T(8,128)(2,1)S(1)} %collective-permute-done.15.refs_17_), channel_id=1, source_target_pairs={{0,2},{1,15},{2,4},{3,1},{4,6},{5,3},{6,8},{7,5},{8,10},{9,7},{10,... | collective-permute-start | bytes 786440 | tf_op jit(solution)/shard_map/ppermute | solution.py:41
  50.3 17.4 %collective-permute-start.18 = (bf16[112,2048]{1,0:T(8,128)(2,1)}, bf16[112,2048]{1,0:T(8,128)(2,1)S(1)}, u32[]{:S(2)}, u32[]{:S(2)}) collective-permute-start(bf16[112,2048]{1,0:T(8,128)(2,1)} %slice_dynamic-update-slice_fusion), channel_id=1, source_target_pairs={{0,1},{1,0},{2,3},{3,2},{4,5},{5,4},{6,7},{7,6},{8,9},{9,8},{10,11... | collective-permute-start | bytes 1376264 | tf_op jit(solution)/shard_map/ppermute | solution.py:41
  55.0 8.8 %collective-permute-start.8 = (bf16[48,2048]{1,0:T(8,128)(2,1)S(1)}, bf16[48,2048]{1,0:T(8,128)(2,1)S(1)}, u32[]{:S(2)}, u32[]{:S(2)}) collective-permute-start(bf16[48,2048]{1,0:T(8,128)(2,1)S(1)} %collective-permute-done.6.refs_8_), channel_id=1, source_target_pairs={{0,14},{1,3},{2,0},{3,5},{4,2},{5,7},{6,4},{7,9},{8,6},{9,11},{10,... | collective-permute-start | bytes 589832 | tf_op jit(solution)/shard_map/ppermute | solution.py:41
  57.7 10.0 %collective-permute-start.9 = (bf16[48,2048]{1,0:T(8,128)(2,1)S(1)}, bf16[48,2048]{1,0:T(8,128)(2,1)S(1)}, u32[]{:S(2)}, u32[]{:S(2)}) collective-permute-start(bf16[48,2048]{1,0:T(8,128)(2,1)S(1)} %collective-permute-done.7.refs_9_), channel_id=1, source_target_pairs={{0,2},{1,15},{2,4},{3,1},{4,6},{5,3},{6,8},{7,5},{8,10},{9,7},{10,... | collective-permute-start | bytes 589832 | tf_op jit(solution)/shard_map/ppermute | solution.py:41
  64.6 11.6 %collective-permute-start.26 = (bf16[256,512]{1,0:T(8,128)(2,1)S(1)}, bf16[256,512]{1,0:T(8,128)(2,1)S(1)}, u32[]{:S(2)}, u32[]{:S(2)}) collective-permute-start(bf16[256,512]{1,0:T(8,128)(2,1)S(1)} %pad_maximum_fusion.4.refs_0_), channel_id=1, source_target_pairs={{0,2},{1,15},{2,4},{3,1},{4,6},{5,3},{6,8},{7,5},{8,10},{9,7},{10,... | collective-permute-start | bytes 786440 | tf_op jit(solution)/shard_map/ppermute | solution.py:41
  72.5 14.5 %collective-permute-start.20 = (bf16[512,512]{1,0:T(8,128)(2,1)S(1)}, bf16[512,512]{1,0:T(8,128)(2,1)S(1)}, u32[]{:S(2)}, u32[]{:S(2)}) collective-permute-start(bf16[512,512]{1,0:T(8,128)(2,1)S(1)} %get-tuple-element.14), channel_id=1, source_target_pairs={{0,1},{1,0},{2,3},{3,2},{4,5},{5,4},{6,7},{7,6},{8,9},{9,8},{10,11... | collective-permute-start | bytes 1572872 | tf_op jit(solution)/shard_map/ppermute | solution.py:41
  76.2 8.1 %collective-permute-start.27 = (bf16[256,512]{1,0:T(8,128)(2,1)S(1)}, bf16[256,512]{1,0:T(8,128)(2,1)S(1)}, u32[]{:S(2)}, u32[]{:S(2)}) collective-permute-start(bf16[256,512]{1,0:T(8,128)(2,1)S(1)} %pad_maximum_fusion.4.refs_0_), channel_id=1, source_target_pairs={{0,14},{1,3},{2,0},{3,5},{4,2},{5,7},{6,4},{7,9},{8,6},{9,11},{10,... | collective-permute-start | bytes 786440 | tf_op jit(solution)/shard_map/ppermute | solution.py:41
  76.2 8.1 %collective-permute-start.28 = (bf16[256,512]{1,0:T(8,128)(2,1)S(1)}, bf16[256,512]{1,0:T(8,128)(2,1)S(1)}, u32[]{:S(2)}, u32[]{:S(2)}) collective-permute-start(bf16[256,512]{1,0:T(8,128)(2,1)S(1)} %collective-permute-done.26.refs_1_), channel_id=1, source_target_pairs={{0,2},{1,15},{2,4},{3,1},{4,6},{5,3},{6,8},{7,5},{8,10},{9,7},{10,... | collective-permute-start | bytes 786440 | tf_op jit(solution)/shard_map/ppermute | solution.py:41
  84.3 7.2 %collective-permute-start.29 = (bf16[256,512]{1,0:T(8,128)(2,1)S(1)}, bf16[256,512]{1,0:T(8,128)(2,1)S(1)}, u32[]{:S(2)}, u32[]{:S(2)}) collective-permute-start(bf16[256,512]{1,0:T(8,128)(2,1)S(1)} %collective-permute-done.27.refs_2_), channel_id=1, source_target_pairs={{0,14},{1,3},{2,0},{3,5},{4,2},{5,7},{6,4},{7,9},{8,6},{9,11},{10,... | collective-permute-start | bytes 786440 | tf_op jit(solution)/shard_map/ppermute | solution.py:41
  84.4 7.8 %collective-permute-start.30 = (bf16[256,512]{1,0:T(8,128)(2,1)S(1)}, bf16[256,512]{1,0:T(8,128)(2,1)S(1)}, u32[]{:S(2)}, u32[]{:S(2)}) collective-permute-start(bf16[256,512]{1,0:T(8,128)(2,1)S(1)} %collective-permute-done.28.refs_3_), channel_id=1, source_target_pairs={{0,2},{1,15},{2,4},{3,1},{4,6},{5,3},{6,8},{7,5},{8,10},{9,7},{10,... | collective-permute-start | bytes 786440 | tf_op jit(solution)/shard_map/ppermute | solution.py:41
  87.8 9.8 %collective-permute-start.21 = (bf16[256,512]{1,0:T(8,128)(2,1)}, bf16[256,512]{1,0:T(8,128)(2,1)S(1)}, u32[]{:S(2)}, u32[]{:S(2)}) collective-permute-start(bf16[256,512]{1,0:T(8,128)(2,1)} %pad_maximum_fusion.2), channel_id=1, source_target_pairs={{0,2},{1,3},{2,4},{3,5},{4,6},{5,7},{6,8},{7,9},{8,10},{9,11},{10,... | collective-permute-start | bytes 786440 | tf_op jit(solution)/shard_map/ppermute | solution.py:41
  88.5 9.1 %collective-permute-start.22 = (bf16[256,512]{1,0:T(8,128)(2,1)}, bf16[256,512]{1,0:T(8,128)(2,1)S(1)}, u32[]{:S(2)}, u32[]{:S(2)}) collective-permute-start(bf16[256,512]{1,0:T(8,128)(2,1)} %pad_maximum_fusion.3), channel_id=1, source_target_pairs={{0,14},{1,15},{2,0},{3,1},{4,2},{5,3},{6,4},{7,5},{8,6},{9,7},{10,... | collective-permute-start | bytes 786440 | tf_op jit(solution)/shard_map/ppermute | solution.py:41
  91.5 11.7 %collective-permute-start.31 = (bf16[256,512]{1,0:T(8,128)(2,1)S(1)}, bf16[256,512]{1,0:T(8,128)(2,1)S(1)}, u32[]{:S(2)}, u32[]{:S(2)}) collective-permute-start(bf16[256,512]{1,0:T(8,128)(2,1)S(1)} %collective-permute-done.29.refs_4_), channel_id=1, source_target_pairs={{0,14},{1,3},{2,0},{3,5},{4,2},{5,7},{6,4},{7,9},{8,6},{9,11},{10,... | collective-permute-start | bytes 786440 | tf_op jit(solution)/shard_map/ppermute | solution.py:41
  92.2 11.0 %collective-permute-start.32 = (bf16[256,512]{1,0:T(8,128)(2,1)S(1)}, bf16[256,512]{1,0:T(8,128)(2,1)S(1)}, u32[]{:S(2)}, u32[]{:S(2)}) collective-permute-start(bf16[256,512]{1,0:T(8,128)(2,1)S(1)} %collective-permute-done.30.refs_5_), channel_id=1, source_target_pairs={{0,2},{1,15},{2,4},{3,1},{4,6},{5,3},{6,8},{7,5},{8,10},{9,7},{10,... | collective-permute-start | bytes 786440 | tf_op jit(solution)/shard_map/ppermute | solution.py:41
  101.5 3.9 %collective-permute-start.23 = (bf16[256,256]{1,0:T(8,128)(2,1)S(1)}, bf16[256,256]{1,0:T(8,128)(2,1)S(1)}, u32[]{:S(2)}, u32[]{:S(2)}) collective-permute-start(bf16[256,256]{1,0:T(8,128)(2,1)S(1)} %get-tuple-element.35), channel_id=1, source_target_pairs={{0,16},{1,17},{2,18},{3,19},{4,20},{5,21},{6,22},{7,23},{8,24},{9,... | collective-permute-start | bytes 393224 | tf_op jit(solution)/shard_map/ppermute | solution.py:41
  106.8 7.0 %collective-permute-start.33 = (bf16[128,2048]{1,0:T(8,128)(2,1)S(1)}, bf16[128,2048]{1,0:T(8,128)(2,1)S(1)}, u32[]{:S(2)}, u32[]{:S(2)}) collective-permute-start(bf16[128,2048]{1,0:T(8,128)(2,1)S(1)} %get-tuple-element.18), channel_id=1, source_target_pairs={{0,1},{1,0},{2,3},{3,2},{4,5},{5,4},{6,7},{7,6},{8,9},{9,8},{10,11... | collective-permute-start | bytes 1572872 | tf_op jit(solution)/shard_map/ppermute | solution.py:41
  (13 other events, 55.2 us)
where the time goes:
time: 115 us
  starting transfers between devices  62.8 us (55%)
  waiting for transfers between devices  30.1 us (26%)
  Pallas kernels  9.24 us (8%)
  other arithmetic  6.32 us (5%)
  local copies, waits for them, and re-layouts  5.2 us (5%)
    ppermute x34, starting transfers between devices, send(): return lax.ppermute(value, 'seq', route)  62.8 us
    ppermute x34, waiting for transfers between devices, send(): return lax.ppermute(value, 'seq', route)  30.1 us
    pallas_call x3, Pallas kernels, on_chip(): pl.pallas_call(kernel, out_shape=out_shape, in_specs=[pl.BlockSpec(memory...  9.24 us
    unnamed x27, local copies, waits for them, and re-layouts  3.99 us
  transfers between devices with their start and end apart: 34, of which 13 were waited for; matrix products, arithmetic and copies ran while one was open for 7% of the time, Pallas kernels for 7%

commit v1 on v0

--- a/solution.py
+++ b/solution.py
@@ -66,43 +66,49 @@
 
 def project_kernel(index, *refs):
     blocks, firsts, seconds = refs[:4], refs[4 : 4 + SHARDS], refs[4 + SHARDS : 4 + 2 * SHARDS]
-    g_most, g_last, keep_ref, send_ref, rows, g_rows, table = refs[4 + 2 * SHARDS :]
+    keep_ref, send_ref, g_rows, far_table, rows, table = refs[4 + 2 * SHARDS :]
     z, core, x = index[0], index[1], index[2]
     low_core = core == 0
     for ref, bx, bc in zip(blocks, (x, 1 - x, x, 1 - x), (core, core, 1 - core, 1 - core)):
         rows[pl.ds(pl.multiple_of((bx * 2 + bc) * TOK, TOK), TOK), :] = ref[...]
-    g_own = pl.multiple_of(core * G_ROWS, G_ROWS)
-    g_other = pl.multiple_of((1 - core) * G_ROWS, G_ROWS)
     for j, (way, hops) in enumerate(STEPS):
         at = z_of(z, core, way, hops) * HALF
         for kind in range(3):
-            here = pl.multiple_of(kind * 256 + at, 16)
-            table[pl.ds(here, 16), :] = firsts[j][kind * 16 : kind * 16 + 16, :]
-            there = pl.multiple_of(kind * 256 + at + 16, 16)
-            table[pl.ds(there, 16), :] = seconds[j][kind * 16 : kind * 16 + 16, :]
-        g_rows[pl.ds(g_own + j * 16, 16), :] = seconds[j][48:64, :]
-    g_rows[pl.ds(g_other, 112), :] = g_most[...]
-    g_rows[pl.ds(g_other + 112, 16), :] = g_last[...]
+            into = table if kind == 0 else far_table
+            base = 0 if kind == 0 else kind * 256 - 256
+            here = pl.multiple_of(base + at, 16)
+            into[pl.ds(here, 16), :] = firsts[j][kind * 16 : kind * 16 + 16, :]
+            there = pl.multiple_of(base + at + 16, 16)
+            into[pl.ds(there, 16), :] = seconds[j][kind * 16 : kind * 16 + 16, :]
+        g_rows[j * 16 : j * 16 + 16, :] = seconds[j][48:64, :]
     for kind in range(3):
-        out = dot_nt(rows[...], table[kind * 256 : kind * 256 + 256, :]).astype(jnp.bfloat16)
+        columns = table[...] if kind == 0 else far_table[kind * 256 - 256 : kind * 256, :]
+        out = dot_nt(rows[...], columns).astype(jnp.bfloat16)
         lanes = slice(kind * 128, kind * 128 + 128)
         keep_ref[:, lanes] = jnp.where(low_core, out[:, :128], out[:, 128:])
         send_ref[:, lanes] = jnp.where(low_core, out[:, 128:], out[:, :128])
-    for kind in (1, 2):
-        out = dot_nt(g_rows[...], table[kind * 256 : kind * 256 + 256, :]).astype(jnp.bfloat16)
-        at = slice((kind - 1) * 256, kind * 256)
-        keep_ref[at, 384:] = jnp.where(low_core, out[:, :128], out[:, 128:])
-        send_ref[at, 384:] = jnp.where(low_core, out[:, 128:], out[:, :128])
-
-
-def attention_kernel(index, far_pos, keep_ref, got_ref, below_ref, above_ref, out_ref):
+
+
+def far_kernel(index, own_ref, other_ref, table, keep_ref, send_ref):
+    low_core = index[1] == 0
+    for source in range(2):
+        rows = jnp.where(index[1] == source, own_ref[...], other_ref[...])
+        at = slice(source * G_ROWS, source * G_ROWS + G_ROWS)
+        for kind in range(2):
+            out = dot_nt(rows, table[kind * 256 : kind * 256 + 256, :]).astype(jnp.bfloat16)
+            lanes = slice(kind * 128, kind * 128 + 128)
+            keep_ref[at, lanes] = jnp.where(low_core, out[:, :128], out[:, 128:])
+            send_ref[at, lanes] = jnp.where(low_core, out[:, 128:], out[:, :128])
+
+
+def attention_kernel(index, far_pos, keep_ref, got_ref, g_keep, g_got, below_ref, above_ref, out_ref):
     z, x, limit = index[0], index[2], index[3]
     lane_head = (lax.broadcasted_iota(jnp.int32, (TOK, WIDE), 1) % 128) // HALF
     row = lax.broadcasted_iota(jnp.int32, (HEADS_LOCAL * TOK, TOK), 0) % TOK
     col = lax.broadcasted_iota(jnp.int32, (HEADS_LOCAL * TOK, TOK), 1)
     far_ok = far_pos[...] < limit
-    far_keys = jnp.concatenate([keep_ref[:256, 384:], got_ref[:256, 384:]], axis=1)
-    far_values = jnp.concatenate([keep_ref[256:, 384:], got_ref[256:, 384:]], axis=1)
+    far_keys = jnp.concatenate([g_keep[:, :128], g_got[:, :128]], axis=1)
+    far_values = jnp.concatenate([g_keep[:, 128:], g_got[:, 128:]], axis=1)
 
     def local(kind, at):
         lanes = slice(kind * 128, kind * 128 + 128)
@@ -165,20 +171,18 @@
             out_ref[mine, part * TOK : (part + 1) * TOK, :] = context.astype(jnp.bfloat16)
 
 
-def output_kernel(index, own_ref, there_ref, *refs):
-    blocks, keep_ref, send_ref = refs[:SHARDS], refs[SHARDS], refs[SHARDS + 1]
-    z, core, x = index[0], index[1], index[2]
+def output_kernel(index, own_ref, there_ref, weights, keep_ref, send_ref):
+    core, x = index[1], index[2]
     own, there = own_ref[...], there_ref[...]
     full = jnp.concatenate([jnp.where(x == 0, own, there), jnp.where(x == 0, there, own)], axis=1)
-    for j, (way, hops) in enumerate(STEPS):
-        zj = z_of(z, core, way, hops)
-        out = dot_nt(full, blocks[j][...])
+    for zj in range(Z):
+        out = dot_nt(full, weights[zj * 256 : zj * 256 + 256, :])
         keep = jnp.where(core == 0, out[:TOK], out[TOK:])
         sent = jnp.where(core == 0, out[TOK:], out[:TOK]).astype(jnp.bfloat16)
         for side in range(X):
-            lanes = pl.ds(pl.multiple_of((side * Z + zj) * 128, 128), 128)
-            keep_ref[:, lanes] = keep[:, side * 128 : side * 128 + 128]
-            send_ref[:, lanes] = sent[:, side * 128 : side * 128 + 128]
+            at = (side * Z + zj) * 128
+            keep_ref[:, at : at + 128] = keep[:, side * 128 : side * 128 + 128]
+            send_ref[:, at : at + 128] = sent[:, side * 128 : side * 128 + 128]
 
 
 def on_chip(kernel, out_shape, flops, exps, args, scratch=()):
@@ -230,9 +234,14 @@
     one, two = {(0, 0): first}, {(0, 0): second}
     a_one, a_two, b_one, b_two = first, second, first, second
     for step in range(1, 5):
+        if step > 1:
+            before = (two[0, step - 2], two[1, step - 2]) if step > 2 else ()
+            a_one, b_one = lax.optimization_barrier((a_one, b_one, *before))[:2]
         one[0, step] = a_one = send(a_one, AHEAD)
         if step < 4:
             one[1, step] = b_one = send(b_one, BEHIND)
+        if step > 1:
+            a_two, b_two = lax.optimization_barrier((a_two, b_two, one[0, step - 1], one[1, step - 1]))[:2]
         two[0, step] = a_two = send(a_two, AHEAD)
         if step < 4:
             two[1, step] = b_two = send(b_two, BEHIND)
@@ -244,26 +253,35 @@
     beside = send(to_send, OTHER_CORE)
     beside_across = send(across, OTHER_CORE)
 
-    g_most = send(jnp.concatenate([s[48:] for s in seconds[:-1]], axis=0), OTHER_CORE)
-    g_last = send(seconds[-1][48:], OTHER_CORE)
-
-    half = jax.ShapeDtypeStruct((ROWS, 4 * 128), bf16)
-    keep, to_swap = on_chip(
+    half = jax.ShapeDtypeStruct((ROWS, 3 * 128), bf16)
+    keep, to_swap, g_own, far_table = on_chip(
         project_kernel,
-        (half, half),
-        2 * 768 * 768 * width,
+        (
+            half,
+            half,
+            jax.ShapeDtypeStruct((G_ROWS, width), bf16),
+            jax.ShapeDtypeStruct((2 * Z * HALF, width), bf16),
+        ),
+        2 * ROWS * 768 * width,
         0,
-        (index, normed, across, beside, beside_across, *firsts, *seconds, g_most, g_last),
-        (pltpu.VMEM((ROWS, width), bf16), pltpu.VMEM((2 * G_ROWS, width), bf16), pltpu.VMEM((768, width), bf16)),
+        (index, normed, across, beside, beside_across, *firsts, *seconds),
+        (pltpu.VMEM((ROWS, width), bf16), pltpu.VMEM((Z * HALF, width), bf16)),
     )
     got = send(to_swap, OTHER_CORE)
+    g_other = send(g_own, OTHER_CORE)
 
     def edge(part):
-        tables = [t.reshape(2, 2, TOK, 512)[:, part, :, 128:384].reshape(2 * TOK, 256) for t in (keep, got)]
+        tables = [t.reshape(2, 2, TOK, 384)[:, part, :, 128:384].reshape(2 * TOK, 256) for t in (keep, got)]
         return jnp.concatenate(tables, axis=1)
 
     below = send(edge(1), UP)
     above = send(edge(0), DOWN)
+
+    far_half = jax.ShapeDtypeStruct((2 * G_ROWS, 256), bf16)
+    g_keep, g_swap = on_chip(
+        far_kernel, (far_half, far_half), 2 * 256 * 512 * width, 0, (index, g_own, g_other, far_table)
+    )
+    g_got = send(g_swap, OTHER_CORE)
 
     deltas = jnp.asarray([-h if w == 0 else h for w, h in STEPS], jnp.int32)
     g_core = jnp.arange(C, dtype=jnp.int32)[:, None, None, None]
@@ -276,10 +294,10 @@
         jax.ShapeDtypeStruct((2, 2 * TOK, WIDE), bf16),
         4 * 4 * TOK * 640 * WIDE * 4,
         4 * 4 * TOK * 640,
-        (index, far_pos, keep, got, below, above),
-    )
-
-    out_t = after(w_out, one[0, 2]).T.reshape(64, X, 2, HEADS_LOCAL, 2, HALF)
+        (index, far_pos, keep, got, g_keep, g_got, below, above),
+    )
+
+    out_t = after(w_out, one[0, 1]).T.reshape(64, X, 2, HEADS_LOCAL, 2, HALF)
     out_t = jnp.transpose(out_t, (0, 2, 1, 4, 3, 5))
     group_0 = out_t[:, 0].reshape(64, 2 * WIDE)
     group_1 = out_t[:, 1, :, ::-1].reshape(64, 2 * WIDE)
@@ -288,12 +306,8 @@
     chip = jnp.concatenate([jnp.where(core == 0, kept, passed), jnp.where(core == 0, passed, kept)], axis=0)
     chip_there = send(chip, OTHER_X)
     both = jnp.concatenate([jnp.where(x == 0, chip, chip_there), jnp.where(x == 0, chip_there, chip)], axis=0)
-    out_blocks = {(0, 0): both}
-    ahead = behind = after(both, two[0, 4], two[1, 3])
-    for step in range(1, 5):
-        out_blocks[0, step] = ahead = send(ahead, AHEAD)
-        if step < 4:
-            out_blocks[1, step] = behind = send(behind, BEHIND)
+    columns = [[place(i, k, c) for k in range(Z)] for i in range(X) for c in range(C)]
+    out_weights = lax.all_gather(both, "seq", axis_index_groups=columns, axis=0, tiled=True)
 
     there = send(context[1], OTHER_X)
     kept_part, sent_part = on_chip(
@@ -301,7 +315,7 @@
         (jax.ShapeDtypeStruct((TOK, width), jnp.float32), jax.ShapeDtypeStruct((TOK, width), bf16)),
         2 * 256 * 512 * width,
         0,
-        (index, context[0], there, *[out_blocks[s] for s in STEPS]),
+        (index, context[0], there, out_weights),
     )
     return (kept_part + send(sent_part, OTHER_CORE).astype(jnp.float32)).astype(bf16)
 

time: 115 us -> 127 us (1.10)
  starting transfers between devices: 62.8 us -> 35.6 us
  waiting for transfers between devices: 30.1 us -> 52.4 us
  between operations: 1.05 us -> 14.3 us
  Pallas kernels: 9.24 us -> 11.6 us
  local copies, waits for them, and re-layouts: 5.2 us -> 7.13 us
    ppermute x34 -> x27, starting transfers between devices: 62.8 us -> 35.6 us  [send(): return lax.ppermute(value, 'seq', route)]
    ppermute x34 -> x27, waiting for transfers between devices: 30.1 us -> 52.4 us  [send(): return lax.ppermute(value, 'seq', route)]
    unnamed x27 -> x30, local copies, waits for them, and re-layouts: 3.99 us -> 6.55 us
    pallas_call x3 -> x4, Pallas kernels: 9.24 us -> 11.6 us  [on_chip(): pl.pallas_call(kernel, out_shape=out_shape, in_specs=[pl.BlockSpec(memory...]
    concatenate x2, other arithmetic: 1.45 us -> 0.04 us  [edge(): return jnp.concatenate(tables, axis=1)]
    unnamed x2 -> x0, other arithmetic: 1.38 us -> none
  transfers between devices with their start and end apart: 34 -> 28, of which waited for: 13 -> 14; matrix products, arithmetic and copies ran while one was open for 7% -> 3% of each run, Pallas kernels for 7% -> 8%
where the time goes in v1:
time: 127 us; the launch traced here: 126 us
  waiting for transfers between devices  52.4 us (41%)
  starting transfers between devices  35.6 us (28%)
  between operations  14.3 us (11%)
  Pallas kernels  11.6 us (9%)
  local copies, waits for them, and re-layouts  7.13 us (6%)
  other arithmetic  5.41 us (4%)
    ppermute x27, waiting for transfers between devices, send(): return lax.ppermute(value, 'seq', route)  52.4 us
    ppermute x27, starting transfers between devices, send(): return lax.ppermute(value, 'seq', route)  35.6 us
    pallas_call x4, Pallas kernels, on_chip(): pl.pallas_call(kernel, out_shape=out_shape, in_specs=[pl.BlockSpec(memory...  11.6 us
    unnamed x30, local copies, waits for them, and re-layouts  6.55 us
  transfers between devices with their start and end apart: 28, of which 14 were waited for; matrix products, arithmetic and copies ran while one was open for 3% of the time, Pallas kernels for 8%

profile of v1, /device:TPU:1, one launch (start us, length us, event | category | flops | bytes accessed | tf_op | source)
XLA Modules:
  0.0 126.5 jit_solution(12936093482472473363)
XLA Ops:
  7.7 6.5 %collective-permute-start = (bf16[48,2048]{1,0:T(8,128)(2,1)S(1)}, bf16[48,2048]{1,0:T(8,128)(2,1)S(1)}, u32[]{:S(2)}, u32[]{:S(2)}) collective-permute-start(bf16[48,2048]{1,0:T(8,128)(2,1)S(1)} %bitcast.49), channel_id=1, source_target_pairs={{0,2},{1,15},{2,4},{3,1},{4,6},{5,3},{6,8},{7,5},{8,10},{9,7},{10,... | collective-permute-start | bytes 589832 | tf_op jit(solution)/shard_map/ppermute | solution.py:41
  14.9 1.2 fusion
  18.1 1.5 %collective-permute-start.24 = (bf16[64,512]{1,0:T(8,128)(2,1)S(1)}, bf16[64,512]{1,0:T(8,128)(2,1)S(1)}, u32[]{:S(2)}, u32[]{:S(2)}) collective-permute-start(bf16[64,512]{1,0:T(8,128)(2,1)S(1)} %copy.28), channel_id=1, source_target_pairs={{0,1},{1,0},{2,3},{3,2},{4,5},{5,4},{6,7},{7,6},{8,9},{9,8},{10,11... | collective-permute-start | bytes 196616 | tf_op jit(solution)/shard_map/ppermute | solution.py:41
  20.5 1.3 %collective-permute-start.25 = (bf16[128,512]{1,0:T(8,128)(2,1)S(1)}, bf16[128,512]{1,0:T(8,128)(2,1)S(1)}, u32[]{:S(2)}, u32[]{:S(2)}) collective-permute-start(bf16[128,512]{1,0:T(8,128)(2,1)S(1)} %pad_maximum_fusion.5), channel_id=1, source_target_pairs={{0,16},{1,17},{2,18},{3,19},{4,20},{5,21},{6,22},{7,23},{8,24},{9,... | collective-permute-start | bytes 393224 | tf_op jit(solution)/shard_map/ppermute | solution.py:41
  22.2 3.1 %collective-permute-done.25 = bf16[128,512]{1,0:T(8,128)(2,1)S(1)} collective-permute-done((bf16[128,512]{1,0:T(8,128)(2,1)S(1)}, bf16[128,512]{1,0:T(8,128)(2,1)S(1)}, u32[]{:S(2)}, u32[]{:S(2)}) %collective-permute-start.25) | collective-permute-done | bytes 131104 | tf_op jit(solution)/shard_map/ppermute | solution.py:41
  26.2 3.3 %collective-permute-start.8 = (bf16[64,2048]{1,0:T(8,128)(2,1)S(1)}, bf16[64,2048]{1,0:T(8,128)(2,1)S(1)}, u32[]{:S(2)}, u32[]{:S(2)}) collective-permute-start(bf16[64,2048]{1,0:T(8,128)(2,1)S(1)} %pad_maximum_fusion.1.refs_12_), channel_id=1, source_target_pairs={{0,2},{1,15},{2,4},{3,1},{4,6},{5,3},{6,8},{7,5},{8,10},{9,7},{10,... | collective-permute-start | bytes 786440 | tf_op jit(solution)/shard_map/ppermute | solution.py:41
  29.5 1.2 collective-permute-start.1
  30.7 2.7 %collective-permute-start.5 = (bf16[48,2048]{1,0:T(8,128)(2,1)S(1)}, bf16[48,2048]{1,0:T(8,128)(2,1)}, u32[]{:S(2)}, u32[]{:S(2)}) collective-permute-start(bf16[48,2048]{1,0:T(8,128)(2,1)S(1)} %collective-permute-done.refs_5_), channel_id=1, source_target_pairs={{0,2},{1,15},{2,4},{3,1},{4,6},{5,3},{6,8},{7,5},{8,10},{9,7},{10,... | collective-permute-start | bytes 589832 | tf_op jit(solution)/shard_map/ppermute | solution.py:41
  34.1 4.8 %collective-permute-done.9.refs_14_ = bf16[64,2048]{1,0:T(8,128)(2,1)S(1)} collective-permute-done((bf16[64,2048]{1,0:T(8,128)(2,1)S(1)}, bf16[64,2048]{1,0:T(8,128)(2,1)S(1)}, u32[]{:S(2)}, u32[]{:S(2)}) %collective-permute-start.9) | collective-permute-done | bytes 262176 | tf_op jit(solution)/shard_map/ppermute | solution.py:41
  38.9 1.5 %collective-permute-start.13 = (bf16[64,2048]{1,0:T(8,128)(2,1)S(1)}, bf16[64,2048]{1,0:T(8,128)(2,1)S(1)}, u32[]{:S(2)}, u32[]{:S(2)}) collective-permute-start(bf16[64,2048]{1,0:T(8,128)(2,1)S(1)} %collective-permute-done.9.refs_14_), channel_id=1, source_target_pairs={{0,14},{1,3},{2,0},{3,5},{4,2},{5,7},{6,4},{7,9},{8,6},{9,11},{10,... | collective-permute-start | bytes 786440 | tf_op jit(solution)/shard_map/ppermute | solution.py:41
  40.4 1.7 %collective-permute-done.6.refs_8_ = bf16[48,2048]{1,0:T(8,128)(2,1)} collective-permute-done((bf16[48,2048]{1,0:T(8,128)(2,1)S(1)}, bf16[48,2048]{1,0:T(8,128)(2,1)}, u32[]{:S(2)}, u32[]{:S(2)}) %collective-permute-start.6) | collective-permute-done | bytes 196640 | tf_op jit(solution)/shard_map/ppermute | solution.py:41
  42.1 10.2 %collective-permute-done.12.refs_15_ = bf16[64,2048]{1,0:T(8,128)(2,1)S(1)} collective-permute-done((bf16[64,2048]{1,0:T(8,128)(2,1)S(1)}, bf16[64,2048]{1,0:T(8,128)(2,1)S(1)}, u32[]{:S(2)}, u32[]{:S(2)}) %collective-permute-start.12) | collective-permute-done | bytes 262176 | tf_op jit(solution)/shard_map/ppermute | solution.py:41
  52.4 1.3 collective-permute-done.13.refs_16_
  53.6 1.5 %collective-permute-start.16 = (bf16[64,2048]{1,0:T(8,128)(2,1)S(1)}, bf16[64,2048]{1,0:T(8,128)(2,1)S(1)}, u32[]{:S(2)}, u32[]{:S(2)}) collective-permute-start(bf16[64,2048]{1,0:T(8,128)(2,1)S(1)} %collective-permute-done.13.refs_16_), channel_id=1, source_target_pairs={{0,14},{1,3},{2,0},{3,5},{4,2},{5,7},{6,4},{7,9},{8,6},{9,11},{10,... | collective-permute-start | bytes 786440 | tf_op jit(solution)/shard_map/ppermute | solution.py:41
  55.1 2.7 %collective-permute-start.2 = (bf16[128,2048]{1,0:T(8,128)(2,1)S(1)}, bf16[128,2048]{1,0:T(8,128)(2,1)S(1)}, u32[]{:S(2)}, u32[]{:S(2)}) collective-permute-start(bf16[128,2048]{1,0:T(8,128)(2,1)S(1)} %get-tuple-element.25.refs_0_), channel_id=1, source_target_pairs={{0,1},{1,0},{2,3},{3,2},{4,5},{5,4},{6,7},{7,6},{8,9},{9,8},{10,11... | collective-permute-start | bytes 1572872 | tf_op jit(solution)/shard_map/ppermute | solution.py:41
  57.8 1.7 %collective-permute-done.10.refs_9_ = bf16[48,2048]{1,0:T(8,128)(2,1)S(1)} collective-permute-done((bf16[48,2048]{1,0:T(8,128)(2,1)}, bf16[48,2048]{1,0:T(8,128)(2,1)S(1)}, u32[]{:S(2)}, u32[]{:S(2)}) %collective-permute-start.10) | collective-permute-done | bytes 196640 | tf_op jit(solution)/shard_map/ppermute | solution.py:41
  59.5 2.8 %collective-permute-start.3 = (bf16[128,2048]{1,0:T(8,128)(2,1)S(1)}, bf16[128,2048]{1,0:T(8,128)(2,1)S(1)}, u32[]{:S(2)}, u32[]{:S(2)}) collective-permute-start(bf16[128,2048]{1,0:T(8,128)(2,1)S(1)} %collective-permute-done.1.refs_1_), channel_id=1, source_target_pairs={{0,1},{1,0},{2,3},{3,2},{4,5},{5,4},{6,7},{7,6},{8,9},{9,8},{10,11... | collective-permute-start | bytes 1572872 | tf_op jit(solution)/shard_map/ppermute | solution.py:41
  62.3 13.3 %collective-permute-done.11.refs_10_ = bf16[48,2048]{1,0:T(8,128)(2,1)S(1)} collective-permute-done((bf16[48,2048]{1,0:T(8,128)(2,1)}, bf16[48,2048]{1,0:T(8,128)(2,1)S(1)}, u32[]{:S(2)}, u32[]{:S(2)}) %collective-permute-start.11) | collective-permute-done | bytes 196640 | tf_op jit(solution)/shard_map/ppermute | solution.py:41
  76.5 6.7 %collective-permute-done.14.refs_11_ = bf16[48,2048]{1,0:T(8,128)(2,1)S(1)} collective-permute-done((bf16[48,2048]{1,0:T(8,128)(2,1)S(1)}, bf16[48,2048]{1,0:T(8,128)(2,1)S(1)}, u32[]{:S(2)}, u32[]{:S(2)}) %collective-permute-start.14) | collective-permute-done | bytes 196640 | tf_op jit(solution)/shard_map/ppermute | solution.py:41
  86.8 4.3 %shard_map.91 = (bf16[512,384]{1,0:T(8,128)(2,1)S(1)}, bf16[512,384]{1,0:T(8,128)(2,1)S(1)}, bf16[128,2048]{1,0:T(8,128)(2,1)S(1)}, bf16[512,2048]{1,0:T(8,128)(2,1)}) custom-call(s32[4]{0:T(128)S(1)} %pad_add_fusion.index, bf16[128,2048]{1,0:T(8,128)(2,1)S(1)} %get-tuple-element.25.refs_0_, bf16[128,2048]{1,0:T(8,128)(2,1)S(1)} %collective-permute-done.1.refs_1_, ...), custom_call_target="tpu_custom_call" | custom-call | flops 1610612736 | bytes 4194304 | tf_op jit(solution)/shard_map/pallas_call | solution.py:190
  91.2 2.6 %collective-permute-start.18 = (bf16[512,384]{1,0:T(8,128)(2,1)S(1)}, bf16[512,384]{1,0:T(8,128)(2,1)S(1)}, u32[]{:S(2)}, u32[]{:S(2)}) collective-permute-start(bf16[512,384]{1,0:T(8,128)(2,1)S(1)} %get-tuple-element.37), channel_id=1, source_target_pairs={{0,1},{1,0},{2,3},{3,2},{4,5},{5,4},{6,7},{7,6},{8,9},{9,8},{10,11... | collective-permute-start | bytes 1179656 | tf_op jit(solution)/shard_map/ppermute | solution.py:41
  95.3 2.7 %collective-permute-start.22 = (bf16[256,512]{1,0:T(8,128)(2,1)S(1)}, bf16[256,512]{1,0:T(8,128)(2,1)S(1)}, u32[]{:S(2)}, u32[]{:S(2)}) collective-permute-start(bf16[256,512]{1,0:T(8,128)(2,1)S(1)} %pad_maximum_fusion.3), channel_id=1, source_target_pairs={{0,14},{1,15},{2,0},{3,1},{4,2},{5,3},{6,4},{7,5},{8,6},{9,7},{10,... | collective-permute-start | bytes 786440 | tf_op jit(solution)/shard_map/ppermute | solution.py:41
  98.0 2.1 %shard_map.92 = (bf16[256,256]{1,0:T(8,128)(2,1)S(1)}, bf16[256,256]{1,0:T(8,128)(2,1)S(1)}) custom-call(s32[4]{0:T(128)S(1)} %pad_add_fusion.index, bf16[128,2048]{1,0:T(8,128)(2,1)S(1)} %get-tuple-element.38.own_ref, bf16[128,2048]{1,0:T(8,128)(2,1)S(1)} %collective-permute-done.19.other_ref, bf16[512,2048]{1,0:T(8,128)(2,1)S(1)} %copy-done.1), custom_call_target="tpu_custom_call" | custom-call | flops 536870912 | bytes 4194304 | tf_op jit(solution)/shard_map/pallas_call | solution.py:190
  100.1 1.2 collective-permute-start.20
  101.5 2.5 %collective-permute-done.21.below_ref = bf16[256,512]{1,0:T(8,128)(2,1)S(1)} collective-permute-done((bf16[256,512]{1,0:T(8,128)(2,1)S(1)}, bf16[256,512]{1,0:T(8,128)(2,1)S(1)}, u32[]{:S(2)}, u32[]{:S(2)}) %collective-permute-start.21) | collective-permute-done | bytes 262176 | tf_op jit(solution)/shard_map/ppermute | solution.py:41
  104.0 3.9 %shard_map.93 = bf16[2,256,256]{2,1,0:T(8,128)(2,1)S(1)} custom-call(s32[4]{0:T(128)S(1)} %pad_add_fusion.index, s32[1,256]{1,0:T(1,128)S(1)} %add.107.far_pos, bf16[512,384]{1,0:T(8,128)(2,1)S(1)} %get-tuple-element.36.keep_ref, bf16[512,384]{1,0:T(8,128)(2,1)S(1)} %collective-permute-done.18.got_ref, bf16[256,256]{1,0:T(8,128)(2,1)S(1)} %get-tuple-element.40.g_keep, ...), custom_call_target="tpu_custom_call" | custom-call | flops 1342177280 | bytes 4194304 | tf_op jit(solution)/shard_map/pallas_call | solution.py:190
  108.0 1.3 %collective-permute-start.23 = (bf16[256,256]{1,0:T(8,128)(2,1)S(1)}, bf16[256,256]{1,0:T(8,128)(2,1)S(1)}, u32[]{:S(2)}, u32[]{:S(2)}) collective-permute-start(bf16[256,256]{1,0:T(8,128)(2,1)S(1)} %get-tuple-element.57), channel_id=1, source_target_pairs={{0,16},{1,17},{2,18},{3,19},{4,20},{5,21},{6,22},{7,23},{8,24},{9,... | collective-permute-start | bytes 393224 | tf_op jit(solution)/shard_map/ppermute | solution.py:41
  109.2 2.6 %collective-permute-done.23.there_ref = bf16[256,256]{1,0:T(8,128)(2,1)S(1)} collective-permute-done((bf16[256,256]{1,0:T(8,128)(2,1)S(1)}, bf16[256,256]{1,0:T(8,128)(2,1)S(1)}, u32[]{:S(2)}, u32[]{:S(2)}) %collective-permute-start.23) | collective-permute-done | bytes 131104 | tf_op jit(solution)/shard_map/ppermute | solution.py:41
  111.9 1.6 %copy-done = bf16[2048,512]{1,0:T(8,128)(2,1)S(1)} copy-done((bf16[2048,512]{1,0:T(8,128)(2,1)S(1)}, bf16[2048,512]{1,0:T(8,128)(2,1)}, u32[]{:S(2)}) %copy-start) | copy-done | bytes 2097176
  113.5 1.3 %shard_map.94 = (f32[128,2048]{1,0:T(8,128)S(1)}, bf16[128,2048]{1,0:T(8,128)(2,1)S(1)}) custom-call(s32[4]{0:T(128)S(1)} %pad_add_fusion.index, bf16[256,256]{1,0:T(8,128)(2,1)S(1)} %get-tuple-element.58.own_ref, bf16[256,256]{1,0:T(8,128)(2,1)S(1)} %collective-permute-done.23.there_ref, bf16[2048,512]{1,0:T(8,128)(2,1)S(1)} %copy-done), custom_call_target="tpu_custom_call" | custom-call | flops 536870912 | bytes 4194304 | tf_op jit(solution)/shard_map/pallas_call | solution.py:190
  114.8 2.4 %collective-permute-start.26 = (bf16[128,2048]{1,0:T(8,128)(2,1)S(1)}, bf16[128,2048]{1,0:T(8,128)(2,1)S(1)}, u32[]{:S(2)}, u32[]{:S(2)}) collective-permute-start(bf16[128,2048]{1,0:T(8,128)(2,1)S(1)} %get-tuple-element.44), channel_id=1, source_target_pairs={{0,1},{1,0},{2,3},{3,2},{4,5},{5,4},{6,7},{7,6},{8,9},{9,8},{10,11... | collective-permute-start | bytes 1572872 | tf_op jit(solution)/shard_map/ppermute | solution.py:41
  117.2 1.5 %collective-permute-done.26 = bf16[128,2048]{1,0:T(8,128)(2,1)S(1)} collective-permute-done((bf16[128,2048]{1,0:T(8,128)(2,1)S(1)}, bf16[128,2048]{1,0:T(8,128)(2,1)S(1)}, u32[]{:S(2)}, u32[]{:S(2)}) %collective-permute-start.26) | collective-permute-done | bytes 524320 | tf_op jit(solution)/shard_map/ppermute | solution.py:41
  (95 shorter events, 13.0 us)
Async XLA Ops:
  6.5 9.6 %copy-start.11 = (f32[2048]{0:T(1024)S(1)}, f32[2048]{0:T(1024)}, u32[]{:S(2)}) copy-start(f32[2048]{0:T(1024)} %param.11) | copy-start | bytes 24580
  6.5 11.1 %copy-start.9 = (bf16[1024,64]{0,1:T(8,128)(2,1)S(1)}, bf16[1024,64]{0,1:T(8,128)(2,1)}, u32[]{:S(2)}) copy-start(bf16[1024,64]{0,1:T(8,128)(2,1)} %param.16) | copy-start | bytes 393220
  6.5 105.3 %all-gather.2.cloned.1.call-start = ((), (), s32[]{:S(2)}) async-start(), calls=%async_computation | async-start | bytes 2359296 | tf_op jit(solution)/shard_map/all_gather | solution.py:310
  7.7 9.9 %collective-permute-start = (bf16[48,2048]{1,0:T(8,128)(2,1)S(1)}, bf16[48,2048]{1,0:T(8,128)(2,1)S(1)}, u32[]{:S(2)}, u32[]{:S(2)}) collective-permute-start(bf16[48,2048]{1,0:T(8,128)(2,1)S(1)} %bitcast.49), channel_id=1, source_target_pairs={{0,2},{1,15},{2,4},{3,1},{4,6},{5,3},{6,8},{7,5},{8,10},{9,7},{10,... | collective-permute-start | bytes 589832 | tf_op jit(solution)/shard_map/ppermute | solution.py:41
  14.2 16.5 %collective-permute-start.4 = (bf16[48,2048]{1,0:T(8,128)(2,1)S(1)}, bf16[48,2048]{1,0:T(8,128)(2,1)S(1)}, u32[]{:S(2)}, u32[]{:S(2)}) collective-permute-start(bf16[48,2048]{1,0:T(8,128)(2,1)S(1)} %bitcast.50), channel_id=1, source_target_pairs={{0,14},{1,3},{2,0},{3,5},{4,2},{5,7},{6,4},{7,9},{8,6},{9,11},{10,... | collective-permute-start | bytes 589832 | tf_op jit(solution)/shard_map/ppermute | solution.py:41
  17.7 13.1 %copy-start.2 = (bf16[48,2048]{1,0:T(8,128)(2,1)}, bf16[48,2048]{1,0:T(8,128)(2,1)S(1)}, u32[]{:S(2)}) copy-start(bf16[48,2048]{1,0:T(8,128)(2,1)S(1)} %collective-permute-done.refs_5_) | copy-start | bytes 589828
  17.9 58.6 %copy-start.12 = (s32[8]{0:T(128)S(1)}, s32[8]{0:T(128)}, u32[]{:S(2)}) copy-start(s32[8]{0:T(128)} %constant.9.clone) | copy-start | bytes 100
  18.1 2.4 %collective-permute-start.24 = (bf16[64,512]{1,0:T(8,128)(2,1)S(1)}, bf16[64,512]{1,0:T(8,128)(2,1)S(1)}, u32[]{:S(2)}, u32[]{:S(2)}) collective-permute-start(bf16[64,512]{1,0:T(8,128)(2,1)S(1)} %copy.28), channel_id=1, source_target_pairs={{0,1},{1,0},{2,3},{3,2},{4,5},{5,4},{6,7},{7,6},{8,9},{9,8},{10,11... | collective-permute-start | bytes 196616 | tf_op jit(solution)/shard_map/ppermute | solution.py:41
  20.5 4.8 %collective-permute-start.25 = (bf16[128,512]{1,0:T(8,128)(2,1)S(1)}, bf16[128,512]{1,0:T(8,128)(2,1)S(1)}, u32[]{:S(2)}, u32[]{:S(2)}) collective-permute-start(bf16[128,512]{1,0:T(8,128)(2,1)S(1)} %pad_maximum_fusion.5), channel_id=1, source_target_pairs={{0,16},{1,17},{2,18},{3,19},{4,20},{5,21},{6,22},{7,23},{8,24},{9,... | collective-permute-start | bytes 393224 | tf_op jit(solution)/shard_map/ppermute | solution.py:41
  21.8 4.3 %collective-permute-start.7 = (bf16[8,2048]{1,0:T(8,128)(2,1)S(1)}, bf16[8,2048]{1,0:T(8,128)(2,1)S(1)}, u32[]{:S(2)}, u32[]{:S(2)}) collective-permute-start(bf16[8,2048]{1,0:T(8,128)(2,1)S(1)} %multiply_convert_fusion), channel_id=1, source_target_pairs={{0,16},{1,17},{2,18},{3,19},{4,20},{5,21},{6,22},{7,23},{8,24},{9,... | collective-permute-start | bytes 98312 | tf_op jit(solution)/shard_map/ppermute | solution.py:41
  26.2 7.9 %collective-permute-start.8 = (bf16[64,2048]{1,0:T(8,128)(2,1)S(1)}, bf16[64,2048]{1,0:T(8,128)(2,1)S(1)}, u32[]{:S(2)}, u32[]{:S(2)}) collective-permute-start(bf16[64,2048]{1,0:T(8,128)(2,1)S(1)} %pad_maximum_fusion.1.refs_12_), channel_id=1, source_target_pairs={{0,2},{1,15},{2,4},{3,1},{4,6},{5,3},{6,8},{7,5},{8,10},{9,7},{10,... | collective-permute-start | bytes 786440 | tf_op jit(solution)/shard_map/ppermute | solution.py:41
  29.5 9.4 %collective-permute-start.9 = (bf16[64,2048]{1,0:T(8,128)(2,1)S(1)}, bf16[64,2048]{1,0:T(8,128)(2,1)S(1)}, u32[]{:S(2)}, u32[]{:S(2)}) collective-permute-start(bf16[64,2048]{1,0:T(8,128)(2,1)S(1)} %pad_maximum_fusion.1.refs_12_), channel_id=1, source_target_pairs={{0,14},{1,3},{2,0},{3,5},{4,2},{5,7},{6,4},{7,9},{8,6},{9,11},{10,... | collective-permute-start | bytes 786440 | tf_op jit(solution)/shard_map/ppermute | solution.py:41
  29.5 30.0 %collective-permute-start.1 = (bf16[128,2048]{1,0:T(8,128)(2,1)S(1)}, bf16[128,2048]{1,0:T(8,128)(2,1)S(1)}, u32[]{:S(2)}, u32[]{:S(2)}) collective-permute-start(bf16[128,2048]{1,0:T(8,128)(2,1)S(1)} %get-tuple-element.25.refs_0_), channel_id=1, source_target_pairs={{0,16},{1,17},{2,18},{3,19},{4,20},{5,21},{6,22},{7,23},{8,24},{9,... | collective-permute-start | bytes 1572872 | tf_op jit(solution)/shard_map/ppermute | solution.py:41
  30.7 9.7 %collective-permute-start.5 = (bf16[48,2048]{1,0:T(8,128)(2,1)S(1)}, bf16[48,2048]{1,0:T(8,128)(2,1)}, u32[]{:S(2)}, u32[]{:S(2)}) collective-permute-start(bf16[48,2048]{1,0:T(8,128)(2,1)S(1)} %collective-permute-done.refs_5_), channel_id=1, source_target_pairs={{0,2},{1,15},{2,4},{3,1},{4,6},{5,3},{6,8},{7,5},{8,10},{9,7},{10,... | collective-permute-start | bytes 589832 | tf_op jit(solution)/shard_map/ppermute | solution.py:41
  33.4 8.7 %collective-permute-start.6 = (bf16[48,2048]{1,0:T(8,128)(2,1)S(1)}, bf16[48,2048]{1,0:T(8,128)(2,1)}, u32[]{:S(2)}, u32[]{:S(2)}) collective-permute-start(bf16[48,2048]{1,0:T(8,128)(2,1)S(1)} %collective-permute-done.4.refs_6_), channel_id=1, source_target_pairs={{0,14},{1,3},{2,0},{3,5},{4,2},{5,7},{6,4},{7,9},{8,6},{9,11},{10,... | collective-permute-start | bytes 589832 | tf_op jit(solution)/shard_map/ppermute | solution.py:41
  38.9 13.4 %collective-permute-start.12 = (bf16[64,2048]{1,0:T(8,128)(2,1)S(1)}, bf16[64,2048]{1,0:T(8,128)(2,1)S(1)}, u32[]{:S(2)}, u32[]{:S(2)}) collective-permute-start(bf16[64,2048]{1,0:T(8,128)(2,1)S(1)} %collective-permute-done.8.refs_13_), channel_id=1, source_target_pairs={{0,2},{1,15},{2,4},{3,1},{4,6},{5,3},{6,8},{7,5},{8,10},{9,7},{10,... | collective-permute-start | bytes 786440 | tf_op jit(solution)/shard_map/ppermute | solution.py:41
  38.9 14.7 %collective-permute-start.13 = (bf16[64,2048]{1,0:T(8,128)(2,1)S(1)}, bf16[64,2048]{1,0:T(8,128)(2,1)S(1)}, u32[]{:S(2)}, u32[]{:S(2)}) collective-permute-start(bf16[64,2048]{1,0:T(8,128)(2,1)S(1)} %collective-permute-done.9.refs_14_), channel_id=1, source_target_pairs={{0,14},{1,3},{2,0},{3,5},{4,2},{5,7},{6,4},{7,9},{8,6},{9,11},{10,... | collective-permute-start | bytes 786440 | tf_op jit(solution)/shard_map/ppermute | solution.py:41
  42.1 17.4 %collective-permute-start.10 = (bf16[48,2048]{1,0:T(8,128)(2,1)}, bf16[48,2048]{1,0:T(8,128)(2,1)S(1)}, u32[]{:S(2)}, u32[]{:S(2)}) collective-permute-start(bf16[48,2048]{1,0:T(8,128)(2,1)} %collective-permute-done.5.refs_7_), channel_id=1, source_target_pairs={{0,2},{1,15},{2,4},{3,1},{4,6},{5,3},{6,8},{7,5},{8,10},{9,7},{10,... | collective-permute-start | bytes 589832 | tf_op jit(solution)/shard_map/ppermute | solution.py:41
  53.6 22.0 %collective-permute-start.15 = (bf16[64,2048]{1,0:T(8,128)(2,1)S(1)}, bf16[64,2048]{1,0:T(8,128)(2,1)S(1)}, u32[]{:S(2)}, u32[]{:S(2)}) collective-permute-start(bf16[64,2048]{1,0:T(8,128)(2,1)S(1)} %collective-permute-done.12.refs_15_), channel_id=1, source_target_pairs={{0,2},{1,15},{2,4},{3,1},{4,6},{5,3},{6,8},{7,5},{8,10},{9,7},{10,... | collective-permute-start | bytes 786440 | tf_op jit(solution)/shard_map/ppermute | solution.py:41
  53.6 22.0 %collective-permute-start.16 = (bf16[64,2048]{1,0:T(8,128)(2,1)S(1)}, bf16[64,2048]{1,0:T(8,128)(2,1)S(1)}, u32[]{:S(2)}, u32[]{:S(2)}) collective-permute-start(bf16[64,2048]{1,0:T(8,128)(2,1)S(1)} %collective-permute-done.13.refs_16_), channel_id=1, source_target_pairs={{0,14},{1,3},{2,0},{3,5},{4,2},{5,7},{6,4},{7,9},{8,6},{9,11},{10,... | collective-permute-start | bytes 786440 | tf_op jit(solution)/shard_map/ppermute | solution.py:41
  55.1 21.4 %collective-permute-start.2 = (bf16[128,2048]{1,0:T(8,128)(2,1)S(1)}, bf16[128,2048]{1,0:T(8,128)(2,1)S(1)}, u32[]{:S(2)}, u32[]{:S(2)}) collective-permute-start(bf16[128,2048]{1,0:T(8,128)(2,1)S(1)} %get-tuple-element.25.refs_0_), channel_id=1, source_target_pairs={{0,1},{1,0},{2,3},{3,2},{4,5},{5,4},{6,7},{7,6},{8,9},{9,8},{10,11... | collective-permute-start | bytes 1572872 | tf_op jit(solution)/shard_map/ppermute | solution.py:41
  59.5 16.1 %collective-permute-start.11 = (bf16[48,2048]{1,0:T(8,128)(2,1)}, bf16[48,2048]{1,0:T(8,128)(2,1)S(1)}, u32[]{:S(2)}, u32[]{:S(2)}) collective-permute-start(bf16[48,2048]{1,0:T(8,128)(2,1)} %collective-permute-done.6.refs_8_), channel_id=1, source_target_pairs={{0,14},{1,3},{2,0},{3,5},{4,2},{5,7},{6,4},{7,9},{8,6},{9,11},{10,... | collective-permute-start | bytes 589832 | tf_op jit(solution)/shard_map/ppermute | solution.py:41
  59.5 23.8 %collective-permute-start.3 = (bf16[128,2048]{1,0:T(8,128)(2,1)S(1)}, bf16[128,2048]{1,0:T(8,128)(2,1)S(1)}, u32[]{:S(2)}, u32[]{:S(2)}) collective-permute-start(bf16[128,2048]{1,0:T(8,128)(2,1)S(1)} %collective-permute-done.1.refs_1_), channel_id=1, source_target_pairs={{0,1},{1,0},{2,3},{3,2},{4,5},{5,4},{6,7},{7,6},{8,9},{9,8},{10,11... | collective-permute-start | bytes 1572872 | tf_op jit(solution)/shard_map/ppermute | solution.py:41
  75.6 7.6 %collective-permute-start.17 = (bf16[64,2048]{1,0:T(8,128)(2,1)S(1)}, bf16[64,2048]{1,0:T(8,128)(2,1)S(1)}, u32[]{:S(2)}, u32[]{:S(2)}) collective-permute-start(bf16[64,2048]{1,0:T(8,128)(2,1)S(1)} %collective-permute-done.15.refs_17_), channel_id=1, source_target_pairs={{0,2},{1,15},{2,4},{3,1},{4,6},{5,3},{6,8},{7,5},{8,10},{9,7},{10,... | collective-permute-start | bytes 786440 | tf_op jit(solution)/shard_map/ppermute | solution.py:41
  75.7 7.5 %collective-permute-start.14 = (bf16[48,2048]{1,0:T(8,128)(2,1)S(1)}, bf16[48,2048]{1,0:T(8,128)(2,1)S(1)}, u32[]{:S(2)}, u32[]{:S(2)}) collective-permute-start(bf16[48,2048]{1,0:T(8,128)(2,1)S(1)} %collective-permute-done.10.refs_9_), channel_id=1, source_target_pairs={{0,2},{1,15},{2,4},{3,1},{4,6},{5,3},{6,8},{7,5},{8,10},{9,7},{10,... | collective-permute-start | bytes 589832 | tf_op jit(solution)/shard_map/ppermute | solution.py:41
  91.2 3.9 %collective-permute-start.18 = (bf16[512,384]{1,0:T(8,128)(2,1)S(1)}, bf16[512,384]{1,0:T(8,128)(2,1)S(1)}, u32[]{:S(2)}, u32[]{:S(2)}) collective-permute-start(bf16[512,384]{1,0:T(8,128)(2,1)S(1)} %get-tuple-element.37), channel_id=1, source_target_pairs={{0,1},{1,0},{2,3},{3,2},{4,5},{5,4},{6,7},{7,6},{8,9},{9,8},{10,11... | collective-permute-start | bytes 1179656 | tf_op jit(solution)/shard_map/ppermute | solution.py:41
  93.8 4.2 %collective-permute-start.19 = (bf16[128,2048]{1,0:T(8,128)(2,1)S(1)}, bf16[128,2048]{1,0:T(8,128)(2,1)S(1)}, u32[]{:S(2)}, u32[]{:S(2)}) collective-permute-start(bf16[128,2048]{1,0:T(8,128)(2,1)S(1)} %get-tuple-element.38.own_ref), channel_id=1, source_target_pairs={{0,1},{1,0},{2,3},{3,2},{4,5},{5,4},{6,7},{7,6},{8,9},{9,8},{10,11... | collective-permute-start | bytes 1572872 | tf_op jit(solution)/shard_map/ppermute | solution.py:41
  95.2 8.8 %collective-permute-start.21 = (bf16[256,512]{1,0:T(8,128)(2,1)S(1)}, bf16[256,512]{1,0:T(8,128)(2,1)S(1)}, u32[]{:S(2)}, u32[]{:S(2)}) collective-permute-start(bf16[256,512]{1,0:T(8,128)(2,1)S(1)} %pad_maximum_fusion.2), channel_id=1, source_target_pairs={{0,2},{1,3},{2,4},{3,5},{4,6},{5,7},{6,8},{7,9},{8,10},{9,11},{10,... | collective-permute-start | bytes 786440 | tf_op jit(solution)/shard_map/ppermute | solution.py:41
  95.3 8.7 %collective-permute-start.22 = (bf16[256,512]{1,0:T(8,128)(2,1)S(1)}, bf16[256,512]{1,0:T(8,128)(2,1)S(1)}, u32[]{:S(2)}, u32[]{:S(2)}) collective-permute-start(bf16[256,512]{1,0:T(8,128)(2,1)S(1)} %pad_maximum_fusion.3), channel_id=1, source_target_pairs={{0,14},{1,15},{2,0},{3,1},{4,2},{5,3},{6,4},{7,5},{8,6},{9,7},{10,... | collective-permute-start | bytes 786440 | tf_op jit(solution)/shard_map/ppermute | solution.py:41
  100.1 3.9 %collective-permute-start.20 = (bf16[256,256]{1,0:T(8,128)(2,1)S(1)}, bf16[256,256]{1,0:T(8,128)(2,1)S(1)}, u32[]{:S(2)}, u32[]{:S(2)}) collective-permute-start(bf16[256,256]{1,0:T(8,128)(2,1)S(1)} %get-tuple-element.41), channel_id=1, source_target_pairs={{0,1},{1,0},{2,3},{3,2},{4,5},{5,4},{6,7},{7,6},{8,9},{9,8},{10,11... | collective-permute-start | bytes 393224 | tf_op jit(solution)/shard_map/ppermute | solution.py:41
  108.0 3.9 %collective-permute-start.23 = (bf16[256,256]{1,0:T(8,128)(2,1)S(1)}, bf16[256,256]{1,0:T(8,128)(2,1)S(1)}, u32[]{:S(2)}, u32[]{:S(2)}) collective-permute-start(bf16[256,256]{1,0:T(8,128)(2,1)S(1)} %get-tuple-element.57), channel_id=1, source_target_pairs={{0,16},{1,17},{2,18},{3,19},{4,20},{5,21},{6,22},{7,23},{8,24},{9,... | collective-permute-start | bytes 393224 | tf_op jit(solution)/shard_map/ppermute | solution.py:41
  114.8 4.0 %collective-permute-start.26 = (bf16[128,2048]{1,0:T(8,128)(2,1)S(1)}, bf16[128,2048]{1,0:T(8,128)(2,1)S(1)}, u32[]{:S(2)}, u32[]{:S(2)}) collective-permute-start(bf16[128,2048]{1,0:T(8,128)(2,1)S(1)} %get-tuple-element.44), channel_id=1, source_target_pairs={{0,1},{1,0},{2,3},{3,2},{4,5},{5,4},{6,7},{7,6},{8,9},{9,8},{10,11... | collective-permute-start | bytes 1572872 | tf_op jit(solution)/shard_map/ppermute | solution.py:41
  (11 other events, 36.6 us)
Sparse Core Ops, SparseCore 0:
  26.2 51.4 all-gather.1

commit v2 on v1

--- a/solution.py
+++ b/solution.py
@@ -56,7 +56,7 @@
 SHARDS = len(STEPS)
 ROWS = 4 * TOK
 G_ROWS = Z * 16
-VMEM_LIMIT = 48 * 1024 * 1024
+VMEM_LIMIT = 24 * 1024 * 1024
 
 
 def z_of(z, core, way, hops):
@@ -171,18 +171,20 @@
             out_ref[mine, part * TOK : (part + 1) * TOK, :] = context.astype(jnp.bfloat16)
 
 
-def output_kernel(index, own_ref, there_ref, weights, keep_ref, send_ref):
-    core, x = index[1], index[2]
+def output_kernel(index, own_ref, there_ref, *refs):
+    blocks, keep_ref, send_ref = refs[:SHARDS], refs[SHARDS], refs[SHARDS + 1]
+    z, core, x = index[0], index[1], index[2]
     own, there = own_ref[...], there_ref[...]
     full = jnp.concatenate([jnp.where(x == 0, own, there), jnp.where(x == 0, there, own)], axis=1)
-    for zj in range(Z):
-        out = dot_nt(full, weights[zj * 256 : zj * 256 + 256, :])
+    for j, (way, hops) in enumerate(STEPS):
+        zj = z_of(z, core, way, hops)
+        out = dot_nt(full, blocks[j][...])
         keep = jnp.where(core == 0, out[:TOK], out[TOK:])
         sent = jnp.where(core == 0, out[TOK:], out[:TOK]).astype(jnp.bfloat16)
         for side in range(X):
-            at = (side * Z + zj) * 128
-            keep_ref[:, at : at + 128] = keep[:, side * 128 : side * 128 + 128]
-            send_ref[:, at : at + 128] = sent[:, side * 128 : side * 128 + 128]
+            lanes = pl.ds(pl.multiple_of((side * Z + zj) * 128, 128), 128)
+            keep_ref[:, lanes] = keep[:, side * 128 : side * 128 + 128]
+            send_ref[:, lanes] = sent[:, side * 128 : side * 128 + 128]
 
 
 def on_chip(kernel, out_shape, flops, exps, args, scratch=()):
@@ -274,8 +276,9 @@
         tables = [t.reshape(2, 2, TOK, 384)[:, part, :, 128:384].reshape(2 * TOK, 256) for t in (keep, got)]
         return jnp.concatenate(tables, axis=1)
 
-    below = send(edge(1), UP)
-    above = send(edge(0), DOWN)
+    low_edge, high_edge = edge(0), edge(1)
+    below = send(high_edge, UP)
+    above = send(low_edge, DOWN)
 
     far_half = jax.ShapeDtypeStruct((2 * G_ROWS, 256), bf16)
     g_keep, g_swap = on_chip(
@@ -297,7 +300,7 @@
         (index, far_pos, keep, got, g_keep, g_got, below, above),
     )
 
-    out_t = after(w_out, one[0, 1]).T.reshape(64, X, 2, HEADS_LOCAL, 2, HALF)
+    out_t = after(w_out, two[0, 1], two[1, 1]).T.reshape(64, X, 2, HEADS_LOCAL, 2, HALF)
     out_t = jnp.transpose(out_t, (0, 2, 1, 4, 3, 5))
     group_0 = out_t[:, 0].reshape(64, 2 * WIDE)
     group_1 = out_t[:, 1, :, ::-1].reshape(64, 2 * WIDE)
@@ -306,8 +309,14 @@
     chip = jnp.concatenate([jnp.where(core == 0, kept, passed), jnp.where(core == 0, passed, kept)], axis=0)
     chip_there = send(chip, OTHER_X)
     both = jnp.concatenate([jnp.where(x == 0, chip, chip_there), jnp.where(x == 0, chip_there, chip)], axis=0)
-    columns = [[place(i, k, c) for k in range(Z)] for i in range(X) for c in range(C)]
-    out_weights = lax.all_gather(both, "seq", axis_index_groups=columns, axis=0, tiled=True)
+    out_blocks = {(0, 0): both}
+    ahead = behind = after(both, one[0, 4], two[0, 4])
+    for step in range(1, 5):
+        if step == 2:
+            ahead, behind = lax.optimization_barrier((ahead, behind, low_edge, high_edge))[:2]
+        out_blocks[0, step] = ahead = send(ahead, AHEAD)
+        if step < 4:
+            out_blocks[1, step] = behind = send(behind, BEHIND)
 
     there = send(context[1], OTHER_X)
     kept_part, sent_part = on_chip(
@@ -315,7 +324,7 @@
         (jax.ShapeDtypeStruct((TOK, width), jnp.float32), jax.ShapeDtypeStruct((TOK, width), bf16)),
         2 * 256 * 512 * width,
         0,
-        (index, context[0], there, out_weights),
+        (index, context[0], there, *[out_blocks[s] for s in STEPS]),
     )
     return (kept_part + send(sent_part, OTHER_CORE).astype(jnp.float32)).astype(bf16)
 

time: 127 us -> 109 us (0.86)
  waiting for transfers between devices: 52.4 us -> 28.8 us
  starting transfers between devices: 35.6 us -> 50 us
  between operations: 14.3 us -> 0.95 us
  other arithmetic: 5.41 us -> 10 us
    ppermute x27 -> x34, waiting for transfers between devices: 52.4 us -> 28.8 us  [send(): return lax.ppermute(value, 'seq', route)]
    ppermute x27 -> x34, starting transfers between devices: 35.6 us -> 50 us  [send(): return lax.ppermute(value, 'seq', route)]
    unnamed x30 -> x24, local copies, waits for them, and re-layouts: 6.55 us -> 4.43 us
  transfers between devices with their start and end apart: 28 -> 34, of which waited for: 14 -> 12; matrix products, arithmetic and copies ran while one was open for 3% -> 8% of each run, Pallas kernels for 8% -> 9%
where the time goes in v2:
time: 109 us; the launch traced here: 108 us
  starting transfers between devices  50 us (46%)
  waiting for transfers between devices  28.8 us (26%)
  Pallas kernels  10.8 us (10%)
  other arithmetic  10 us (9%)
  local copies, waits for them, and re-layouts  7.9 us (7%)
    ppermute x34, starting transfers between devices, send(): return lax.ppermute(value, 'seq', route)  50 us
    ppermute x34, waiting for transfers between devices, send(): return lax.ppermute(value, 'seq', route)  28.8 us
    pallas_call x4, Pallas kernels, on_chip(): pl.pallas_call(kernel, out_shape=out_shape, in_specs=[pl.BlockSpec(memory...  10.8 us
    unnamed x24, local copies, waits for them, and re-layouts  4.43 us
  transfers between devices with their start and end apart: 34, of which 12 were waited for; matrix products, arithmetic and copies ran while one was open for 8% of the time, Pallas kernels for 9%

profile of v2, /device:TPU:1, one launch (start us, length us, event | category | flops | bytes accessed | tf_op | source)
XLA Modules:
  0.0 108.5 jit_solution(7181189027766270703)
XLA Ops:
  1.9 1.6 %bitcast_reduce_fusion = (f32[8,2048]{1,0:T(8,128)S(1)}, bf16[128,2048]{1,0:T(8,128)(2,1)S(1)}) fusion(f32[128]{0:T(128)S(1)} %compare_convert_fusion, f32[2048]{0:T(1024)} %param.11, f32[128]{0:T(128)S(1)} %add_rsqrt_fusion.1, bf16[128,2048]{1,0:T(8,128)(2,1)} %param.9), kind=kLoop, calls=%fused_computation.5 | loop fusion | flops 1818624 | bytes 1123328 | tf_op jit(solution)/shard_map/reduce_sum | solution.py:222
  4.5 2.1 %collective-permute-start.7 = (bf16[8,2048]{1,0:T(8,128)(2,1)S(1)}, bf16[8,2048]{1,0:T(8,128)(2,1)S(1)}, u32[]{:S(2)}, u32[]{:S(2)}) collective-permute-start(bf16[8,2048]{1,0:T(8,128)(2,1)S(1)} %multiply_convert_fusion), channel_id=1, source_target_pairs={{0,16},{1,17},{2,18},{3,19},{4,20},{5,21},{6,22},{7,23},{8,24},{9,... | collective-permute-start | bytes 98312 | tf_op jit(solution)/shard_map/ppermute | solution.py:41
  7.7 5.7 %collective-permute-start = (bf16[48,2048]{1,0:T(8,128)(2,1)S(1)}, bf16[48,2048]{1,0:T(8,128)(2,1)S(1)}, u32[]{:S(2)}, u32[]{:S(2)}) collective-permute-start(bf16[48,2048]{1,0:T(8,128)(2,1)S(1)} %bitcast.49), channel_id=1, source_target_pairs={{0,2},{1,15},{2,4},{3,1},{4,6},{5,3},{6,8},{7,5},{8,10},{9,7},{10,... | collective-permute-start | bytes 589832 | tf_op jit(solution)/shard_map/ppermute | solution.py:41
  13.5 2.7 %collective-permute-start.8 = (bf16[64,2048]{1,0:T(8,128)(2,1)S(1)}, bf16[64,2048]{1,0:T(8,128)(2,1)S(1)}, u32[]{:S(2)}, u32[]{:S(2)}) collective-permute-start(bf16[64,2048]{1,0:T(8,128)(2,1)S(1)} %pad_maximum_fusion.1.refs_12_), channel_id=1, source_target_pairs={{0,2},{1,15},{2,4},{3,1},{4,6},{5,3},{6,8},{7,5},{8,10},{9,7},{10,... | collective-permute-start | bytes 786440 | tf_op jit(solution)/shard_map/ppermute | solution.py:41
  16.8 3.8 %collective-permute-done.4.refs_6_ = bf16[48,2048]{1,0:T(8,128)(2,1)S(1)} collective-permute-done((bf16[48,2048]{1,0:T(8,128)(2,1)S(1)}, bf16[48,2048]{1,0:T(8,128)(2,1)S(1)}, u32[]{:S(2)}, u32[]{:S(2)}) %collective-permute-start.4) | collective-permute-done | bytes 196640 | tf_op jit(solution)/shard_map/ppermute | solution.py:41
  20.6 1.5 %collective-permute-start.6 = (bf16[48,2048]{1,0:T(8,128)(2,1)S(1)}, bf16[48,2048]{1,0:T(8,128)(2,1)}, u32[]{:S(2)}, u32[]{:S(2)}) collective-permute-start(bf16[48,2048]{1,0:T(8,128)(2,1)S(1)} %collective-permute-done.4.refs_6_), channel_id=1, source_target_pairs={{0,14},{1,3},{2,0},{3,5},{4,2},{5,7},{6,4},{7,9},{8,6},{9,11},{10,... | collective-permute-start | bytes 589832 | tf_op jit(solution)/shard_map/ppermute | solution.py:41
  22.8 3.5 %collective-permute-done.9.refs_14_ = bf16[64,2048]{1,0:T(8,128)(2,1)S(1)} collective-permute-done((bf16[64,2048]{1,0:T(8,128)(2,1)S(1)}, bf16[64,2048]{1,0:T(8,128)(2,1)S(1)}, u32[]{:S(2)}, u32[]{:S(2)}) %collective-permute-start.9) | collective-permute-done | bytes 262176 | tf_op jit(solution)/shard_map/ppermute | solution.py:41
  26.2 1.5 %collective-permute-start.13 = (bf16[64,2048]{1,0:T(8,128)(2,1)S(1)}, bf16[64,2048]{1,0:T(8,128)(2,1)}, u32[]{:S(2)}, u32[]{:S(2)}) collective-permute-start(bf16[64,2048]{1,0:T(8,128)(2,1)S(1)} %collective-permute-done.9.refs_14_), channel_id=1, source_target_pairs={{0,14},{1,3},{2,0},{3,5},{4,2},{5,7},{6,4},{7,9},{8,6},{9,11},{10,... | collective-permute-start | bytes 786440 | tf_op jit(solution)/shard_map/ppermute | solution.py:41
  28.3 1.4 %collective-permute-done.6.refs_8_ = bf16[48,2048]{1,0:T(8,128)(2,1)} collective-permute-done((bf16[48,2048]{1,0:T(8,128)(2,1)S(1)}, bf16[48,2048]{1,0:T(8,128)(2,1)}, u32[]{:S(2)}, u32[]{:S(2)}) %collective-permute-start.6) | collective-permute-done | bytes 196640 | tf_op jit(solution)/shard_map/ppermute | solution.py:41
  30.4 2.2 %collective-permute-start.2 = (bf16[128,2048]{1,0:T(8,128)(2,1)S(1)}, bf16[128,2048]{1,0:T(8,128)(2,1)S(1)}, u32[]{:S(2)}, u32[]{:S(2)}) collective-permute-start(bf16[128,2048]{1,0:T(8,128)(2,1)S(1)} %get-tuple-element.28.refs_0_), channel_id=1, source_target_pairs={{0,1},{1,0},{2,3},{3,2},{4,5},{5,4},{6,7},{7,6},{8,9},{9,8},{10,11... | collective-permute-start | bytes 1572872 | tf_op jit(solution)/shard_map/ppermute | solution.py:41
  34.4 1.6 %collective-permute-start.11 = (bf16[48,2048]{1,0:T(8,128)(2,1)}, bf16[48,2048]{1,0:T(8,128)(2,1)}, u32[]{:S(2)}, u32[]{:S(2)}) collective-permute-start(bf16[48,2048]{1,0:T(8,128)(2,1)} %collective-permute-done.6.refs_8_), channel_id=1, source_target_pairs={{0,14},{1,3},{2,0},{3,5},{4,2},{5,7},{6,4},{7,9},{8,6},{9,11},{10,... | collective-permute-start | bytes 589832 | tf_op jit(solution)/shard_map/ppermute | solution.py:41
  37.7 2.8 %collective-permute-start.3 = (bf16[128,2048]{1,0:T(8,128)(2,1)S(1)}, bf16[128,2048]{1,0:T(8,128)(2,1)S(1)}, u32[]{:S(2)}, u32[]{:S(2)}) collective-permute-start(bf16[128,2048]{1,0:T(8,128)(2,1)S(1)} %collective-permute-done.1.refs_1_), channel_id=1, source_target_pairs={{0,1},{1,0},{2,3},{3,2},{4,5},{5,4},{6,7},{7,6},{8,9},{9,8},{10,11... | collective-permute-start | bytes 1572872 | tf_op jit(solution)/shard_map/ppermute | solution.py:41
  42.2 2.0 %collective-permute-start.24 = (bf16[64,512]{1,0:T(8,128)(2,1)}, bf16[64,512]{1,0:T(8,128)(2,1)}, u32[]{:S(2)}, u32[]{:S(2)}) collective-permute-start(bf16[64,512]{1,0:T(8,128)(2,1)} %copy.28), channel_id=1, source_target_pairs={{0,1},{1,0},{2,3},{3,2},{4,5},{5,4},{6,7},{7,6},{8,9},{9,8},{10,11... | collective-permute-start | bytes 196616 | tf_op jit(solution)/shard_map/ppermute | solution.py:41
  44.5 2.2 %collective-permute-start.14 = (bf16[48,2048]{1,0:T(8,128)(2,1)}, bf16[48,2048]{1,0:T(8,128)(2,1)S(1)}, u32[]{:S(2)}, u32[]{:S(2)}) collective-permute-start(bf16[48,2048]{1,0:T(8,128)(2,1)} %collective-permute-done.10.refs_9_), channel_id=1, source_target_pairs={{0,2},{1,15},{2,4},{3,1},{4,6},{5,3},{6,8},{7,5},{8,10},{9,7},{10,... | collective-permute-start | bytes 589832 | tf_op jit(solution)/shard_map/ppermute | solution.py:41
  48.0 1.6 %collective-permute-done.14.refs_11_ = bf16[48,2048]{1,0:T(8,128)(2,1)S(1)} collective-permute-done((bf16[48,2048]{1,0:T(8,128)(2,1)}, bf16[48,2048]{1,0:T(8,128)(2,1)S(1)}, u32[]{:S(2)}, u32[]{:S(2)}) %collective-permute-start.14) | collective-permute-done | bytes 196640 | tf_op jit(solution)/shard_map/ppermute | solution.py:41
  49.6 3.1 %collective-permute-done.17.refs_19_ = bf16[64,2048]{1,0:T(8,128)(2,1)S(1)} collective-permute-done((bf16[64,2048]{1,0:T(8,128)(2,1)}, bf16[64,2048]{1,0:T(8,128)(2,1)S(1)}, u32[]{:S(2)}, u32[]{:S(2)}) %collective-permute-start.17) | collective-permute-done | bytes 262176 | tf_op jit(solution)/shard_map/ppermute | solution.py:41
  56.4 3.5 %shard_map.91 = (bf16[512,384]{1,0:T(8,128)(2,1)S(1)}, bf16[512,384]{1,0:T(8,128)(2,1)S(1)}, bf16[128,2048]{1,0:T(8,128)(2,1)S(1)}, bf16[512,2048]{1,0:T(8,128)(2,1)S(1)}) custom-call(s32[4]{0:T(128)S(1)} %pad_add_fusion.index, bf16[128,2048]{1,0:T(8,128)(2,1)S(1)} %get-tuple-element.28.refs_0_, bf16[128,2048]{1,0:T(8,128)(2,1)S(1)} %collective-permute-done.1.refs_1_, ...), custom_call_target="tpu_custom_call" | custom-call | flops 1610612736 | bytes 4194304 | tf_op jit(solution)/shard_map/pallas_call | solution.py:192
  60.0 4.7 %collective-permute-start.18 = (bf16[512,384]{1,0:T(8,128)(2,1)S(1)}, bf16[512,384]{1,0:T(8,128)(2,1)S(1)}, u32[]{:S(2)}, u32[]{:S(2)}) collective-permute-start(bf16[512,384]{1,0:T(8,128)(2,1)S(1)} %get-tuple-element.40), channel_id=1, source_target_pairs={{0,1},{1,0},{2,3},{3,2},{4,5},{5,4},{6,7},{7,6},{8,9},{9,8},{10,11... | collective-permute-start | bytes 1179656 | tf_op jit(solution)/shard_map/ppermute | solution.py:41
  64.9 1.5 %collective-permute-start.27 = (bf16[256,512]{1,0:T(8,128)(2,1)S(1)}, bf16[256,512]{1,0:T(8,128)(2,1)S(1)}, u32[]{:S(2)}, u32[]{:S(2)}) collective-permute-start(bf16[256,512]{1,0:T(8,128)(2,1)S(1)} %pad_maximum_fusion.4.refs_0_), channel_id=1, source_target_pairs={{0,14},{1,3},{2,0},{3,5},{4,2},{5,7},{6,4},{7,9},{8,6},{9,11},{10,... | collective-permute-start | bytes 786440 | tf_op jit(solution)/shard_map/ppermute | solution.py:41
  66.3 1.8 %collective-permute-start.19 = (bf16[128,2048]{1,0:T(8,128)(2,1)S(1)}, bf16[128,2048]{1,0:T(8,128)(2,1)S(1)}, u32[]{:S(2)}, u32[]{:S(2)}) collective-permute-start(bf16[128,2048]{1,0:T(8,128)(2,1)S(1)} %get-tuple-element.41.own_ref), channel_id=1, source_target_pairs={{0,1},{1,0},{2,3},{3,2},{4,5},{5,4},{6,7},{7,6},{8,9},{9,8},{10,11... | collective-permute-start | bytes 1572872 | tf_op jit(solution)/shard_map/ppermute | solution.py:41
  68.9 3.7 %collective-permute-done.26.refs_1_ = bf16[256,512]{1,0:T(8,128)(2,1)S(1)} collective-permute-done((bf16[256,512]{1,0:T(8,128)(2,1)S(1)}, bf16[256,512]{1,0:T(8,128)(2,1)S(1)}, u32[]{:S(2)}, u32[]{:S(2)}) %collective-permute-start.26) | collective-permute-done | bytes 262176 | tf_op jit(solution)/shard_map/ppermute | solution.py:41
  72.6 1.5 %collective-permute-done.27.refs_2_ = bf16[256,512]{1,0:T(8,128)(2,1)S(1)} collective-permute-done((bf16[256,512]{1,0:T(8,128)(2,1)S(1)}, bf16[256,512]{1,0:T(8,128)(2,1)S(1)}, u32[]{:S(2)}, u32[]{:S(2)}) %collective-permute-start.27) | collective-permute-done | bytes 262176 | tf_op jit(solution)/shard_map/ppermute | solution.py:41
  74.2 1.5 %collective-permute-start.21 = (bf16[256,512]{1,0:T(8,128)(2,1)S(1)}, bf16[256,512]{1,0:T(8,128)(2,1)S(1)}, u32[]{:S(2)}, u32[]{:S(2)}) collective-permute-start(bf16[256,512]{1,0:T(8,128)(2,1)S(1)} %pad_maximum_fusion.2), channel_id=1, source_target_pairs={{0,2},{1,3},{2,4},{3,5},{4,6},{5,7},{6,8},{7,9},{8,10},{9,11},{10,... | collective-permute-start | bytes 786440 | tf_op jit(solution)/shard_map/ppermute | solution.py:41
  77.2 2.1 %shard_map.92 = (bf16[256,256]{1,0:T(8,128)(2,1)S(1)}, bf16[256,256]{1,0:T(8,128)(2,1)S(1)}) custom-call(s32[4]{0:T(128)S(1)} %pad_add_fusion.index, bf16[128,2048]{1,0:T(8,128)(2,1)S(1)} %get-tuple-element.41.own_ref, bf16[128,2048]{1,0:T(8,128)(2,1)S(1)} %collective-permute-done.19.other_ref, bf16[512,2048]{1,0:T(8,128)(2,1)S(1)} %get-tuple-element.42.table), custom_call_target="tpu_custom_call" | custom-call | flops 536870912 | bytes 4194304 | tf_op jit(solution)/shard_map/pallas_call | solution.py:192
  79.3 3.1 %collective-permute-start.20 = (bf16[256,256]{1,0:T(8,128)(2,1)S(1)}, bf16[256,256]{1,0:T(8,128)(2,1)S(1)}, u32[]{:S(2)}, u32[]{:S(2)}) collective-permute-start(bf16[256,256]{1,0:T(8,128)(2,1)S(1)} %get-tuple-element.44), channel_id=1, source_target_pairs={{0,1},{1,0},{2,3},{3,2},{4,5},{5,4},{6,7},{7,6},{8,9},{9,8},{10,11... | collective-permute-start | bytes 393224 | tf_op jit(solution)/shard_map/ppermute | solution.py:41
  83.9 4.5 %collective-permute-done.29.refs_4_ = bf16[256,512]{1,0:T(8,128)(2,1)S(1)} collective-permute-done((bf16[256,512]{1,0:T(8,128)(2,1)S(1)}, bf16[256,512]{1,0:T(8,128)(2,1)S(1)}, u32[]{:S(2)}, u32[]{:S(2)}) %collective-permute-start.29) | collective-permute-done | bytes 262176 | tf_op jit(solution)/shard_map/ppermute | solution.py:41
  89.6 3.9 %shard_map.93 = bf16[2,256,256]{2,1,0:T(8,128)(2,1)S(1)} custom-call(s32[4]{0:T(128)S(1)} %pad_add_fusion.index, s32[1,256]{1,0:T(1,128)S(1)} %add.107.far_pos, bf16[512,384]{1,0:T(8,128)(2,1)S(1)} %get-tuple-element.39.keep_ref, bf16[512,384]{1,0:T(8,128)(2,1)S(1)} %collective-permute-done.18.got_ref, bf16[256,256]{1,0:T(8,128)(2,1)S(1)} %get-tuple-element.43.g_keep, ...), custom_call_target="tpu_custom_call" | custom-call | flops 1342177280 | bytes 4194304 | tf_op jit(solution)/shard_map/pallas_call | solution.py:192
  93.6 1.5 %collective-permute-start.32 = (bf16[256,512]{1,0:T(8,128)(2,1)S(1)}, bf16[256,512]{1,0:T(8,128)(2,1)S(1)}, u32[]{:S(2)}, u32[]{:S(2)}) collective-permute-start(bf16[256,512]{1,0:T(8,128)(2,1)S(1)} %collective-permute-done.30.refs_5_), channel_id=1, source_target_pairs={{0,2},{1,15},{2,4},{3,1},{4,6},{5,3},{6,8},{7,5},{8,10},{9,7},{10,... | collective-permute-start | bytes 786440 | tf_op jit(solution)/shard_map/ppermute | solution.py:41
  95.3 3.6 %collective-permute-done.23.there_ref = bf16[256,256]{1,0:T(8,128)(2,1)S(1)} collective-permute-done((bf16[256,256]{1,0:T(8,128)(2,1)S(1)}, bf16[256,256]{1,0:T(8,128)(2,1)S(1)}, u32[]{:S(2)}, u32[]{:S(2)}) %collective-permute-start.23) | collective-permute-done | bytes 131104 | tf_op jit(solution)/shard_map/ppermute | solution.py:41
  99.3 1.3 %shard_map.94 = (f32[128,2048]{1,0:T(8,128)S(1)}, bf16[128,2048]{1,0:T(8,128)(2,1)S(1)}) custom-call(s32[4]{0:T(128)S(1)} %pad_add_fusion.index, bf16[256,256]{1,0:T(8,128)(2,1)S(1)} %get-tuple-element.64.own_ref, bf16[256,256]{1,0:T(8,128)(2,1)S(1)} %collective-permute-done.23.there_ref, bf16[256,512]{1,0:T(8,128)(2,1)S(1)} %pad_maximum_fusion.4.refs_0_, ...), custom_call_target="tpu_custom_call" | custom-call | flops 536870912 | bytes 4194304 | tf_op jit(solution)/shard_map/pallas_call | solution.py:192
  100.6 5.4 %collective-permute-start.33 = (bf16[128,2048]{1,0:T(8,128)(2,1)S(1)}, bf16[128,2048]{1,0:T(8,128)(2,1)S(1)}, u32[]{:S(2)}, u32[]{:S(2)}) collective-permute-start(bf16[128,2048]{1,0:T(8,128)(2,1)S(1)} %get-tuple-element.50), channel_id=1, source_target_pairs={{0,1},{1,0},{2,3},{3,2},{4,5},{5,4},{6,7},{7,6},{8,9},{9,8},{10,11... | collective-permute-start | bytes 1572872 | tf_op jit(solution)/shard_map/ppermute | solution.py:41
  106.0 1.5 %collective-permute-done.33 = bf16[128,2048]{1,0:T(8,128)(2,1)S(1)} collective-permute-done((bf16[128,2048]{1,0:T(8,128)(2,1)S(1)}, bf16[128,2048]{1,0:T(8,128)(2,1)S(1)}, u32[]{:S(2)}, u32[]{:S(2)}) %collective-permute-start.33) | collective-permute-done | bytes 524320 | tf_op jit(solution)/shard_map/ppermute | solution.py:41
  (100 shorter events, 23.2 us)
Async XLA Ops:
  4.5 8.9 %collective-permute-start.7 = (bf16[8,2048]{1,0:T(8,128)(2,1)S(1)}, bf16[8,2048]{1,0:T(8,128)(2,1)S(1)}, u32[]{:S(2)}, u32[]{:S(2)}) collective-permute-start(bf16[8,2048]{1,0:T(8,128)(2,1)S(1)} %multiply_convert_fusion), channel_id=1, source_target_pairs={{0,16},{1,17},{2,18},{3,19},{4,20},{5,21},{6,22},{7,23},{8,24},{9,... | collective-permute-start | bytes 98312 | tf_op jit(solution)/shard_map/ppermute | solution.py:41
  7.7 8.8 %collective-permute-start = (bf16[48,2048]{1,0:T(8,128)(2,1)S(1)}, bf16[48,2048]{1,0:T(8,128)(2,1)S(1)}, u32[]{:S(2)}, u32[]{:S(2)}) collective-permute-start(bf16[48,2048]{1,0:T(8,128)(2,1)S(1)} %bitcast.49), channel_id=1, source_target_pairs={{0,2},{1,15},{2,4},{3,1},{4,6},{5,3},{6,8},{7,5},{8,10},{9,7},{10,... | collective-permute-start | bytes 589832 | tf_op jit(solution)/shard_map/ppermute | solution.py:41
  13.4 7.2 %collective-permute-start.4 = (bf16[48,2048]{1,0:T(8,128)(2,1)S(1)}, bf16[48,2048]{1,0:T(8,128)(2,1)S(1)}, u32[]{:S(2)}, u32[]{:S(2)}) collective-permute-start(bf16[48,2048]{1,0:T(8,128)(2,1)S(1)} %bitcast.50), channel_id=1, source_target_pairs={{0,14},{1,3},{2,0},{3,5},{4,2},{5,7},{6,4},{7,9},{8,6},{9,11},{10,... | collective-permute-start | bytes 589832 | tf_op jit(solution)/shard_map/ppermute | solution.py:41
  13.5 9.3 %collective-permute-start.8 = (bf16[64,2048]{1,0:T(8,128)(2,1)S(1)}, bf16[64,2048]{1,0:T(8,128)(2,1)S(1)}, u32[]{:S(2)}, u32[]{:S(2)}) collective-permute-start(bf16[64,2048]{1,0:T(8,128)(2,1)S(1)} %pad_maximum_fusion.1.refs_12_), channel_id=1, source_target_pairs={{0,2},{1,15},{2,4},{3,1},{4,6},{5,3},{6,8},{7,5},{8,10},{9,7},{10,... | collective-permute-start | bytes 786440 | tf_op jit(solution)/shard_map/ppermute | solution.py:41
  16.3 10.0 %collective-permute-start.9 = (bf16[64,2048]{1,0:T(8,128)(2,1)S(1)}, bf16[64,2048]{1,0:T(8,128)(2,1)S(1)}, u32[]{:S(2)}, u32[]{:S(2)}) collective-permute-start(bf16[64,2048]{1,0:T(8,128)(2,1)S(1)} %pad_maximum_fusion.1.refs_12_), channel_id=1, source_target_pairs={{0,14},{1,3},{2,0},{3,5},{4,2},{5,7},{6,4},{7,9},{8,6},{9,11},{10,... | collective-permute-start | bytes 786440 | tf_op jit(solution)/shard_map/ppermute | solution.py:41
  16.5 21.2 %collective-permute-start.1 = (bf16[128,2048]{1,0:T(8,128)(2,1)S(1)}, bf16[128,2048]{1,0:T(8,128)(2,1)S(1)}, u32[]{:S(2)}, u32[]{:S(2)}) collective-permute-start(bf16[128,2048]{1,0:T(8,128)(2,1)S(1)} %get-tuple-element.28.refs_0_), channel_id=1, source_target_pairs={{0,16},{1,17},{2,18},{3,19},{4,20},{5,21},{6,22},{7,23},{8,24},{9,... | collective-permute-start | bytes 1572872 | tf_op jit(solution)/shard_map/ppermute | solution.py:41
  20.6 7.7 %collective-permute-start.5 = (bf16[48,2048]{1,0:T(8,128)(2,1)S(1)}, bf16[48,2048]{1,0:T(8,128)(2,1)S(1)}, u32[]{:S(2)}, u32[]{:S(2)}) collective-permute-start(bf16[48,2048]{1,0:T(8,128)(2,1)S(1)} %collective-permute-done.refs_5_), channel_id=1, source_target_pairs={{0,2},{1,15},{2,4},{3,1},{4,6},{5,3},{6,8},{7,5},{8,10},{9,7},{10,... | collective-permute-start | bytes 589832 | tf_op jit(solution)/shard_map/ppermute | solution.py:41
  20.6 9.0 %collective-permute-start.6 = (bf16[48,2048]{1,0:T(8,128)(2,1)S(1)}, bf16[48,2048]{1,0:T(8,128)(2,1)}, u32[]{:S(2)}, u32[]{:S(2)}) collective-permute-start(bf16[48,2048]{1,0:T(8,128)(2,1)S(1)} %collective-permute-done.4.refs_6_), channel_id=1, source_target_pairs={{0,14},{1,3},{2,0},{3,5},{4,2},{5,7},{6,4},{7,9},{8,6},{9,11},{10,... | collective-permute-start | bytes 589832 | tf_op jit(solution)/shard_map/ppermute | solution.py:41
  26.2 8.2 %collective-permute-start.12 = (bf16[64,2048]{1,0:T(8,128)(2,1)S(1)}, bf16[64,2048]{1,0:T(8,128)(2,1)}, u32[]{:S(2)}, u32[]{:S(2)}) collective-permute-start(bf16[64,2048]{1,0:T(8,128)(2,1)S(1)} %collective-permute-done.8.refs_13_), channel_id=1, source_target_pairs={{0,2},{1,15},{2,4},{3,1},{4,6},{5,3},{6,8},{7,5},{8,10},{9,7},{10,... | collective-permute-start | bytes 786440 | tf_op jit(solution)/shard_map/ppermute | solution.py:41
  26.2 9.7 %collective-permute-start.13 = (bf16[64,2048]{1,0:T(8,128)(2,1)S(1)}, bf16[64,2048]{1,0:T(8,128)(2,1)}, u32[]{:S(2)}, u32[]{:S(2)}) collective-permute-start(bf16[64,2048]{1,0:T(8,128)(2,1)S(1)} %collective-permute-done.9.refs_14_), channel_id=1, source_target_pairs={{0,14},{1,3},{2,0},{3,5},{4,2},{5,7},{6,4},{7,9},{8,6},{9,11},{10,... | collective-permute-start | bytes 786440 | tf_op jit(solution)/shard_map/ppermute | solution.py:41
  29.6 7.5 %collective-permute-start.10 = (bf16[48,2048]{1,0:T(8,128)(2,1)S(1)}, bf16[48,2048]{1,0:T(8,128)(2,1)}, u32[]{:S(2)}, u32[]{:S(2)}) collective-permute-start(bf16[48,2048]{1,0:T(8,128)(2,1)S(1)} %collective-permute-done.5.refs_7_), channel_id=1, source_target_pairs={{0,2},{1,15},{2,4},{3,1},{4,6},{5,3},{6,8},{7,5},{8,10},{9,7},{10,... | collective-permute-start | bytes 589832 | tf_op jit(solution)/shard_map/ppermute | solution.py:41
  30.4 17.6 %collective-permute-start.2 = (bf16[128,2048]{1,0:T(8,128)(2,1)S(1)}, bf16[128,2048]{1,0:T(8,128)(2,1)S(1)}, u32[]{:S(2)}, u32[]{:S(2)}) collective-permute-start(bf16[128,2048]{1,0:T(8,128)(2,1)S(1)} %get-tuple-element.28.refs_0_), channel_id=1, source_target_pairs={{0,1},{1,0},{2,3},{3,2},{4,5},{5,4},{6,7},{7,6},{8,9},{9,8},{10,11... | collective-permute-start | bytes 1572872 | tf_op jit(solution)/shard_map/ppermute | solution.py:41
  34.4 7.9 %collective-permute-start.11 = (bf16[48,2048]{1,0:T(8,128)(2,1)}, bf16[48,2048]{1,0:T(8,128)(2,1)}, u32[]{:S(2)}, u32[]{:S(2)}) collective-permute-start(bf16[48,2048]{1,0:T(8,128)(2,1)} %collective-permute-done.6.refs_8_), channel_id=1, source_target_pairs={{0,14},{1,3},{2,0},{3,5},{4,2},{5,7},{6,4},{7,9},{8,6},{9,11},{10,... | collective-permute-start | bytes 589832 | tf_op jit(solution)/shard_map/ppermute | solution.py:41
  36.0 8.5 %collective-permute-start.15 = (bf16[64,2048]{1,0:T(8,128)(2,1)}, bf16[64,2048]{1,0:T(8,128)(2,1)}, u32[]{:S(2)}, u32[]{:S(2)}) collective-permute-start(bf16[64,2048]{1,0:T(8,128)(2,1)} %collective-permute-done.12.refs_15_), channel_id=1, source_target_pairs={{0,2},{1,15},{2,4},{3,1},{4,6},{5,3},{6,8},{7,5},{8,10},{9,7},{10,... | collective-permute-start | bytes 786440 | tf_op jit(solution)/shard_map/ppermute | solution.py:41
  37.1 9.6 %collective-permute-start.16 = (bf16[64,2048]{1,0:T(8,128)(2,1)}, bf16[64,2048]{1,0:T(8,128)(2,1)}, u32[]{:S(2)}, u32[]{:S(2)}) collective-permute-start(bf16[64,2048]{1,0:T(8,128)(2,1)} %collective-permute-done.13.refs_16_), channel_id=1, source_target_pairs={{0,14},{1,3},{2,0},{3,5},{4,2},{5,7},{6,4},{7,9},{8,6},{9,11},{10,... | collective-permute-start | bytes 786440 | tf_op jit(solution)/shard_map/ppermute | solution.py:41
  37.7 15.0 %collective-permute-start.3 = (bf16[128,2048]{1,0:T(8,128)(2,1)S(1)}, bf16[128,2048]{1,0:T(8,128)(2,1)S(1)}, u32[]{:S(2)}, u32[]{:S(2)}) collective-permute-start(bf16[128,2048]{1,0:T(8,128)(2,1)S(1)} %collective-permute-done.1.refs_1_), channel_id=1, source_target_pairs={{0,1},{1,0},{2,3},{3,2},{4,5},{5,4},{6,7},{7,6},{8,9},{9,8},{10,11... | collective-permute-start | bytes 1572872 | tf_op jit(solution)/shard_map/ppermute | solution.py:41
  44.5 5.1 %collective-permute-start.14 = (bf16[48,2048]{1,0:T(8,128)(2,1)}, bf16[48,2048]{1,0:T(8,128)(2,1)S(1)}, u32[]{:S(2)}, u32[]{:S(2)}) collective-permute-start(bf16[48,2048]{1,0:T(8,128)(2,1)} %collective-permute-done.10.refs_9_), channel_id=1, source_target_pairs={{0,2},{1,15},{2,4},{3,1},{4,6},{5,3},{6,8},{7,5},{8,10},{9,7},{10,... | collective-permute-start | bytes 589832 | tf_op jit(solution)/shard_map/ppermute | solution.py:41
  46.7 6.0 %collective-permute-start.17 = (bf16[64,2048]{1,0:T(8,128)(2,1)}, bf16[64,2048]{1,0:T(8,128)(2,1)S(1)}, u32[]{:S(2)}, u32[]{:S(2)}) collective-permute-start(bf16[64,2048]{1,0:T(8,128)(2,1)} %collective-permute-done.15.refs_17_), channel_id=1, source_target_pairs={{0,2},{1,15},{2,4},{3,1},{4,6},{5,3},{6,8},{7,5},{8,10},{9,7},{10,... | collective-permute-start | bytes 786440 | tf_op jit(solution)/shard_map/ppermute | solution.py:41
  47.7 17.0 %collective-permute-start.25 = (bf16[128,512]{1,0:T(8,128)(2,1)S(1)}, bf16[128,512]{1,0:T(8,128)(2,1)S(1)}, u32[]{:S(2)}, u32[]{:S(2)}) collective-permute-start(bf16[128,512]{1,0:T(8,128)(2,1)S(1)} %pad_maximum_fusion.5), channel_id=1, source_target_pairs={{0,16},{1,17},{2,18},{3,19},{4,20},{5,21},{6,22},{7,23},{8,24},{9,... | collective-permute-start | bytes 393224 | tf_op jit(solution)/shard_map/ppermute | solution.py:41
  60.0 8.1 %collective-permute-start.18 = (bf16[512,384]{1,0:T(8,128)(2,1)S(1)}, bf16[512,384]{1,0:T(8,128)(2,1)S(1)}, u32[]{:S(2)}, u32[]{:S(2)}) collective-permute-start(bf16[512,384]{1,0:T(8,128)(2,1)S(1)} %get-tuple-element.40), channel_id=1, source_target_pairs={{0,1},{1,0},{2,3},{3,2},{4,5},{5,4},{6,7},{7,6},{8,9},{9,8},{10,11... | collective-permute-start | bytes 1179656 | tf_op jit(solution)/shard_map/ppermute | solution.py:41
  64.8 7.8 %collective-permute-start.26 = (bf16[256,512]{1,0:T(8,128)(2,1)S(1)}, bf16[256,512]{1,0:T(8,128)(2,1)S(1)}, u32[]{:S(2)}, u32[]{:S(2)}) collective-permute-start(bf16[256,512]{1,0:T(8,128)(2,1)S(1)} %pad_maximum_fusion.4.refs_0_), channel_id=1, source_target_pairs={{0,2},{1,15},{2,4},{3,1},{4,6},{5,3},{6,8},{7,5},{8,10},{9,7},{10,... | collective-permute-start | bytes 786440 | tf_op jit(solution)/shard_map/ppermute | solution.py:41
  64.9 9.3 %collective-permute-start.27 = (bf16[256,512]{1,0:T(8,128)(2,1)S(1)}, bf16[256,512]{1,0:T(8,128)(2,1)S(1)}, u32[]{:S(2)}, u32[]{:S(2)}) collective-permute-start(bf16[256,512]{1,0:T(8,128)(2,1)S(1)} %pad_maximum_fusion.4.refs_0_), channel_id=1, source_target_pairs={{0,14},{1,3},{2,0},{3,5},{4,2},{5,7},{6,4},{7,9},{8,6},{9,11},{10,... | collective-permute-start | bytes 786440 | tf_op jit(solution)/shard_map/ppermute | solution.py:41
  66.3 10.9 %collective-permute-start.19 = (bf16[128,2048]{1,0:T(8,128)(2,1)S(1)}, bf16[128,2048]{1,0:T(8,128)(2,1)S(1)}, u32[]{:S(2)}, u32[]{:S(2)}) collective-permute-start(bf16[128,2048]{1,0:T(8,128)(2,1)S(1)} %get-tuple-element.41.own_ref), channel_id=1, source_target_pairs={{0,1},{1,0},{2,3},{3,2},{4,5},{5,4},{6,7},{7,6},{8,9},{9,8},{10,11... | collective-permute-start | bytes 1572872 | tf_op jit(solution)/shard_map/ppermute | solution.py:41
  74.2 8.2 %collective-permute-start.28 = (bf16[256,512]{1,0:T(8,128)(2,1)S(1)}, bf16[256,512]{1,0:T(8,128)(2,1)S(1)}, u32[]{:S(2)}, u32[]{:S(2)}) collective-permute-start(bf16[256,512]{1,0:T(8,128)(2,1)S(1)} %collective-permute-done.26.refs_1_), channel_id=1, source_target_pairs={{0,2},{1,15},{2,4},{3,1},{4,6},{5,3},{6,8},{7,5},{8,10},{9,7},{10,... | collective-permute-start | bytes 786440 | tf_op jit(solution)/shard_map/ppermute | solution.py:41
  74.2 15.4 %collective-permute-start.21 = (bf16[256,512]{1,0:T(8,128)(2,1)S(1)}, bf16[256,512]{1,0:T(8,128)(2,1)S(1)}, u32[]{:S(2)}, u32[]{:S(2)}) collective-permute-start(bf16[256,512]{1,0:T(8,128)(2,1)S(1)} %pad_maximum_fusion.2), channel_id=1, source_target_pairs={{0,2},{1,3},{2,4},{3,5},{4,6},{5,7},{6,8},{7,9},{8,10},{9,11},{10,... | collective-permute-start | bytes 786440 | tf_op jit(solution)/shard_map/ppermute | solution.py:41
  75.7 13.9 %collective-permute-start.22 = (bf16[256,512]{1,0:T(8,128)(2,1)}, bf16[256,512]{1,0:T(8,128)(2,1)S(1)}, u32[]{:S(2)}, u32[]{:S(2)}) collective-permute-start(bf16[256,512]{1,0:T(8,128)(2,1)} %pad_maximum_fusion.3), channel_id=1, source_target_pairs={{0,14},{1,15},{2,0},{3,1},{4,2},{5,3},{6,4},{7,5},{8,6},{9,7},{10,... | collective-permute-start | bytes 786440 | tf_op jit(solution)/shard_map/ppermute | solution.py:41
  76.9 11.4 %collective-permute-start.29 = (bf16[256,512]{1,0:T(8,128)(2,1)S(1)}, bf16[256,512]{1,0:T(8,128)(2,1)S(1)}, u32[]{:S(2)}, u32[]{:S(2)}) collective-permute-start(bf16[256,512]{1,0:T(8,128)(2,1)S(1)} %collective-permute-done.27.refs_2_), channel_id=1, source_target_pairs={{0,14},{1,3},{2,0},{3,5},{4,2},{5,7},{6,4},{7,9},{8,6},{9,11},{10,... | collective-permute-start | bytes 786440 | tf_op jit(solution)/shard_map/ppermute | solution.py:41
  79.3 10.4 %collective-permute-start.20 = (bf16[256,256]{1,0:T(8,128)(2,1)S(1)}, bf16[256,256]{1,0:T(8,128)(2,1)S(1)}, u32[]{:S(2)}, u32[]{:S(2)}) collective-permute-start(bf16[256,256]{1,0:T(8,128)(2,1)S(1)} %get-tuple-element.44), channel_id=1, source_target_pairs={{0,1},{1,0},{2,3},{3,2},{4,5},{5,4},{6,7},{7,6},{8,9},{9,8},{10,11... | collective-permute-start | bytes 393224 | tf_op jit(solution)/shard_map/ppermute | solution.py:41
  82.4 11.2 %collective-permute-start.30 = (bf16[256,512]{1,0:T(8,128)(2,1)S(1)}, bf16[256,512]{1,0:T(8,128)(2,1)S(1)}, u32[]{:S(2)}, u32[]{:S(2)}) collective-permute-start(bf16[256,512]{1,0:T(8,128)(2,1)S(1)} %collective-permute-done.28.refs_3_), channel_id=1, source_target_pairs={{0,2},{1,15},{2,4},{3,1},{4,6},{5,3},{6,8},{7,5},{8,10},{9,7},{10,... | collective-permute-start | bytes 786440 | tf_op jit(solution)/shard_map/ppermute | solution.py:41
  88.3 10.6 %collective-permute-start.31 = (bf16[256,512]{1,0:T(8,128)(2,1)S(1)}, bf16[256,512]{1,0:T(8,128)(2,1)S(1)}, u32[]{:S(2)}, u32[]{:S(2)}) collective-permute-start(bf16[256,512]{1,0:T(8,128)(2,1)S(1)} %collective-permute-done.29.refs_4_), channel_id=1, source_target_pairs={{0,14},{1,3},{2,0},{3,5},{4,2},{5,7},{6,4},{7,9},{8,6},{9,11},{10,... | collective-permute-start | bytes 786440 | tf_op jit(solution)/shard_map/ppermute | solution.py:41
  93.6 5.7 %collective-permute-start.32 = (bf16[256,512]{1,0:T(8,128)(2,1)S(1)}, bf16[256,512]{1,0:T(8,128)(2,1)S(1)}, u32[]{:S(2)}, u32[]{:S(2)}) collective-permute-start(bf16[256,512]{1,0:T(8,128)(2,1)S(1)} %collective-permute-done.30.refs_5_), channel_id=1, source_target_pairs={{0,2},{1,15},{2,4},{3,1},{4,6},{5,3},{6,8},{7,5},{8,10},{9,7},{10,... | collective-permute-start | bytes 786440 | tf_op jit(solution)/shard_map/ppermute | solution.py:41
  100.6 7.0 %collective-permute-start.33 = (bf16[128,2048]{1,0:T(8,128)(2,1)S(1)}, bf16[128,2048]{1,0:T(8,128)(2,1)S(1)}, u32[]{:S(2)}, u32[]{:S(2)}) collective-permute-start(bf16[128,2048]{1,0:T(8,128)(2,1)S(1)} %get-tuple-element.50), channel_id=1, source_target_pairs={{0,1},{1,0},{2,3},{3,2},{4,5},{5,4},{6,7},{7,6},{8,9},{9,8},{10,11... | collective-permute-start | bytes 1572872 | tf_op jit(solution)/shard_map/ppermute | solution.py:41
  (14 other events, 175.5 us)

commit v3 on v2

--- a/solution.py
+++ b/solution.py
@@ -37,13 +37,27 @@
 DOWN = pairs(lambda x, z, c: (x, (z - 1) % Z, c))
 
 
-def send(value, route):
-    return lax.ppermute(value, "seq", route)
+Y = 4
+Y_UP = [(d, (d & 4) | ((d + 1) & 3)) for d in range(2 * Y)]
+Y_DOWN = [(d, (d & 4) | ((d - 1) & 3)) for d in range(2 * Y)]
+
+
+def send(value, route, axis="seq"):
+    return lax.ppermute(value, axis, route)
 
 
 def rms_norm(values, gain_row):
     mean_square = jnp.mean(values * values, axis=-1, keepdims=True)
     return values * lax.rsqrt(mean_square + EPSILON) * gain_row
+
+
+def norm_kernel(index, hidden, gain, global_gain, normed_ref, blocks_ref):
+    normed = rms_norm(hidden[...].astype(jnp.float32), gain[...]).astype(jnp.bfloat16)
+    normed_ref[...] = normed
+    at = index[4] + lax.broadcasted_iota(jnp.int32, (TOK, 1), 0)
+    valid = (at < index[3]).astype(jnp.float32)
+    kept = (normed.astype(jnp.float32) * valid).reshape(TOK // BLOCK, BLOCK, normed.shape[1])
+    blocks_ref[...] = rms_norm(jnp.sum(kept, axis=1), global_gain[...]).astype(jnp.bfloat16)
 
 
 def dot_nt(left, right):
@@ -56,7 +70,7 @@
 SHARDS = len(STEPS)
 ROWS = 4 * TOK
 G_ROWS = Z * 16
-VMEM_LIMIT = 24 * 1024 * 1024
+VMEM_LIMIT = 32 * 1024 * 1024
 
 
 def z_of(z, core, way, hops):
@@ -66,11 +80,14 @@
 
 def project_kernel(index, *refs):
     blocks, firsts, seconds = refs[:4], refs[4 : 4 + SHARDS], refs[4 + SHARDS : 4 + 2 * SHARDS]
-    keep_ref, send_ref, g_rows, far_table, rows, table = refs[4 + 2 * SHARDS :]
+    keep_ref, send_ref, g_rows, far_table, out_rows, rows, table, sems = refs[4 + 2 * SHARDS :]
     z, core, x = index[0], index[1], index[2]
     low_core = core == 0
-    for ref, bx, bc in zip(blocks, (x, 1 - x, x, 1 - x), (core, core, 1 - core, 1 - core)):
-        rows[pl.ds(pl.multiple_of((bx * 2 + bc) * TOK, TOK), TOK), :] = ref[...]
+    copies = []
+    for i, (ref, bx, bc) in enumerate(zip(blocks, (x, 1 - x, x, 1 - x), (core, core, 1 - core, 1 - core))):
+        into = rows.at[pl.ds(pl.multiple_of((bx * 2 + bc) * TOK, TOK), TOK), :]
+        copies.append(pltpu.make_async_copy(ref, into, sems.at[i]))
+        copies[-1].start()
     for j, (way, hops) in enumerate(STEPS):
         at = z_of(z, core, way, hops) * HALF
         for kind in range(3):
@@ -81,6 +98,9 @@
             there = pl.multiple_of(base + at + 16, 16)
             into[pl.ds(there, 16), :] = seconds[j][kind * 16 : kind * 16 + 16, :]
         g_rows[j * 16 : j * 16 + 16, :] = seconds[j][48:64, :]
+        out_rows[j * 16 : j * 16 + 16, :] = seconds[j][64:80, :]
+    for copy in copies:
+        copy.wait()
     for kind in range(3):
         columns = table[...] if kind == 0 else far_table[kind * 256 - 256 : kind * 256, :]
         out = dot_nt(rows[...], columns).astype(jnp.bfloat16)
@@ -101,12 +121,25 @@
             send_ref[at, lanes] = jnp.where(low_core, out[:, 128:], out[:, :128])
 
 
-def attention_kernel(index, far_pos, keep_ref, got_ref, g_keep, g_got, below_ref, above_ref, out_ref):
+def edge_kernel(keep_ref, got_ref, low_ref, high_ref):
+    for seg in range(2):
+        into = slice(seg * TOK, seg * TOK + TOK)
+        for part, out in ((0, low_ref), (1, high_ref)):
+            at = slice((seg * 2 + part) * TOK, (seg * 2 + part + 1) * TOK)
+            out[into, :256] = keep_ref[at, 128:]
+            out[into, 256:] = got_ref[at, 128:]
+
+
+def attention_kernel(index, keep_ref, got_ref, g_keep, g_got, below_ref, above_ref, out_ref):
     z, x, limit = index[0], index[2], index[3]
     lane_head = (lax.broadcasted_iota(jnp.int32, (TOK, WIDE), 1) % 128) // HALF
     row = lax.broadcasted_iota(jnp.int32, (HEADS_LOCAL * TOK, TOK), 0) % TOK
     col = lax.broadcasted_iota(jnp.int32, (HEADS_LOCAL * TOK, TOK), 1)
-    far_ok = far_pos[...] < limit
+    far = lax.broadcasted_iota(jnp.int32, (1, 2 * G_ROWS), 1)
+    far_core, j, far_x, far_k = far >> 7, (far >> 4) & 7, (far >> 3) & 1, far & 7
+    delta = jnp.where((j & 1) == 1, -((j + 1) >> 1), j >> 1)
+    far_z = (z + delta * (1 - 2 * far_core)) & (Z - 1)
+    far_ok = ((far_x * Z + far_z) * C + far_core) * TOK + far_k * BLOCK < limit
     far_keys = jnp.concatenate([g_keep[:, :128], g_got[:, :128]], axis=1)
     far_values = jnp.concatenate([g_keep[:, 128:], g_got[:, 128:]], axis=1)
 
@@ -171,14 +204,24 @@
             out_ref[mine, part * TOK : (part + 1) * TOK, :] = context.astype(jnp.bfloat16)
 
 
-def output_kernel(index, own_ref, there_ref, *refs):
-    blocks, keep_ref, send_ref = refs[:SHARDS], refs[SHARDS], refs[SHARDS + 1]
-    z, core, x = index[0], index[1], index[2]
+def output_kernel(index, own_ref, there_ref, mine, prev, nxt, far_a, far_b, keep_ref, send_ref, table):
+    z, core, x, y = index[0], index[1], index[2], index[5]
     own, there = own_ref[...], there_ref[...]
-    full = jnp.concatenate([jnp.where(x == 0, own, there), jnp.where(x == 0, there, own)], axis=1)
+    for side in range(X):
+        mixed = jnp.where(x == side, own, there)
+        table[2 * side] = mixed[:, :128]
+        table[2 * side + 1] = mixed[:, 128:]
+    full = jnp.concatenate([table[(y + turn) & 3] for turn in (0, 3, 1, 2)], axis=1)
     for j, (way, hops) in enumerate(STEPS):
         zj = z_of(z, core, way, hops)
-        out = dot_nt(full, blocks[j][...])
+        here = j * 16
+        far = (far_a, here) if j < 4 else (far_b, here - 64)
+        weights = [
+            ref[at : at + 16, i * 256 : i * 256 + 256]
+            for ref, at in ((mine, here), (prev, here), (nxt, here), far)
+            for i in range(8)
+        ]
+        out = jnp.dot(full, jnp.concatenate(weights, axis=0), preferred_element_type=jnp.float32)
         keep = jnp.where(core == 0, out[:TOK], out[TOK:])
         sent = jnp.where(core == 0, out[TOK:], out[:TOK]).astype(jnp.bfloat16)
         for side in range(X):
@@ -187,12 +230,14 @@
             send_ref[:, lanes] = sent[:, side * 128 : side * 128 + 128]
 
 
-def on_chip(kernel, out_shape, flops, exps, args, scratch=()):
+def on_chip(kernel, out_shape, flops, exps, args, scratch=(), in_hbm=0):
     vmem = pl.BlockSpec(memory_space=pltpu.VMEM)
+    specs = [pl.BlockSpec(memory_space=pltpu.SMEM)] + [pl.BlockSpec(memory_space=pltpu.HBM)] * in_hbm
+    specs += [vmem] * (len(args) - len(specs))
     return pl.pallas_call(
         kernel,
         out_shape=out_shape,
-        in_specs=[pl.BlockSpec(memory_space=pltpu.SMEM)] + [vmem] * (len(args) - 1),
+        in_specs=specs,
         out_specs=jax.tree.map(lambda _: vmem, out_shape),
         scratch_shapes=list(scratch),
         compiler_params=pltpu.CompilerParams(vmem_limit_bytes=VMEM_LIMIT),
@@ -212,23 +257,39 @@
     x = me >> 4
     limit = length[0]
     bf16 = jnp.bfloat16
-    index = jnp.stack([z, core, x, limit]).astype(jnp.int32)
+    y = lax.axis_index("doc") & (Y - 1)
+    index = jnp.stack([z, core, x, limit, me * TOK, y]).astype(jnp.int32)
 
     mine = jnp.stack([w_query.T, w_key.T, w_value.T]).reshape(3, 2, 16, width)
     first = mine[:, 0].reshape(48, width)
 
-    normed = rms_norm(hidden_in.astype(jnp.float32), attn_gain).astype(bf16)
-    is_valid = (me * TOK + jnp.arange(TOK, dtype=jnp.int32) < limit).astype(jnp.float32)
-    block_sums = jnp.sum(
-        (normed.astype(jnp.float32) * is_valid[:, None]).reshape(TOK // BLOCK, BLOCK, width), axis=1
-    )
-    global_mine = rms_norm(block_sums, global_gain).astype(bf16)
+    normed, global_mine = on_chip(
+        norm_kernel,
+        (jax.ShapeDtypeStruct((TOK, width), bf16), jax.ShapeDtypeStruct((TOK // BLOCK, width), bf16)),
+        8 * TOK * width,
+        0,
+        (index, hidden_in, attn_gain[None], global_gain[None]),
+    )
     global_there = send(global_mine, OTHER_X)
+
+    split = w_out.reshape(X, 2, HEADS_LOCAL, 2, HALF, 64)
+
+    def slab(group):
+        at = (y >> 1, group, 0, (y & 1) ^ group, 0, 0)
+        return lax.dynamic_slice(split, at, (1, 1, HEADS_LOCAL, 1, HALF, 64)).reshape(128, 64)
+
+    kept = slab(core)
+    passed = send(slab(1 - core), OTHER_CORE)
+    chip = jnp.concatenate([jnp.where(core == 0, kept, passed), jnp.where(core == 0, passed, kept)], axis=1)
+    chip_there = send(chip, OTHER_X)
+    both = jnp.concatenate([jnp.where(x == 0, chip, chip_there), jnp.where(x == 0, chip_there, chip)], axis=1)
+
     second = jnp.concatenate(
         [
             mine[:, 1].reshape(48, width),
             jnp.where(x == 0, global_mine, global_there),
             jnp.where(x == 0, global_there, global_mine),
+            jnp.concatenate([both[i * 16 : i * 16 + 16] for i in range(8)], axis=1),
         ],
         axis=0,
     )
@@ -256,27 +317,29 @@
     beside_across = send(across, OTHER_CORE)
 
     half = jax.ShapeDtypeStruct((ROWS, 3 * 128), bf16)
-    keep, to_swap, g_own, far_table = on_chip(
+    keep, to_swap, g_own, far_table, out_own = on_chip(
         project_kernel,
         (
             half,
             half,
             jax.ShapeDtypeStruct((G_ROWS, width), bf16),
             jax.ShapeDtypeStruct((2 * Z * HALF, width), bf16),
+            jax.ShapeDtypeStruct((128, width), bf16),
         ),
         2 * ROWS * 768 * width,
         0,
         (index, normed, across, beside, beside_across, *firsts, *seconds),
-        (pltpu.VMEM((ROWS, width), bf16), pltpu.VMEM((Z * HALF, width), bf16)),
+        (pltpu.VMEM((ROWS, width), bf16), pltpu.VMEM((Z * HALF, width), bf16), pltpu.SemaphoreType.DMA((4,))),
+        in_hbm=4,
     )
     got = send(to_swap, OTHER_CORE)
     g_other = send(g_own, OTHER_CORE)
 
-    def edge(part):
-        tables = [t.reshape(2, 2, TOK, 384)[:, part, :, 128:384].reshape(2 * TOK, 256) for t in (keep, got)]
-        return jnp.concatenate(tables, axis=1)
-
-    low_edge, high_edge = edge(0), edge(1)
+    vmem = pl.BlockSpec(memory_space=pltpu.VMEM)
+    edge_shape = jax.ShapeDtypeStruct((2 * TOK, 512), bf16)
+    low_edge, high_edge = pl.pallas_call(
+        edge_kernel, out_shape=(edge_shape, edge_shape), in_specs=[vmem] * 2, out_specs=(vmem, vmem)
+    )(keep, got)
     below = send(high_edge, UP)
     above = send(low_edge, DOWN)
 
@@ -286,37 +349,19 @@
     )
     g_got = send(g_swap, OTHER_CORE)
 
-    deltas = jnp.asarray([-h if w == 0 else h for w, h in STEPS], jnp.int32)
-    g_core = jnp.arange(C, dtype=jnp.int32)[:, None, None, None]
-    g_z = (z + deltas[None, :, None, None] * (1 - 2 * g_core)) & (Z - 1)
-    g_x = jnp.arange(X, dtype=jnp.int32)[None, None, :, None]
-    g_k = jnp.arange(8, dtype=jnp.int32)[None, None, None, :]
-    far_pos = (((g_x * Z + g_z) * C + g_core) * TOK + g_k * BLOCK).reshape(1, 2 * G_ROWS)
+    to_pass = after(out_own, low_edge, high_edge)
+    out_prev = send(to_pass, Y_UP, "doc")
+    out_next = send(to_pass, Y_DOWN, "doc")
+    out_far_a = send(out_prev[:64], Y_UP, "doc")
+    out_far_b = send(out_next[64:], Y_DOWN, "doc")
+
     context = on_chip(
         attention_kernel,
         jax.ShapeDtypeStruct((2, 2 * TOK, WIDE), bf16),
         4 * 4 * TOK * 640 * WIDE * 4,
         4 * 4 * TOK * 640,
-        (index, far_pos, keep, got, g_keep, g_got, below, above),
-    )
-
-    out_t = after(w_out, two[0, 1], two[1, 1]).T.reshape(64, X, 2, HEADS_LOCAL, 2, HALF)
-    out_t = jnp.transpose(out_t, (0, 2, 1, 4, 3, 5))
-    group_0 = out_t[:, 0].reshape(64, 2 * WIDE)
-    group_1 = out_t[:, 1, :, ::-1].reshape(64, 2 * WIDE)
-    kept = jnp.where(core == 0, group_0, group_1)
-    passed = send(jnp.where(core == 0, group_1, group_0), OTHER_CORE)
-    chip = jnp.concatenate([jnp.where(core == 0, kept, passed), jnp.where(core == 0, passed, kept)], axis=0)
-    chip_there = send(chip, OTHER_X)
-    both = jnp.concatenate([jnp.where(x == 0, chip, chip_there), jnp.where(x == 0, chip_there, chip)], axis=0)
-    out_blocks = {(0, 0): both}
-    ahead = behind = after(both, one[0, 4], two[0, 4])
-    for step in range(1, 5):
-        if step == 2:
-            ahead, behind = lax.optimization_barrier((ahead, behind, low_edge, high_edge))[:2]
-        out_blocks[0, step] = ahead = send(ahead, AHEAD)
-        if step < 4:
-            out_blocks[1, step] = behind = send(behind, BEHIND)
+        (index, keep, got, g_keep, g_got, below, above),
+    )
 
     there = send(context[1], OTHER_X)
     kept_part, sent_part = on_chip(
@@ -324,7 +369,8 @@
         (jax.ShapeDtypeStruct((TOK, width), jnp.float32), jax.ShapeDtypeStruct((TOK, width), bf16)),
         2 * 256 * 512 * width,
         0,
-        (index, context[0], there, *[out_blocks[s] for s in STEPS]),
+        (index, context[0], there, out_own, out_prev, out_next, out_far_a, out_far_b),
+        (pltpu.VMEM((4, 2 * TOK, 128), bf16),),
     )
     return (kept_part + send(sent_part, OTHER_CORE).astype(jnp.float32)).astype(bf16)
 

time: 109 us -> 113 us (1.037)
  waiting for transfers between devices: 28.8 us -> 43.7 us
  other arithmetic: 10 us -> 2.24 us
  Pallas kernels: 10.8 us -> 14.3 us
  local copies, waits for them, and re-layouts: 7.9 us -> 4.44 us
  starting transfers between devices: 50 us -> 46.7 us
    ppermute x34 -> x31, waiting for transfers between devices: 28.8 us -> 43.7 us  [send(): return lax.ppermute(value, axis, route)]
    pallas_call x4 -> x6, Pallas kernels: 10.8 us -> 14.3 us  [the longest x5 12.3 us: on_chip(): pl.pallas_call(kernel, out_shape=out_shape, in_specs=specs, out_specs=jax...]
    ppermute x34 -> x31, starting transfers between devices: 50 us -> 46.7 us  [send(): return lax.ppermute(value, axis, route)]
    reduce_sum x3 -> x0, other arithmetic: 3 us -> none  [the longest x1 1.64 us: per_device(): jnp.sum((normed.astype(jnp.float32) * is_valid[:, None]).reshape(TOK // B...]
    unnamed x24 -> x11, local copies, waits for them, and re-layouts: 4.43 us -> 4.25 us
  transfers between devices with their start and end apart: 34 -> 31, of which waited for: 12 -> 12; matrix products, arithmetic and copies ran while one was open for 8% -> 1% of each run, Pallas kernels for 9% -> 9%
where the time goes in v3:
time: 113 us; the launch traced here: 112 us
  starting transfers between devices  46.7 us (41%)
  waiting for transfers between devices  43.7 us (39%)
  Pallas kernels  14.3 us (13%)
  local copies, waits for them, and re-layouts  4.44 us (4%)
  other arithmetic  2.24 us (2%)
    ppermute x31, starting transfers between devices, send(): return lax.ppermute(value, axis, route)  46.7 us
    ppermute x31, waiting for transfers between devices, send(): return lax.ppermute(value, axis, route)  43.7 us
    pallas_call x5, Pallas kernels, on_chip(): pl.pallas_call(kernel, out_shape=out_shape, in_specs=specs, out_specs=jax...  12.3 us
    unnamed x11, local copies, waits for them, and re-layouts  4.25 us
  transfers between devices with their start and end apart: 31, of which 12 were waited for; matrix products, arithmetic and copies ran while one was open for 1% of the time, Pallas kernels for 9%

profile of v3, /device:TPU:1, one launch (start us, length us, event | category | flops | bytes accessed | tf_op | source)
XLA Modules:
  0.0 112.3 jit_solution(12292646451071566451)
XLA Ops:
  1.1 3.3 %collective-permute-start.8 = (bf16[128,64]{1,0:T(8,128)(2,1)S(1)}, bf16[128,64]{1,0:T(8,128)(2,1)S(1)}, u32[]{:S(2)}, u32[]{:S(2)}) collective-permute-start(bf16[128,64]{1,0:T(8,128)(2,1)S(1)} %bitcast.43), channel_id=1, source_target_pairs={{0,1},{1,0},{2,3},{3,2},{4,5},{5,4},{6,7},{7,6},{8,9},{9,8},{10,11... | collective-permute-start | bytes 49160 | tf_op jit(solution)/shard_map/ppermute | solution.py:46
  10.1 1.5 %collective-permute-start.9 = (bf16[128,128]{1,0:T(8,128)(2,1)S(1)}, bf16[128,128]{1,0:T(8,128)(2,1)S(1)}, u32[]{:S(2)}, u32[]{:S(2)}) collective-permute-start(bf16[128,128]{1,0:T(8,128)(2,1)S(1)} %pad_maximum_fusion.2), channel_id=1, source_target_pairs={{0,16},{1,17},{2,18},{3,19},{4,20},{5,21},{6,22},{7,23},{8,24},{9,... | collective-permute-start | bytes 98312 | tf_op jit(solution)/shard_map/ppermute | solution.py:46
  11.7 1.3 %collective-permute-done.9 = bf16[128,128]{1,0:T(8,128)(2,1)S(1)} collective-permute-done((bf16[128,128]{1,0:T(8,128)(2,1)S(1)}, bf16[128,128]{1,0:T(8,128)(2,1)S(1)}, u32[]{:S(2)}, u32[]{:S(2)}) %collective-permute-start.9) | collective-permute-done | bytes 32800 | tf_op jit(solution)/shard_map/ppermute | solution.py:46
  14.4 4.0 %collective-permute-start.10 = (bf16[80,2048]{1,0:T(8,128)(2,1)S(1)}, bf16[80,2048]{1,0:T(8,128)(2,1)S(1)}, u32[]{:S(2)}, u32[]{:S(2)}) collective-permute-start(bf16[80,2048]{1,0:T(8,128)(2,1)S(1)} %pad_maximum_fusion.1.refs_12_), channel_id=1, source_target_pairs={{0,2},{1,15},{2,4},{3,1},{4,6},{5,3},{6,8},{7,5},{8,10},{9,7},{10,... | collective-permute-start | bytes 983048 | tf_op jit(solution)/shard_map/ppermute | solution.py:46
  18.4 1.4 %collective-permute-start = (bf16[48,2048]{1,0:T(8,128)(2,1)S(1)}, bf16[48,2048]{1,0:T(8,128)(2,1)S(1)}, u32[]{:S(2)}, u32[]{:S(2)}) collective-permute-start(bf16[48,2048]{1,0:T(8,128)(2,1)S(1)} %bitcast.33), channel_id=1, source_target_pairs={{0,2},{1,15},{2,4},{3,1},{4,6},{5,3},{6,8},{7,5},{8,10},{9,7},{10,... | collective-permute-start | bytes 589832 | tf_op jit(solution)/shard_map/ppermute | solution.py:46
  19.9 8.4 %collective-permute-done.refs_5_ = bf16[48,2048]{1,0:T(8,128)(2,1)S(1)} collective-permute-done((bf16[48,2048]{1,0:T(8,128)(2,1)S(1)}, bf16[48,2048]{1,0:T(8,128)(2,1)S(1)}, u32[]{:S(2)}, u32[]{:S(2)}) %collective-permute-start) | collective-permute-done | bytes 196640 | tf_op jit(solution)/shard_map/ppermute | solution.py:46
  28.5 3.5 %collective-permute-start.14 = (bf16[80,2048]{1,0:T(8,128)(2,1)S(1)}, bf16[80,2048]{1,0:T(8,128)(2,1)S(1)}, u32[]{:S(2)}, u32[]{:S(2)}) collective-permute-start(bf16[80,2048]{1,0:T(8,128)(2,1)S(1)} %collective-permute-done.10.refs_13_), channel_id=1, source_target_pairs={{0,2},{1,15},{2,4},{3,1},{4,6},{5,3},{6,8},{7,5},{8,10},{9,7},{10,... | collective-permute-start | bytes 983048 | tf_op jit(solution)/shard_map/ppermute | solution.py:46
  32.0 2.7 %collective-permute-start.5 = (bf16[48,2048]{1,0:T(8,128)(2,1)S(1)}, bf16[48,2048]{1,0:T(8,128)(2,1)S(1)}, u32[]{:S(2)}, u32[]{:S(2)}) collective-permute-start(bf16[48,2048]{1,0:T(8,128)(2,1)S(1)} %collective-permute-done.refs_5_), channel_id=1, source_target_pairs={{0,2},{1,15},{2,4},{3,1},{4,6},{5,3},{6,8},{7,5},{8,10},{9,7},{10,... | collective-permute-start | bytes 589832 | tf_op jit(solution)/shard_map/ppermute | solution.py:46
  34.7 5.2 %collective-permute-done.5.refs_7_ = bf16[48,2048]{1,0:T(8,128)(2,1)S(1)} collective-permute-done((bf16[48,2048]{1,0:T(8,128)(2,1)S(1)}, bf16[48,2048]{1,0:T(8,128)(2,1)S(1)}, u32[]{:S(2)}, u32[]{:S(2)}) %collective-permute-start.5) | collective-permute-done | bytes 196640 | tf_op jit(solution)/shard_map/ppermute | solution.py:46
  39.9 6.4 %collective-permute-done.6.refs_8_ = bf16[48,2048]{1,0:T(8,128)(2,1)S(1)} collective-permute-done((bf16[48,2048]{1,0:T(8,128)(2,1)S(1)}, bf16[48,2048]{1,0:T(8,128)(2,1)S(1)}, u32[]{:S(2)}, u32[]{:S(2)}) %collective-permute-start.6) | collective-permute-done | bytes 196640 | tf_op jit(solution)/shard_map/ppermute | solution.py:46
  47.9 1.4 %collective-permute-start.13 = (bf16[48,2048]{1,0:T(8,128)(2,1)S(1)}, bf16[48,2048]{1,0:T(8,128)(2,1)S(1)}, u32[]{:S(2)}, u32[]{:S(2)}) collective-permute-start(bf16[48,2048]{1,0:T(8,128)(2,1)S(1)} %collective-permute-done.6.refs_8_), channel_id=1, source_target_pairs={{0,14},{1,3},{2,0},{3,5},{4,2},{5,7},{6,4},{7,9},{8,6},{9,11},{10,... | collective-permute-start | bytes 589832 | tf_op jit(solution)/shard_map/ppermute | solution.py:46
  49.2 1.6 %collective-permute-done.12.refs_9_ = bf16[48,2048]{1,0:T(8,128)(2,1)S(1)} collective-permute-done((bf16[48,2048]{1,0:T(8,128)(2,1)S(1)}, bf16[48,2048]{1,0:T(8,128)(2,1)S(1)}, u32[]{:S(2)}, u32[]{:S(2)}) %collective-permute-start.12) | collective-permute-done | bytes 196640 | tf_op jit(solution)/shard_map/ppermute | solution.py:46
  50.8 5.8 %collective-permute-start.2 = (bf16[128,2048]{1,0:T(8,128)(2,1)S(1)}, bf16[128,2048]{1,0:T(8,128)(2,1)S(1)}, u32[]{:S(2)}, u32[]{:S(2)}) collective-permute-start(bf16[128,2048]{1,0:T(8,128)(2,1)S(1)} %get-tuple-element.31.refs_0_), channel_id=1, source_target_pairs={{0,1},{1,0},{2,3},{3,2},{4,5},{5,4},{6,7},{7,6},{8,9},{9,8},{10,11... | collective-permute-start | bytes 1572872 | tf_op jit(solution)/shard_map/ppermute | solution.py:46
  56.6 3.6 %collective-permute-done.13.refs_10_ = bf16[48,2048]{1,0:T(8,128)(2,1)S(1)} collective-permute-done((bf16[48,2048]{1,0:T(8,128)(2,1)S(1)}, bf16[48,2048]{1,0:T(8,128)(2,1)S(1)}, u32[]{:S(2)}, u32[]{:S(2)}) %collective-permute-start.13) | collective-permute-done | bytes 196640 | tf_op jit(solution)/shard_map/ppermute | solution.py:46
  60.2 1.9 %collective-permute-start.19 = (bf16[80,2048]{1,0:T(8,128)(2,1)S(1)}, bf16[80,2048]{1,0:T(8,128)(2,1)S(1)}, u32[]{:S(2)}, u32[]{:S(2)}) collective-permute-start(bf16[80,2048]{1,0:T(8,128)(2,1)S(1)} %collective-permute-done.17.refs_17_), channel_id=1, source_target_pairs={{0,2},{1,15},{2,4},{3,1},{4,6},{5,3},{6,8},{7,5},{8,10},{9,7},{10,... | collective-permute-start | bytes 983048 | tf_op jit(solution)/shard_map/ppermute | solution.py:46
  62.2 6.4 %collective-permute-done.16.refs_11_ = bf16[48,2048]{1,0:T(8,128)(2,1)S(1)} collective-permute-done((bf16[48,2048]{1,0:T(8,128)(2,1)S(1)}, bf16[48,2048]{1,0:T(8,128)(2,1)S(1)}, u32[]{:S(2)}, u32[]{:S(2)}) %collective-permute-start.16) | collective-permute-done | bytes 196640 | tf_op jit(solution)/shard_map/ppermute | solution.py:46
  68.6 2.8 %shard_map.83 = (bf16[512,384]{1,0:T(8,128)(2,1)S(1)}, bf16[512,384]{1,0:T(8,128)(2,1)S(1)}, bf16[128,2048]{1,0:T(8,128)(2,1)}, bf16[512,2048]{1,0:T(8,128)(2,1)S(1)}, bf16[128,2048]{1,0:T(8,128)(2,1)S(1)}) custom-call(s32[6]{0:T(128)S(1)} %stack.35.index, bf16[128,2048]{1,0:T(8,128)(2,1)S(1)} %get-tuple-element.31.refs_0_, ...), custom_call_target="tpu_custom_call" | custom-call | flops 1610612736 | bytes 4194304 | tf_op jit(solution)/shard_map/pallas_call | solution.py:237
  72.2 4.0 %collective-permute-start.20 = (bf16[512,384]{1,0:T(8,128)(2,1)S(1)}, bf16[512,384]{1,0:T(8,128)(2,1)}, u32[]{:S(2)}, u32[]{:S(2)}) collective-permute-start(bf16[512,384]{1,0:T(8,128)(2,1)S(1)} %get-tuple-element.44), channel_id=1, source_target_pairs={{0,1},{1,0},{2,3},{3,2},{4,5},{5,4},{6,7},{7,6},{8,9},{9,8},{10,11... | collective-permute-start | bytes 1179656 | tf_op jit(solution)/shard_map/ppermute | solution.py:46
  76.1 2.0 %collective-permute-done.20.got_ref = bf16[512,384]{1,0:T(8,128)(2,1)} collective-permute-done((bf16[512,384]{1,0:T(8,128)(2,1)S(1)}, bf16[512,384]{1,0:T(8,128)(2,1)}, u32[]{:S(2)}, u32[]{:S(2)}) %collective-permute-start.20) | collective-permute-done | bytes 393248 | tf_op jit(solution)/shard_map/ppermute | solution.py:46
  78.2 2.0 %shard_map.85 = (bf16[256,512]{1,0:T(8,128)(2,1)}, bf16[256,512]{1,0:T(8,128)(2,1)}) custom-call(bf16[512,384]{1,0:T(8,128)(2,1)} %copy-done.1, bf16[512,384]{1,0:T(8,128)(2,1)} %collective-permute-done.20.got_ref), custom_call_target="tpu_custom_call" | custom-call | tf_op jit(solution)/shard_map/pallas_call | solution.py:340
  80.1 2.7 %collective-permute-start.27 = (bf16[128,2048]{1,0:T(8,128)(2,1)S(1)}, bf16[128,2048]{1,0:T(8,128)(2,1)S(1)}, u32[]{:S(2)}, u32[]{:S(2)}) collective-permute-start(bf16[128,2048]{1,0:T(8,128)(2,1)S(1)} %get-tuple-element.52.mine), channel_id=1, source_target_pairs={{0,96},{32,0},{64,32},{96,64},{128,224},{160,128},{192,160},{224,1... | collective-permute-start | bytes 1572872 | tf_op jit(solution)/shard_map/ppermute | solution.py:46
  82.9 2.7 %collective-permute-start.24 = (bf16[256,512]{1,0:T(8,128)(2,1)}, bf16[256,512]{1,0:T(8,128)(2,1)S(1)}, u32[]{:S(2)}, u32[]{:S(2)}) collective-permute-start(bf16[256,512]{1,0:T(8,128)(2,1)} %get-tuple-element.50), channel_id=1, source_target_pairs={{0,14},{1,15},{2,0},{3,1},{4,2},{5,3},{6,4},{7,5},{8,6},{9,7},{10,... | collective-permute-start | bytes 786440 | tf_op jit(solution)/shard_map/ppermute | solution.py:46
  85.5 2.6 %shard_map.84 = (bf16[256,256]{1,0:T(8,128)(2,1)S(1)}, bf16[256,256]{1,0:T(8,128)(2,1)S(1)}) custom-call(s32[6]{0:T(128)S(1)} %stack.35.index, bf16[128,2048]{1,0:T(8,128)(2,1)} %get-tuple-element.45.own_ref, bf16[128,2048]{1,0:T(8,128)(2,1)S(1)} %collective-permute-done.21.other_ref, bf16[512,2048]{1,0:T(8,128)(2,1)S(1)} %get-tuple-element.46.table), custom_call_target="tpu_custom_call" | custom-call | flops 536870912 | bytes 4194304 | tf_op jit(solution)/shard_map/pallas_call | solution.py:237
  88.1 1.5 %collective-permute-start.22 = (bf16[256,256]{1,0:T(8,128)(2,1)S(1)}, bf16[256,256]{1,0:T(8,128)(2,1)S(1)}, u32[]{:S(2)}, u32[]{:S(2)}) collective-permute-start(bf16[256,256]{1,0:T(8,128)(2,1)S(1)} %get-tuple-element.48), channel_id=1, source_target_pairs={{0,1},{1,0},{2,3},{3,2},{4,5},{5,4},{6,7},{7,6},{8,9},{9,8},{10,11... | collective-permute-start | bytes 393224 | tf_op jit(solution)/shard_map/ppermute | solution.py:46
  89.7 1.8 %collective-permute-done.23.below_ref = bf16[256,512]{1,0:T(8,128)(2,1)S(1)} collective-permute-done((bf16[256,512]{1,0:T(8,128)(2,1)}, bf16[256,512]{1,0:T(8,128)(2,1)S(1)}, u32[]{:S(2)}, u32[]{:S(2)}) %collective-permute-start.23) | collective-permute-done | bytes 262176 | tf_op jit(solution)/shard_map/ppermute | solution.py:46
  91.5 4.5 %shard_map.86 = bf16[2,256,256]{2,1,0:T(8,128)(2,1)S(1)} custom-call(s32[6]{0:T(128)S(1)} %stack.35.index, bf16[512,384]{1,0:T(8,128)(2,1)S(1)} %copy-done.2, bf16[512,384]{1,0:T(8,128)(2,1)} %collective-permute-done.20.got_ref, bf16[256,256]{1,0:T(8,128)(2,1)S(1)} %get-tuple-element.47.g_keep, bf16[256,256]{1,0:T(8,128)(2,1)S(1)} %collective-permute-done.22.g_got, ...), custom_call_target="tpu_custom_call" | custom-call | flops 1342177280 | bytes 4194304 | tf_op jit(solution)/shard_map/pallas_call | solution.py:237
  96.0 2.4 %collective-permute-start.29 = (bf16[64,2048]{1,0:T(8,128)(2,1)S(1)}, bf16[64,2048]{1,0:T(8,128)(2,1)S(1)}, u32[]{:S(2)}, u32[]{:S(2)}) collective-permute-start(bf16[64,2048]{1,0:T(8,128)(2,1)S(1)} %slice.75), channel_id=1, source_target_pairs={{0,96},{32,0},{64,32},{96,64},{128,224},{160,128},{192,160},{224,1... | collective-permute-start | bytes 786440 | tf_op jit(solution)/shard_map/ppermute | solution.py:46
  98.6 1.4 %collective-permute-start.25 = (bf16[256,256]{1,0:T(8,128)(2,1)S(1)}, bf16[256,256]{1,0:T(8,128)(2,1)S(1)}, u32[]{:S(2)}, u32[]{:S(2)}) collective-permute-start(bf16[256,256]{1,0:T(8,128)(2,1)S(1)} %get-tuple-element.57), channel_id=1, source_target_pairs={{0,16},{1,17},{2,18},{3,19},{4,20},{5,21},{6,22},{7,23},{8,24},{9,... | collective-permute-start | bytes 393224 | tf_op jit(solution)/shard_map/ppermute | solution.py:46
  100.0 2.8 %collective-permute-done.25.there_ref = bf16[256,256]{1,0:T(8,128)(2,1)S(1)} collective-permute-done((bf16[256,256]{1,0:T(8,128)(2,1)S(1)}, bf16[256,256]{1,0:T(8,128)(2,1)S(1)}, u32[]{:S(2)}, u32[]{:S(2)}) %collective-permute-start.25) | collective-permute-done | bytes 131104 | tf_op jit(solution)/shard_map/ppermute | solution.py:46
  102.8 2.6 %collective-permute-done.28.far_a = bf16[64,2048]{1,0:T(8,128)(2,1)S(1)} collective-permute-done((bf16[64,2048]{1,0:T(8,128)(2,1)S(1)}, bf16[64,2048]{1,0:T(8,128)(2,1)S(1)}, u32[]{:S(2)}, u32[]{:S(2)}) %collective-permute-start.28) | collective-permute-done | bytes 262176 | tf_op jit(solution)/shard_map/ppermute | solution.py:46
  106.7 3.1 %collective-permute-start.30 = (bf16[128,2048]{1,0:T(8,128)(2,1)S(1)}, bf16[128,2048]{1,0:T(8,128)(2,1)S(1)}, u32[]{:S(2)}, u32[]{:S(2)}) collective-permute-start(bf16[128,2048]{1,0:T(8,128)(2,1)S(1)} %get-tuple-element.54), channel_id=1, source_target_pairs={{0,1},{1,0},{2,3},{3,2},{4,5},{5,4},{6,7},{7,6},{8,9},{9,8},{10,11... | collective-permute-start | bytes 1572872 | tf_op jit(solution)/shard_map/ppermute | solution.py:46
  109.8 1.5 %collective-permute-done.30 = bf16[128,2048]{1,0:T(8,128)(2,1)S(1)} collective-permute-done((bf16[128,2048]{1,0:T(8,128)(2,1)S(1)}, bf16[128,2048]{1,0:T(8,128)(2,1)S(1)}, u32[]{:S(2)}, u32[]{:S(2)}) %collective-permute-start.30) | collective-permute-done | bytes 524320 | tf_op jit(solution)/shard_map/ppermute | solution.py:46
  (68 shorter events, 12.5 us)
Async XLA Ops:
  1.1 8.9 %collective-permute-start.8 = (bf16[128,64]{1,0:T(8,128)(2,1)S(1)}, bf16[128,64]{1,0:T(8,128)(2,1)S(1)}, u32[]{:S(2)}, u32[]{:S(2)}) collective-permute-start(bf16[128,64]{1,0:T(8,128)(2,1)S(1)} %bitcast.43), channel_id=1, source_target_pairs={{0,1},{1,0},{2,3},{3,2},{4,5},{5,4},{6,7},{7,6},{8,9},{9,8},{10,11... | collective-permute-start | bytes 49160 | tf_op jit(solution)/shard_map/ppermute | solution.py:46
  8.8 2.9 %collective-permute-start.7 = (bf16[8,2048]{1,0:T(8,128)(2,1)S(1)}, bf16[8,2048]{1,0:T(8,128)(2,1)S(1)}, u32[]{:S(2)}, u32[]{:S(2)}) collective-permute-start(bf16[8,2048]{1,0:T(8,128)(2,1)S(1)} %get-tuple-element.34), channel_id=1, source_target_pairs={{0,16},{1,17},{2,18},{3,19},{4,20},{5,21},{6,22},{7,23},{8,24},{9,... | collective-permute-start | bytes 98312 | tf_op jit(solution)/shard_map/ppermute | solution.py:46
  10.1 2.9 %collective-permute-start.9 = (bf16[128,128]{1,0:T(8,128)(2,1)S(1)}, bf16[128,128]{1,0:T(8,128)(2,1)S(1)}, u32[]{:S(2)}, u32[]{:S(2)}) collective-permute-start(bf16[128,128]{1,0:T(8,128)(2,1)S(1)} %pad_maximum_fusion.2), channel_id=1, source_target_pairs={{0,16},{1,17},{2,18},{3,19},{4,20},{5,21},{6,22},{7,23},{8,24},{9,... | collective-permute-start | bytes 98312 | tf_op jit(solution)/shard_map/ppermute | solution.py:46
  13.2 15.3 %collective-permute-start.11 = (bf16[80,2048]{1,0:T(8,128)(2,1)S(1)}, bf16[80,2048]{1,0:T(8,128)(2,1)S(1)}, u32[]{:S(2)}, u32[]{:S(2)}) collective-permute-start(bf16[80,2048]{1,0:T(8,128)(2,1)S(1)} %pad_maximum_fusion.1.refs_12_), channel_id=1, source_target_pairs={{0,14},{1,3},{2,0},{3,5},{4,2},{5,7},{6,4},{7,9},{8,6},{9,11},{10,... | collective-permute-start | bytes 983048 | tf_op jit(solution)/shard_map/ppermute | solution.py:46
  14.4 14.2 %collective-permute-start.10 = (bf16[80,2048]{1,0:T(8,128)(2,1)S(1)}, bf16[80,2048]{1,0:T(8,128)(2,1)S(1)}, u32[]{:S(2)}, u32[]{:S(2)}) collective-permute-start(bf16[80,2048]{1,0:T(8,128)(2,1)S(1)} %pad_maximum_fusion.1.refs_12_), channel_id=1, source_target_pairs={{0,2},{1,15},{2,4},{3,1},{4,6},{5,3},{6,8},{7,5},{8,10},{9,7},{10,... | collective-permute-start | bytes 983048 | tf_op jit(solution)/shard_map/ppermute | solution.py:46
  18.4 9.9 %collective-permute-start = (bf16[48,2048]{1,0:T(8,128)(2,1)S(1)}, bf16[48,2048]{1,0:T(8,128)(2,1)S(1)}, u32[]{:S(2)}, u32[]{:S(2)}) collective-permute-start(bf16[48,2048]{1,0:T(8,128)(2,1)S(1)} %bitcast.33), channel_id=1, source_target_pairs={{0,2},{1,15},{2,4},{3,1},{4,6},{5,3},{6,8},{7,5},{8,10},{9,7},{10,... | collective-permute-start | bytes 589832 | tf_op jit(solution)/shard_map/ppermute | solution.py:46
  19.8 8.7 %collective-permute-start.4 = (bf16[48,2048]{1,0:T(8,128)(2,1)S(1)}, bf16[48,2048]{1,0:T(8,128)(2,1)S(1)}, u32[]{:S(2)}, u32[]{:S(2)}) collective-permute-start(bf16[48,2048]{1,0:T(8,128)(2,1)S(1)} %bitcast.34), channel_id=1, source_target_pairs={{0,14},{1,3},{2,0},{3,5},{4,2},{5,7},{6,4},{7,9},{8,6},{9,11},{10,... | collective-permute-start | bytes 589832 | tf_op jit(solution)/shard_map/ppermute | solution.py:46
  28.3 28.4 %collective-permute-start.1 = (bf16[128,2048]{1,0:T(8,128)(2,1)S(1)}, bf16[128,2048]{1,0:T(8,128)(2,1)S(1)}, u32[]{:S(2)}, u32[]{:S(2)}) collective-permute-start(bf16[128,2048]{1,0:T(8,128)(2,1)S(1)} %get-tuple-element.31.refs_0_), channel_id=1, source_target_pairs={{0,16},{1,17},{2,18},{3,19},{4,20},{5,21},{6,22},{7,23},{8,24},{9,... | collective-permute-start | bytes 1572872 | tf_op jit(solution)/shard_map/ppermute | solution.py:46
  28.5 17.8 %collective-permute-start.14 = (bf16[80,2048]{1,0:T(8,128)(2,1)S(1)}, bf16[80,2048]{1,0:T(8,128)(2,1)S(1)}, u32[]{:S(2)}, u32[]{:S(2)}) collective-permute-start(bf16[80,2048]{1,0:T(8,128)(2,1)S(1)} %collective-permute-done.10.refs_13_), channel_id=1, source_target_pairs={{0,2},{1,15},{2,4},{3,1},{4,6},{5,3},{6,8},{7,5},{8,10},{9,7},{10,... | collective-permute-start | bytes 983048 | tf_op jit(solution)/shard_map/ppermute | solution.py:46
  32.0 14.3 %collective-permute-start.15 = (bf16[80,2048]{1,0:T(8,128)(2,1)S(1)}, bf16[80,2048]{1,0:T(8,128)(2,1)S(1)}, u32[]{:S(2)}, u32[]{:S(2)}) collective-permute-start(bf16[80,2048]{1,0:T(8,128)(2,1)S(1)} %collective-permute-done.11.refs_14_), channel_id=1, source_target_pairs={{0,14},{1,3},{2,0},{3,5},{4,2},{5,7},{6,4},{7,9},{8,6},{9,11},{10,... | collective-permute-start | bytes 983048 | tf_op jit(solution)/shard_map/ppermute | solution.py:46
  32.0 7.8 %collective-permute-start.5 = (bf16[48,2048]{1,0:T(8,128)(2,1)S(1)}, bf16[48,2048]{1,0:T(8,128)(2,1)S(1)}, u32[]{:S(2)}, u32[]{:S(2)}) collective-permute-start(bf16[48,2048]{1,0:T(8,128)(2,1)S(1)} %collective-permute-done.refs_5_), channel_id=1, source_target_pairs={{0,2},{1,15},{2,4},{3,1},{4,6},{5,3},{6,8},{7,5},{8,10},{9,7},{10,... | collective-permute-start | bytes 589832 | tf_op jit(solution)/shard_map/ppermute | solution.py:46
  34.7 11.6 %collective-permute-start.6 = (bf16[48,2048]{1,0:T(8,128)(2,1)S(1)}, bf16[48,2048]{1,0:T(8,128)(2,1)S(1)}, u32[]{:S(2)}, u32[]{:S(2)}) collective-permute-start(bf16[48,2048]{1,0:T(8,128)(2,1)S(1)} %collective-permute-done.4.refs_6_), channel_id=1, source_target_pairs={{0,14},{1,3},{2,0},{3,5},{4,2},{5,7},{6,4},{7,9},{8,6},{9,11},{10,... | collective-permute-start | bytes 589832 | tf_op jit(solution)/shard_map/ppermute | solution.py:46
  46.3 4.5 %collective-permute-start.12 = (bf16[48,2048]{1,0:T(8,128)(2,1)S(1)}, bf16[48,2048]{1,0:T(8,128)(2,1)S(1)}, u32[]{:S(2)}, u32[]{:S(2)}) collective-permute-start(bf16[48,2048]{1,0:T(8,128)(2,1)S(1)} %collective-permute-done.5.refs_7_), channel_id=1, source_target_pairs={{0,2},{1,15},{2,4},{3,1},{4,6},{5,3},{6,8},{7,5},{8,10},{9,7},{10,... | collective-permute-start | bytes 589832 | tf_op jit(solution)/shard_map/ppermute | solution.py:46
  46.3 13.9 %collective-permute-start.17 = (bf16[80,2048]{1,0:T(8,128)(2,1)S(1)}, bf16[80,2048]{1,0:T(8,128)(2,1)S(1)}, u32[]{:S(2)}, u32[]{:S(2)}) collective-permute-start(bf16[80,2048]{1,0:T(8,128)(2,1)S(1)} %collective-permute-done.14.refs_15_), channel_id=1, source_target_pairs={{0,2},{1,15},{2,4},{3,1},{4,6},{5,3},{6,8},{7,5},{8,10},{9,7},{10,... | collective-permute-start | bytes 983048 | tf_op jit(solution)/shard_map/ppermute | solution.py:46
  46.6 13.6 %collective-permute-start.18 = (bf16[80,2048]{1,0:T(8,128)(2,1)S(1)}, bf16[80,2048]{1,0:T(8,128)(2,1)S(1)}, u32[]{:S(2)}, u32[]{:S(2)}) collective-permute-start(bf16[80,2048]{1,0:T(8,128)(2,1)S(1)} %collective-permute-done.15.refs_16_), channel_id=1, source_target_pairs={{0,14},{1,3},{2,0},{3,5},{4,2},{5,7},{6,4},{7,9},{8,6},{9,11},{10,... | collective-permute-start | bytes 983048 | tf_op jit(solution)/shard_map/ppermute | solution.py:46
  47.9 12.4 %collective-permute-start.13 = (bf16[48,2048]{1,0:T(8,128)(2,1)S(1)}, bf16[48,2048]{1,0:T(8,128)(2,1)S(1)}, u32[]{:S(2)}, u32[]{:S(2)}) collective-permute-start(bf16[48,2048]{1,0:T(8,128)(2,1)S(1)} %collective-permute-done.6.refs_8_), channel_id=1, source_target_pairs={{0,14},{1,3},{2,0},{3,5},{4,2},{5,7},{6,4},{7,9},{8,6},{9,11},{10,... | collective-permute-start | bytes 589832 | tf_op jit(solution)/shard_map/ppermute | solution.py:46
  50.8 11.4 %collective-permute-start.2 = (bf16[128,2048]{1,0:T(8,128)(2,1)S(1)}, bf16[128,2048]{1,0:T(8,128)(2,1)S(1)}, u32[]{:S(2)}, u32[]{:S(2)}) collective-permute-start(bf16[128,2048]{1,0:T(8,128)(2,1)S(1)} %get-tuple-element.31.refs_0_), channel_id=1, source_target_pairs={{0,1},{1,0},{2,3},{3,2},{4,5},{5,4},{6,7},{7,6},{8,9},{9,8},{10,11... | collective-permute-start | bytes 1572872 | tf_op jit(solution)/shard_map/ppermute | solution.py:46
  56.6 11.9 %collective-permute-start.3 = (bf16[128,2048]{1,0:T(8,128)(2,1)S(1)}, bf16[128,2048]{1,0:T(8,128)(2,1)S(1)}, u32[]{:S(2)}, u32[]{:S(2)}) collective-permute-start(bf16[128,2048]{1,0:T(8,128)(2,1)S(1)} %collective-permute-done.1.refs_1_), channel_id=1, source_target_pairs={{0,1},{1,0},{2,3},{3,2},{4,5},{5,4},{6,7},{7,6},{8,9},{9,8},{10,11... | collective-permute-start | bytes 1572872 | tf_op jit(solution)/shard_map/ppermute | solution.py:46
  60.2 8.3 %collective-permute-start.19 = (bf16[80,2048]{1,0:T(8,128)(2,1)S(1)}, bf16[80,2048]{1,0:T(8,128)(2,1)S(1)}, u32[]{:S(2)}, u32[]{:S(2)}) collective-permute-start(bf16[80,2048]{1,0:T(8,128)(2,1)S(1)} %collective-permute-done.17.refs_17_), channel_id=1, source_target_pairs={{0,2},{1,15},{2,4},{3,1},{4,6},{5,3},{6,8},{7,5},{8,10},{9,7},{10,... | collective-permute-start | bytes 983048 | tf_op jit(solution)/shard_map/ppermute | solution.py:46
  62.1 6.5 %collective-permute-start.16 = (bf16[48,2048]{1,0:T(8,128)(2,1)S(1)}, bf16[48,2048]{1,0:T(8,128)(2,1)S(1)}, u32[]{:S(2)}, u32[]{:S(2)}) collective-permute-start(bf16[48,2048]{1,0:T(8,128)(2,1)S(1)} %collective-permute-done.12.refs_9_), channel_id=1, source_target_pairs={{0,2},{1,15},{2,4},{3,1},{4,6},{5,3},{6,8},{7,5},{8,10},{9,7},{10,... | collective-permute-start | bytes 589832 | tf_op jit(solution)/shard_map/ppermute | solution.py:46
  72.2 6.0 %collective-permute-start.20 = (bf16[512,384]{1,0:T(8,128)(2,1)S(1)}, bf16[512,384]{1,0:T(8,128)(2,1)}, u32[]{:S(2)}, u32[]{:S(2)}) collective-permute-start(bf16[512,384]{1,0:T(8,128)(2,1)S(1)} %get-tuple-element.44), channel_id=1, source_target_pairs={{0,1},{1,0},{2,3},{3,2},{4,5},{5,4},{6,7},{7,6},{8,9},{9,8},{10,11... | collective-permute-start | bytes 1179656 | tf_op jit(solution)/shard_map/ppermute | solution.py:46
  76.1 9.4 %collective-permute-start.21 = (bf16[128,2048]{1,0:T(8,128)(2,1)}, bf16[128,2048]{1,0:T(8,128)(2,1)S(1)}, u32[]{:S(2)}, u32[]{:S(2)}) collective-permute-start(bf16[128,2048]{1,0:T(8,128)(2,1)} %get-tuple-element.45.own_ref), channel_id=1, source_target_pairs={{0,1},{1,0},{2,3},{3,2},{4,5},{5,4},{6,7},{7,6},{8,9},{9,8},{10,11... | collective-permute-start | bytes 1572872 | tf_op jit(solution)/shard_map/ppermute | solution.py:46
  80.1 11.4 %copy-start.2 = (bf16[512,384]{1,0:T(8,128)(2,1)S(1)}, bf16[512,384]{1,0:T(8,128)(2,1)}, u32[]{:S(2)}) copy-start(bf16[512,384]{1,0:T(8,128)(2,1)} %copy-done.1) | copy-start | bytes 1179652
  80.1 15.8 %collective-permute-start.27 = (bf16[128,2048]{1,0:T(8,128)(2,1)S(1)}, bf16[128,2048]{1,0:T(8,128)(2,1)S(1)}, u32[]{:S(2)}, u32[]{:S(2)}) collective-permute-start(bf16[128,2048]{1,0:T(8,128)(2,1)S(1)} %get-tuple-element.52.mine), channel_id=1, source_target_pairs={{0,96},{32,0},{64,32},{96,64},{128,224},{160,128},{192,160},{224,1... | collective-permute-start | bytes 1572872 | tf_op jit(solution)/shard_map/ppermute | solution.py:46
  82.9 15.6 %collective-permute-start.26 = (bf16[128,2048]{1,0:T(8,128)(2,1)S(1)}, bf16[128,2048]{1,0:T(8,128)(2,1)S(1)}, u32[]{:S(2)}, u32[]{:S(2)}) collective-permute-start(bf16[128,2048]{1,0:T(8,128)(2,1)S(1)} %get-tuple-element.52.mine), channel_id=1, source_target_pairs={{0,32},{32,64},{64,96},{96,0},{128,160},{160,192},{192,224},{224,1... | collective-permute-start | bytes 1572872 | tf_op jit(solution)/shard_map/ppermute | solution.py:46
  82.9 8.6 %collective-permute-start.23 = (bf16[256,512]{1,0:T(8,128)(2,1)}, bf16[256,512]{1,0:T(8,128)(2,1)S(1)}, u32[]{:S(2)}, u32[]{:S(2)}) collective-permute-start(bf16[256,512]{1,0:T(8,128)(2,1)} %get-tuple-element.49), channel_id=1, source_target_pairs={{0,2},{1,3},{2,4},{3,5},{4,6},{5,7},{6,8},{7,9},{8,10},{9,11},{10,... | collective-permute-start | bytes 786440 | tf_op jit(solution)/shard_map/ppermute | solution.py:46
  82.9 8.6 %collective-permute-start.24 = (bf16[256,512]{1,0:T(8,128)(2,1)}, bf16[256,512]{1,0:T(8,128)(2,1)S(1)}, u32[]{:S(2)}, u32[]{:S(2)}) collective-permute-start(bf16[256,512]{1,0:T(8,128)(2,1)} %get-tuple-element.50), channel_id=1, source_target_pairs={{0,14},{1,15},{2,0},{3,1},{4,2},{5,3},{6,4},{7,5},{8,6},{9,7},{10,... | collective-permute-start | bytes 786440 | tf_op jit(solution)/shard_map/ppermute | solution.py:46
  88.1 3.3 %collective-permute-start.22 = (bf16[256,256]{1,0:T(8,128)(2,1)S(1)}, bf16[256,256]{1,0:T(8,128)(2,1)S(1)}, u32[]{:S(2)}, u32[]{:S(2)}) collective-permute-start(bf16[256,256]{1,0:T(8,128)(2,1)S(1)} %get-tuple-element.48), channel_id=1, source_target_pairs={{0,1},{1,0},{2,3},{3,2},{4,5},{5,4},{6,7},{7,6},{8,9},{9,8},{10,11... | collective-permute-start | bytes 393224 | tf_op jit(solution)/shard_map/ppermute | solution.py:46
  96.0 6.8 %collective-permute-start.29 = (bf16[64,2048]{1,0:T(8,128)(2,1)S(1)}, bf16[64,2048]{1,0:T(8,128)(2,1)S(1)}, u32[]{:S(2)}, u32[]{:S(2)}) collective-permute-start(bf16[64,2048]{1,0:T(8,128)(2,1)S(1)} %slice.75), channel_id=1, source_target_pairs={{0,96},{32,0},{64,32},{96,64},{128,224},{160,128},{192,160},{224,1... | collective-permute-start | bytes 786440 | tf_op jit(solution)/shard_map/ppermute | solution.py:46
  98.4 7.0 %collective-permute-start.28 = (bf16[64,2048]{1,0:T(8,128)(2,1)S(1)}, bf16[64,2048]{1,0:T(8,128)(2,1)S(1)}, u32[]{:S(2)}, u32[]{:S(2)}) collective-permute-start(bf16[64,2048]{1,0:T(8,128)(2,1)S(1)} %slice.74), channel_id=1, source_target_pairs={{0,32},{32,64},{64,96},{96,0},{128,160},{160,192},{192,224},{224,1... | collective-permute-start | bytes 786440 | tf_op jit(solution)/shard_map/ppermute | solution.py:46
  98.6 4.2 %collective-permute-start.25 = (bf16[256,256]{1,0:T(8,128)(2,1)S(1)}, bf16[256,256]{1,0:T(8,128)(2,1)S(1)}, u32[]{:S(2)}, u32[]{:S(2)}) collective-permute-start(bf16[256,256]{1,0:T(8,128)(2,1)S(1)} %get-tuple-element.57), channel_id=1, source_target_pairs={{0,16},{1,17},{2,18},{3,19},{4,20},{5,21},{6,22},{7,23},{8,24},{9,... | collective-permute-start | bytes 393224 | tf_op jit(solution)/shard_map/ppermute | solution.py:46
  106.7 4.7 %collective-permute-start.30 = (bf16[128,2048]{1,0:T(8,128)(2,1)S(1)}, bf16[128,2048]{1,0:T(8,128)(2,1)S(1)}, u32[]{:S(2)}, u32[]{:S(2)}) collective-permute-start(bf16[128,2048]{1,0:T(8,128)(2,1)S(1)} %get-tuple-element.54), channel_id=1, source_target_pairs={{0,1},{1,0},{2,3},{3,2},{4,5},{5,4},{6,7},{7,6},{8,9},{9,8},{10,11... | collective-permute-start | bytes 1572872 | tf_op jit(solution)/shard_map/ppermute | solution.py:46
  (4 other events, 3.2 us)

commit v4 on v3

--- a/solution.py
+++ b/solution.py
@@ -42,6 +42,10 @@
 Y_DOWN = [(d, (d & 4) | ((d - 1) & 3)) for d in range(2 * Y)]
 
 
+UP_CROSS = pairs(lambda x, z, c: (x, (z + 1) % Z, 1 - c))
+DOWN_CROSS = pairs(lambda x, z, c: (x, (z - 1) % Z, 1 - c))
+
+
 def send(value, route, axis="seq"):
     return lax.ppermute(value, axis, route)
 
@@ -51,7 +55,15 @@
     return values * lax.rsqrt(mean_square + EPSILON) * gain_row
 
 
-def norm_kernel(index, hidden, gain, global_gain, normed_ref, blocks_ref):
+def norm_kernel(index, hidden_in, gain_in, global_in, normed_ref, blocks_ref, hidden, gain, global_gain, sems):
+    copies = [
+        pltpu.make_async_copy(source, into, sems.at[i])
+        for i, (source, into) in enumerate(((hidden_in, hidden), (gain_in, gain), (global_in, global_gain)))
+    ]
+    for copy in copies:
+        copy.start()
+    for copy in copies:
+        copy.wait()
     normed = rms_norm(hidden[...].astype(jnp.float32), gain[...]).astype(jnp.bfloat16)
     normed_ref[...] = normed
     at = index[4] + lax.broadcasted_iota(jnp.int32, (TOK, 1), 0)
@@ -80,7 +92,7 @@
 
 def project_kernel(index, *refs):
     blocks, firsts, seconds = refs[:4], refs[4 : 4 + SHARDS], refs[4 + SHARDS : 4 + 2 * SHARDS]
-    keep_ref, send_ref, g_rows, far_table, out_rows, rows, table, sems = refs[4 + 2 * SHARDS :]
+    keep_ref, send_ref, g_rows, far_table, out_rows, *edges, rows, table, sems = refs[4 + 2 * SHARDS :]
     z, core, x = index[0], index[1], index[2]
     low_core = core == 0
     copies = []
@@ -107,6 +119,14 @@
         lanes = slice(kind * 128, kind * 128 + 128)
         keep_ref[:, lanes] = jnp.where(low_core, out[:, :128], out[:, 128:])
         send_ref[:, lanes] = jnp.where(low_core, out[:, 128:], out[:, :128])
+        if kind:
+            lanes_out = slice(kind * 128 - 128, kind * 128)
+            for part in range(2):
+                for seg in range(2):
+                    at = slice((seg * 2 + part) * TOK, (seg * 2 + part + 1) * TOK)
+                    into = slice(seg * TOK, seg * TOK + TOK)
+                    edges[2 * part][into, lanes_out] = keep_ref[at, lanes]
+                    edges[2 * part + 1][into, lanes_out] = send_ref[at, lanes]
 
 
 def far_kernel(index, own_ref, other_ref, table, keep_ref, send_ref):
@@ -121,16 +141,7 @@
             send_ref[at, lanes] = jnp.where(low_core, out[:, 128:], out[:, :128])
 
 
-def edge_kernel(keep_ref, got_ref, low_ref, high_ref):
-    for seg in range(2):
-        into = slice(seg * TOK, seg * TOK + TOK)
-        for part, out in ((0, low_ref), (1, high_ref)):
-            at = slice((seg * 2 + part) * TOK, (seg * 2 + part + 1) * TOK)
-            out[into, :256] = keep_ref[at, 128:]
-            out[into, 256:] = got_ref[at, 128:]
-
-
-def attention_kernel(index, keep_ref, got_ref, g_keep, g_got, below_ref, above_ref, out_ref):
+def attention_kernel(index, keep_ref, got_ref, g_keep, g_got, below_ref, below_got, above_ref, above_got, out_ref):
     z, x, limit = index[0], index[2], index[3]
     lane_head = (lax.broadcasted_iota(jnp.int32, (TOK, WIDE), 1) % 128) // HALF
     row = lax.broadcasted_iota(jnp.int32, (HEADS_LOCAL * TOK, TOK), 0) % TOK
@@ -147,10 +158,10 @@
         lanes = slice(kind * 128, kind * 128 + 128)
         return jnp.concatenate([keep_ref[at : at + TOK, lanes], got_ref[at : at + TOK, lanes]], axis=1)
 
-    def halo(ref, kind, seg):
+    def halo(ref, got, kind, seg):
         at = pl.ds(pl.multiple_of(seg * TOK, TOK), TOK)
-        lanes = kind * 128 - 128
-        return jnp.concatenate([ref[at, lanes : lanes + 128], ref[at, lanes + 256 : lanes + 384]], axis=1)
+        lanes = slice(kind * 128 - 128, kind * 128)
+        return jnp.concatenate([ref[at, lanes], got[at, lanes]], axis=1)
 
     for seg in range(2):
         below_seg = jnp.where(z == 0, 1 - seg, seg)
@@ -166,8 +177,8 @@
 
             def neighbours(kind):
                 if part == 0:
-                    return halo(below_ref, kind, below_seg), local(kind, at), local(kind, at + TOK)
-                return local(kind, at - TOK), local(kind, at), halo(above_ref, kind, above_seg)
+                    return halo(below_ref, below_got, kind, below_seg), local(kind, at), local(kind, at + TOK)
+                return local(kind, at - TOK), local(kind, at), halo(above_ref, above_got, kind, above_seg)
 
             k_left, k_mid, k_right = neighbours(1)
             v_left, v_mid, v_right = neighbours(2)
@@ -268,11 +279,18 @@
         (jax.ShapeDtypeStruct((TOK, width), bf16), jax.ShapeDtypeStruct((TOK // BLOCK, width), bf16)),
         8 * TOK * width,
         0,
-        (index, hidden_in, attn_gain[None], global_gain[None]),
+        (index, after(hidden_in, first), attn_gain[None], global_gain[None]),
+        (
+            pltpu.VMEM((TOK, width), bf16),
+            pltpu.VMEM((1, width), jnp.float32),
+            pltpu.VMEM((1, width), jnp.float32),
+            pltpu.SemaphoreType.DMA((3,)),
+        ),
+        in_hbm=3,
     )
     global_there = send(global_mine, OTHER_X)
 
-    split = w_out.reshape(X, 2, HEADS_LOCAL, 2, HALF, 64)
+    split = after(w_out, first).reshape(X, 2, HEADS_LOCAL, 2, HALF, 64)
 
     def slab(group):
         at = (y >> 1, group, 0, (y & 1) ^ group, 0, 0)
@@ -303,7 +321,9 @@
         one[0, step] = a_one = send(a_one, AHEAD)
         if step < 4:
             one[1, step] = b_one = send(b_one, BEHIND)
-        if step > 1:
+        if step == 1:
+            a_two = b_two = after(second, a_one, b_one)
+        else:
             a_two, b_two = lax.optimization_barrier((a_two, b_two, one[0, step - 1], one[1, step - 1]))[:2]
         two[0, step] = a_two = send(a_two, AHEAD)
         if step < 4:
@@ -317,7 +337,7 @@
     beside_across = send(across, OTHER_CORE)
 
     half = jax.ShapeDtypeStruct((ROWS, 3 * 128), bf16)
-    keep, to_swap, g_own, far_table, out_own = on_chip(
+    keep, to_swap, g_own, far_table, out_own, *edges = on_chip(
         project_kernel,
         (
             half,
@@ -325,6 +345,7 @@
             jax.ShapeDtypeStruct((G_ROWS, width), bf16),
             jax.ShapeDtypeStruct((2 * Z * HALF, width), bf16),
             jax.ShapeDtypeStruct((128, width), bf16),
+            *[jax.ShapeDtypeStruct((2 * TOK, 256), bf16)] * 4,
         ),
         2 * ROWS * 768 * width,
         0,
@@ -335,21 +356,15 @@
     got = send(to_swap, OTHER_CORE)
     g_other = send(g_own, OTHER_CORE)
 
-    vmem = pl.BlockSpec(memory_space=pltpu.VMEM)
-    edge_shape = jax.ShapeDtypeStruct((2 * TOK, 512), bf16)
-    low_edge, high_edge = pl.pallas_call(
-        edge_kernel, out_shape=(edge_shape, edge_shape), in_specs=[vmem] * 2, out_specs=(vmem, vmem)
-    )(keep, got)
-    below = send(high_edge, UP)
-    above = send(low_edge, DOWN)
-
+    below = send(edges[2], UP), send(edges[3], UP_CROSS)
+    above = send(edges[0], DOWN), send(edges[1], DOWN_CROSS)
     far_half = jax.ShapeDtypeStruct((2 * G_ROWS, 256), bf16)
     g_keep, g_swap = on_chip(
         far_kernel, (far_half, far_half), 2 * 256 * 512 * width, 0, (index, g_own, g_other, far_table)
     )
     g_got = send(g_swap, OTHER_CORE)
 
-    to_pass = after(out_own, low_edge, high_edge)
+    to_pass = after(out_own, got, g_other)
     out_prev = send(to_pass, Y_UP, "doc")
     out_next = send(to_pass, Y_DOWN, "doc")
     out_far_a = send(out_prev[:64], Y_UP, "doc")
@@ -360,7 +375,7 @@
         jax.ShapeDtypeStruct((2, 2 * TOK, WIDE), bf16),
         4 * 4 * TOK * 640 * WIDE * 4,
         4 * 4 * TOK * 640,
-        (index, keep, got, g_keep, g_got, below, above),
+        (index, keep, got, g_keep, g_got, *below, *above),
     )
 
     there = send(context[1], OTHER_X)

time: 113 us -> 109 us (0.965)
  local copies, waits for them, and re-layouts: 4.44 us -> 1.28 us
  Pallas kernels: 14.3 us -> 11.5 us
  waiting for transfers between devices: 43.7 us -> 45.3 us
    unnamed x11 -> x6, local copies, waits for them, and re-layouts: 4.25 us -> 0.01 us
    pallas_call x1 -> x0, Pallas kernels: 1.96 us -> none  [per_device(): pl.pallas_call(edge_kernel, out_shape=(edge_shape, edge_shape), in_specs=...]
    ppermute x31 -> x33, waiting for transfers between devices: 43.7 us -> 45.3 us  [send(): return lax.ppermute(value, axis, route)]
    ppermute x31 -> x33, starting transfers between devices: 46.7 us -> 46.8 us  [send(): return lax.ppermute(value, axis, route)]
  transfers between devices with their start and end apart: 31 -> 33, of which waited for: 12 -> 17; matrix products, arithmetic and copies ran while one was open for 1% -> 0% of each run, Pallas kernels for 9% -> 7%
where the time goes in v4:
time: 109 us; the launch traced here: 108 us
  starting transfers between devices  46.8 us (43%)
  waiting for transfers between devices  45.3 us (42%)
  Pallas kernels  11.5 us (11%)
  other arithmetic  2.31 us (2%)
  local copies, waits for them, and re-layouts  1.28 us (1%)
    ppermute x33, starting transfers between devices, send(): return lax.ppermute(value, axis, route)  46.8 us
    ppermute x33, waiting for transfers between devices, send(): return lax.ppermute(value, axis, route)  45.3 us
    pallas_call x5, Pallas kernels, on_chip(): pl.pallas_call(kernel, out_shape=out_shape, in_specs=specs, out_specs=jax...  11.5 us
  transfers between devices with their start and end apart: 33, of which 17 were waited for; matrix products, arithmetic and copies ran while one was open for 0% of the time, Pallas kernels for 7%

profile of v4, /device:TPU:1, one launch (start us, length us, event | category | flops | bytes accessed | tf_op | source)
XLA Modules:
  0.0 108.2 jit_solution(2763683820626192010)
XLA Ops:
  2.3 3.3 %collective-permute-start.8 = (bf16[128,64]{1,0:T(8,128)(2,1)S(1)}, bf16[128,64]{1,0:T(8,128)(2,1)S(1)}, u32[]{:S(2)}, u32[]{:S(2)}) collective-permute-start(bf16[128,64]{1,0:T(8,128)(2,1)S(1)} %bitcast.43), channel_id=1, source_target_pairs={{0,1},{1,0},{2,3},{3,2},{4,5},{5,4},{6,7},{7,6},{8,9},{9,8},{10,11... | collective-permute-start | bytes 49160 | tf_op jit(solution)/shard_map/ppermute | solution.py:50
  5.6 3.9 %collective-permute-start = (bf16[48,2048]{1,0:T(8,128)(2,1)S(1)}, bf16[48,2048]{1,0:T(8,128)(2,1)S(1)}, u32[]{:S(2)}, u32[]{:S(2)}) collective-permute-start(bf16[48,2048]{1,0:T(8,128)(2,1)S(1)} %bitcast.34), channel_id=1, source_target_pairs={{0,2},{1,15},{2,4},{3,1},{4,6},{5,3},{6,8},{7,5},{8,10},{9,7},{10,... | collective-permute-start | bytes 589832 | tf_op jit(solution)/shard_map/ppermute | solution.py:50
  10.3 1.3 %shard_map.82 = (bf16[128,2048]{1,0:T(8,128)(2,1)S(1)}, bf16[8,2048]{1,0:T(8,128)(2,1)S(1)}) custom-call(s32[6]{0:T(128)S(1)} %stack.35.index, bf16[128,2048]{1,0:T(8,128)(2,1)S(1)} %copy-done, f32[1,2048]{1,0:T(1,128)S(1)} %bitcast.36, f32[1,2048]{1,0:T(1,128)S(1)} %bitcast.37), custom_call_target="tpu_custom_call" | custom-call | flops 2097152 | bytes 4194304 | tf_op jit(solution)/shard_map/pallas_call | solution.py:248
  11.5 1.3 %collective-permute-start.7 = (bf16[8,2048]{1,0:T(8,128)(2,1)S(1)}, bf16[8,2048]{1,0:T(8,128)(2,1)S(1)}, u32[]{:S(2)}, u32[]{:S(2)}) collective-permute-start(bf16[8,2048]{1,0:T(8,128)(2,1)S(1)} %get-tuple-element.40), channel_id=1, source_target_pairs={{0,16},{1,17},{2,18},{3,19},{4,20},{5,21},{6,22},{7,23},{8,24},{9,... | collective-permute-start | bytes 98312 | tf_op jit(solution)/shard_map/ppermute | solution.py:50
  13.3 1.4 %collective-permute-done.7 = bf16[8,2048]{1,0:T(8,128)(2,1)S(1)} collective-permute-done((bf16[8,2048]{1,0:T(8,128)(2,1)S(1)}, bf16[8,2048]{1,0:T(8,128)(2,1)S(1)}, u32[]{:S(2)}, u32[]{:S(2)}) %collective-permute-start.7) | collective-permute-done | bytes 32800 | tf_op jit(solution)/shard_map/ppermute | solution.py:50
  14.7 1.4 %collective-permute-done.9 = bf16[128,128]{1,0:T(8,128)(2,1)S(1)} collective-permute-done((bf16[128,128]{1,0:T(8,128)(2,1)S(1)}, bf16[128,128]{1,0:T(8,128)(2,1)S(1)}, u32[]{:S(2)}, u32[]{:S(2)}) %collective-permute-start.9) | collective-permute-done | bytes 32800 | tf_op jit(solution)/shard_map/ppermute | solution.py:50
  16.4 2.7 %collective-permute-start.10 = (bf16[80,2048]{1,0:T(8,128)(2,1)S(1)}, bf16[80,2048]{1,0:T(8,128)(2,1)S(1)}, u32[]{:S(2)}, u32[]{:S(2)}) collective-permute-start(bf16[80,2048]{1,0:T(8,128)(2,1)S(1)} %pad_maximum_fusion.1.refs_12_), channel_id=1, source_target_pairs={{0,2},{1,15},{2,4},{3,1},{4,6},{5,3},{6,8},{7,5},{8,10},{9,7},{10,... | collective-permute-start | bytes 983048 | tf_op jit(solution)/shard_map/ppermute | solution.py:50
  19.3 4.2 %collective-permute-done.11.refs_14_ = bf16[80,2048]{1,0:T(8,128)(2,1)S(1)} collective-permute-done((bf16[80,2048]{1,0:T(8,128)(2,1)S(1)}, bf16[80,2048]{1,0:T(8,128)(2,1)S(1)}, u32[]{:S(2)}, u32[]{:S(2)}) %collective-permute-start.11) | collective-permute-done | bytes 327712 | tf_op jit(solution)/shard_map/ppermute | solution.py:50
  24.3 3.4 %collective-permute-start.14 = (bf16[80,2048]{1,0:T(8,128)(2,1)S(1)}, bf16[80,2048]{1,0:T(8,128)(2,1)S(1)}, u32[]{:S(2)}, u32[]{:S(2)}) collective-permute-start(bf16[80,2048]{1,0:T(8,128)(2,1)S(1)} %collective-permute-done.10.refs_13_), channel_id=1, source_target_pairs={{0,2},{1,15},{2,4},{3,1},{4,6},{5,3},{6,8},{7,5},{8,10},{9,7},{10,... | collective-permute-start | bytes 983048 | tf_op jit(solution)/shard_map/ppermute | solution.py:50
  27.7 2.7 %collective-permute-start.5 = (bf16[48,2048]{1,0:T(8,128)(2,1)S(1)}, bf16[48,2048]{1,0:T(8,128)(2,1)S(1)}, u32[]{:S(2)}, u32[]{:S(2)}) collective-permute-start(bf16[48,2048]{1,0:T(8,128)(2,1)S(1)} %collective-permute-done.refs_5_), channel_id=1, source_target_pairs={{0,2},{1,15},{2,4},{3,1},{4,6},{5,3},{6,8},{7,5},{8,10},{9,7},{10,... | collective-permute-start | bytes 589832 | tf_op jit(solution)/shard_map/ppermute | solution.py:50
  30.4 3.9 %collective-permute-done.5.refs_7_ = bf16[48,2048]{1,0:T(8,128)(2,1)S(1)} collective-permute-done((bf16[48,2048]{1,0:T(8,128)(2,1)S(1)}, bf16[48,2048]{1,0:T(8,128)(2,1)S(1)}, u32[]{:S(2)}, u32[]{:S(2)}) %collective-permute-start.5) | collective-permute-done | bytes 196640 | tf_op jit(solution)/shard_map/ppermute | solution.py:50
  34.3 6.4 %collective-permute-done.6.refs_8_ = bf16[48,2048]{1,0:T(8,128)(2,1)S(1)} collective-permute-done((bf16[48,2048]{1,0:T(8,128)(2,1)S(1)}, bf16[48,2048]{1,0:T(8,128)(2,1)S(1)}, u32[]{:S(2)}, u32[]{:S(2)}) %collective-permute-start.6) | collective-permute-done | bytes 196640 | tf_op jit(solution)/shard_map/ppermute | solution.py:50
  40.7 2.2 %collective-permute-start.17 = (bf16[80,2048]{1,0:T(8,128)(2,1)S(1)}, bf16[80,2048]{1,0:T(8,128)(2,1)S(1)}, u32[]{:S(2)}, u32[]{:S(2)}) collective-permute-start(bf16[80,2048]{1,0:T(8,128)(2,1)S(1)} %collective-permute-done.14.refs_15_), channel_id=1, source_target_pairs={{0,2},{1,15},{2,4},{3,1},{4,6},{5,3},{6,8},{7,5},{8,10},{9,7},{10,... | collective-permute-start | bytes 983048 | tf_op jit(solution)/shard_map/ppermute | solution.py:50
  43.6 1.6 %collective-permute-done.12.refs_9_ = bf16[48,2048]{1,0:T(8,128)(2,1)S(1)} collective-permute-done((bf16[48,2048]{1,0:T(8,128)(2,1)S(1)}, bf16[48,2048]{1,0:T(8,128)(2,1)S(1)}, u32[]{:S(2)}, u32[]{:S(2)}) %collective-permute-start.12) | collective-permute-done | bytes 196640 | tf_op jit(solution)/shard_map/ppermute | solution.py:50
  45.2 7.0 %collective-permute-start.2 = (bf16[128,2048]{1,0:T(8,128)(2,1)S(1)}, bf16[128,2048]{1,0:T(8,128)(2,1)S(1)}, u32[]{:S(2)}, u32[]{:S(2)}) collective-permute-start(bf16[128,2048]{1,0:T(8,128)(2,1)S(1)} %get-tuple-element.37.refs_0_), channel_id=1, source_target_pairs={{0,1},{1,0},{2,3},{3,2},{4,5},{5,4},{6,7},{7,6},{8,9},{9,8},{10,11... | collective-permute-start | bytes 1572872 | tf_op jit(solution)/shard_map/ppermute | solution.py:50
  52.3 4.9 %collective-permute-done.13.refs_10_ = bf16[48,2048]{1,0:T(8,128)(2,1)S(1)} collective-permute-done((bf16[48,2048]{1,0:T(8,128)(2,1)S(1)}, bf16[48,2048]{1,0:T(8,128)(2,1)S(1)}, u32[]{:S(2)}, u32[]{:S(2)}) %collective-permute-start.13) | collective-permute-done | bytes 196640 | tf_op jit(solution)/shard_map/ppermute | solution.py:50
  58.3 7.3 %collective-permute-done.16.refs_11_ = bf16[48,2048]{1,0:T(8,128)(2,1)S(1)} collective-permute-done((bf16[48,2048]{1,0:T(8,128)(2,1)S(1)}, bf16[48,2048]{1,0:T(8,128)(2,1)S(1)}, u32[]{:S(2)}, u32[]{:S(2)}) %collective-permute-start.16) | collective-permute-done | bytes 196640 | tf_op jit(solution)/shard_map/ppermute | solution.py:50
  65.5 2.9 %shard_map.83 = (bf16[512,384]{1,0:T(8,128)(2,1)S(1)}, bf16[512,384]{1,0:T(8,128)(2,1)S(1)}, bf16[128,2048]{1,0:T(8,128)(2,1)S(1)}, bf16[512,2048]{1,0:T(8,128)(...) custom-call(s32[6]{0:T(128)S(1)} %stack.35.index, ...), custom_call_target="tpu_custom_call" | custom-call | flops 1610612736 | bytes 4194304 | tf_op jit(solution)/shard_map/pallas_call | solution.py:248
  68.5 3.4 %collective-permute-start.21 = (bf16[128,2048]{1,0:T(8,128)(2,1)S(1)}, bf16[128,2048]{1,0:T(8,128)(2,1)S(1)}, u32[]{:S(2)}, u32[]{:S(2)}) collective-permute-start(bf16[128,2048]{1,0:T(8,128)(2,1)S(1)} %get-tuple-element.53.own_ref), channel_id=1, source_target_pairs={{0,1},{1,0},{2,3},{3,2},{4,5},{5,4},{6,7},{7,6},{8,9},{9,8},{10,11... | collective-permute-start | bytes 1572872 | tf_op jit(solution)/shard_map/ppermute | solution.py:50
  72.0 2.0 %collective-permute-done.20.got_ref = bf16[512,384]{1,0:T(8,128)(2,1)S(1)} collective-permute-done((bf16[512,384]{1,0:T(8,128)(2,1)S(1)}, bf16[512,384]{1,0:T(8,128)(2,1)S(1)}, u32[]{:S(2)}, u32[]{:S(2)}) %collective-permute-start.20) | collective-permute-done | bytes 393248 | tf_op jit(solution)/shard_map/ppermute | solution.py:50
  74.0 2.7 %collective-permute-start.29 = (bf16[128,2048]{1,0:T(8,128)(2,1)S(1)}, bf16[128,2048]{1,0:T(8,128)(2,1)S(1)}, u32[]{:S(2)}, u32[]{:S(2)}) collective-permute-start(bf16[128,2048]{1,0:T(8,128)(2,1)S(1)} %get-tuple-element.62.mine), channel_id=1, source_target_pairs={{0,96},{32,0},{64,32},{96,64},{128,224},{160,128},{192,160},{224,1... | collective-permute-start | bytes 1572872 | tf_op jit(solution)/shard_map/ppermute | solution.py:50
  76.7 3.2 %collective-permute-start.25 = (bf16[256,256]{1,0:T(8,128)(2,1)S(1)}, bf16[256,256]{1,0:T(8,128)(2,1)S(1)}, u32[]{:S(2)}, u32[]{:S(2)}) collective-permute-start(bf16[256,256]{1,0:T(8,128)(2,1)S(1)} %get-tuple-element.59), channel_id=1, source_target_pairs={{0,14},{1,15},{2,0},{3,1},{4,2},{5,3},{6,4},{7,5},{8,6},{9,7},{10,... | collective-permute-start | bytes 393224 | tf_op jit(solution)/shard_map/ppermute | solution.py:50
  80.0 2.1 %shard_map.84 = (bf16[256,256]{1,0:T(8,128)(2,1)S(1)}, bf16[256,256]{1,0:T(8,128)(2,1)S(1)}) custom-call(s32[6]{0:T(128)S(1)} %stack.35.index, bf16[128,2048]{1,0:T(8,128)(2,1)S(1)} %get-tuple-element.53.own_ref, bf16[128,2048]{1,0:T(8,128)(2,1)S(1)} %collective-permute-done.21.other_ref, bf16[512,2048]{1,0:T(8,128)(2,1)S(1)} %get-tuple-element.54.table), custom_call_target="tpu_custom_call" | custom-call | flops 536870912 | bytes 4194304 | tf_op jit(solution)/shard_map/pallas_call | solution.py:248
  82.3 1.8 %collective-permute-start.26 = (bf16[256,256]{1,0:T(8,128)(2,1)S(1)}, bf16[256,256]{1,0:T(8,128)(2,1)S(1)}, u32[]{:S(2)}, u32[]{:S(2)}) collective-permute-start(bf16[256,256]{1,0:T(8,128)(2,1)S(1)} %get-tuple-element.60), channel_id=1, source_target_pairs={{0,15},{1,14},{2,1},{3,0},{4,3},{5,2},{6,5},{7,4},{8,7},{9,6},{10,... | collective-permute-start | bytes 393224 | tf_op jit(solution)/shard_map/ppermute | solution.py:50
  84.1 2.1 %collective-permute-done.24.below_got = bf16[256,256]{1,0:T(8,128)(2,1)S(1)} collective-permute-done((bf16[256,256]{1,0:T(8,128)(2,1)S(1)}, bf16[256,256]{1,0:T(8,128)(2,1)S(1)}, u32[]{:S(2)}, u32[]{:S(2)}) %collective-permute-start.24) | collective-permute-done | bytes 131104 | tf_op jit(solution)/shard_map/ppermute | solution.py:50
  87.6 4.0 %shard_map.85 = bf16[2,256,256]{2,1,0:T(8,128)(2,1)S(1)} custom-call(s32[6]{0:T(128)S(1)} %stack.35.index, bf16[512,384]{1,0:T(8,128)(2,1)S(1)} %get-tuple-element.51.keep_ref, bf16[512,384]{1,0:T(8,128)(2,1)S(1)} %collective-permute-done.20.got_ref, bf16[256,256]{1,0:T(8,128)(2,1)S(1)} %get-tuple-element.55.g_keep, ...), custom_call_target="tpu_custom_call" | custom-call | flops 1342177280 | bytes 4194304 | tf_op jit(solution)/shard_map/pallas_call | solution.py:248
  91.6 2.8 %collective-permute-start.31 = (bf16[64,2048]{1,0:T(8,128)(2,1)S(1)}, bf16[64,2048]{1,0:T(8,128)(2,1)S(1)}, u32[]{:S(2)}, u32[]{:S(2)}) collective-permute-start(bf16[64,2048]{1,0:T(8,128)(2,1)S(1)} %slice.75), channel_id=1, source_target_pairs={{0,96},{32,0},{64,32},{96,64},{128,224},{160,128},{192,160},{224,1... | collective-permute-start | bytes 786440 | tf_op jit(solution)/shard_map/ppermute | solution.py:50
  94.7 4.0 %collective-permute-done.27.there_ref = bf16[256,256]{1,0:T(8,128)(2,1)S(1)} collective-permute-done((bf16[256,256]{1,0:T(8,128)(2,1)S(1)}, bf16[256,256]{1,0:T(8,128)(2,1)S(1)}, u32[]{:S(2)}, u32[]{:S(2)}) %collective-permute-start.27) | collective-permute-done | bytes 131104 | tf_op jit(solution)/shard_map/ppermute | solution.py:50
  98.7 2.2 %collective-permute-done.30.far_a = bf16[64,2048]{1,0:T(8,128)(2,1)S(1)} collective-permute-done((bf16[64,2048]{1,0:T(8,128)(2,1)S(1)}, bf16[64,2048]{1,0:T(8,128)(2,1)S(1)}, u32[]{:S(2)}, u32[]{:S(2)}) %collective-permute-start.30) | collective-permute-done | bytes 262176 | tf_op jit(solution)/shard_map/ppermute | solution.py:50
  100.9 1.3 %shard_map.86 = (f32[128,2048]{1,0:T(8,128)S(1)}, bf16[128,2048]{1,0:T(8,128)(2,1)S(1)}) custom-call(s32[6]{0:T(128)S(1)} %stack.35.index, bf16[256,256]{1,0:T(8,128)(2,1)S(1)} %get-tuple-element.68.own_ref, bf16[256,256]{1,0:T(8,128)(2,1)S(1)} %collective-permute-done.27.there_ref, bf16[128,2048]{1,0:T(8,128)(2,1)S(1)} %get-tuple-element.62.mine, ...), custom_call_target="tpu_custom_call" | custom-call | flops 536870912 | bytes 4194304 | tf_op jit(solution)/shard_map/pallas_call | solution.py:248
  102.2 3.6 %collective-permute-start.32 = (bf16[128,2048]{1,0:T(8,128)(2,1)S(1)}, bf16[128,2048]{1,0:T(8,128)(2,1)S(1)}, u32[]{:S(2)}, u32[]{:S(2)}) collective-permute-start(bf16[128,2048]{1,0:T(8,128)(2,1)S(1)} %get-tuple-element.64), channel_id=1, source_target_pairs={{0,1},{1,0},{2,3},{3,2},{4,5},{5,4},{6,7},{7,6},{8,9},{9,8},{10,11... | collective-permute-start | bytes 1572872 | tf_op jit(solution)/shard_map/ppermute | solution.py:50
  105.8 1.5 %collective-permute-done.32 = bf16[128,2048]{1,0:T(8,128)(2,1)S(1)} collective-permute-done((bf16[128,2048]{1,0:T(8,128)(2,1)S(1)}, bf16[128,2048]{1,0:T(8,128)(2,1)S(1)}, u32[]{:S(2)}, u32[]{:S(2)}) %collective-permute-start.32) | collective-permute-done | bytes 524320 | tf_op jit(solution)/shard_map/ppermute | solution.py:50
  (67 shorter events, 8.9 us)
Async XLA Ops:
  2.3 10.5 %collective-permute-start.8 = (bf16[128,64]{1,0:T(8,128)(2,1)S(1)}, bf16[128,64]{1,0:T(8,128)(2,1)S(1)}, u32[]{:S(2)}, u32[]{:S(2)}) collective-permute-start(bf16[128,64]{1,0:T(8,128)(2,1)S(1)} %bitcast.43), channel_id=1, source_target_pairs={{0,1},{1,0},{2,3},{3,2},{4,5},{5,4},{6,7},{7,6},{8,9},{9,8},{10,11... | collective-permute-start | bytes 49160 | tf_op jit(solution)/shard_map/ppermute | solution.py:50
  5.6 10.7 %collective-permute-start.4 = (bf16[48,2048]{1,0:T(8,128)(2,1)S(1)}, bf16[48,2048]{1,0:T(8,128)(2,1)S(1)}, u32[]{:S(2)}, u32[]{:S(2)}) collective-permute-start(bf16[48,2048]{1,0:T(8,128)(2,1)S(1)} %bitcast.33), channel_id=1, source_target_pairs={{0,14},{1,3},{2,0},{3,5},{4,2},{5,7},{6,4},{7,9},{8,6},{9,11},{10,... | collective-permute-start | bytes 589832 | tf_op jit(solution)/shard_map/ppermute | solution.py:50
  5.6 10.7 %collective-permute-start = (bf16[48,2048]{1,0:T(8,128)(2,1)S(1)}, bf16[48,2048]{1,0:T(8,128)(2,1)S(1)}, u32[]{:S(2)}, u32[]{:S(2)}) collective-permute-start(bf16[48,2048]{1,0:T(8,128)(2,1)S(1)} %bitcast.34), channel_id=1, source_target_pairs={{0,2},{1,15},{2,4},{3,1},{4,6},{5,3},{6,8},{7,5},{8,10},{9,7},{10,... | collective-permute-start | bytes 589832 | tf_op jit(solution)/shard_map/ppermute | solution.py:50
  11.5 3.1 %collective-permute-start.7 = (bf16[8,2048]{1,0:T(8,128)(2,1)S(1)}, bf16[8,2048]{1,0:T(8,128)(2,1)S(1)}, u32[]{:S(2)}, u32[]{:S(2)}) collective-permute-start(bf16[8,2048]{1,0:T(8,128)(2,1)S(1)} %get-tuple-element.40), channel_id=1, source_target_pairs={{0,16},{1,17},{2,18},{3,19},{4,20},{5,21},{6,22},{7,23},{8,24},{9,... | collective-permute-start | bytes 98312 | tf_op jit(solution)/shard_map/ppermute | solution.py:50
  12.9 3.1 %collective-permute-start.9 = (bf16[128,128]{1,0:T(8,128)(2,1)S(1)}, bf16[128,128]{1,0:T(8,128)(2,1)S(1)}, u32[]{:S(2)}, u32[]{:S(2)}) collective-permute-start(bf16[128,128]{1,0:T(8,128)(2,1)S(1)} %pad_maximum_fusion.2), channel_id=1, source_target_pairs={{0,16},{1,17},{2,18},{3,19},{4,20},{5,21},{6,22},{7,23},{8,24},{9,... | collective-permute-start | bytes 98312 | tf_op jit(solution)/shard_map/ppermute | solution.py:50
  16.3 7.2 %collective-permute-start.11 = (bf16[80,2048]{1,0:T(8,128)(2,1)S(1)}, bf16[80,2048]{1,0:T(8,128)(2,1)S(1)}, u32[]{:S(2)}, u32[]{:S(2)}) collective-permute-start(bf16[80,2048]{1,0:T(8,128)(2,1)S(1)} %pad_maximum_fusion.1.refs_12_), channel_id=1, source_target_pairs={{0,14},{1,3},{2,0},{3,5},{4,2},{5,7},{6,4},{7,9},{8,6},{9,11},{10,... | collective-permute-start | bytes 983048 | tf_op jit(solution)/shard_map/ppermute | solution.py:50
  16.4 7.9 %collective-permute-start.10 = (bf16[80,2048]{1,0:T(8,128)(2,1)S(1)}, bf16[80,2048]{1,0:T(8,128)(2,1)S(1)}, u32[]{:S(2)}, u32[]{:S(2)}) collective-permute-start(bf16[80,2048]{1,0:T(8,128)(2,1)S(1)} %pad_maximum_fusion.1.refs_12_), channel_id=1, source_target_pairs={{0,2},{1,15},{2,4},{3,1},{4,6},{5,3},{6,8},{7,5},{8,10},{9,7},{10,... | collective-permute-start | bytes 983048 | tf_op jit(solution)/shard_map/ppermute | solution.py:50
  19.1 33.2 %collective-permute-start.1 = (bf16[128,2048]{1,0:T(8,128)(2,1)S(1)}, bf16[128,2048]{1,0:T(8,128)(2,1)S(1)}, u32[]{:S(2)}, u32[]{:S(2)}) collective-permute-start(bf16[128,2048]{1,0:T(8,128)(2,1)S(1)} %get-tuple-element.37.refs_0_), channel_id=1, source_target_pairs={{0,16},{1,17},{2,18},{3,19},{4,20},{5,21},{6,22},{7,23},{8,24},{9,... | collective-permute-start | bytes 1572872 | tf_op jit(solution)/shard_map/ppermute | solution.py:50
  24.3 16.4 %collective-permute-start.14 = (bf16[80,2048]{1,0:T(8,128)(2,1)S(1)}, bf16[80,2048]{1,0:T(8,128)(2,1)S(1)}, u32[]{:S(2)}, u32[]{:S(2)}) collective-permute-start(bf16[80,2048]{1,0:T(8,128)(2,1)S(1)} %collective-permute-done.10.refs_13_), channel_id=1, source_target_pairs={{0,2},{1,15},{2,4},{3,1},{4,6},{5,3},{6,8},{7,5},{8,10},{9,7},{10,... | collective-permute-start | bytes 983048 | tf_op jit(solution)/shard_map/ppermute | solution.py:50
  27.7 13.0 %collective-permute-start.15 = (bf16[80,2048]{1,0:T(8,128)(2,1)S(1)}, bf16[80,2048]{1,0:T(8,128)(2,1)S(1)}, u32[]{:S(2)}, u32[]{:S(2)}) collective-permute-start(bf16[80,2048]{1,0:T(8,128)(2,1)S(1)} %collective-permute-done.11.refs_14_), channel_id=1, source_target_pairs={{0,14},{1,3},{2,0},{3,5},{4,2},{5,7},{6,4},{7,9},{8,6},{9,11},{10,... | collective-permute-start | bytes 983048 | tf_op jit(solution)/shard_map/ppermute | solution.py:50
  27.7 6.6 %collective-permute-start.5 = (bf16[48,2048]{1,0:T(8,128)(2,1)S(1)}, bf16[48,2048]{1,0:T(8,128)(2,1)S(1)}, u32[]{:S(2)}, u32[]{:S(2)}) collective-permute-start(bf16[48,2048]{1,0:T(8,128)(2,1)S(1)} %collective-permute-done.refs_5_), channel_id=1, source_target_pairs={{0,2},{1,15},{2,4},{3,1},{4,6},{5,3},{6,8},{7,5},{8,10},{9,7},{10,... | collective-permute-start | bytes 589832 | tf_op jit(solution)/shard_map/ppermute | solution.py:50
  30.4 10.3 %collective-permute-start.6 = (bf16[48,2048]{1,0:T(8,128)(2,1)S(1)}, bf16[48,2048]{1,0:T(8,128)(2,1)S(1)}, u32[]{:S(2)}, u32[]{:S(2)}) collective-permute-start(bf16[48,2048]{1,0:T(8,128)(2,1)S(1)} %collective-permute-done.4.refs_6_), channel_id=1, source_target_pairs={{0,14},{1,3},{2,0},{3,5},{4,2},{5,7},{6,4},{7,9},{8,6},{9,11},{10,... | collective-permute-start | bytes 589832 | tf_op jit(solution)/shard_map/ppermute | solution.py:50
  40.7 4.5 %collective-permute-start.12 = (bf16[48,2048]{1,0:T(8,128)(2,1)S(1)}, bf16[48,2048]{1,0:T(8,128)(2,1)S(1)}, u32[]{:S(2)}, u32[]{:S(2)}) collective-permute-start(bf16[48,2048]{1,0:T(8,128)(2,1)S(1)} %collective-permute-done.5.refs_7_), channel_id=1, source_target_pairs={{0,2},{1,15},{2,4},{3,1},{4,6},{5,3},{6,8},{7,5},{8,10},{9,7},{10,... | collective-permute-start | bytes 589832 | tf_op jit(solution)/shard_map/ppermute | solution.py:50
  40.7 16.5 %collective-permute-start.17 = (bf16[80,2048]{1,0:T(8,128)(2,1)S(1)}, bf16[80,2048]{1,0:T(8,128)(2,1)S(1)}, u32[]{:S(2)}, u32[]{:S(2)}) collective-permute-start(bf16[80,2048]{1,0:T(8,128)(2,1)S(1)} %collective-permute-done.14.refs_15_), channel_id=1, source_target_pairs={{0,2},{1,15},{2,4},{3,1},{4,6},{5,3},{6,8},{7,5},{8,10},{9,7},{10,... | collective-permute-start | bytes 983048 | tf_op jit(solution)/shard_map/ppermute | solution.py:50
  42.9 14.3 %collective-permute-start.18 = (bf16[80,2048]{1,0:T(8,128)(2,1)S(1)}, bf16[80,2048]{1,0:T(8,128)(2,1)S(1)}, u32[]{:S(2)}, u32[]{:S(2)}) collective-permute-start(bf16[80,2048]{1,0:T(8,128)(2,1)S(1)} %collective-permute-done.15.refs_16_), channel_id=1, source_target_pairs={{0,14},{1,3},{2,0},{3,5},{4,2},{5,7},{6,4},{7,9},{8,6},{9,11},{10,... | collective-permute-start | bytes 983048 | tf_op jit(solution)/shard_map/ppermute | solution.py:50
  42.9 14.3 %collective-permute-start.13 = (bf16[48,2048]{1,0:T(8,128)(2,1)S(1)}, bf16[48,2048]{1,0:T(8,128)(2,1)S(1)}, u32[]{:S(2)}, u32[]{:S(2)}) collective-permute-start(bf16[48,2048]{1,0:T(8,128)(2,1)S(1)} %collective-permute-done.6.refs_8_), channel_id=1, source_target_pairs={{0,14},{1,3},{2,0},{3,5},{4,2},{5,7},{6,4},{7,9},{8,6},{9,11},{10,... | collective-permute-start | bytes 589832 | tf_op jit(solution)/shard_map/ppermute | solution.py:50
  45.2 13.1 %collective-permute-start.2 = (bf16[128,2048]{1,0:T(8,128)(2,1)S(1)}, bf16[128,2048]{1,0:T(8,128)(2,1)S(1)}, u32[]{:S(2)}, u32[]{:S(2)}) collective-permute-start(bf16[128,2048]{1,0:T(8,128)(2,1)S(1)} %get-tuple-element.37.refs_0_), channel_id=1, source_target_pairs={{0,1},{1,0},{2,3},{3,2},{4,5},{5,4},{6,7},{7,6},{8,9},{9,8},{10,11... | collective-permute-start | bytes 1572872 | tf_op jit(solution)/shard_map/ppermute | solution.py:50
  52.2 13.3 %collective-permute-start.3 = (bf16[128,2048]{1,0:T(8,128)(2,1)S(1)}, bf16[128,2048]{1,0:T(8,128)(2,1)S(1)}, u32[]{:S(2)}, u32[]{:S(2)}) collective-permute-start(bf16[128,2048]{1,0:T(8,128)(2,1)S(1)} %collective-permute-done.1.refs_1_), channel_id=1, source_target_pairs={{0,1},{1,0},{2,3},{3,2},{4,5},{5,4},{6,7},{7,6},{8,9},{9,8},{10,11... | collective-permute-start | bytes 1572872 | tf_op jit(solution)/shard_map/ppermute | solution.py:50
  57.2 8.3 %collective-permute-start.19 = (bf16[80,2048]{1,0:T(8,128)(2,1)S(1)}, bf16[80,2048]{1,0:T(8,128)(2,1)S(1)}, u32[]{:S(2)}, u32[]{:S(2)}) collective-permute-start(bf16[80,2048]{1,0:T(8,128)(2,1)S(1)} %collective-permute-done.17.refs_17_), channel_id=1, source_target_pairs={{0,2},{1,15},{2,4},{3,1},{4,6},{5,3},{6,8},{7,5},{8,10},{9,7},{10,... | collective-permute-start | bytes 983048 | tf_op jit(solution)/shard_map/ppermute | solution.py:50
  58.2 7.4 %collective-permute-start.16 = (bf16[48,2048]{1,0:T(8,128)(2,1)S(1)}, bf16[48,2048]{1,0:T(8,128)(2,1)S(1)}, u32[]{:S(2)}, u32[]{:S(2)}) collective-permute-start(bf16[48,2048]{1,0:T(8,128)(2,1)S(1)} %collective-permute-done.12.refs_9_), channel_id=1, source_target_pairs={{0,2},{1,15},{2,4},{3,1},{4,6},{5,3},{6,8},{7,5},{8,10},{9,7},{10,... | collective-permute-start | bytes 589832 | tf_op jit(solution)/shard_map/ppermute | solution.py:50
  68.5 5.5 %collective-permute-start.21 = (bf16[128,2048]{1,0:T(8,128)(2,1)S(1)}, bf16[128,2048]{1,0:T(8,128)(2,1)S(1)}, u32[]{:S(2)}, u32[]{:S(2)}) collective-permute-start(bf16[128,2048]{1,0:T(8,128)(2,1)S(1)} %get-tuple-element.53.own_ref), channel_id=1, source_target_pairs={{0,1},{1,0},{2,3},{3,2},{4,5},{5,4},{6,7},{7,6},{8,9},{9,8},{10,11... | collective-permute-start | bytes 1572872 | tf_op jit(solution)/shard_map/ppermute | solution.py:50
  71.9 2.1 %collective-permute-start.20 = (bf16[512,384]{1,0:T(8,128)(2,1)S(1)}, bf16[512,384]{1,0:T(8,128)(2,1)S(1)}, u32[]{:S(2)}, u32[]{:S(2)}) collective-permute-start(bf16[512,384]{1,0:T(8,128)(2,1)S(1)} %get-tuple-element.52), channel_id=1, source_target_pairs={{0,1},{1,0},{2,3},{3,2},{4,5},{5,4},{6,7},{7,6},{8,9},{9,8},{10,11... | collective-permute-start | bytes 1179656 | tf_op jit(solution)/shard_map/ppermute | solution.py:50
  74.0 17.6 %collective-permute-start.29 = (bf16[128,2048]{1,0:T(8,128)(2,1)S(1)}, bf16[128,2048]{1,0:T(8,128)(2,1)S(1)}, u32[]{:S(2)}, u32[]{:S(2)}) collective-permute-start(bf16[128,2048]{1,0:T(8,128)(2,1)S(1)} %get-tuple-element.62.mine), channel_id=1, source_target_pairs={{0,96},{32,0},{64,32},{96,64},{128,224},{160,128},{192,160},{224,1... | collective-permute-start | bytes 1572872 | tf_op jit(solution)/shard_map/ppermute | solution.py:50
  76.7 17.6 %collective-permute-start.28 = (bf16[128,2048]{1,0:T(8,128)(2,1)S(1)}, bf16[128,2048]{1,0:T(8,128)(2,1)S(1)}, u32[]{:S(2)}, u32[]{:S(2)}) collective-permute-start(bf16[128,2048]{1,0:T(8,128)(2,1)S(1)} %get-tuple-element.62.mine), channel_id=1, source_target_pairs={{0,32},{32,64},{64,96},{96,0},{128,160},{160,192},{192,224},{224,1... | collective-permute-start | bytes 1572872 | tf_op jit(solution)/shard_map/ppermute | solution.py:50
  76.7 5.6 %collective-permute-start.23 = (bf16[256,256]{1,0:T(8,128)(2,1)S(1)}, bf16[256,256]{1,0:T(8,128)(2,1)S(1)}, u32[]{:S(2)}, u32[]{:S(2)}) collective-permute-start(bf16[256,256]{1,0:T(8,128)(2,1)S(1)} %get-tuple-element.57), channel_id=1, source_target_pairs={{0,2},{1,3},{2,4},{3,5},{4,6},{5,7},{6,8},{7,9},{8,10},{9,11},{10,... | collective-permute-start | bytes 393224 | tf_op jit(solution)/shard_map/ppermute | solution.py:50
  76.7 9.5 %collective-permute-start.24 = (bf16[256,256]{1,0:T(8,128)(2,1)S(1)}, bf16[256,256]{1,0:T(8,128)(2,1)S(1)}, u32[]{:S(2)}, u32[]{:S(2)}) collective-permute-start(bf16[256,256]{1,0:T(8,128)(2,1)S(1)} %get-tuple-element.58), channel_id=1, source_target_pairs={{0,3},{1,2},{2,5},{3,4},{4,7},{5,6},{6,9},{7,8},{8,11},{9,10},{10,... | collective-permute-start | bytes 393224 | tf_op jit(solution)/shard_map/ppermute | solution.py:50
  76.7 9.5 %collective-permute-start.25 = (bf16[256,256]{1,0:T(8,128)(2,1)S(1)}, bf16[256,256]{1,0:T(8,128)(2,1)S(1)}, u32[]{:S(2)}, u32[]{:S(2)}) collective-permute-start(bf16[256,256]{1,0:T(8,128)(2,1)S(1)} %get-tuple-element.59), channel_id=1, source_target_pairs={{0,14},{1,15},{2,0},{3,1},{4,2},{5,3},{6,4},{7,5},{8,6},{9,7},{10,... | collective-permute-start | bytes 393224 | tf_op jit(solution)/shard_map/ppermute | solution.py:50
  82.3 4.7 %collective-permute-start.26 = (bf16[256,256]{1,0:T(8,128)(2,1)S(1)}, bf16[256,256]{1,0:T(8,128)(2,1)S(1)}, u32[]{:S(2)}, u32[]{:S(2)}) collective-permute-start(bf16[256,256]{1,0:T(8,128)(2,1)S(1)} %get-tuple-element.60), channel_id=1, source_target_pairs={{0,15},{1,14},{2,1},{3,0},{4,3},{5,2},{6,5},{7,4},{8,7},{9,6},{10,... | collective-permute-start | bytes 393224 | tf_op jit(solution)/shard_map/ppermute | solution.py:50
  91.6 7.1 %collective-permute-start.31 = (bf16[64,2048]{1,0:T(8,128)(2,1)S(1)}, bf16[64,2048]{1,0:T(8,128)(2,1)S(1)}, u32[]{:S(2)}, u32[]{:S(2)}) collective-permute-start(bf16[64,2048]{1,0:T(8,128)(2,1)S(1)} %slice.75), channel_id=1, source_target_pairs={{0,96},{32,0},{64,32},{96,64},{128,224},{160,128},{192,160},{224,1... | collective-permute-start | bytes 786440 | tf_op jit(solution)/shard_map/ppermute | solution.py:50
  94.4 6.5 %collective-permute-start.30 = (bf16[64,2048]{1,0:T(8,128)(2,1)S(1)}, bf16[64,2048]{1,0:T(8,128)(2,1)S(1)}, u32[]{:S(2)}, u32[]{:S(2)}) collective-permute-start(bf16[64,2048]{1,0:T(8,128)(2,1)S(1)} %slice.74), channel_id=1, source_target_pairs={{0,32},{32,64},{64,96},{96,0},{128,160},{160,192},{192,224},{224,1... | collective-permute-start | bytes 786440 | tf_op jit(solution)/shard_map/ppermute | solution.py:50
  94.5 4.2 %collective-permute-start.27 = (bf16[256,256]{1,0:T(8,128)(2,1)S(1)}, bf16[256,256]{1,0:T(8,128)(2,1)S(1)}, u32[]{:S(2)}, u32[]{:S(2)}) collective-permute-start(bf16[256,256]{1,0:T(8,128)(2,1)S(1)} %get-tuple-element.67), channel_id=1, source_target_pairs={{0,16},{1,17},{2,18},{3,19},{4,20},{5,21},{6,22},{7,23},{8,24},{9,... | collective-permute-start | bytes 393224 | tf_op jit(solution)/shard_map/ppermute | solution.py:50
  102.2 5.1 %collective-permute-start.32 = (bf16[128,2048]{1,0:T(8,128)(2,1)S(1)}, bf16[128,2048]{1,0:T(8,128)(2,1)S(1)}, u32[]{:S(2)}, u32[]{:S(2)}) collective-permute-start(bf16[128,2048]{1,0:T(8,128)(2,1)S(1)} %get-tuple-element.64), channel_id=1, source_target_pairs={{0,1},{1,0},{2,3},{3,2},{4,5},{5,4},{6,7},{7,6},{8,9},{9,8},{10,11... | collective-permute-start | bytes 1572872 | tf_op jit(solution)/shard_map/ppermute | solution.py:50
  (4 other events, 32.1 us)

commit v5 on v4

--- a/solution.py
+++ b/solution.py
@@ -91,8 +91,8 @@
 
 
 def project_kernel(index, *refs):
-    blocks, firsts, seconds = refs[:4], refs[4 : 4 + SHARDS], refs[4 + SHARDS : 4 + 2 * SHARDS]
-    keep_ref, send_ref, g_rows, far_table, out_rows, *edges, rows, table, sems = refs[4 + 2 * SHARDS :]
+    blocks, shards = refs[:4], refs[4 : 4 + SHARDS]
+    keep_ref, send_ref, far_table, *edges, rows, table, sems = refs[4 + SHARDS :]
     z, core, x = index[0], index[1], index[2]
     low_core = core == 0
     copies = []
@@ -105,12 +105,8 @@
         for kind in range(3):
             into = table if kind == 0 else far_table
             base = 0 if kind == 0 else kind * 256 - 256
-            here = pl.multiple_of(base + at, 16)
-            into[pl.ds(here, 16), :] = firsts[j][kind * 16 : kind * 16 + 16, :]
-            there = pl.multiple_of(base + at + 16, 16)
-            into[pl.ds(there, 16), :] = seconds[j][kind * 16 : kind * 16 + 16, :]
-        g_rows[j * 16 : j * 16 + 16, :] = seconds[j][48:64, :]
-        out_rows[j * 16 : j * 16 + 16, :] = seconds[j][64:80, :]
+            here = pl.multiple_of(base + at, HALF)
+            into[pl.ds(here, HALF), :] = shards[j][kind * HALF : kind * HALF + HALF, :]
     for copy in copies:
         copy.wait()
     for kind in range(3):
@@ -127,6 +123,13 @@
                     into = slice(seg * TOK, seg * TOK + TOK)
                     edges[2 * part][into, lanes_out] = keep_ref[at, lanes]
                     edges[2 * part + 1][into, lanes_out] = send_ref[at, lanes]
+
+
+def collect_kernel(*refs):
+    riders, g_rows, out_rows = refs[1 : 1 + SHARDS], refs[1 + SHARDS], refs[2 + SHARDS]
+    for j in range(SHARDS):
+        g_rows[j * 16 : j * 16 + 16, :] = riders[j][:16, :]
+        out_rows[j * 16 : j * 16 + 16, :] = riders[j][16:, :]
 
 
 def far_kernel(index, own_ref, other_ref, table, keep_ref, send_ref):
@@ -271,8 +274,7 @@
     y = lax.axis_index("doc") & (Y - 1)
     index = jnp.stack([z, core, x, limit, me * TOK, y]).astype(jnp.int32)
 
-    mine = jnp.stack([w_query.T, w_key.T, w_value.T]).reshape(3, 2, 16, width)
-    first = mine[:, 0].reshape(48, width)
+    first = jnp.concatenate([w_query.T, w_key.T, w_value.T], axis=0)
 
     normed, global_mine = on_chip(
         norm_kernel,
@@ -304,7 +306,6 @@
 
     second = jnp.concatenate(
         [
-            mine[:, 1].reshape(48, width),
             jnp.where(x == 0, global_mine, global_there),
             jnp.where(x == 0, global_there, global_mine),
             jnp.concatenate([both[i * 16 : i * 16 + 16] for i in range(8)], axis=1),
@@ -315,21 +316,19 @@
     one, two = {(0, 0): first}, {(0, 0): second}
     a_one, a_two, b_one, b_two = first, second, first, second
     for step in range(1, 5):
-        if step > 1:
-            before = (two[0, step - 2], two[1, step - 2]) if step > 2 else ()
+        if step > 2:
+            before = two[0, step - 2], two[1, step - 2]
             a_one, b_one = lax.optimization_barrier((a_one, b_one, *before))[:2]
         one[0, step] = a_one = send(a_one, AHEAD)
         if step < 4:
             one[1, step] = b_one = send(b_one, BEHIND)
-        if step == 1:
-            a_two = b_two = after(second, a_one, b_one)
-        else:
-            a_two, b_two = lax.optimization_barrier((a_two, b_two, one[0, step - 1], one[1, step - 1]))[:2]
+        before = one[0, max(step - 1, 1)], one[1, max(step - 1, 1)]
+        a_two, b_two = lax.optimization_barrier((a_two, b_two, *before))[:2]
         two[0, step] = a_two = send(a_two, AHEAD)
         if step < 4:
             two[1, step] = b_two = send(b_two, BEHIND)
-    firsts = [one[s] for s in STEPS]
-    seconds = [two[s] for s in STEPS]
+    shards = [one[s] for s in STEPS]
+    riders = [two[s] for s in STEPS]
 
     to_send = after(normed, one[0, 1])
     across = send(to_send, OTHER_X)
@@ -337,23 +336,23 @@
     beside_across = send(across, OTHER_CORE)
 
     half = jax.ShapeDtypeStruct((ROWS, 3 * 128), bf16)
-    keep, to_swap, g_own, far_table, out_own, *edges = on_chip(
+    keep, to_swap, far_table, *edges = on_chip(
         project_kernel,
         (
             half,
             half,
-            jax.ShapeDtypeStruct((G_ROWS, width), bf16),
             jax.ShapeDtypeStruct((2 * Z * HALF, width), bf16),
-            jax.ShapeDtypeStruct((128, width), bf16),
             *[jax.ShapeDtypeStruct((2 * TOK, 256), bf16)] * 4,
         ),
         2 * ROWS * 768 * width,
         0,
-        (index, normed, across, beside, beside_across, *firsts, *seconds),
+        (index, normed, across, beside, beside_across, *shards),
         (pltpu.VMEM((ROWS, width), bf16), pltpu.VMEM((Z * HALF, width), bf16), pltpu.SemaphoreType.DMA((4,))),
         in_hbm=4,
     )
     got = send(to_swap, OTHER_CORE)
+    block = jax.ShapeDtypeStruct((G_ROWS, width), bf16)
+    g_own, out_own = on_chip(collect_kernel, (block, block), 0, 0, (index, *riders))
     g_other = send(g_own, OTHER_CORE)
 
     below = send(edges[2], UP), send(edges[3], UP_CROSS)
@@ -364,7 +363,7 @@
     )
     g_got = send(g_swap, OTHER_CORE)
 
-    to_pass = after(out_own, got, g_other)
+    to_pass = after(out_own, below[0], above[0])
     out_prev = send(to_pass, Y_UP, "doc")
     out_next = send(to_pass, Y_DOWN, "doc")
     out_far_a = send(out_prev[:64], Y_UP, "doc")

time: 109 us -> 109 us (level)
  starting transfers between devices: 46.8 us -> 41.6 us
  waiting for transfers between devices: 45.3 us -> 48.7 us
  local copies, waits for them, and re-layouts: 1.28 us -> 3.67 us
    ppermute x33, starting transfers between devices: 46.8 us -> 41.6 us  [send(): return lax.ppermute(value, axis, route)]
    ppermute x33, waiting for transfers between devices: 45.3 us -> 48.7 us  [send(): return lax.ppermute(value, axis, route)]
    unnamed x6, local copies, waits for them, and re-layouts: 0.01 us -> 2.44 us
    another operation x1 -> x0, other arithmetic: 1.13 us -> none  [per_device(): mine = jnp.stack([w_query.T, w_key.T, w_value.T]).reshape(3, 2, 16, width)]
    pallas_call x5 -> x6, Pallas kernels: 11.5 us -> 12.1 us  [on_chip(): pl.pallas_call(kernel, out_shape=out_shape, in_specs=specs, out_specs=jax...]
  transfers between devices with their start and end apart: 33 -> 33, of which waited for: 17 -> 13; matrix products, arithmetic and copies ran while one was open for 0% -> 0% of each run, Pallas kernels for 7% -> 10%
where the time goes in v5:
time: 109 us
  waiting for transfers between devices  48.7 us (45%)
  starting transfers between devices  41.6 us (38%)
  Pallas kernels  12.1 us (11%)
  local copies, waits for them, and re-layouts  3.67 us (3%)
  other arithmetic  2.22 us (2%)
    ppermute x33, waiting for transfers between devices, send(): return lax.ppermute(value, axis, route)  48.7 us
    ppermute x33, starting transfers between devices, send(): return lax.ppermute(value, axis, route)  41.6 us
    pallas_call x6, Pallas kernels, on_chip(): pl.pallas_call(kernel, out_shape=out_shape, in_specs=specs, out_specs=jax...  12.1 us
    unnamed x6, local copies, waits for them, and re-layouts  2.44 us
  transfers between devices with their start and end apart: 33, of which 13 were waited for; matrix products, arithmetic and copies ran while one was open for 0% of the time, Pallas kernels for 10%

profile of v5, /device:TPU:1, one launch (start us, length us, event | category | flops | bytes accessed | tf_op | source)
XLA Modules:
  0.0 109.2 jit_solution(16037271083240481174)
XLA Ops:
  2.2 3.3 %collective-permute-start.8 = (bf16[128,64]{1,0:T(8,128)(2,1)S(1)}, bf16[128,64]{1,0:T(8,128)(2,1)S(1)}, u32[]{:S(2)}, u32[]{:S(2)}) collective-permute-start(bf16[128,64]{1,0:T(8,128)(2,1)S(1)} %bitcast.25), channel_id=1, source_target_pairs={{0,1},{1,0},{2,3},{3,2},{4,5},{5,4},{6,7},{7,6},{8,9},{9,8},{10,11... | collective-permute-start | bytes 49160 | tf_op jit(solution)/shard_map/ppermute | solution.py:50
  5.5 3.8 %collective-permute-start = (bf16[96,2048]{1,0:T(8,128)(2,1)S(1)}, bf16[96,2048]{1,0:T(8,128)(2,1)S(1)}, u32[]{:S(2)}, u32[]{:S(2)}) collective-permute-start(bf16[96,2048]{1,0:T(8,128)(2,1)S(1)} %pad_maximum_fusion.refs_4_), channel_id=1, source_target_pairs={{0,2},{1,15},{2,4},{3,1},{4,6},{5,3},{6,8},{7,5},{8,10},{9,7},{10,... | collective-permute-start | bytes 1179656 | tf_op jit(solution)/shard_map/ppermute | solution.py:50
  13.8 1.3 %collective-permute-start.7 = (bf16[8,2048]{1,0:T(8,128)(2,1)S(1)}, bf16[8,2048]{1,0:T(8,128)(2,1)S(1)}, u32[]{:S(2)}, u32[]{:S(2)}) collective-permute-start(bf16[8,2048]{1,0:T(8,128)(2,1)S(1)} %get-tuple-element.37), channel_id=1, source_target_pairs={{0,16},{1,17},{2,18},{3,19},{4,20},{5,21},{6,22},{7,23},{8,24},{9,... | collective-permute-start | bytes 98312 | tf_op jit(solution)/shard_map/ppermute | solution.py:50
  15.5 1.3 %collective-permute-done.7 = bf16[8,2048]{1,0:T(8,128)(2,1)S(1)} collective-permute-done((bf16[8,2048]{1,0:T(8,128)(2,1)S(1)}, bf16[8,2048]{1,0:T(8,128)(2,1)S(1)}, u32[]{:S(2)}, u32[]{:S(2)}) %collective-permute-start.7) | collective-permute-done | bytes 32800 | tf_op jit(solution)/shard_map/ppermute | solution.py:50
  18.2 3.2 %collective-permute-start.5 = (bf16[96,2048]{1,0:T(8,128)(2,1)S(1)}, bf16[96,2048]{1,0:T(8,128)(2,1)S(1)}, u32[]{:S(2)}, u32[]{:S(2)}) collective-permute-start(bf16[96,2048]{1,0:T(8,128)(2,1)S(1)} %collective-permute-done.refs_5_), channel_id=1, source_target_pairs={{0,2},{1,15},{2,4},{3,1},{4,6},{5,3},{6,8},{7,5},{8,10},{9,7},{10,... | collective-permute-start | bytes 1179656 | tf_op jit(solution)/shard_map/ppermute | solution.py:50
  22.4 2.7 %collective-permute-start.10 = (bf16[32,2048]{1,0:T(8,128)(2,1)S(1)}, bf16[32,2048]{1,0:T(8,128)(2,1)S(1)}, u32[]{:S(2)}, u32[]{:S(2)}) collective-permute-start(bf16[32,2048]{1,0:T(8,128)(2,1)S(1)} %pad_maximum_fusion.1.refs_1_), channel_id=1, source_target_pairs={{0,2},{1,15},{2,4},{3,1},{4,6},{5,3},{6,8},{7,5},{8,10},{9,7},{10,... | collective-permute-start | bytes 393224 | tf_op jit(solution)/shard_map/ppermute | solution.py:50
  25.1 5.9 %collective-permute-done.10.refs_2_ = bf16[32,2048]{1,0:T(8,128)(2,1)S(1)} collective-permute-done((bf16[32,2048]{1,0:T(8,128)(2,1)S(1)}, bf16[32,2048]{1,0:T(8,128)(2,1)S(1)}, u32[]{:S(2)}, u32[]{:S(2)}) %collective-permute-start.10) | collective-permute-done | bytes 131104 | tf_op jit(solution)/shard_map/ppermute | solution.py:50
  31.0 4.6 %collective-permute-done.11.refs_3_ = bf16[32,2048]{1,0:T(8,128)(2,1)S(1)} collective-permute-done((bf16[32,2048]{1,0:T(8,128)(2,1)S(1)}, bf16[32,2048]{1,0:T(8,128)(2,1)S(1)}, u32[]{:S(2)}, u32[]{:S(2)}) %collective-permute-start.11) | collective-permute-done | bytes 131104 | tf_op jit(solution)/shard_map/ppermute | solution.py:50
  35.5 1.5 %collective-permute-start.13 = (bf16[96,2048]{1,0:T(8,128)(2,1)S(1)}, bf16[96,2048]{1,0:T(8,128)(2,1)S(1)}, u32[]{:S(2)}, u32[]{:S(2)}) collective-permute-start(bf16[96,2048]{1,0:T(8,128)(2,1)S(1)} %collective-permute-done.6.refs_8_), channel_id=1, source_target_pairs={{0,14},{1,3},{2,0},{3,5},{4,2},{5,7},{6,4},{7,9},{8,6},{9,11},{10,... | collective-permute-start | bytes 1179656 | tf_op jit(solution)/shard_map/ppermute | solution.py:50
  37.0 1.3 %collective-permute-start.14 = (bf16[32,2048]{1,0:T(8,128)(2,1)S(1)}, bf16[32,2048]{1,0:T(8,128)(2,1)S(1)}, u32[]{:S(2)}, u32[]{:S(2)}) collective-permute-start(bf16[32,2048]{1,0:T(8,128)(2,1)S(1)} %collective-permute-done.10.refs_2_), channel_id=1, source_target_pairs={{0,2},{1,15},{2,4},{3,1},{4,6},{5,3},{6,8},{7,5},{8,10},{9,7},{10,... | collective-permute-start | bytes 393224 | tf_op jit(solution)/shard_map/ppermute | solution.py:50
  38.5 10.5 %collective-permute-done.14.refs_4_ = bf16[32,2048]{1,0:T(8,128)(2,1)S(1)} collective-permute-done((bf16[32,2048]{1,0:T(8,128)(2,1)S(1)}, bf16[32,2048]{1,0:T(8,128)(2,1)S(1)}, u32[]{:S(2)}, u32[]{:S(2)}) %collective-permute-start.14) | collective-permute-done | bytes 131104 | tf_op jit(solution)/shard_map/ppermute | solution.py:50
  49.0 2.1 %collective-permute-start.2 = (bf16[128,2048]{1,0:T(8,128)(2,1)S(1)}, bf16[128,2048]{1,0:T(8,128)(2,1)S(1)}, u32[]{:S(2)}, u32[]{:S(2)}) collective-permute-start(bf16[128,2048]{1,0:T(8,128)(2,1)S(1)} %get-tuple-element.36.refs_0_), channel_id=1, source_target_pairs={{0,1},{1,0},{2,3},{3,2},{4,5},{5,4},{6,7},{7,6},{8,9},{9,8},{10,11... | collective-permute-start | bytes 1572872 | tf_op jit(solution)/shard_map/ppermute | solution.py:50
  51.6 1.5 %collective-permute-start.19 = (bf16[32,2048]{1,0:T(8,128)(2,1)S(1)}, bf16[32,2048]{1,0:T(8,128)(2,1)S(1)}, u32[]{:S(2)}, u32[]{:S(2)}) collective-permute-start(bf16[32,2048]{1,0:T(8,128)(2,1)S(1)} %collective-permute-done.15.refs_5_), channel_id=1, source_target_pairs={{0,14},{1,3},{2,0},{3,5},{4,2},{5,7},{6,4},{7,9},{8,6},{9,11},{10,... | collective-permute-start | bytes 393224 | tf_op jit(solution)/shard_map/ppermute | solution.py:50
  53.0 8.2 %collective-permute-done.18.refs_6_ = bf16[32,2048]{1,0:T(8,128)(2,1)S(1)} collective-permute-done((bf16[32,2048]{1,0:T(8,128)(2,1)S(1)}, bf16[32,2048]{1,0:T(8,128)(2,1)S(1)}, u32[]{:S(2)}, u32[]{:S(2)}) %collective-permute-start.18) | collective-permute-done | bytes 131104 | tf_op jit(solution)/shard_map/ppermute | solution.py:50
  62.3 2.8 %collective-permute-done.20.refs_8_ = bf16[32,2048]{1,0:T(8,128)(2,1)S(1)} collective-permute-done((bf16[32,2048]{1,0:T(8,128)(2,1)S(1)}, bf16[32,2048]{1,0:T(8,128)(2,1)S(1)}, u32[]{:S(2)}, u32[]{:S(2)}) %collective-permute-start.20) | collective-permute-done | bytes 131104 | tf_op jit(solution)/shard_map/ppermute | solution.py:50
  65.6 4.2 %collective-permute-start.21 = (bf16[128,2048]{1,0:T(8,128)(2,1)S(1)}, bf16[128,2048]{1,0:T(8,128)(2,1)S(1)}, u32[]{:S(2)}, u32[]{:S(2)}) collective-permute-start(bf16[128,2048]{1,0:T(8,128)(2,1)S(1)} %get-tuple-element.51.own_ref), channel_id=1, source_target_pairs={{0,1},{1,0},{2,3},{3,2},{4,5},{5,4},{6,7},{7,6},{8,9},{9,8},{10,11... | collective-permute-start | bytes 1572872 | tf_op jit(solution)/shard_map/ppermute | solution.py:50
  69.9 2.9 %shard_map.83 = (bf16[512,384]{1,0:T(8,128)(2,1)S(1)}, bf16[512,384]{1,0:T(8,128)(2,1)S(1)}, bf16[512,2048]{1,0:T(8,128)(2,1)S(1)}, bf16[256,256]{1,0:T(8,128)(2...) custom-call(s32[6]{0:T(128)S(1)} %stack.23.index.refs_0_, ...), custom_call_target="tpu_custom_call" | custom-call | flops 1610612736 | bytes 4194304 | tf_op jit(solution)/shard_map/pallas_call | solution.py:251
  72.9 2.7 %collective-permute-start.25 = (bf16[256,256]{1,0:T(8,128)(2,1)S(1)}, bf16[256,256]{1,0:T(8,128)(2,1)S(1)}, u32[]{:S(2)}, u32[]{:S(2)}) collective-permute-start(bf16[256,256]{1,0:T(8,128)(2,1)S(1)} %get-tuple-element.57), channel_id=1, source_target_pairs={{0,14},{1,15},{2,0},{3,1},{4,2},{5,3},{6,4},{7,5},{8,6},{9,7},{10,... | collective-permute-start | bytes 393224 | tf_op jit(solution)/shard_map/ppermute | solution.py:50
  75.5 3.6 %collective-permute-done.23.below_ref = bf16[256,256]{1,0:T(8,128)(2,1)S(1)} collective-permute-done((bf16[256,256]{1,0:T(8,128)(2,1)S(1)}, bf16[256,256]{1,0:T(8,128)(2,1)S(1)}, u32[]{:S(2)}, u32[]{:S(2)}) %collective-permute-start.23) | collective-permute-done | bytes 131104 | tf_op jit(solution)/shard_map/ppermute | solution.py:50
  79.1 1.3 %collective-permute-start.28 = (bf16[128,2048]{1,0:T(8,128)(2,1)S(1)}, bf16[128,2048]{1,0:T(8,128)(2,1)S(1)}, u32[]{:S(2)}, u32[]{:S(2)}) collective-permute-start(bf16[128,2048]{1,0:T(8,128)(2,1)S(1)} %get-tuple-element.60.mine), channel_id=1, source_target_pairs={{0,32},{32,64},{64,96},{96,0},{128,160},{160,192},{192,224},{224,1... | collective-permute-start | bytes 1572872 | tf_op jit(solution)/shard_map/ppermute | solution.py:50
  80.4 1.4 %collective-permute-start.29 = (bf16[128,2048]{1,0:T(8,128)(2,1)S(1)}, bf16[128,2048]{1,0:T(8,128)(2,1)S(1)}, u32[]{:S(2)}, u32[]{:S(2)}) collective-permute-start(bf16[128,2048]{1,0:T(8,128)(2,1)S(1)} %get-tuple-element.60.mine), channel_id=1, source_target_pairs={{0,96},{32,0},{64,32},{96,64},{128,224},{160,128},{192,160},{224,1... | collective-permute-start | bytes 1572872 | tf_op jit(solution)/shard_map/ppermute | solution.py:50
  81.9 1.3 %collective-permute-start.17 = (bf16[512,384]{1,0:T(8,128)(2,1)S(1)}, bf16[512,384]{1,0:T(8,128)(2,1)S(1)}, u32[]{:S(2)}, u32[]{:S(2)}) collective-permute-start(bf16[512,384]{1,0:T(8,128)(2,1)S(1)} %get-tuple-element.47), channel_id=1, source_target_pairs={{0,1},{1,0},{2,3},{3,2},{4,5},{5,4},{6,7},{7,6},{8,9},{9,8},{10,11... | collective-permute-start | bytes 1179656 | tf_op jit(solution)/shard_map/ppermute | solution.py:50
  83.2 3.0 %collective-permute-start.26 = (bf16[256,256]{1,0:T(8,128)(2,1)S(1)}, bf16[256,256]{1,0:T(8,128)(2,1)S(1)}, u32[]{:S(2)}, u32[]{:S(2)}) collective-permute-start(bf16[256,256]{1,0:T(8,128)(2,1)S(1)} %get-tuple-element.58), channel_id=1, source_target_pairs={{0,15},{1,14},{2,1},{3,0},{4,3},{5,2},{6,5},{7,4},{8,7},{9,6},{10,... | collective-permute-start | bytes 393224 | tf_op jit(solution)/shard_map/ppermute | solution.py:50
  86.2 2.1 %shard_map.85 = (bf16[256,256]{1,0:T(8,128)(2,1)S(1)}, bf16[256,256]{1,0:T(8,128)(2,1)S(1)}) custom-call(s32[6]{0:T(128)S(1)} %stack.23.index.refs_0_, bf16[128,2048]{1,0:T(8,128)(2,1)S(1)} %get-tuple-element.51.own_ref, bf16[128,2048]{1,0:T(8,128)(2,1)S(1)} %collective-permute-done.21.other_ref, bf16[512,2048]{1,0:T(8,128)(2,1)S(1)} %get-tuple-element.52.table), custom_call_target="tpu_custom_call" | custom-call | flops 536870912 | bytes 4194304 | tf_op jit(solution)/shard_map/pallas_call | solution.py:251
  88.2 1.7 %collective-permute-done.24.below_got = bf16[256,256]{1,0:T(8,128)(2,1)S(1)} collective-permute-done((bf16[256,256]{1,0:T(8,128)(2,1)S(1)}, bf16[256,256]{1,0:T(8,128)(2,1)S(1)}, u32[]{:S(2)}, u32[]{:S(2)}) %collective-permute-start.24) | collective-permute-done | bytes 131104 | tf_op jit(solution)/shard_map/ppermute | solution.py:50
  89.9 1.3 %collective-permute-done.22.g_got = bf16[256,256]{1,0:T(8,128)(2,1)S(1)} collective-permute-done((bf16[256,256]{1,0:T(8,128)(2,1)S(1)}, bf16[256,256]{1,0:T(8,128)(2,1)S(1)}, u32[]{:S(2)}, u32[]{:S(2)}) %collective-permute-start.22) | collective-permute-done | bytes 131104 | tf_op jit(solution)/shard_map/ppermute | solution.py:50
  91.3 4.0 %shard_map.86 = bf16[2,256,256]{2,1,0:T(8,128)(2,1)S(1)} custom-call(s32[6]{0:T(128)S(1)} %stack.23.index.refs_0_, bf16[512,384]{1,0:T(8,128)(2,1)S(1)} %get-tuple-element.46.keep_ref, bf16[512,384]{1,0:T(8,128)(2,1)S(1)} %collective-permute-done.17.got_ref, bf16[256,256]{1,0:T(8,128)(2,1)S(1)} %get-tuple-element.53.g_keep, ...), custom_call_target="tpu_custom_call" | custom-call | flops 1342177280 | bytes 4194304 | tf_op jit(solution)/shard_map/pallas_call | solution.py:251
  95.4 2.7 %collective-permute-start.31 = (bf16[64,2048]{1,0:T(8,128)(2,1)S(1)}, bf16[64,2048]{1,0:T(8,128)(2,1)S(1)}, u32[]{:S(2)}, u32[]{:S(2)}) collective-permute-start(bf16[64,2048]{1,0:T(8,128)(2,1)S(1)} %slice.65), channel_id=1, source_target_pairs={{0,96},{32,0},{64,32},{96,64},{128,224},{160,128},{192,160},{224,1... | collective-permute-start | bytes 786440 | tf_op jit(solution)/shard_map/ppermute | solution.py:50
  98.3 4.3 %collective-permute-done.27.there_ref = bf16[256,256]{1,0:T(8,128)(2,1)S(1)} collective-permute-done((bf16[256,256]{1,0:T(8,128)(2,1)S(1)}, bf16[256,256]{1,0:T(8,128)(2,1)S(1)}, u32[]{:S(2)}, u32[]{:S(2)}) %collective-permute-start.27) | collective-permute-done | bytes 131104 | tf_op jit(solution)/shard_map/ppermute | solution.py:50
  102.6 1.8 %collective-permute-done.30.far_a = bf16[64,2048]{1,0:T(8,128)(2,1)S(1)} collective-permute-done((bf16[64,2048]{1,0:T(8,128)(2,1)S(1)}, bf16[64,2048]{1,0:T(8,128)(2,1)S(1)}, u32[]{:S(2)}, u32[]{:S(2)}) %collective-permute-start.30) | collective-permute-done | bytes 262176 | tf_op jit(solution)/shard_map/ppermute | solution.py:50
  104.4 1.3 %shard_map.87 = (f32[128,2048]{1,0:T(8,128)S(1)}, bf16[128,2048]{1,0:T(8,128)(2,1)S(1)}) custom-call(s32[6]{0:T(128)S(1)} %stack.23.index.refs_0_, bf16[256,256]{1,0:T(8,128)(2,1)S(1)} %get-tuple-element.64.own_ref, bf16[256,256]{1,0:T(8,128)(2,1)S(1)} %collective-permute-done.27.there_ref, bf16[128,2048]{1,0:T(8,128)(2,1)S(1)} %get-tuple-element.60.mine, ...), custom_call_target="tpu_custom_call" | custom-call | flops 536870912 | bytes 4194304 | tf_op jit(solution)/shard_map/pallas_call | solution.py:251
  106.7 1.5 %collective-permute-done.32 = bf16[128,2048]{1,0:T(8,128)(2,1)S(1)} collective-permute-done((bf16[128,2048]{1,0:T(8,128)(2,1)S(1)}, bf16[128,2048]{1,0:T(8,128)(2,1)S(1)}, u32[]{:S(2)}, u32[]{:S(2)}) %collective-permute-start.32) | collective-permute-done | bytes 524320 | tf_op jit(solution)/shard_map/ppermute | solution.py:50
  (67 shorter events, 13.3 us)
Async XLA Ops:
  2.2 12.9 %collective-permute-start.8 = (bf16[128,64]{1,0:T(8,128)(2,1)S(1)}, bf16[128,64]{1,0:T(8,128)(2,1)S(1)}, u32[]{:S(2)}, u32[]{:S(2)}) collective-permute-start(bf16[128,64]{1,0:T(8,128)(2,1)S(1)} %bitcast.25), channel_id=1, source_target_pairs={{0,1},{1,0},{2,3},{3,2},{4,5},{5,4},{6,7},{7,6},{8,9},{9,8},{10,11... | collective-permute-start | bytes 49160 | tf_op jit(solution)/shard_map/ppermute | solution.py:50
  5.5 12.7 %collective-permute-start = (bf16[96,2048]{1,0:T(8,128)(2,1)S(1)}, bf16[96,2048]{1,0:T(8,128)(2,1)S(1)}, u32[]{:S(2)}, u32[]{:S(2)}) collective-permute-start(bf16[96,2048]{1,0:T(8,128)(2,1)S(1)} %pad_maximum_fusion.refs_4_), channel_id=1, source_target_pairs={{0,2},{1,15},{2,4},{3,1},{4,6},{5,3},{6,8},{7,5},{8,10},{9,7},{10,... | collective-permute-start | bytes 1179656 | tf_op jit(solution)/shard_map/ppermute | solution.py:50
  9.3 12.1 %collective-permute-start.4 = (bf16[96,2048]{1,0:T(8,128)(2,1)S(1)}, bf16[96,2048]{1,0:T(8,128)(2,1)S(1)}, u32[]{:S(2)}, u32[]{:S(2)}) collective-permute-start(bf16[96,2048]{1,0:T(8,128)(2,1)S(1)} %pad_maximum_fusion.refs_4_), channel_id=1, source_target_pairs={{0,14},{1,3},{2,0},{3,5},{4,2},{5,7},{6,4},{7,9},{8,6},{9,11},{10,... | collective-permute-start | bytes 1179656 | tf_op jit(solution)/shard_map/ppermute | solution.py:50
  13.8 3.0 %collective-permute-start.7 = (bf16[8,2048]{1,0:T(8,128)(2,1)S(1)}, bf16[8,2048]{1,0:T(8,128)(2,1)S(1)}, u32[]{:S(2)}, u32[]{:S(2)}) collective-permute-start(bf16[8,2048]{1,0:T(8,128)(2,1)S(1)} %get-tuple-element.37), channel_id=1, source_target_pairs={{0,16},{1,17},{2,18},{3,19},{4,20},{5,21},{6,22},{7,23},{8,24},{9,... | collective-permute-start | bytes 98312 | tf_op jit(solution)/shard_map/ppermute | solution.py:50
  15.2 2.9 %collective-permute-start.9 = (bf16[128,128]{1,0:T(8,128)(2,1)S(1)}, bf16[128,128]{1,0:T(8,128)(2,1)S(1)}, u32[]{:S(2)}, u32[]{:S(2)}) collective-permute-start(bf16[128,128]{1,0:T(8,128)(2,1)S(1)} %pad_maximum_fusion.2), channel_id=1, source_target_pairs={{0,16},{1,17},{2,18},{3,19},{4,20},{5,21},{6,22},{7,23},{8,24},{9,... | collective-permute-start | bytes 98312 | tf_op jit(solution)/shard_map/ppermute | solution.py:50
  18.2 17.3 %collective-permute-start.5 = (bf16[96,2048]{1,0:T(8,128)(2,1)S(1)}, bf16[96,2048]{1,0:T(8,128)(2,1)S(1)}, u32[]{:S(2)}, u32[]{:S(2)}) collective-permute-start(bf16[96,2048]{1,0:T(8,128)(2,1)S(1)} %collective-permute-done.refs_5_), channel_id=1, source_target_pairs={{0,2},{1,15},{2,4},{3,1},{4,6},{5,3},{6,8},{7,5},{8,10},{9,7},{10,... | collective-permute-start | bytes 1179656 | tf_op jit(solution)/shard_map/ppermute | solution.py:50
  21.5 14.1 %collective-permute-start.6 = (bf16[96,2048]{1,0:T(8,128)(2,1)S(1)}, bf16[96,2048]{1,0:T(8,128)(2,1)S(1)}, u32[]{:S(2)}, u32[]{:S(2)}) collective-permute-start(bf16[96,2048]{1,0:T(8,128)(2,1)S(1)} %collective-permute-done.4.refs_6_), channel_id=1, source_target_pairs={{0,14},{1,3},{2,0},{3,5},{4,2},{5,7},{6,4},{7,9},{8,6},{9,11},{10,... | collective-permute-start | bytes 1179656 | tf_op jit(solution)/shard_map/ppermute | solution.py:50
  21.5 29.7 %collective-permute-start.1 = (bf16[128,2048]{1,0:T(8,128)(2,1)S(1)}, bf16[128,2048]{1,0:T(8,128)(2,1)S(1)}, u32[]{:S(2)}, u32[]{:S(2)}) collective-permute-start(bf16[128,2048]{1,0:T(8,128)(2,1)S(1)} %get-tuple-element.36.refs_0_), channel_id=1, source_target_pairs={{0,16},{1,17},{2,18},{3,19},{4,20},{5,21},{6,22},{7,23},{8,24},{9,... | collective-permute-start | bytes 1572872 | tf_op jit(solution)/shard_map/ppermute | solution.py:50
  22.4 8.5 %collective-permute-start.10 = (bf16[32,2048]{1,0:T(8,128)(2,1)S(1)}, bf16[32,2048]{1,0:T(8,128)(2,1)S(1)}, u32[]{:S(2)}, u32[]{:S(2)}) collective-permute-start(bf16[32,2048]{1,0:T(8,128)(2,1)S(1)} %pad_maximum_fusion.1.refs_1_), channel_id=1, source_target_pairs={{0,2},{1,15},{2,4},{3,1},{4,6},{5,3},{6,8},{7,5},{8,10},{9,7},{10,... | collective-permute-start | bytes 393224 | tf_op jit(solution)/shard_map/ppermute | solution.py:50
  25.1 10.4 %collective-permute-start.11 = (bf16[32,2048]{1,0:T(8,128)(2,1)S(1)}, bf16[32,2048]{1,0:T(8,128)(2,1)S(1)}, u32[]{:S(2)}, u32[]{:S(2)}) collective-permute-start(bf16[32,2048]{1,0:T(8,128)(2,1)S(1)} %pad_maximum_fusion.1.refs_1_), channel_id=1, source_target_pairs={{0,14},{1,3},{2,0},{3,5},{4,2},{5,7},{6,4},{7,9},{8,6},{9,11},{10,... | collective-permute-start | bytes 393224 | tf_op jit(solution)/shard_map/ppermute | solution.py:50
  35.5 15.7 %collective-permute-start.12 = (bf16[96,2048]{1,0:T(8,128)(2,1)S(1)}, bf16[96,2048]{1,0:T(8,128)(2,1)S(1)}, u32[]{:S(2)}, u32[]{:S(2)}) collective-permute-start(bf16[96,2048]{1,0:T(8,128)(2,1)S(1)} %collective-permute-done.5.refs_7_), channel_id=1, source_target_pairs={{0,2},{1,15},{2,4},{3,1},{4,6},{5,3},{6,8},{7,5},{8,10},{9,7},{10,... | collective-permute-start | bytes 1179656 | tf_op jit(solution)/shard_map/ppermute | solution.py:50
  35.5 15.7 %collective-permute-start.13 = (bf16[96,2048]{1,0:T(8,128)(2,1)S(1)}, bf16[96,2048]{1,0:T(8,128)(2,1)S(1)}, u32[]{:S(2)}, u32[]{:S(2)}) collective-permute-start(bf16[96,2048]{1,0:T(8,128)(2,1)S(1)} %collective-permute-done.6.refs_8_), channel_id=1, source_target_pairs={{0,14},{1,3},{2,0},{3,5},{4,2},{5,7},{6,4},{7,9},{8,6},{9,11},{10,... | collective-permute-start | bytes 1179656 | tf_op jit(solution)/shard_map/ppermute | solution.py:50
  37.0 12.0 %collective-permute-start.14 = (bf16[32,2048]{1,0:T(8,128)(2,1)S(1)}, bf16[32,2048]{1,0:T(8,128)(2,1)S(1)}, u32[]{:S(2)}, u32[]{:S(2)}) collective-permute-start(bf16[32,2048]{1,0:T(8,128)(2,1)S(1)} %collective-permute-done.10.refs_2_), channel_id=1, source_target_pairs={{0,2},{1,15},{2,4},{3,1},{4,6},{5,3},{6,8},{7,5},{8,10},{9,7},{10,... | collective-permute-start | bytes 393224 | tf_op jit(solution)/shard_map/ppermute | solution.py:50
  38.3 12.9 %collective-permute-start.15 = (bf16[32,2048]{1,0:T(8,128)(2,1)S(1)}, bf16[32,2048]{1,0:T(8,128)(2,1)S(1)}, u32[]{:S(2)}, u32[]{:S(2)}) collective-permute-start(bf16[32,2048]{1,0:T(8,128)(2,1)S(1)} %collective-permute-done.11.refs_3_), channel_id=1, source_target_pairs={{0,14},{1,3},{2,0},{3,5},{4,2},{5,7},{6,4},{7,9},{8,6},{9,11},{10,... | collective-permute-start | bytes 393224 | tf_op jit(solution)/shard_map/ppermute | solution.py:50
  49.0 20.8 %collective-permute-start.2 = (bf16[128,2048]{1,0:T(8,128)(2,1)S(1)}, bf16[128,2048]{1,0:T(8,128)(2,1)S(1)}, u32[]{:S(2)}, u32[]{:S(2)}) collective-permute-start(bf16[128,2048]{1,0:T(8,128)(2,1)S(1)} %get-tuple-element.36.refs_0_), channel_id=1, source_target_pairs={{0,1},{1,0},{2,3},{3,2},{4,5},{5,4},{6,7},{7,6},{8,9},{9,8},{10,11... | collective-permute-start | bytes 1572872 | tf_op jit(solution)/shard_map/ppermute | solution.py:50
  51.2 18.7 %collective-permute-start.3 = (bf16[128,2048]{1,0:T(8,128)(2,1)S(1)}, bf16[128,2048]{1,0:T(8,128)(2,1)S(1)}, u32[]{:S(2)}, u32[]{:S(2)}) collective-permute-start(bf16[128,2048]{1,0:T(8,128)(2,1)S(1)} %collective-permute-done.1.refs_1_), channel_id=1, source_target_pairs={{0,1},{1,0},{2,3},{3,2},{4,5},{5,4},{6,7},{7,6},{8,9},{9,8},{10,11... | collective-permute-start | bytes 1572872 | tf_op jit(solution)/shard_map/ppermute | solution.py:50
  51.2 18.7 %collective-permute-start.16 = (bf16[96,2048]{1,0:T(8,128)(2,1)S(1)}, bf16[96,2048]{1,0:T(8,128)(2,1)S(1)}, u32[]{:S(2)}, u32[]{:S(2)}) collective-permute-start(bf16[96,2048]{1,0:T(8,128)(2,1)S(1)} %collective-permute-done.12.refs_9_), channel_id=1, source_target_pairs={{0,2},{1,15},{2,4},{3,1},{4,6},{5,3},{6,8},{7,5},{8,10},{9,7},{10,... | collective-permute-start | bytes 1179656 | tf_op jit(solution)/shard_map/ppermute | solution.py:50
  51.5 9.7 %collective-permute-start.18 = (bf16[32,2048]{1,0:T(8,128)(2,1)S(1)}, bf16[32,2048]{1,0:T(8,128)(2,1)S(1)}, u32[]{:S(2)}, u32[]{:S(2)}) collective-permute-start(bf16[32,2048]{1,0:T(8,128)(2,1)S(1)} %collective-permute-done.14.refs_4_), channel_id=1, source_target_pairs={{0,2},{1,15},{2,4},{3,1},{4,6},{5,3},{6,8},{7,5},{8,10},{9,7},{10,... | collective-permute-start | bytes 393224 | tf_op jit(solution)/shard_map/ppermute | solution.py:50
  51.6 9.6 %collective-permute-start.19 = (bf16[32,2048]{1,0:T(8,128)(2,1)S(1)}, bf16[32,2048]{1,0:T(8,128)(2,1)S(1)}, u32[]{:S(2)}, u32[]{:S(2)}) collective-permute-start(bf16[32,2048]{1,0:T(8,128)(2,1)S(1)} %collective-permute-done.15.refs_5_), channel_id=1, source_target_pairs={{0,14},{1,3},{2,0},{3,5},{4,2},{5,7},{6,4},{7,9},{8,6},{9,11},{10,... | collective-permute-start | bytes 393224 | tf_op jit(solution)/shard_map/ppermute | solution.py:50
  61.2 3.8 %collective-permute-start.20 = (bf16[32,2048]{1,0:T(8,128)(2,1)S(1)}, bf16[32,2048]{1,0:T(8,128)(2,1)S(1)}, u32[]{:S(2)}, u32[]{:S(2)}) collective-permute-start(bf16[32,2048]{1,0:T(8,128)(2,1)S(1)} %collective-permute-done.18.refs_6_), channel_id=1, source_target_pairs={{0,2},{1,15},{2,4},{3,1},{4,6},{5,3},{6,8},{7,5},{8,10},{9,7},{10,... | collective-permute-start | bytes 393224 | tf_op jit(solution)/shard_map/ppermute | solution.py:50
  65.6 17.6 %collective-permute-start.21 = (bf16[128,2048]{1,0:T(8,128)(2,1)S(1)}, bf16[128,2048]{1,0:T(8,128)(2,1)S(1)}, u32[]{:S(2)}, u32[]{:S(2)}) collective-permute-start(bf16[128,2048]{1,0:T(8,128)(2,1)S(1)} %get-tuple-element.51.own_ref), channel_id=1, source_target_pairs={{0,1},{1,0},{2,3},{3,2},{4,5},{5,4},{6,7},{7,6},{8,9},{9,8},{10,11... | collective-permute-start | bytes 1572872 | tf_op jit(solution)/shard_map/ppermute | solution.py:50
  72.8 6.4 %collective-permute-start.23 = (bf16[256,256]{1,0:T(8,128)(2,1)S(1)}, bf16[256,256]{1,0:T(8,128)(2,1)S(1)}, u32[]{:S(2)}, u32[]{:S(2)}) collective-permute-start(bf16[256,256]{1,0:T(8,128)(2,1)S(1)} %get-tuple-element.55), channel_id=1, source_target_pairs={{0,2},{1,3},{2,4},{3,5},{4,6},{5,7},{6,8},{7,9},{8,10},{9,11},{10,... | collective-permute-start | bytes 393224 | tf_op jit(solution)/shard_map/ppermute | solution.py:50
  72.9 6.3 %collective-permute-start.25 = (bf16[256,256]{1,0:T(8,128)(2,1)S(1)}, bf16[256,256]{1,0:T(8,128)(2,1)S(1)}, u32[]{:S(2)}, u32[]{:S(2)}) collective-permute-start(bf16[256,256]{1,0:T(8,128)(2,1)S(1)} %get-tuple-element.57), channel_id=1, source_target_pairs={{0,14},{1,15},{2,0},{3,1},{4,2},{5,3},{6,4},{7,5},{8,6},{9,7},{10,... | collective-permute-start | bytes 393224 | tf_op jit(solution)/shard_map/ppermute | solution.py:50
  79.1 16.1 %collective-permute-start.28 = (bf16[128,2048]{1,0:T(8,128)(2,1)S(1)}, bf16[128,2048]{1,0:T(8,128)(2,1)S(1)}, u32[]{:S(2)}, u32[]{:S(2)}) collective-permute-start(bf16[128,2048]{1,0:T(8,128)(2,1)S(1)} %get-tuple-element.60.mine), channel_id=1, source_target_pairs={{0,32},{32,64},{64,96},{96,0},{128,160},{160,192},{192,224},{224,1... | collective-permute-start | bytes 1572872 | tf_op jit(solution)/shard_map/ppermute | solution.py:50
  80.4 15.0 %collective-permute-start.29 = (bf16[128,2048]{1,0:T(8,128)(2,1)S(1)}, bf16[128,2048]{1,0:T(8,128)(2,1)S(1)}, u32[]{:S(2)}, u32[]{:S(2)}) collective-permute-start(bf16[128,2048]{1,0:T(8,128)(2,1)S(1)} %get-tuple-element.60.mine), channel_id=1, source_target_pairs={{0,96},{32,0},{64,32},{96,64},{128,224},{160,128},{192,160},{224,1... | collective-permute-start | bytes 1572872 | tf_op jit(solution)/shard_map/ppermute | solution.py:50
  81.9 8.1 %collective-permute-start.17 = (bf16[512,384]{1,0:T(8,128)(2,1)S(1)}, bf16[512,384]{1,0:T(8,128)(2,1)S(1)}, u32[]{:S(2)}, u32[]{:S(2)}) collective-permute-start(bf16[512,384]{1,0:T(8,128)(2,1)S(1)} %get-tuple-element.47), channel_id=1, source_target_pairs={{0,1},{1,0},{2,3},{3,2},{4,5},{5,4},{6,7},{7,6},{8,9},{9,8},{10,11... | collective-permute-start | bytes 1179656 | tf_op jit(solution)/shard_map/ppermute | solution.py:50
  83.2 6.7 %collective-permute-start.24 = (bf16[256,256]{1,0:T(8,128)(2,1)S(1)}, bf16[256,256]{1,0:T(8,128)(2,1)S(1)}, u32[]{:S(2)}, u32[]{:S(2)}) collective-permute-start(bf16[256,256]{1,0:T(8,128)(2,1)S(1)} %get-tuple-element.56), channel_id=1, source_target_pairs={{0,3},{1,2},{2,5},{3,4},{4,7},{5,6},{6,9},{7,8},{8,11},{9,10},{10,... | collective-permute-start | bytes 393224 | tf_op jit(solution)/shard_map/ppermute | solution.py:50
  83.2 6.7 %collective-permute-start.26 = (bf16[256,256]{1,0:T(8,128)(2,1)S(1)}, bf16[256,256]{1,0:T(8,128)(2,1)S(1)}, u32[]{:S(2)}, u32[]{:S(2)}) collective-permute-start(bf16[256,256]{1,0:T(8,128)(2,1)S(1)} %get-tuple-element.58), channel_id=1, source_target_pairs={{0,15},{1,14},{2,1},{3,0},{4,3},{5,2},{6,5},{7,4},{8,7},{9,6},{10,... | collective-permute-start | bytes 393224 | tf_op jit(solution)/shard_map/ppermute | solution.py:50
  95.3 9.0 %collective-permute-start.30 = (bf16[64,2048]{1,0:T(8,128)(2,1)S(1)}, bf16[64,2048]{1,0:T(8,128)(2,1)S(1)}, u32[]{:S(2)}, u32[]{:S(2)}) collective-permute-start(bf16[64,2048]{1,0:T(8,128)(2,1)S(1)} %slice.64), channel_id=1, source_target_pairs={{0,32},{32,64},{64,96},{96,0},{128,160},{160,192},{192,224},{224,1... | collective-permute-start | bytes 786440 | tf_op jit(solution)/shard_map/ppermute | solution.py:50
  95.4 8.9 %collective-permute-start.31 = (bf16[64,2048]{1,0:T(8,128)(2,1)S(1)}, bf16[64,2048]{1,0:T(8,128)(2,1)S(1)}, u32[]{:S(2)}, u32[]{:S(2)}) collective-permute-start(bf16[64,2048]{1,0:T(8,128)(2,1)S(1)} %slice.65), channel_id=1, source_target_pairs={{0,96},{32,0},{64,32},{96,64},{128,224},{160,128},{192,160},{224,1... | collective-permute-start | bytes 786440 | tf_op jit(solution)/shard_map/ppermute | solution.py:50
  98.2 4.4 %collective-permute-start.27 = (bf16[256,256]{1,0:T(8,128)(2,1)S(1)}, bf16[256,256]{1,0:T(8,128)(2,1)S(1)}, u32[]{:S(2)}, u32[]{:S(2)}) collective-permute-start(bf16[256,256]{1,0:T(8,128)(2,1)S(1)} %get-tuple-element.63), channel_id=1, source_target_pairs={{0,16},{1,17},{2,18},{3,19},{4,20},{5,21},{6,22},{7,23},{8,24},{9,... | collective-permute-start | bytes 393224 | tf_op jit(solution)/shard_map/ppermute | solution.py:50
  105.6 2.6 %collective-permute-start.32 = (bf16[128,2048]{1,0:T(8,128)(2,1)S(1)}, bf16[128,2048]{1,0:T(8,128)(2,1)S(1)}, u32[]{:S(2)}, u32[]{:S(2)}) collective-permute-start(bf16[128,2048]{1,0:T(8,128)(2,1)S(1)} %get-tuple-element.62), channel_id=1, source_target_pairs={{0,1},{1,0},{2,3},{3,2},{4,5},{5,4},{6,7},{7,6},{8,9},{9,8},{10,11... | collective-permute-start | bytes 1572872 | tf_op jit(solution)/shard_map/ppermute | solution.py:50
  (4 other events, 3.8 us)

commit v6 on v4

--- a/solution.py
+++ b/solution.py
@@ -92,7 +92,7 @@
 
 def project_kernel(index, *refs):
     blocks, firsts, seconds = refs[:4], refs[4 : 4 + SHARDS], refs[4 + SHARDS : 4 + 2 * SHARDS]
-    keep_ref, send_ref, g_rows, far_table, out_rows, *edges, rows, table, sems = refs[4 + 2 * SHARDS :]
+    keep_ref, send_ref, g_rows, far_table, *edges, rows, table, sems = refs[4 + 2 * SHARDS :]
     z, core, x = index[0], index[1], index[2]
     low_core = core == 0
     copies = []
@@ -110,7 +110,6 @@
             there = pl.multiple_of(base + at + 16, 16)
             into[pl.ds(there, 16), :] = seconds[j][kind * 16 : kind * 16 + 16, :]
         g_rows[j * 16 : j * 16 + 16, :] = seconds[j][48:64, :]
-        out_rows[j * 16 : j * 16 + 16, :] = seconds[j][64:80, :]
     for copy in copies:
         copy.wait()
     for kind in range(3):
@@ -127,6 +126,11 @@
                     into = slice(seg * TOK, seg * TOK + TOK)
                     edges[2 * part][into, lanes_out] = keep_ref[at, lanes]
                     edges[2 * part + 1][into, lanes_out] = send_ref[at, lanes]
+
+
+def collect_kernel(*refs):
+    for j, ref in enumerate(refs[1 : 1 + SHARDS]):
+        refs[1 + SHARDS][j * 16 : j * 16 + 16, :] = ref[ref.shape[0] - 16 :, :]
 
 
 def far_kernel(index, own_ref, other_ref, table, keep_ref, send_ref):
@@ -302,12 +306,13 @@
     chip_there = send(chip, OTHER_X)
     both = jnp.concatenate([jnp.where(x == 0, chip, chip_there), jnp.where(x == 0, chip_there, chip)], axis=1)
 
+    joining = jnp.concatenate([both[i * 16 : i * 16 + 16] for i in range(8)], axis=1)
+
     second = jnp.concatenate(
         [
             mine[:, 1].reshape(48, width),
             jnp.where(x == 0, global_mine, global_there),
             jnp.where(x == 0, global_there, global_mine),
-            jnp.concatenate([both[i * 16 : i * 16 + 16] for i in range(8)], axis=1),
         ],
         axis=0,
     )
@@ -321,13 +326,17 @@
         one[0, step] = a_one = send(a_one, AHEAD)
         if step < 4:
             one[1, step] = b_one = send(b_one, BEHIND)
-        if step == 1:
-            a_two = b_two = after(second, a_one, b_one)
-        else:
+        if step > 1:
             a_two, b_two = lax.optimization_barrier((a_two, b_two, one[0, step - 1], one[1, step - 1]))[:2]
+        if step == 2:
+            a_two = jnp.concatenate([a_two, joining], axis=0)
+            b_two = jnp.concatenate([b_two, joining], axis=0)
         two[0, step] = a_two = send(a_two, AHEAD)
         if step < 4:
             two[1, step] = b_two = send(b_two, BEHIND)
+    last_b = send(two[1, 3][64:], BEHIND)
+    last_a = send(two[0, 4][64:], AHEAD)
+    joined = [joining, two[0, 2], two[1, 2], two[0, 3], two[1, 3], two[0, 4], last_b, last_a]
     firsts = [one[s] for s in STEPS]
     seconds = [two[s] for s in STEPS]
 
@@ -337,14 +346,13 @@
     beside_across = send(across, OTHER_CORE)
 
     half = jax.ShapeDtypeStruct((ROWS, 3 * 128), bf16)
-    keep, to_swap, g_own, far_table, out_own, *edges = on_chip(
+    keep, to_swap, g_own, far_table, *edges = on_chip(
         project_kernel,
         (
             half,
             half,
             jax.ShapeDtypeStruct((G_ROWS, width), bf16),
             jax.ShapeDtypeStruct((2 * Z * HALF, width), bf16),
-            jax.ShapeDtypeStruct((128, width), bf16),
             *[jax.ShapeDtypeStruct((2 * TOK, 256), bf16)] * 4,
         ),
         2 * ROWS * 768 * width,
@@ -364,7 +372,8 @@
     )
     g_got = send(g_swap, OTHER_CORE)
 
-    to_pass = after(out_own, got, g_other)
+    out_own = on_chip(collect_kernel, jax.ShapeDtypeStruct((128, width), bf16), 0, 0, (index, *joined))
+    to_pass = after(out_own, got)
     out_prev = send(to_pass, Y_UP, "doc")
     out_next = send(to_pass, Y_DOWN, "doc")
     out_far_a = send(out_prev[:64], Y_UP, "doc")

time: 109 us -> 108 us (level); the launches traced: 108 us -> 108 us
  starting transfers between devices: 46.8 us -> 45.4 us
    ppermute x33 -> x35, starting transfers between devices: 46.8 us -> 45.4 us  [send(): return lax.ppermute(value, axis, route)]
    ppermute x33 -> x35, waiting for transfers between devices: 45.3 us -> 46.3 us  [send(): return lax.ppermute(value, axis, route)]
    pallas_call x5 -> x6, Pallas kernels: 11.5 us -> 12 us  [on_chip(): pl.pallas_call(kernel, out_shape=out_shape, in_specs=specs, out_specs=jax...]
  transfers between devices with their start and end apart: 33 -> 35, of which waited for: 17 -> 14; matrix products, arithmetic and copies ran while one was open for 0% -> 0% of each run, Pallas kernels for 7% -> 7%
where the time goes in v6:
time: 108 us
  waiting for transfers between devices  46.3 us (43%)
  starting transfers between devices  45.4 us (42%)
  Pallas kernels  12 us (11%)
  other arithmetic  2.36 us (2%)
  local copies, waits for them, and re-layouts  1.29 us (1%)
    ppermute x35, waiting for transfers between devices, send(): return lax.ppermute(value, axis, route)  46.3 us
    ppermute x35, starting transfers between devices, send(): return lax.ppermute(value, axis, route)  45.4 us
    pallas_call x6, Pallas kernels, on_chip(): pl.pallas_call(kernel, out_shape=out_shape, in_specs=specs, out_specs=jax...  12 us
  transfers between devices with their start and end apart: 35, of which 14 were waited for; matrix products, arithmetic and copies ran while one was open for 0% of the time, Pallas kernels for 7%

profile of v6, /device:TPU:1, one launch (start us, length us, event | category | flops | bytes accessed | tf_op | source)
XLA Modules:
  0.0 108.4 jit_solution(12535999462377631971)
XLA Ops:
  2.3 3.3 %collective-permute-start.12 = (bf16[128,64]{1,0:T(8,128)(2,1)S(1)}, bf16[128,64]{1,0:T(8,128)(2,1)S(1)}, u32[]{:S(2)}, u32[]{:S(2)}) collective-permute-start(bf16[128,64]{1,0:T(8,128)(2,1)S(1)} %bitcast.43), channel_id=1, source_target_pairs={{0,1},{1,0},{2,3},{3,2},{4,5},{5,4},{6,7},{7,6},{8,9},{9,8},{10,11... | collective-permute-start | bytes 49160 | tf_op jit(solution)/shard_map/ppermute | solution.py:50
  5.6 3.9 %collective-permute-start = (bf16[48,2048]{1,0:T(8,128)(2,1)S(1)}, bf16[48,2048]{1,0:T(8,128)(2,1)S(1)}, u32[]{:S(2)}, u32[]{:S(2)}) collective-permute-start(bf16[48,2048]{1,0:T(8,128)(2,1)S(1)} %bitcast.33), channel_id=1, source_target_pairs={{0,2},{1,15},{2,4},{3,1},{4,6},{5,3},{6,8},{7,5},{8,10},{9,7},{10,... | collective-permute-start | bytes 589832 | tf_op jit(solution)/shard_map/ppermute | solution.py:50
  11.5 1.3 %collective-permute-start.7 = (bf16[8,2048]{1,0:T(8,128)(2,1)S(1)}, bf16[8,2048]{1,0:T(8,128)(2,1)S(1)}, u32[]{:S(2)}, u32[]{:S(2)}) collective-permute-start(bf16[8,2048]{1,0:T(8,128)(2,1)S(1)} %get-tuple-element.38), channel_id=1, source_target_pairs={{0,16},{1,17},{2,18},{3,19},{4,20},{5,21},{6,22},{7,23},{8,24},{9,... | collective-permute-start | bytes 98312 | tf_op jit(solution)/shard_map/ppermute | solution.py:50
  14.4 3.3 %collective-permute-start.8 = (bf16[64,2048]{1,0:T(8,128)(2,1)S(1)}, bf16[64,2048]{1,0:T(8,128)(2,1)S(1)}, u32[]{:S(2)}, u32[]{:S(2)}) collective-permute-start(bf16[64,2048]{1,0:T(8,128)(2,1)S(1)} %pad_maximum_fusion.3.refs_12_), channel_id=1, source_target_pairs={{0,2},{1,15},{2,4},{3,1},{4,6},{5,3},{6,8},{7,5},{8,10},{9,7},{10,... | collective-permute-start | bytes 786440 | tf_op jit(solution)/shard_map/ppermute | solution.py:50
  17.9 1.3 %collective-permute-start.1 = (bf16[128,2048]{1,0:T(8,128)(2,1)S(1)}, bf16[128,2048]{1,0:T(8,128)(2,1)S(1)}, u32[]{:S(2)}, u32[]{:S(2)}) collective-permute-start(bf16[128,2048]{1,0:T(8,128)(2,1)S(1)} %get-tuple-element.35.refs_0_), channel_id=1, source_target_pairs={{0,16},{1,17},{2,18},{3,19},{4,20},{5,21},{6,22},{7,23},{8,24},{9,... | collective-permute-start | bytes 1572872 | tf_op jit(solution)/shard_map/ppermute | solution.py:50
  19.2 2.7 %collective-permute-done.8.refs_13_ = bf16[64,2048]{1,0:T(8,128)(2,1)S(1)} collective-permute-done((bf16[64,2048]{1,0:T(8,128)(2,1)S(1)}, bf16[64,2048]{1,0:T(8,128)(2,1)S(1)}, u32[]{:S(2)}, u32[]{:S(2)}) %collective-permute-start.8) | collective-permute-done | bytes 262176 | tf_op jit(solution)/shard_map/ppermute | solution.py:50
  21.9 3.8 %collective-permute-done.9.refs_14_ = bf16[64,2048]{1,0:T(8,128)(2,1)S(1)} collective-permute-done((bf16[64,2048]{1,0:T(8,128)(2,1)S(1)}, bf16[64,2048]{1,0:T(8,128)(2,1)S(1)}, u32[]{:S(2)}, u32[]{:S(2)}) %collective-permute-start.9) | collective-permute-done | bytes 262176 | tf_op jit(solution)/shard_map/ppermute | solution.py:50
  25.9 1.5 %collective-permute-start.15 = (bf16[80,2048]{1,0:T(8,128)(2,1)S(1)}, bf16[80,2048]{1,0:T(8,128)(2,1)S(1)}, u32[]{:S(2)}, u32[]{:S(2)}) collective-permute-start(bf16[80,2048]{1,0:T(8,128)(2,1)S(1)} %get-tuple-element.67), channel_id=1, source_target_pairs={{0,14},{1,3},{2,0},{3,5},{4,2},{5,7},{6,4},{7,9},{8,6},{9,11},{10,... | collective-permute-start | bytes 983048 | tf_op jit(solution)/shard_map/ppermute | solution.py:50
  27.4 1.3 %collective-permute-start.5 = (bf16[48,2048]{1,0:T(8,128)(2,1)S(1)}, bf16[48,2048]{1,0:T(8,128)(2,1)S(1)}, u32[]{:S(2)}, u32[]{:S(2)}) collective-permute-start(bf16[48,2048]{1,0:T(8,128)(2,1)S(1)} %collective-permute-done.refs_5_), channel_id=1, source_target_pairs={{0,2},{1,15},{2,4},{3,1},{4,6},{5,3},{6,8},{7,5},{8,10},{9,7},{10,... | collective-permute-start | bytes 589832 | tf_op jit(solution)/shard_map/ppermute | solution.py:50
  28.9 10.9 %collective-permute-done.5.refs_7_ = bf16[48,2048]{1,0:T(8,128)(2,1)S(1)} collective-permute-done((bf16[48,2048]{1,0:T(8,128)(2,1)S(1)}, bf16[48,2048]{1,0:T(8,128)(2,1)S(1)}, u32[]{:S(2)}, u32[]{:S(2)}) %collective-permute-start.5) | collective-permute-done | bytes 196640 | tf_op jit(solution)/shard_map/ppermute | solution.py:50
  41.1 1.5 %collective-permute-start.18 = (bf16[80,2048]{1,0:T(8,128)(2,1)S(1)}, bf16[80,2048]{1,0:T(8,128)(2,1)S(1)}, u32[]{:S(2)}, u32[]{:S(2)}) collective-permute-start(bf16[80,2048]{1,0:T(8,128)(2,1)S(1)} %collective-permute-done.15.refs_16_.refs_3_), channel_id=1, source_target_pairs={{0,14},{1,3},{2,0},{3,5},{4,2},{5,7},{6,4},{7,9},{8,6},{9,11},{10,... | collective-permute-start | bytes 983048 | tf_op jit(solution)/shard_map/ppermute | solution.py:50
  42.5 1.4 %collective-permute-start.11 = (bf16[48,2048]{1,0:T(8,128)(2,1)S(1)}, bf16[48,2048]{1,0:T(8,128)(2,1)S(1)}, u32[]{:S(2)}, u32[]{:S(2)}) collective-permute-start(bf16[48,2048]{1,0:T(8,128)(2,1)S(1)} %collective-permute-done.6.refs_8_), channel_id=1, source_target_pairs={{0,14},{1,3},{2,0},{3,5},{4,2},{5,7},{6,4},{7,9},{8,6},{9,11},{10,... | collective-permute-start | bytes 589832 | tf_op jit(solution)/shard_map/ppermute | solution.py:50
  43.9 2.9 %collective-permute-done.10.refs_9_ = bf16[48,2048]{1,0:T(8,128)(2,1)S(1)} collective-permute-done((bf16[48,2048]{1,0:T(8,128)(2,1)S(1)}, bf16[48,2048]{1,0:T(8,128)(2,1)S(1)}, u32[]{:S(2)}, u32[]{:S(2)}) %collective-permute-start.10) | collective-permute-done | bytes 196640 | tf_op jit(solution)/shard_map/ppermute | solution.py:50
  46.8 3.5 %collective-permute-start.2 = (bf16[128,2048]{1,0:T(8,128)(2,1)S(1)}, bf16[128,2048]{1,0:T(8,128)(2,1)S(1)}, u32[]{:S(2)}, u32[]{:S(2)}) collective-permute-start(bf16[128,2048]{1,0:T(8,128)(2,1)S(1)} %get-tuple-element.35.refs_0_), channel_id=1, source_target_pairs={{0,1},{1,0},{2,3},{3,2},{4,5},{5,4},{6,7},{7,6},{8,9},{9,8},{10,11... | collective-permute-start | bytes 1572872 | tf_op jit(solution)/shard_map/ppermute | solution.py:50
  50.3 5.4 %collective-permute-done.11.refs_10_ = bf16[48,2048]{1,0:T(8,128)(2,1)S(1)} collective-permute-done((bf16[48,2048]{1,0:T(8,128)(2,1)S(1)}, bf16[48,2048]{1,0:T(8,128)(2,1)S(1)}, u32[]{:S(2)}, u32[]{:S(2)}) %collective-permute-start.11) | collective-permute-done | bytes 196640 | tf_op jit(solution)/shard_map/ppermute | solution.py:50
  55.8 8.2 %collective-permute-done.16.refs_11_ = bf16[48,2048]{1,0:T(8,128)(2,1)S(1)} collective-permute-done((bf16[48,2048]{1,0:T(8,128)(2,1)S(1)}, bf16[48,2048]{1,0:T(8,128)(2,1)S(1)}, u32[]{:S(2)}, u32[]{:S(2)}) %collective-permute-start.16) | collective-permute-done | bytes 196640 | tf_op jit(solution)/shard_map/ppermute | solution.py:50
  64.0 2.9 %shard_map.83 = (bf16[512,384]{1,0:T(8,128)(2,1)S(1)}, bf16[512,384]{1,0:T(8,128)(2,1)S(1)}, bf16[128,2048]{1,0:T(8,128)(2,1)S(1)}, bf16[512,2048]{1,0:T(8,128)(...) custom-call(s32[6]{0:T(128)S(1)} %stack.35.index.refs_0_, ...), custom_call_target="tpu_custom_call" | custom-call | flops 1610612736 | bytes 4194304 | tf_op jit(solution)/shard_map/pallas_call | solution.py:252
  66.9 3.2 %collective-permute-start.20 = (bf16[512,384]{1,0:T(8,128)(2,1)S(1)}, bf16[512,384]{1,0:T(8,128)(2,1)S(1)}, u32[]{:S(2)}, u32[]{:S(2)}) collective-permute-start(bf16[512,384]{1,0:T(8,128)(2,1)S(1)} %get-tuple-element.49), channel_id=1, source_target_pairs={{0,1},{1,0},{2,3},{3,2},{4,5},{5,4},{6,7},{7,6},{8,9},{9,8},{10,11... | collective-permute-start | bytes 1179656 | tf_op jit(solution)/shard_map/ppermute | solution.py:50
  70.2 2.7 %collective-permute-start.29 = (bf16[16,2048]{1,0:T(8,128)(2,1)S(1)}, bf16[16,2048]{1,0:T(8,128)(2,1)S(1)}, u32[]{:S(2)}, u32[]{:S(2)}) collective-permute-start(bf16[16,2048]{1,0:T(8,128)(2,1)S(1)} %slice.83), channel_id=1, source_target_pairs={{0,2},{1,15},{2,4},{3,1},{4,6},{5,3},{6,8},{7,5},{8,10},{9,7},{10,... | collective-permute-start | bytes 196616 | tf_op jit(solution)/shard_map/ppermute | solution.py:50
  72.9 1.6 %collective-permute-done.28.refs_7_ = bf16[16,2048]{1,0:T(8,128)(2,1)S(1)} collective-permute-done((bf16[16,2048]{1,0:T(8,128)(2,1)S(1)}, bf16[16,2048]{1,0:T(8,128)(2,1)S(1)}, u32[]{:S(2)}, u32[]{:S(2)}) %collective-permute-start.28) | collective-permute-done | bytes 65568 | tf_op jit(solution)/shard_map/ppermute | solution.py:50
  75.1 1.4 %collective-permute-start.30 = (bf16[128,2048]{1,0:T(8,128)(2,1)S(1)}, bf16[128,2048]{1,0:T(8,128)(2,1)S(1)}, u32[]{:S(2)}, u32[]{:S(2)}) collective-permute-start(bf16[128,2048]{1,0:T(8,128)(2,1)S(1)} %shard_map.86.mine), channel_id=1, source_target_pairs={{0,32},{32,64},{64,96},{96,0},{128,160},{160,192},{192,224},{224,1... | collective-permute-start | bytes 1572872 | tf_op jit(solution)/shard_map/ppermute | solution.py:50
  76.5 1.5 %collective-permute-start.31 = (bf16[128,2048]{1,0:T(8,128)(2,1)S(1)}, bf16[128,2048]{1,0:T(8,128)(2,1)S(1)}, u32[]{:S(2)}, u32[]{:S(2)}) collective-permute-start(bf16[128,2048]{1,0:T(8,128)(2,1)S(1)} %shard_map.86.mine), channel_id=1, source_target_pairs={{0,96},{32,0},{64,32},{96,64},{128,224},{160,128},{192,160},{224,1... | collective-permute-start | bytes 1572872 | tf_op jit(solution)/shard_map/ppermute | solution.py:50
  78.0 2.4 %collective-permute-start.24 = (bf16[256,256]{1,0:T(8,128)(2,1)S(1)}, bf16[256,256]{1,0:T(8,128)(2,1)S(1)}, u32[]{:S(2)}, u32[]{:S(2)}) collective-permute-start(bf16[256,256]{1,0:T(8,128)(2,1)S(1)} %get-tuple-element.55), channel_id=1, source_target_pairs={{0,3},{1,2},{2,5},{3,4},{4,7},{5,6},{6,9},{7,8},{8,11},{9,10},{10,... | collective-permute-start | bytes 393224 | tf_op jit(solution)/shard_map/ppermute | solution.py:50
  80.5 2.9 %collective-permute-start.25 = (bf16[256,256]{1,0:T(8,128)(2,1)S(1)}, bf16[256,256]{1,0:T(8,128)(2,1)S(1)}, u32[]{:S(2)}, u32[]{:S(2)}) collective-permute-start(bf16[256,256]{1,0:T(8,128)(2,1)S(1)} %get-tuple-element.56), channel_id=1, source_target_pairs={{0,14},{1,15},{2,0},{3,1},{4,2},{5,3},{6,4},{7,5},{8,6},{9,7},{10,... | collective-permute-start | bytes 393224 | tf_op jit(solution)/shard_map/ppermute | solution.py:50
  83.4 2.0 %shard_map.84 = (bf16[256,256]{1,0:T(8,128)(2,1)S(1)}, bf16[256,256]{1,0:T(8,128)(2,1)S(1)}) custom-call(s32[6]{0:T(128)S(1)} %stack.35.index.refs_0_, bf16[128,2048]{1,0:T(8,128)(2,1)S(1)} %get-tuple-element.50.own_ref, bf16[128,2048]{1,0:T(8,128)(2,1)S(1)} %collective-permute-done.21.other_ref, bf16[512,2048]{1,0:T(8,128)(2,1)S(1)} %get-tuple-element.51.table), custom_call_target="tpu_custom_call" | custom-call | flops 536870912 | bytes 4194304 | tf_op jit(solution)/shard_map/pallas_call | solution.py:252
  86.7 2.0 %collective-permute-done.24.below_got = bf16[256,256]{1,0:T(8,128)(2,1)S(1)} collective-permute-done((bf16[256,256]{1,0:T(8,128)(2,1)S(1)}, bf16[256,256]{1,0:T(8,128)(2,1)S(1)}, u32[]{:S(2)}, u32[]{:S(2)}) %collective-permute-start.24) | collective-permute-done | bytes 131104 | tf_op jit(solution)/shard_map/ppermute | solution.py:50
  88.7 1.6 %collective-permute-done.26.above_got = bf16[256,256]{1,0:T(8,128)(2,1)S(1)} collective-permute-done((bf16[256,256]{1,0:T(8,128)(2,1)S(1)}, bf16[256,256]{1,0:T(8,128)(2,1)S(1)}, u32[]{:S(2)}, u32[]{:S(2)}) %collective-permute-start.26) | collective-permute-done | bytes 131104 | tf_op jit(solution)/shard_map/ppermute | solution.py:50
  90.3 4.0 %shard_map.85 = bf16[2,256,256]{2,1,0:T(8,128)(2,1)S(1)} custom-call(s32[6]{0:T(128)S(1)} %stack.35.index.refs_0_, bf16[512,384]{1,0:T(8,128)(2,1)S(1)} %get-tuple-element.48.keep_ref, bf16[512,384]{1,0:T(8,128)(2,1)S(1)} %collective-permute-done.20.got_ref, bf16[256,256]{1,0:T(8,128)(2,1)S(1)} %get-tuple-element.52.g_keep, ...), custom_call_target="tpu_custom_call" | custom-call | flops 1342177280 | bytes 4194304 | tf_op jit(solution)/shard_map/pallas_call | solution.py:252
  94.5 2.7 %collective-permute-start.33 = (bf16[64,2048]{1,0:T(8,128)(2,1)S(1)}, bf16[64,2048]{1,0:T(8,128)(2,1)S(1)}, u32[]{:S(2)}, u32[]{:S(2)}) collective-permute-start(bf16[64,2048]{1,0:T(8,128)(2,1)S(1)} %slice.85), channel_id=1, source_target_pairs={{0,96},{32,0},{64,32},{96,64},{128,224},{160,128},{192,160},{224,1... | collective-permute-start | bytes 786440 | tf_op jit(solution)/shard_map/ppermute | solution.py:50
  98.5 2.9 %collective-permute-done.27.there_ref = bf16[256,256]{1,0:T(8,128)(2,1)S(1)} collective-permute-done((bf16[256,256]{1,0:T(8,128)(2,1)S(1)}, bf16[256,256]{1,0:T(8,128)(2,1)S(1)}, u32[]{:S(2)}, u32[]{:S(2)}) %collective-permute-start.27) | collective-permute-done | bytes 131104 | tf_op jit(solution)/shard_map/ppermute | solution.py:50
  102.9 3.0 %collective-permute-start.34 = (bf16[128,2048]{1,0:T(8,128)(2,1)S(1)}, bf16[128,2048]{1,0:T(8,128)(2,1)S(1)}, u32[]{:S(2)}, u32[]{:S(2)}) collective-permute-start(bf16[128,2048]{1,0:T(8,128)(2,1)S(1)} %get-tuple-element.60), channel_id=1, source_target_pairs={{0,1},{1,0},{2,3},{3,2},{4,5},{5,4},{6,7},{7,6},{8,9},{9,8},{10,11... | collective-permute-start | bytes 1572872 | tf_op jit(solution)/shard_map/ppermute | solution.py:50
  105.9 1.5 %collective-permute-done.34 = bf16[128,2048]{1,0:T(8,128)(2,1)S(1)} collective-permute-done((bf16[128,2048]{1,0:T(8,128)(2,1)S(1)}, bf16[128,2048]{1,0:T(8,128)(2,1)S(1)}, u32[]{:S(2)}, u32[]{:S(2)}) %collective-permute-start.34) | collective-permute-done | bytes 524320 | tf_op jit(solution)/shard_map/ppermute | solution.py:50
  (75 shorter events, 12.9 us)
Async XLA Ops:
  2.3 10.5 %collective-permute-start.12 = (bf16[128,64]{1,0:T(8,128)(2,1)S(1)}, bf16[128,64]{1,0:T(8,128)(2,1)S(1)}, u32[]{:S(2)}, u32[]{:S(2)}) collective-permute-start(bf16[128,64]{1,0:T(8,128)(2,1)S(1)} %bitcast.43), channel_id=1, source_target_pairs={{0,1},{1,0},{2,3},{3,2},{4,5},{5,4},{6,7},{7,6},{8,9},{9,8},{10,11... | collective-permute-start | bytes 49160 | tf_op jit(solution)/shard_map/ppermute | solution.py:50
  5.6 12.3 %collective-permute-start = (bf16[48,2048]{1,0:T(8,128)(2,1)S(1)}, bf16[48,2048]{1,0:T(8,128)(2,1)S(1)}, u32[]{:S(2)}, u32[]{:S(2)}) collective-permute-start(bf16[48,2048]{1,0:T(8,128)(2,1)S(1)} %bitcast.33), channel_id=1, source_target_pairs={{0,2},{1,15},{2,4},{3,1},{4,6},{5,3},{6,8},{7,5},{8,10},{9,7},{10,... | collective-permute-start | bytes 589832 | tf_op jit(solution)/shard_map/ppermute | solution.py:50
  9.5 9.7 %collective-permute-start.4 = (bf16[48,2048]{1,0:T(8,128)(2,1)S(1)}, bf16[48,2048]{1,0:T(8,128)(2,1)S(1)}, u32[]{:S(2)}, u32[]{:S(2)}) collective-permute-start(bf16[48,2048]{1,0:T(8,128)(2,1)S(1)} %bitcast.34), channel_id=1, source_target_pairs={{0,14},{1,3},{2,0},{3,5},{4,2},{5,7},{6,4},{7,9},{8,6},{9,11},{10,... | collective-permute-start | bytes 589832 | tf_op jit(solution)/shard_map/ppermute | solution.py:50
  12.9 4.8 %collective-permute-start.13 = (bf16[128,128]{1,0:T(8,128)(2,1)S(1)}, bf16[128,128]{1,0:T(8,128)(2,1)S(1)}, u32[]{:S(2)}, u32[]{:S(2)}) collective-permute-start(bf16[128,128]{1,0:T(8,128)(2,1)S(1)} %pad_maximum_fusion.4), channel_id=1, source_target_pairs={{0,16},{1,17},{2,18},{3,19},{4,20},{5,21},{6,22},{7,23},{8,24},{9,... | collective-permute-start | bytes 98312 | tf_op jit(solution)/shard_map/ppermute | solution.py:50
  14.4 7.5 %collective-permute-start.8 = (bf16[64,2048]{1,0:T(8,128)(2,1)S(1)}, bf16[64,2048]{1,0:T(8,128)(2,1)S(1)}, u32[]{:S(2)}, u32[]{:S(2)}) collective-permute-start(bf16[64,2048]{1,0:T(8,128)(2,1)S(1)} %pad_maximum_fusion.3.refs_12_), channel_id=1, source_target_pairs={{0,2},{1,15},{2,4},{3,1},{4,6},{5,3},{6,8},{7,5},{8,10},{9,7},{10,... | collective-permute-start | bytes 786440 | tf_op jit(solution)/shard_map/ppermute | solution.py:50
  17.7 8.1 %collective-permute-start.9 = (bf16[64,2048]{1,0:T(8,128)(2,1)S(1)}, bf16[64,2048]{1,0:T(8,128)(2,1)S(1)}, u32[]{:S(2)}, u32[]{:S(2)}) collective-permute-start(bf16[64,2048]{1,0:T(8,128)(2,1)S(1)} %pad_maximum_fusion.3.refs_12_), channel_id=1, source_target_pairs={{0,14},{1,3},{2,0},{3,5},{4,2},{5,7},{6,4},{7,9},{8,6},{9,11},{10,... | collective-permute-start | bytes 786440 | tf_op jit(solution)/shard_map/ppermute | solution.py:50
  17.9 32.4 %collective-permute-start.1 = (bf16[128,2048]{1,0:T(8,128)(2,1)S(1)}, bf16[128,2048]{1,0:T(8,128)(2,1)S(1)}, u32[]{:S(2)}, u32[]{:S(2)}) collective-permute-start(bf16[128,2048]{1,0:T(8,128)(2,1)S(1)} %get-tuple-element.35.refs_0_), channel_id=1, source_target_pairs={{0,16},{1,17},{2,18},{3,19},{4,20},{5,21},{6,22},{7,23},{8,24},{9,... | collective-permute-start | bytes 1572872 | tf_op jit(solution)/shard_map/ppermute | solution.py:50
  25.9 15.1 %collective-permute-start.14 = (bf16[80,2048]{1,0:T(8,128)(2,1)S(1)}, bf16[80,2048]{1,0:T(8,128)(2,1)S(1)}, u32[]{:S(2)}, u32[]{:S(2)}) collective-permute-start(bf16[80,2048]{1,0:T(8,128)(2,1)S(1)} %get-tuple-element.68), channel_id=1, source_target_pairs={{0,2},{1,15},{2,4},{3,1},{4,6},{5,3},{6,8},{7,5},{8,10},{9,7},{10,... | collective-permute-start | bytes 983048 | tf_op jit(solution)/shard_map/ppermute | solution.py:50
  25.9 15.0 %collective-permute-start.15 = (bf16[80,2048]{1,0:T(8,128)(2,1)S(1)}, bf16[80,2048]{1,0:T(8,128)(2,1)S(1)}, u32[]{:S(2)}, u32[]{:S(2)}) collective-permute-start(bf16[80,2048]{1,0:T(8,128)(2,1)S(1)} %get-tuple-element.67), channel_id=1, source_target_pairs={{0,14},{1,3},{2,0},{3,5},{4,2},{5,7},{6,4},{7,9},{8,6},{9,11},{10,... | collective-permute-start | bytes 983048 | tf_op jit(solution)/shard_map/ppermute | solution.py:50
  27.4 12.4 %collective-permute-start.5 = (bf16[48,2048]{1,0:T(8,128)(2,1)S(1)}, bf16[48,2048]{1,0:T(8,128)(2,1)S(1)}, u32[]{:S(2)}, u32[]{:S(2)}) collective-permute-start(bf16[48,2048]{1,0:T(8,128)(2,1)S(1)} %collective-permute-done.refs_5_), channel_id=1, source_target_pairs={{0,2},{1,15},{2,4},{3,1},{4,6},{5,3},{6,8},{7,5},{8,10},{9,7},{10,... | collective-permute-start | bytes 589832 | tf_op jit(solution)/shard_map/ppermute | solution.py:50
  28.7 12.3 %collective-permute-start.6 = (bf16[48,2048]{1,0:T(8,128)(2,1)S(1)}, bf16[48,2048]{1,0:T(8,128)(2,1)S(1)}, u32[]{:S(2)}, u32[]{:S(2)}) collective-permute-start(bf16[48,2048]{1,0:T(8,128)(2,1)S(1)} %collective-permute-done.4.refs_6_), channel_id=1, source_target_pairs={{0,14},{1,3},{2,0},{3,5},{4,2},{5,7},{6,4},{7,9},{8,6},{9,11},{10,... | collective-permute-start | bytes 589832 | tf_op jit(solution)/shard_map/ppermute | solution.py:50
  41.0 5.9 %collective-permute-start.10 = (bf16[48,2048]{1,0:T(8,128)(2,1)S(1)}, bf16[48,2048]{1,0:T(8,128)(2,1)S(1)}, u32[]{:S(2)}, u32[]{:S(2)}) collective-permute-start(bf16[48,2048]{1,0:T(8,128)(2,1)S(1)} %collective-permute-done.5.refs_7_), channel_id=1, source_target_pairs={{0,2},{1,15},{2,4},{3,1},{4,6},{5,3},{6,8},{7,5},{8,10},{9,7},{10,... | collective-permute-start | bytes 589832 | tf_op jit(solution)/shard_map/ppermute | solution.py:50
  41.0 14.7 %collective-permute-start.17 = (bf16[80,2048]{1,0:T(8,128)(2,1)S(1)}, bf16[80,2048]{1,0:T(8,128)(2,1)S(1)}, u32[]{:S(2)}, u32[]{:S(2)}) collective-permute-start(bf16[80,2048]{1,0:T(8,128)(2,1)S(1)} %collective-permute-done.14.refs_15_.refs_2_), channel_id=1, source_target_pairs={{0,2},{1,15},{2,4},{3,1},{4,6},{5,3},{6,8},{7,5},{8,10},{9,7},{10,... | collective-permute-start | bytes 983048 | tf_op jit(solution)/shard_map/ppermute | solution.py:50
  41.1 14.6 %collective-permute-start.18 = (bf16[80,2048]{1,0:T(8,128)(2,1)S(1)}, bf16[80,2048]{1,0:T(8,128)(2,1)S(1)}, u32[]{:S(2)}, u32[]{:S(2)}) collective-permute-start(bf16[80,2048]{1,0:T(8,128)(2,1)S(1)} %collective-permute-done.15.refs_16_.refs_3_), channel_id=1, source_target_pairs={{0,14},{1,3},{2,0},{3,5},{4,2},{5,7},{6,4},{7,9},{8,6},{9,11},{10,... | collective-permute-start | bytes 983048 | tf_op jit(solution)/shard_map/ppermute | solution.py:50
  42.5 13.1 %collective-permute-start.11 = (bf16[48,2048]{1,0:T(8,128)(2,1)S(1)}, bf16[48,2048]{1,0:T(8,128)(2,1)S(1)}, u32[]{:S(2)}, u32[]{:S(2)}) collective-permute-start(bf16[48,2048]{1,0:T(8,128)(2,1)S(1)} %collective-permute-done.6.refs_8_), channel_id=1, source_target_pairs={{0,14},{1,3},{2,0},{3,5},{4,2},{5,7},{6,4},{7,9},{8,6},{9,11},{10,... | collective-permute-start | bytes 589832 | tf_op jit(solution)/shard_map/ppermute | solution.py:50
  46.8 8.9 %collective-permute-start.2 = (bf16[128,2048]{1,0:T(8,128)(2,1)S(1)}, bf16[128,2048]{1,0:T(8,128)(2,1)S(1)}, u32[]{:S(2)}, u32[]{:S(2)}) collective-permute-start(bf16[128,2048]{1,0:T(8,128)(2,1)S(1)} %get-tuple-element.35.refs_0_), channel_id=1, source_target_pairs={{0,1},{1,0},{2,3},{3,2},{4,5},{5,4},{6,7},{7,6},{8,9},{9,8},{10,11... | collective-permute-start | bytes 1572872 | tf_op jit(solution)/shard_map/ppermute | solution.py:50
  50.3 13.7 %collective-permute-start.3 = (bf16[128,2048]{1,0:T(8,128)(2,1)S(1)}, bf16[128,2048]{1,0:T(8,128)(2,1)S(1)}, u32[]{:S(2)}, u32[]{:S(2)}) collective-permute-start(bf16[128,2048]{1,0:T(8,128)(2,1)S(1)} %collective-permute-done.1.refs_1_), channel_id=1, source_target_pairs={{0,1},{1,0},{2,3},{3,2},{4,5},{5,4},{6,7},{7,6},{8,9},{9,8},{10,11... | collective-permute-start | bytes 1572872 | tf_op jit(solution)/shard_map/ppermute | solution.py:50
  55.7 8.3 %collective-permute-start.19 = (bf16[80,2048]{1,0:T(8,128)(2,1)S(1)}, bf16[80,2048]{1,0:T(8,128)(2,1)S(1)}, u32[]{:S(2)}, u32[]{:S(2)}) collective-permute-start(bf16[80,2048]{1,0:T(8,128)(2,1)S(1)} %collective-permute-done.17.refs_17_.refs_4_), channel_id=1, source_target_pairs={{0,2},{1,15},{2,4},{3,1},{4,6},{5,3},{6,8},{7,5},{8,10},{9,7},{10,... | collective-permute-start | bytes 983048 | tf_op jit(solution)/shard_map/ppermute | solution.py:50
  55.7 8.3 %collective-permute-start.16 = (bf16[48,2048]{1,0:T(8,128)(2,1)S(1)}, bf16[48,2048]{1,0:T(8,128)(2,1)S(1)}, u32[]{:S(2)}, u32[]{:S(2)}) collective-permute-start(bf16[48,2048]{1,0:T(8,128)(2,1)S(1)} %collective-permute-done.10.refs_9_), channel_id=1, source_target_pairs={{0,2},{1,15},{2,4},{3,1},{4,6},{5,3},{6,8},{7,5},{8,10},{9,7},{10,... | collective-permute-start | bytes 589832 | tf_op jit(solution)/shard_map/ppermute | solution.py:50
  66.9 8.2 %collective-permute-start.20 = (bf16[512,384]{1,0:T(8,128)(2,1)S(1)}, bf16[512,384]{1,0:T(8,128)(2,1)S(1)}, u32[]{:S(2)}, u32[]{:S(2)}) collective-permute-start(bf16[512,384]{1,0:T(8,128)(2,1)S(1)} %get-tuple-element.49), channel_id=1, source_target_pairs={{0,1},{1,0},{2,3},{3,2},{4,5},{5,4},{6,7},{7,6},{8,9},{9,8},{10,11... | collective-permute-start | bytes 1179656 | tf_op jit(solution)/shard_map/ppermute | solution.py:50
  70.1 10.4 %collective-permute-start.21 = (bf16[128,2048]{1,0:T(8,128)(2,1)S(1)}, bf16[128,2048]{1,0:T(8,128)(2,1)S(1)}, u32[]{:S(2)}, u32[]{:S(2)}) collective-permute-start(bf16[128,2048]{1,0:T(8,128)(2,1)S(1)} %get-tuple-element.50.own_ref), channel_id=1, source_target_pairs={{0,1},{1,0},{2,3},{3,2},{4,5},{5,4},{6,7},{7,6},{8,9},{9,8},{10,11... | collective-permute-start | bytes 1572872 | tf_op jit(solution)/shard_map/ppermute | solution.py:50
  70.2 4.3 %collective-permute-start.28 = (bf16[16,2048]{1,0:T(8,128)(2,1)S(1)}, bf16[16,2048]{1,0:T(8,128)(2,1)S(1)}, u32[]{:S(2)}, u32[]{:S(2)}) collective-permute-start(bf16[16,2048]{1,0:T(8,128)(2,1)S(1)} %slice.82), channel_id=1, source_target_pairs={{0,14},{1,3},{2,0},{3,5},{4,2},{5,7},{6,4},{7,9},{8,6},{9,11},{10,... | collective-permute-start | bytes 196616 | tf_op jit(solution)/shard_map/ppermute | solution.py:50
  70.2 4.3 %collective-permute-start.29 = (bf16[16,2048]{1,0:T(8,128)(2,1)S(1)}, bf16[16,2048]{1,0:T(8,128)(2,1)S(1)}, u32[]{:S(2)}, u32[]{:S(2)}) collective-permute-start(bf16[16,2048]{1,0:T(8,128)(2,1)S(1)} %slice.83), channel_id=1, source_target_pairs={{0,2},{1,15},{2,4},{3,1},{4,6},{5,3},{6,8},{7,5},{8,10},{9,7},{10,... | collective-permute-start | bytes 196616 | tf_op jit(solution)/shard_map/ppermute | solution.py:50
  75.1 19.1 %collective-permute-start.30 = (bf16[128,2048]{1,0:T(8,128)(2,1)S(1)}, bf16[128,2048]{1,0:T(8,128)(2,1)S(1)}, u32[]{:S(2)}, u32[]{:S(2)}) collective-permute-start(bf16[128,2048]{1,0:T(8,128)(2,1)S(1)} %shard_map.86.mine), channel_id=1, source_target_pairs={{0,32},{32,64},{64,96},{96,0},{128,160},{160,192},{192,224},{224,1... | collective-permute-start | bytes 1572872 | tf_op jit(solution)/shard_map/ppermute | solution.py:50
  76.5 18.0 %collective-permute-start.31 = (bf16[128,2048]{1,0:T(8,128)(2,1)S(1)}, bf16[128,2048]{1,0:T(8,128)(2,1)S(1)}, u32[]{:S(2)}, u32[]{:S(2)}) collective-permute-start(bf16[128,2048]{1,0:T(8,128)(2,1)S(1)} %shard_map.86.mine), channel_id=1, source_target_pairs={{0,96},{32,0},{64,32},{96,64},{128,224},{160,128},{192,160},{224,1... | collective-permute-start | bytes 1572872 | tf_op jit(solution)/shard_map/ppermute | solution.py:50
  78.0 7.4 %collective-permute-start.23 = (bf16[256,256]{1,0:T(8,128)(2,1)S(1)}, bf16[256,256]{1,0:T(8,128)(2,1)S(1)}, u32[]{:S(2)}, u32[]{:S(2)}) collective-permute-start(bf16[256,256]{1,0:T(8,128)(2,1)S(1)} %get-tuple-element.54), channel_id=1, source_target_pairs={{0,2},{1,3},{2,4},{3,5},{4,6},{5,7},{6,8},{7,9},{8,10},{9,11},{10,... | collective-permute-start | bytes 393224 | tf_op jit(solution)/shard_map/ppermute | solution.py:50
  78.0 10.7 %collective-permute-start.24 = (bf16[256,256]{1,0:T(8,128)(2,1)S(1)}, bf16[256,256]{1,0:T(8,128)(2,1)S(1)}, u32[]{:S(2)}, u32[]{:S(2)}) collective-permute-start(bf16[256,256]{1,0:T(8,128)(2,1)S(1)} %get-tuple-element.55), channel_id=1, source_target_pairs={{0,3},{1,2},{2,5},{3,4},{4,7},{5,6},{6,9},{7,8},{8,11},{9,10},{10,... | collective-permute-start | bytes 393224 | tf_op jit(solution)/shard_map/ppermute | solution.py:50
  80.5 8.2 %collective-permute-start.25 = (bf16[256,256]{1,0:T(8,128)(2,1)S(1)}, bf16[256,256]{1,0:T(8,128)(2,1)S(1)}, u32[]{:S(2)}, u32[]{:S(2)}) collective-permute-start(bf16[256,256]{1,0:T(8,128)(2,1)S(1)} %get-tuple-element.56), channel_id=1, source_target_pairs={{0,14},{1,15},{2,0},{3,1},{4,2},{5,3},{6,4},{7,5},{8,6},{9,7},{10,... | collective-permute-start | bytes 393224 | tf_op jit(solution)/shard_map/ppermute | solution.py:50
  85.4 4.8 %collective-permute-start.26 = (bf16[256,256]{1,0:T(8,128)(2,1)S(1)}, bf16[256,256]{1,0:T(8,128)(2,1)S(1)}, u32[]{:S(2)}, u32[]{:S(2)}) collective-permute-start(bf16[256,256]{1,0:T(8,128)(2,1)S(1)} %get-tuple-element.57), channel_id=1, source_target_pairs={{0,15},{1,14},{2,1},{3,0},{4,3},{5,2},{6,5},{7,4},{8,7},{9,6},{10,... | collective-permute-start | bytes 393224 | tf_op jit(solution)/shard_map/ppermute | solution.py:50
  94.3 7.3 %collective-permute-start.32 = (bf16[64,2048]{1,0:T(8,128)(2,1)S(1)}, bf16[64,2048]{1,0:T(8,128)(2,1)S(1)}, u32[]{:S(2)}, u32[]{:S(2)}) collective-permute-start(bf16[64,2048]{1,0:T(8,128)(2,1)S(1)} %slice.84), channel_id=1, source_target_pairs={{0,32},{32,64},{64,96},{96,0},{128,160},{160,192},{192,224},{224,1... | collective-permute-start | bytes 786440 | tf_op jit(solution)/shard_map/ppermute | solution.py:50
  94.5 7.2 %collective-permute-start.33 = (bf16[64,2048]{1,0:T(8,128)(2,1)S(1)}, bf16[64,2048]{1,0:T(8,128)(2,1)S(1)}, u32[]{:S(2)}, u32[]{:S(2)}) collective-permute-start(bf16[64,2048]{1,0:T(8,128)(2,1)S(1)} %slice.85), channel_id=1, source_target_pairs={{0,96},{32,0},{64,32},{96,64},{128,224},{160,128},{192,160},{224,1... | collective-permute-start | bytes 786440 | tf_op jit(solution)/shard_map/ppermute | solution.py:50
  102.9 4.5 %collective-permute-start.34 = (bf16[128,2048]{1,0:T(8,128)(2,1)S(1)}, bf16[128,2048]{1,0:T(8,128)(2,1)S(1)}, u32[]{:S(2)}, u32[]{:S(2)}) collective-permute-start(bf16[128,2048]{1,0:T(8,128)(2,1)S(1)} %get-tuple-element.60), channel_id=1, source_target_pairs={{0,1},{1,0},{2,3},{3,2},{4,5},{5,4},{6,7},{7,6},{8,9},{9,8},{10,11... | collective-permute-start | bytes 1572872 | tf_op jit(solution)/shard_map/ppermute | solution.py:50
  (6 other events, 39.3 us)

commit v7 on v4

--- a/solution.py
+++ b/solution.py
@@ -315,19 +315,22 @@
     one, two = {(0, 0): first}, {(0, 0): second}
     a_one, a_two, b_one, b_two = first, second, first, second
     for step in range(1, 5):
+        if step == 2:
+            a_two = b_two = after(second, a_one, b_one)
         if step > 1:
-            before = (two[0, step - 2], two[1, step - 2]) if step > 2 else ()
+            if step > 2:
+                before = one[0, step - 2], one[1, step - 2]
+                a_two, b_two = lax.optimization_barrier((a_two, b_two, *before))[:2]
+            two[0, step - 1] = a_two = send(a_two, AHEAD)
+            two[1, step - 1] = b_two = send(b_two, BEHIND)
+        if step > 2:
+            before = two[0, step - 2], two[1, step - 2]
             a_one, b_one = lax.optimization_barrier((a_one, b_one, *before))[:2]
         one[0, step] = a_one = send(a_one, AHEAD)
         if step < 4:
             one[1, step] = b_one = send(b_one, BEHIND)
-        if step == 1:
-            a_two = b_two = after(second, a_one, b_one)
-        else:
-            a_two, b_two = lax.optimization_barrier((a_two, b_two, one[0, step - 1], one[1, step - 1]))[:2]
-        two[0, step] = a_two = send(a_two, AHEAD)
-        if step < 4:
-            two[1, step] = b_two = send(b_two, BEHIND)
+    a_two = after(a_two, one[0, 3], one[1, 3])
+    two[0, 4] = send(a_two, AHEAD)
     firsts = [one[s] for s in STEPS]
     seconds = [two[s] for s in STEPS]
 
@@ -364,7 +367,7 @@
     )
     g_got = send(g_swap, OTHER_CORE)
 
-    to_pass = after(out_own, got, g_other)
+    to_pass = out_own
     out_prev = send(to_pass, Y_UP, "doc")
     out_next = send(to_pass, Y_DOWN, "doc")
     out_far_a = send(out_prev[:64], Y_UP, "doc")

time: 109 us -> 104 us (0.954)
  starting transfers between devices: 46.8 us -> 42.4 us
    ppermute x33, starting transfers between devices: 46.8 us -> 42.4 us  [send(): return lax.ppermute(value, axis, route)]
  transfers between devices with their start and end apart: 33 -> 33, of which waited for: 17 -> 15; matrix products, arithmetic and copies ran while one was open for 0% -> 0% of each run, Pallas kernels for 7% -> 7%
where the time goes in v7:
time: 104 us
  waiting for transfers between devices  45.5 us (44%)
  starting transfers between devices  42.4 us (41%)
  Pallas kernels  11.5 us (11%)
  other arithmetic  2.31 us (2%)
  local copies, waits for them, and re-layouts  1.28 us (1%)
    ppermute x33, waiting for transfers between devices, send(): return lax.ppermute(value, axis, route)  45.5 us
    ppermute x33, starting transfers between devices, send(): return lax.ppermute(value, axis, route)  42.4 us
    pallas_call x5, Pallas kernels, on_chip(): pl.pallas_call(kernel, out_shape=out_shape, in_specs=specs, out_specs=jax...  11.5 us
  transfers between devices with their start and end apart: 33, of which 15 were waited for; matrix products, arithmetic and copies ran while one was open for 0% of the time, Pallas kernels for 7%

profile of v7, /device:TPU:1, one launch (start us, length us, event | category | flops | bytes accessed | tf_op | source)
XLA Modules:
  0.0 104.0 jit_solution(11704480703305166512)
XLA Ops:
  0.0 1.1 %pad_maximum_fusion = bf16[3,2,16,2048]{3,2,0,1:T(8,128)(2,1)S(1)} fusion(bf16[1,2,16,2048]{3,2,0,1:T(8,128)(2,1)} %bitcast.40, bf16[1,2,16,2048]{3,2,0,1:T(8,128)(2,1)} %bitcast.41, bf16[1,2,16,2048]{3,2,0,1:T(8,128)(2,1)} %bitcast.42), kind=kLoop, calls=%fused_computation.1 | loop fusion | flops 393216 | bytes 786432 | tf_op jit(solution)/shard_map/stack | solution.py:274
  2.3 3.3 %collective-permute-start.8 = (bf16[128,64]{1,0:T(8,128)(2,1)S(1)}, bf16[128,64]{1,0:T(8,128)(2,1)S(1)}, u32[]{:S(2)}, u32[]{:S(2)}) collective-permute-start(bf16[128,64]{1,0:T(8,128)(2,1)S(1)} %bitcast.43), channel_id=1, source_target_pairs={{0,1},{1,0},{2,3},{3,2},{4,5},{5,4},{6,7},{7,6},{8,9},{9,8},{10,11... | collective-permute-start | bytes 49160 | tf_op jit(solution)/shard_map/ppermute | solution.py:50
  5.6 3.9 %collective-permute-start = (bf16[48,2048]{1,0:T(8,128)(2,1)S(1)}, bf16[48,2048]{1,0:T(8,128)(2,1)S(1)}, u32[]{:S(2)}, u32[]{:S(2)}) collective-permute-start(bf16[48,2048]{1,0:T(8,128)(2,1)S(1)} %bitcast.34), channel_id=1, source_target_pairs={{0,2},{1,15},{2,4},{3,1},{4,6},{5,3},{6,8},{7,5},{8,10},{9,7},{10,... | collective-permute-start | bytes 589832 | tf_op jit(solution)/shard_map/ppermute | solution.py:50
  10.3 1.3 %shard_map.82 = (bf16[128,2048]{1,0:T(8,128)(2,1)S(1)}, bf16[8,2048]{1,0:T(8,128)(2,1)S(1)}) custom-call(s32[6]{0:T(128)S(1)} %stack.35.index, bf16[128,2048]{1,0:T(8,128)(2,1)S(1)} %copy-done, f32[1,2048]{1,0:T(1,128)S(1)} %bitcast.36, f32[1,2048]{1,0:T(1,128)S(1)} %bitcast.37), custom_call_target="tpu_custom_call" | custom-call | flops 2097152 | bytes 4194304 | tf_op jit(solution)/shard_map/pallas_call | solution.py:248
  11.5 1.3 %collective-permute-start.7 = (bf16[8,2048]{1,0:T(8,128)(2,1)S(1)}, bf16[8,2048]{1,0:T(8,128)(2,1)S(1)}, u32[]{:S(2)}, u32[]{:S(2)}) collective-permute-start(bf16[8,2048]{1,0:T(8,128)(2,1)S(1)} %get-tuple-element.35), channel_id=1, source_target_pairs={{0,16},{1,17},{2,18},{3,19},{4,20},{5,21},{6,22},{7,23},{8,24},{9,... | collective-permute-start | bytes 98312 | tf_op jit(solution)/shard_map/ppermute | solution.py:50
  13.3 1.4 %collective-permute-done.7 = bf16[8,2048]{1,0:T(8,128)(2,1)S(1)} collective-permute-done((bf16[8,2048]{1,0:T(8,128)(2,1)S(1)}, bf16[8,2048]{1,0:T(8,128)(2,1)S(1)}, u32[]{:S(2)}, u32[]{:S(2)}) %collective-permute-start.7) | collective-permute-done | bytes 32800 | tf_op jit(solution)/shard_map/ppermute | solution.py:50
  14.7 1.4 %collective-permute-done.9 = bf16[128,128]{1,0:T(8,128)(2,1)S(1)} collective-permute-done((bf16[128,128]{1,0:T(8,128)(2,1)S(1)}, bf16[128,128]{1,0:T(8,128)(2,1)S(1)}, u32[]{:S(2)}, u32[]{:S(2)}) %collective-permute-start.9) | collective-permute-done | bytes 32800 | tf_op jit(solution)/shard_map/ppermute | solution.py:50
  16.4 2.7 %collective-permute-start.10 = (bf16[80,2048]{1,0:T(8,128)(2,1)S(1)}, bf16[80,2048]{1,0:T(8,128)(2,1)S(1)}, u32[]{:S(2)}, u32[]{:S(2)}) collective-permute-start(bf16[80,2048]{1,0:T(8,128)(2,1)S(1)} %pad_maximum_fusion.1.refs_12_), channel_id=1, source_target_pairs={{0,2},{1,15},{2,4},{3,1},{4,6},{5,3},{6,8},{7,5},{8,10},{9,7},{10,... | collective-permute-start | bytes 983048 | tf_op jit(solution)/shard_map/ppermute | solution.py:50
  19.3 4.2 %collective-permute-done.11.refs_14_ = bf16[80,2048]{1,0:T(8,128)(2,1)S(1)} collective-permute-done((bf16[80,2048]{1,0:T(8,128)(2,1)S(1)}, bf16[80,2048]{1,0:T(8,128)(2,1)S(1)}, u32[]{:S(2)}, u32[]{:S(2)}) %collective-permute-start.11) | collective-permute-done | bytes 327712 | tf_op jit(solution)/shard_map/ppermute | solution.py:50
  24.3 3.4 %collective-permute-start.14 = (bf16[80,2048]{1,0:T(8,128)(2,1)S(1)}, bf16[80,2048]{1,0:T(8,128)(2,1)S(1)}, u32[]{:S(2)}, u32[]{:S(2)}) collective-permute-start(bf16[80,2048]{1,0:T(8,128)(2,1)S(1)} %collective-permute-done.10.refs_13_), channel_id=1, source_target_pairs={{0,2},{1,15},{2,4},{3,1},{4,6},{5,3},{6,8},{7,5},{8,10},{9,7},{10,... | collective-permute-start | bytes 983048 | tf_op jit(solution)/shard_map/ppermute | solution.py:50
  28.6 1.8 %collective-permute-start.5 = (bf16[48,2048]{1,0:T(8,128)(2,1)S(1)}, bf16[48,2048]{1,0:T(8,128)(2,1)S(1)}, u32[]{:S(2)}, u32[]{:S(2)}) collective-permute-start(bf16[48,2048]{1,0:T(8,128)(2,1)S(1)} %collective-permute-done.refs_5_), channel_id=1, source_target_pairs={{0,2},{1,15},{2,4},{3,1},{4,6},{5,3},{6,8},{7,5},{8,10},{9,7},{10,... | collective-permute-start | bytes 589832 | tf_op jit(solution)/shard_map/ppermute | solution.py:50
  30.4 10.2 %collective-permute-done.6.refs_8_ = bf16[48,2048]{1,0:T(8,128)(2,1)S(1)} collective-permute-done((bf16[48,2048]{1,0:T(8,128)(2,1)S(1)}, bf16[48,2048]{1,0:T(8,128)(2,1)S(1)}, u32[]{:S(2)}, u32[]{:S(2)}) %collective-permute-start.6) | collective-permute-done | bytes 196640 | tf_op jit(solution)/shard_map/ppermute | solution.py:50
  40.8 2.2 %collective-permute-start.12 = (bf16[48,2048]{1,0:T(8,128)(2,1)S(1)}, bf16[48,2048]{1,0:T(8,128)(2,1)S(1)}, u32[]{:S(2)}, u32[]{:S(2)}) collective-permute-start(bf16[48,2048]{1,0:T(8,128)(2,1)S(1)} %collective-permute-done.5.refs_7_), channel_id=1, source_target_pairs={{0,2},{1,15},{2,4},{3,1},{4,6},{5,3},{6,8},{7,5},{8,10},{9,7},{10,... | collective-permute-start | bytes 589832 | tf_op jit(solution)/shard_map/ppermute | solution.py:50
  43.0 3.6 %collective-permute-start.2 = (bf16[128,2048]{1,0:T(8,128)(2,1)S(1)}, bf16[128,2048]{1,0:T(8,128)(2,1)S(1)}, u32[]{:S(2)}, u32[]{:S(2)}) collective-permute-start(bf16[128,2048]{1,0:T(8,128)(2,1)S(1)} %get-tuple-element.34.refs_0_), channel_id=1, source_target_pairs={{0,1},{1,0},{2,3},{3,2},{4,5},{5,4},{6,7},{7,6},{8,9},{9,8},{10,11... | collective-permute-start | bytes 1572872 | tf_op jit(solution)/shard_map/ppermute | solution.py:50
  46.6 2.6 %collective-permute-done.12.refs_9_ = bf16[48,2048]{1,0:T(8,128)(2,1)S(1)} collective-permute-done((bf16[48,2048]{1,0:T(8,128)(2,1)S(1)}, bf16[48,2048]{1,0:T(8,128)(2,1)S(1)}, u32[]{:S(2)}, u32[]{:S(2)}) %collective-permute-start.12) | collective-permute-done | bytes 196640 | tf_op jit(solution)/shard_map/ppermute | solution.py:50
  50.3 3.3 %collective-permute-start.19 = (bf16[80,2048]{1,0:T(8,128)(2,1)S(1)}, bf16[80,2048]{1,0:T(8,128)(2,1)S(1)}, u32[]{:S(2)}, u32[]{:S(2)}) collective-permute-start(bf16[80,2048]{1,0:T(8,128)(2,1)S(1)} %collective-permute-done.17.refs_17_), channel_id=1, source_target_pairs={{0,2},{1,15},{2,4},{3,1},{4,6},{5,3},{6,8},{7,5},{8,10},{9,7},{10,... | collective-permute-start | bytes 983048 | tf_op jit(solution)/shard_map/ppermute | solution.py:50
  54.3 8.1 %collective-permute-done.16.refs_11_ = bf16[48,2048]{1,0:T(8,128)(2,1)S(1)} collective-permute-done((bf16[48,2048]{1,0:T(8,128)(2,1)S(1)}, bf16[48,2048]{1,0:T(8,128)(2,1)S(1)}, u32[]{:S(2)}, u32[]{:S(2)}) %collective-permute-start.16) | collective-permute-done | bytes 196640 | tf_op jit(solution)/shard_map/ppermute | solution.py:50
  62.5 3.0 %shard_map.83 = (bf16[512,384]{1,0:T(8,128)(2,1)S(1)}, bf16[512,384]{1,0:T(8,128)(2,1)S(1)}, bf16[128,2048]{1,0:T(8,128)(2,1)S(1)}, bf16[512,2048]{1,0:T(8,128)(...) custom-call(s32[6]{0:T(128)S(1)} %stack.35.index, ...), custom_call_target="tpu_custom_call" | custom-call | flops 1610612736 | bytes 4194304 | tf_op jit(solution)/shard_map/pallas_call | solution.py:248
  65.5 4.5 %collective-permute-start.21 = (bf16[128,2048]{1,0:T(8,128)(2,1)S(1)}, bf16[128,2048]{1,0:T(8,128)(2,1)S(1)}, u32[]{:S(2)}, u32[]{:S(2)}) collective-permute-start(bf16[128,2048]{1,0:T(8,128)(2,1)S(1)} %get-tuple-element.48.own_ref), channel_id=1, source_target_pairs={{0,1},{1,0},{2,3},{3,2},{4,5},{5,4},{6,7},{7,6},{8,9},{9,8},{10,11... | collective-permute-start | bytes 1572872 | tf_op jit(solution)/shard_map/ppermute | solution.py:50
  70.0 2.7 %collective-permute-start.29 = (bf16[128,2048]{1,0:T(8,128)(2,1)S(1)}, bf16[128,2048]{1,0:T(8,128)(2,1)S(1)}, u32[]{:S(2)}, u32[]{:S(2)}) collective-permute-start(bf16[128,2048]{1,0:T(8,128)(2,1)S(1)} %get-tuple-element.56.mine), channel_id=1, source_target_pairs={{0,96},{32,0},{64,32},{96,64},{128,224},{160,128},{192,160},{224,1... | collective-permute-start | bytes 1572872 | tf_op jit(solution)/shard_map/ppermute | solution.py:50
  74.0 2.1 %shard_map.84 = (bf16[256,256]{1,0:T(8,128)(2,1)S(1)}, bf16[256,256]{1,0:T(8,128)(2,1)S(1)}) custom-call(s32[6]{0:T(128)S(1)} %stack.35.index, bf16[128,2048]{1,0:T(8,128)(2,1)S(1)} %get-tuple-element.48.own_ref, bf16[128,2048]{1,0:T(8,128)(2,1)S(1)} %collective-permute-done.21.other_ref, bf16[512,2048]{1,0:T(8,128)(2,1)S(1)} %get-tuple-element.49.table), custom_call_target="tpu_custom_call" | custom-call | flops 536870912 | bytes 4194304 | tf_op jit(solution)/shard_map/pallas_call | solution.py:248
  76.1 3.2 %collective-permute-done.23.below_ref = bf16[256,256]{1,0:T(8,128)(2,1)S(1)} collective-permute-done((bf16[256,256]{1,0:T(8,128)(2,1)S(1)}, bf16[256,256]{1,0:T(8,128)(2,1)S(1)}, u32[]{:S(2)}, u32[]{:S(2)}) %collective-permute-start.23) | collective-permute-done | bytes 131104 | tf_op jit(solution)/shard_map/ppermute | solution.py:50
  79.3 4.8 %collective-permute-done.29.nxt = bf16[128,2048]{1,0:T(8,128)(2,1)S(1)} collective-permute-done((bf16[128,2048]{1,0:T(8,128)(2,1)S(1)}, bf16[128,2048]{1,0:T(8,128)(2,1)S(1)}, u32[]{:S(2)}, u32[]{:S(2)}) %collective-permute-start.29) | collective-permute-done | bytes 524320 | tf_op jit(solution)/shard_map/ppermute | solution.py:50
  84.9 2.2 %collective-permute-done.28.prev = bf16[128,2048]{1,0:T(8,128)(2,1)S(1)} collective-permute-done((bf16[128,2048]{1,0:T(8,128)(2,1)S(1)}, bf16[128,2048]{1,0:T(8,128)(2,1)S(1)}, u32[]{:S(2)}, u32[]{:S(2)}) %collective-permute-start.28) | collective-permute-done | bytes 524320 | tf_op jit(solution)/shard_map/ppermute | solution.py:50
  87.1 1.2 %collective-permute-start.22 = (bf16[256,256]{1,0:T(8,128)(2,1)S(1)}, bf16[256,256]{1,0:T(8,128)(2,1)S(1)}, u32[]{:S(2)}, u32[]{:S(2)}) collective-permute-start(bf16[256,256]{1,0:T(8,128)(2,1)S(1)} %get-tuple-element.51), channel_id=1, source_target_pairs={{0,1},{1,0},{2,3},{3,2},{4,5},{5,4},{6,7},{7,6},{8,9},{9,8},{10,11... | collective-permute-start | bytes 393224 | tf_op jit(solution)/shard_map/ppermute | solution.py:50
  88.7 1.4 %collective-permute-start.30 = (bf16[64,2048]{1,0:T(8,128)(2,1)S(1)}, bf16[64,2048]{1,0:T(8,128)(2,1)S(1)}, u32[]{:S(2)}, u32[]{:S(2)}) collective-permute-start(bf16[64,2048]{1,0:T(8,128)(2,1)S(1)} %slice.74), channel_id=1, source_target_pairs={{0,32},{32,64},{64,96},{96,0},{128,160},{160,192},{192,224},{224,1... | collective-permute-start | bytes 786440 | tf_op jit(solution)/shard_map/ppermute | solution.py:50
  90.1 4.0 %shard_map.85 = bf16[2,256,256]{2,1,0:T(8,128)(2,1)S(1)} custom-call(s32[6]{0:T(128)S(1)} %stack.35.index, bf16[512,384]{1,0:T(8,128)(2,1)S(1)} %get-tuple-element.46.keep_ref, bf16[512,384]{1,0:T(8,128)(2,1)S(1)} %collective-permute-done.20.got_ref, bf16[256,256]{1,0:T(8,128)(2,1)S(1)} %get-tuple-element.50.g_keep, ...), custom_call_target="tpu_custom_call" | custom-call | flops 1342177280 | bytes 4194304 | tf_op jit(solution)/shard_map/pallas_call | solution.py:248
  94.2 2.4 %collective-permute-done.31.far_b = bf16[64,2048]{1,0:T(8,128)(2,1)S(1)} collective-permute-done((bf16[64,2048]{1,0:T(8,128)(2,1)S(1)}, bf16[64,2048]{1,0:T(8,128)(2,1)S(1)}, u32[]{:S(2)}, u32[]{:S(2)}) %collective-permute-start.31) | collective-permute-done | bytes 262176 | tf_op jit(solution)/shard_map/ppermute | solution.py:50
  97.0 1.7 %collective-permute-done.27.there_ref = bf16[256,256]{1,0:T(8,128)(2,1)S(1)} collective-permute-done((bf16[256,256]{1,0:T(8,128)(2,1)S(1)}, bf16[256,256]{1,0:T(8,128)(2,1)S(1)}, u32[]{:S(2)}, u32[]{:S(2)}) %collective-permute-start.27) | collective-permute-done | bytes 131104 | tf_op jit(solution)/shard_map/ppermute | solution.py:50
  98.7 1.3 %shard_map.86 = (f32[128,2048]{1,0:T(8,128)S(1)}, bf16[128,2048]{1,0:T(8,128)(2,1)S(1)}) custom-call(s32[6]{0:T(128)S(1)} %stack.35.index, bf16[256,256]{1,0:T(8,128)(2,1)S(1)} %get-tuple-element.62.own_ref, bf16[256,256]{1,0:T(8,128)(2,1)S(1)} %collective-permute-done.27.there_ref, bf16[128,2048]{1,0:T(8,128)(2,1)S(1)} %get-tuple-element.56.mine, ...), custom_call_target="tpu_custom_call" | custom-call | flops 536870912 | bytes 4194304 | tf_op jit(solution)/shard_map/pallas_call | solution.py:248
  100.0 1.5 %collective-permute-start.32 = (bf16[128,2048]{1,0:T(8,128)(2,1)S(1)}, bf16[128,2048]{1,0:T(8,128)(2,1)S(1)}, u32[]{:S(2)}, u32[]{:S(2)}) collective-permute-start(bf16[128,2048]{1,0:T(8,128)(2,1)S(1)} %get-tuple-element.58), channel_id=1, source_target_pairs={{0,1},{1,0},{2,3},{3,2},{4,5},{5,4},{6,7},{7,6},{8,9},{9,8},{10,11... | collective-permute-start | bytes 1572872 | tf_op jit(solution)/shard_map/ppermute | solution.py:50
  101.5 1.5 %collective-permute-done.32 = bf16[128,2048]{1,0:T(8,128)(2,1)S(1)} collective-permute-done((bf16[128,2048]{1,0:T(8,128)(2,1)S(1)}, bf16[128,2048]{1,0:T(8,128)(2,1)S(1)}, u32[]{:S(2)}, u32[]{:S(2)}) %collective-permute-start.32) | collective-permute-done | bytes 524320 | tf_op jit(solution)/shard_map/ppermute | solution.py:50
  (67 shorter events, 9.9 us)
Async XLA Ops:
  2.3 10.5 %collective-permute-start.8 = (bf16[128,64]{1,0:T(8,128)(2,1)S(1)}, bf16[128,64]{1,0:T(8,128)(2,1)S(1)}, u32[]{:S(2)}, u32[]{:S(2)}) collective-permute-start(bf16[128,64]{1,0:T(8,128)(2,1)S(1)} %bitcast.43), channel_id=1, source_target_pairs={{0,1},{1,0},{2,3},{3,2},{4,5},{5,4},{6,7},{7,6},{8,9},{9,8},{10,11... | collective-permute-start | bytes 49160 | tf_op jit(solution)/shard_map/ppermute | solution.py:50
  5.6 10.7 %collective-permute-start.4 = (bf16[48,2048]{1,0:T(8,128)(2,1)S(1)}, bf16[48,2048]{1,0:T(8,128)(2,1)S(1)}, u32[]{:S(2)}, u32[]{:S(2)}) collective-permute-start(bf16[48,2048]{1,0:T(8,128)(2,1)S(1)} %bitcast.33), channel_id=1, source_target_pairs={{0,14},{1,3},{2,0},{3,5},{4,2},{5,7},{6,4},{7,9},{8,6},{9,11},{10,... | collective-permute-start | bytes 589832 | tf_op jit(solution)/shard_map/ppermute | solution.py:50
  5.6 10.7 %collective-permute-start = (bf16[48,2048]{1,0:T(8,128)(2,1)S(1)}, bf16[48,2048]{1,0:T(8,128)(2,1)S(1)}, u32[]{:S(2)}, u32[]{:S(2)}) collective-permute-start(bf16[48,2048]{1,0:T(8,128)(2,1)S(1)} %bitcast.34), channel_id=1, source_target_pairs={{0,2},{1,15},{2,4},{3,1},{4,6},{5,3},{6,8},{7,5},{8,10},{9,7},{10,... | collective-permute-start | bytes 589832 | tf_op jit(solution)/shard_map/ppermute | solution.py:50
  11.5 3.1 %collective-permute-start.7 = (bf16[8,2048]{1,0:T(8,128)(2,1)S(1)}, bf16[8,2048]{1,0:T(8,128)(2,1)S(1)}, u32[]{:S(2)}, u32[]{:S(2)}) collective-permute-start(bf16[8,2048]{1,0:T(8,128)(2,1)S(1)} %get-tuple-element.35), channel_id=1, source_target_pairs={{0,16},{1,17},{2,18},{3,19},{4,20},{5,21},{6,22},{7,23},{8,24},{9,... | collective-permute-start | bytes 98312 | tf_op jit(solution)/shard_map/ppermute | solution.py:50
  12.9 3.1 %collective-permute-start.9 = (bf16[128,128]{1,0:T(8,128)(2,1)S(1)}, bf16[128,128]{1,0:T(8,128)(2,1)S(1)}, u32[]{:S(2)}, u32[]{:S(2)}) collective-permute-start(bf16[128,128]{1,0:T(8,128)(2,1)S(1)} %pad_maximum_fusion.2), channel_id=1, source_target_pairs={{0,16},{1,17},{2,18},{3,19},{4,20},{5,21},{6,22},{7,23},{8,24},{9,... | collective-permute-start | bytes 98312 | tf_op jit(solution)/shard_map/ppermute | solution.py:50
  16.3 7.2 %collective-permute-start.11 = (bf16[80,2048]{1,0:T(8,128)(2,1)S(1)}, bf16[80,2048]{1,0:T(8,128)(2,1)S(1)}, u32[]{:S(2)}, u32[]{:S(2)}) collective-permute-start(bf16[80,2048]{1,0:T(8,128)(2,1)S(1)} %pad_maximum_fusion.1.refs_12_), channel_id=1, source_target_pairs={{0,14},{1,3},{2,0},{3,5},{4,2},{5,7},{6,4},{7,9},{8,6},{9,11},{10,... | collective-permute-start | bytes 983048 | tf_op jit(solution)/shard_map/ppermute | solution.py:50
  16.4 7.9 %collective-permute-start.10 = (bf16[80,2048]{1,0:T(8,128)(2,1)S(1)}, bf16[80,2048]{1,0:T(8,128)(2,1)S(1)}, u32[]{:S(2)}, u32[]{:S(2)}) collective-permute-start(bf16[80,2048]{1,0:T(8,128)(2,1)S(1)} %pad_maximum_fusion.1.refs_12_), channel_id=1, source_target_pairs={{0,2},{1,15},{2,4},{3,1},{4,6},{5,3},{6,8},{7,5},{8,10},{9,7},{10,... | collective-permute-start | bytes 983048 | tf_op jit(solution)/shard_map/ppermute | solution.py:50
  19.1 27.5 %collective-permute-start.1 = (bf16[128,2048]{1,0:T(8,128)(2,1)S(1)}, bf16[128,2048]{1,0:T(8,128)(2,1)S(1)}, u32[]{:S(2)}, u32[]{:S(2)}) collective-permute-start(bf16[128,2048]{1,0:T(8,128)(2,1)S(1)} %get-tuple-element.34.refs_0_), channel_id=1, source_target_pairs={{0,16},{1,17},{2,18},{3,19},{4,20},{5,21},{6,22},{7,23},{8,24},{9,... | collective-permute-start | bytes 1572872 | tf_op jit(solution)/shard_map/ppermute | solution.py:50
  24.3 16.4 %collective-permute-start.14 = (bf16[80,2048]{1,0:T(8,128)(2,1)S(1)}, bf16[80,2048]{1,0:T(8,128)(2,1)S(1)}, u32[]{:S(2)}, u32[]{:S(2)}) collective-permute-start(bf16[80,2048]{1,0:T(8,128)(2,1)S(1)} %collective-permute-done.10.refs_13_), channel_id=1, source_target_pairs={{0,2},{1,15},{2,4},{3,1},{4,6},{5,3},{6,8},{7,5},{8,10},{9,7},{10,... | collective-permute-start | bytes 983048 | tf_op jit(solution)/shard_map/ppermute | solution.py:50
  27.7 13.0 %collective-permute-start.15 = (bf16[80,2048]{1,0:T(8,128)(2,1)S(1)}, bf16[80,2048]{1,0:T(8,128)(2,1)S(1)}, u32[]{:S(2)}, u32[]{:S(2)}) collective-permute-start(bf16[80,2048]{1,0:T(8,128)(2,1)S(1)} %collective-permute-done.11.refs_14_), channel_id=1, source_target_pairs={{0,14},{1,3},{2,0},{3,5},{4,2},{5,7},{6,4},{7,9},{8,6},{9,11},{10,... | collective-permute-start | bytes 983048 | tf_op jit(solution)/shard_map/ppermute | solution.py:50
  27.7 12.9 %collective-permute-start.6 = (bf16[48,2048]{1,0:T(8,128)(2,1)S(1)}, bf16[48,2048]{1,0:T(8,128)(2,1)S(1)}, u32[]{:S(2)}, u32[]{:S(2)}) collective-permute-start(bf16[48,2048]{1,0:T(8,128)(2,1)S(1)} %collective-permute-done.4.refs_6_), channel_id=1, source_target_pairs={{0,14},{1,3},{2,0},{3,5},{4,2},{5,7},{6,4},{7,9},{8,6},{9,11},{10,... | collective-permute-start | bytes 589832 | tf_op jit(solution)/shard_map/ppermute | solution.py:50
  28.6 12.0 %collective-permute-start.5 = (bf16[48,2048]{1,0:T(8,128)(2,1)S(1)}, bf16[48,2048]{1,0:T(8,128)(2,1)S(1)}, u32[]{:S(2)}, u32[]{:S(2)}) collective-permute-start(bf16[48,2048]{1,0:T(8,128)(2,1)S(1)} %collective-permute-done.refs_5_), channel_id=1, source_target_pairs={{0,2},{1,15},{2,4},{3,1},{4,6},{5,3},{6,8},{7,5},{8,10},{9,7},{10,... | collective-permute-start | bytes 589832 | tf_op jit(solution)/shard_map/ppermute | solution.py:50
  40.7 9.7 %collective-permute-start.17 = (bf16[80,2048]{1,0:T(8,128)(2,1)S(1)}, bf16[80,2048]{1,0:T(8,128)(2,1)S(1)}, u32[]{:S(2)}, u32[]{:S(2)}) collective-permute-start(bf16[80,2048]{1,0:T(8,128)(2,1)S(1)} %collective-permute-done.14.refs_15_), channel_id=1, source_target_pairs={{0,2},{1,15},{2,4},{3,1},{4,6},{5,3},{6,8},{7,5},{8,10},{9,7},{10,... | collective-permute-start | bytes 983048 | tf_op jit(solution)/shard_map/ppermute | solution.py:50
  40.8 8.4 %collective-permute-start.12 = (bf16[48,2048]{1,0:T(8,128)(2,1)S(1)}, bf16[48,2048]{1,0:T(8,128)(2,1)S(1)}, u32[]{:S(2)}, u32[]{:S(2)}) collective-permute-start(bf16[48,2048]{1,0:T(8,128)(2,1)S(1)} %collective-permute-done.5.refs_7_), channel_id=1, source_target_pairs={{0,2},{1,15},{2,4},{3,1},{4,6},{5,3},{6,8},{7,5},{8,10},{9,7},{10,... | collective-permute-start | bytes 589832 | tf_op jit(solution)/shard_map/ppermute | solution.py:50
  43.0 7.4 %collective-permute-start.13 = (bf16[48,2048]{1,0:T(8,128)(2,1)S(1)}, bf16[48,2048]{1,0:T(8,128)(2,1)S(1)}, u32[]{:S(2)}, u32[]{:S(2)}) collective-permute-start(bf16[48,2048]{1,0:T(8,128)(2,1)S(1)} %collective-permute-done.6.refs_8_), channel_id=1, source_target_pairs={{0,14},{1,3},{2,0},{3,5},{4,2},{5,7},{6,4},{7,9},{8,6},{9,11},{10,... | collective-permute-start | bytes 589832 | tf_op jit(solution)/shard_map/ppermute | solution.py:50
  43.0 11.4 %collective-permute-start.2 = (bf16[128,2048]{1,0:T(8,128)(2,1)S(1)}, bf16[128,2048]{1,0:T(8,128)(2,1)S(1)}, u32[]{:S(2)}, u32[]{:S(2)}) collective-permute-start(bf16[128,2048]{1,0:T(8,128)(2,1)S(1)} %get-tuple-element.34.refs_0_), channel_id=1, source_target_pairs={{0,1},{1,0},{2,3},{3,2},{4,5},{5,4},{6,7},{7,6},{8,9},{9,8},{10,11... | collective-permute-start | bytes 1572872 | tf_op jit(solution)/shard_map/ppermute | solution.py:50
  46.6 15.9 %collective-permute-start.3 = (bf16[128,2048]{1,0:T(8,128)(2,1)S(1)}, bf16[128,2048]{1,0:T(8,128)(2,1)S(1)}, u32[]{:S(2)}, u32[]{:S(2)}) collective-permute-start(bf16[128,2048]{1,0:T(8,128)(2,1)S(1)} %collective-permute-done.1.refs_1_), channel_id=1, source_target_pairs={{0,1},{1,0},{2,3},{3,2},{4,5},{5,4},{6,7},{7,6},{8,9},{9,8},{10,11... | collective-permute-start | bytes 1572872 | tf_op jit(solution)/shard_map/ppermute | solution.py:50
  49.2 13.3 %collective-permute-start.18 = (bf16[80,2048]{1,0:T(8,128)(2,1)S(1)}, bf16[80,2048]{1,0:T(8,128)(2,1)S(1)}, u32[]{:S(2)}, u32[]{:S(2)}) collective-permute-start(bf16[80,2048]{1,0:T(8,128)(2,1)S(1)} %collective-permute-done.15.refs_16_), channel_id=1, source_target_pairs={{0,14},{1,3},{2,0},{3,5},{4,2},{5,7},{6,4},{7,9},{8,6},{9,11},{10,... | collective-permute-start | bytes 983048 | tf_op jit(solution)/shard_map/ppermute | solution.py:50
  50.3 12.1 %collective-permute-start.19 = (bf16[80,2048]{1,0:T(8,128)(2,1)S(1)}, bf16[80,2048]{1,0:T(8,128)(2,1)S(1)}, u32[]{:S(2)}, u32[]{:S(2)}) collective-permute-start(bf16[80,2048]{1,0:T(8,128)(2,1)S(1)} %collective-permute-done.17.refs_17_), channel_id=1, source_target_pairs={{0,2},{1,15},{2,4},{3,1},{4,6},{5,3},{6,8},{7,5},{8,10},{9,7},{10,... | collective-permute-start | bytes 983048 | tf_op jit(solution)/shard_map/ppermute | solution.py:50
  53.7 8.8 %collective-permute-start.16 = (bf16[48,2048]{1,0:T(8,128)(2,1)S(1)}, bf16[48,2048]{1,0:T(8,128)(2,1)S(1)}, u32[]{:S(2)}, u32[]{:S(2)}) collective-permute-start(bf16[48,2048]{1,0:T(8,128)(2,1)S(1)} %collective-permute-done.12.refs_9_), channel_id=1, source_target_pairs={{0,2},{1,15},{2,4},{3,1},{4,6},{5,3},{6,8},{7,5},{8,10},{9,7},{10,... | collective-permute-start | bytes 589832 | tf_op jit(solution)/shard_map/ppermute | solution.py:50
  65.5 8.2 %collective-permute-start.21 = (bf16[128,2048]{1,0:T(8,128)(2,1)S(1)}, bf16[128,2048]{1,0:T(8,128)(2,1)S(1)}, u32[]{:S(2)}, u32[]{:S(2)}) collective-permute-start(bf16[128,2048]{1,0:T(8,128)(2,1)S(1)} %get-tuple-element.48.own_ref), channel_id=1, source_target_pairs={{0,1},{1,0},{2,3},{3,2},{4,5},{5,4},{6,7},{7,6},{8,9},{9,8},{10,11... | collective-permute-start | bytes 1572872 | tf_op jit(solution)/shard_map/ppermute | solution.py:50
  70.0 14.0 %collective-permute-start.29 = (bf16[128,2048]{1,0:T(8,128)(2,1)S(1)}, bf16[128,2048]{1,0:T(8,128)(2,1)S(1)}, u32[]{:S(2)}, u32[]{:S(2)}) collective-permute-start(bf16[128,2048]{1,0:T(8,128)(2,1)S(1)} %get-tuple-element.56.mine), channel_id=1, source_target_pairs={{0,96},{32,0},{64,32},{96,64},{128,224},{160,128},{192,160},{224,1... | collective-permute-start | bytes 1572872 | tf_op jit(solution)/shard_map/ppermute | solution.py:50
  72.7 14.4 %collective-permute-start.28 = (bf16[128,2048]{1,0:T(8,128)(2,1)S(1)}, bf16[128,2048]{1,0:T(8,128)(2,1)S(1)}, u32[]{:S(2)}, u32[]{:S(2)}) collective-permute-start(bf16[128,2048]{1,0:T(8,128)(2,1)S(1)} %get-tuple-element.56.mine), channel_id=1, source_target_pairs={{0,32},{32,64},{64,96},{96,0},{128,160},{160,192},{192,224},{224,1... | collective-permute-start | bytes 1572872 | tf_op jit(solution)/shard_map/ppermute | solution.py:50
  72.7 17.4 %collective-permute-start.20 = (bf16[512,384]{1,0:T(8,128)(2,1)S(1)}, bf16[512,384]{1,0:T(8,128)(2,1)S(1)}, u32[]{:S(2)}, u32[]{:S(2)}) collective-permute-start(bf16[512,384]{1,0:T(8,128)(2,1)S(1)} %get-tuple-element.47), channel_id=1, source_target_pairs={{0,1},{1,0},{2,3},{3,2},{4,5},{5,4},{6,7},{7,6},{8,9},{9,8},{10,11... | collective-permute-start | bytes 1179656 | tf_op jit(solution)/shard_map/ppermute | solution.py:50
  73.1 6.2 %collective-permute-start.23 = (bf16[256,256]{1,0:T(8,128)(2,1)S(1)}, bf16[256,256]{1,0:T(8,128)(2,1)S(1)}, u32[]{:S(2)}, u32[]{:S(2)}) collective-permute-start(bf16[256,256]{1,0:T(8,128)(2,1)S(1)} %get-tuple-element.52), channel_id=1, source_target_pairs={{0,2},{1,3},{2,4},{3,5},{4,6},{5,7},{6,8},{7,9},{8,10},{9,11},{10,... | collective-permute-start | bytes 393224 | tf_op jit(solution)/shard_map/ppermute | solution.py:50
  73.6 14.7 %collective-permute-start.24 = (bf16[256,256]{1,0:T(8,128)(2,1)S(1)}, bf16[256,256]{1,0:T(8,128)(2,1)S(1)}, u32[]{:S(2)}, u32[]{:S(2)}) collective-permute-start(bf16[256,256]{1,0:T(8,128)(2,1)S(1)} %get-tuple-element.53), channel_id=1, source_target_pairs={{0,3},{1,2},{2,5},{3,4},{4,7},{5,6},{6,9},{7,8},{8,11},{9,10},{10,... | collective-permute-start | bytes 393224 | tf_op jit(solution)/shard_map/ppermute | solution.py:50
  79.2 9.5 %collective-permute-start.25 = (bf16[256,256]{1,0:T(8,128)(2,1)S(1)}, bf16[256,256]{1,0:T(8,128)(2,1)S(1)}, u32[]{:S(2)}, u32[]{:S(2)}) collective-permute-start(bf16[256,256]{1,0:T(8,128)(2,1)S(1)} %get-tuple-element.54), channel_id=1, source_target_pairs={{0,14},{1,15},{2,0},{3,1},{4,2},{5,3},{6,4},{7,5},{8,6},{9,7},{10,... | collective-permute-start | bytes 393224 | tf_op jit(solution)/shard_map/ppermute | solution.py:50
  84.0 6.1 %collective-permute-start.26 = (bf16[256,256]{1,0:T(8,128)(2,1)S(1)}, bf16[256,256]{1,0:T(8,128)(2,1)S(1)}, u32[]{:S(2)}, u32[]{:S(2)}) collective-permute-start(bf16[256,256]{1,0:T(8,128)(2,1)S(1)} %get-tuple-element.55), channel_id=1, source_target_pairs={{0,15},{1,14},{2,1},{3,0},{4,3},{5,2},{6,5},{7,4},{8,7},{9,6},{10,... | collective-permute-start | bytes 393224 | tf_op jit(solution)/shard_map/ppermute | solution.py:50
  88.3 8.2 %collective-permute-start.31 = (bf16[64,2048]{1,0:T(8,128)(2,1)S(1)}, bf16[64,2048]{1,0:T(8,128)(2,1)S(1)}, u32[]{:S(2)}, u32[]{:S(2)}) collective-permute-start(bf16[64,2048]{1,0:T(8,128)(2,1)S(1)} %slice.75), channel_id=1, source_target_pairs={{0,96},{32,0},{64,32},{96,64},{128,224},{160,128},{192,160},{224,1... | collective-permute-start | bytes 786440 | tf_op jit(solution)/shard_map/ppermute | solution.py:50
  88.7 8.3 %collective-permute-start.30 = (bf16[64,2048]{1,0:T(8,128)(2,1)S(1)}, bf16[64,2048]{1,0:T(8,128)(2,1)S(1)}, u32[]{:S(2)}, u32[]{:S(2)}) collective-permute-start(bf16[64,2048]{1,0:T(8,128)(2,1)S(1)} %slice.74), channel_id=1, source_target_pairs={{0,32},{32,64},{64,96},{96,0},{128,160},{160,192},{192,224},{224,1... | collective-permute-start | bytes 786440 | tf_op jit(solution)/shard_map/ppermute | solution.py:50
  94.1 4.6 %collective-permute-start.27 = (bf16[256,256]{1,0:T(8,128)(2,1)S(1)}, bf16[256,256]{1,0:T(8,128)(2,1)S(1)}, u32[]{:S(2)}, u32[]{:S(2)}) collective-permute-start(bf16[256,256]{1,0:T(8,128)(2,1)S(1)} %get-tuple-element.61), channel_id=1, source_target_pairs={{0,16},{1,17},{2,18},{3,19},{4,20},{5,21},{6,22},{7,23},{8,24},{9,... | collective-permute-start | bytes 393224 | tf_op jit(solution)/shard_map/ppermute | solution.py:50
  100.0 3.0 %collective-permute-start.32 = (bf16[128,2048]{1,0:T(8,128)(2,1)S(1)}, bf16[128,2048]{1,0:T(8,128)(2,1)S(1)}, u32[]{:S(2)}, u32[]{:S(2)}) collective-permute-start(bf16[128,2048]{1,0:T(8,128)(2,1)S(1)} %get-tuple-element.58), channel_id=1, source_target_pairs={{0,1},{1,0},{2,3},{3,2},{4,5},{5,4},{6,7},{7,6},{8,9},{9,8},{10,11... | collective-permute-start | bytes 1572872 | tf_op jit(solution)/shard_map/ppermute | solution.py:50
  (4 other events, 33.7 us)

commit v8 on v7

--- a/solution.py
+++ b/solution.py
@@ -318,18 +318,18 @@
         if step == 2:
             a_two = b_two = after(second, a_one, b_one)
         if step > 1:
-            if step > 2:
-                before = one[0, step - 2], one[1, step - 2]
+            if step > 3:
+                before = one[0, step - 3], one[1, step - 3]
                 a_two, b_two = lax.optimization_barrier((a_two, b_two, *before))[:2]
             two[0, step - 1] = a_two = send(a_two, AHEAD)
             two[1, step - 1] = b_two = send(b_two, BEHIND)
         if step > 2:
-            before = two[0, step - 2], two[1, step - 2]
+            before = two[0, step - 1], two[1, step - 1]
             a_one, b_one = lax.optimization_barrier((a_one, b_one, *before))[:2]
         one[0, step] = a_one = send(a_one, AHEAD)
         if step < 4:
             one[1, step] = b_one = send(b_one, BEHIND)
-    a_two = after(a_two, one[0, 3], one[1, 3])
+    a_two = after(a_two, one[0, 2], one[1, 2])
     two[0, 4] = send(a_two, AHEAD)
     firsts = [one[s] for s in STEPS]
     seconds = [two[s] for s in STEPS]
@@ -370,8 +370,8 @@
     to_pass = out_own
     out_prev = send(to_pass, Y_UP, "doc")
     out_next = send(to_pass, Y_DOWN, "doc")
-    out_far_a = send(out_prev[:64], Y_UP, "doc")
-    out_far_b = send(out_next[64:], Y_DOWN, "doc")
+    out_far_a = send(after(out_prev[:64], *below, *above), Y_UP, "doc")
+    out_far_b = send(after(out_next[64:], *below, *above), Y_DOWN, "doc")
 
     context = on_chip(
         attention_kernel,

time: 104 us -> 113 us (1.087)
  starting transfers between devices: 42.4 us -> 47.1 us
  waiting for transfers between devices: 45.5 us -> 49.4 us
    ppermute x33, starting transfers between devices: 42.4 us -> 47.1 us  [send(): return lax.ppermute(value, axis, route)]
    ppermute x33, waiting for transfers between devices: 45.5 us -> 49.4 us  [send(): return lax.ppermute(value, axis, route)]
  transfers between devices with their start and end apart: 33 -> 33, of which waited for: 15 -> 16; matrix products, arithmetic and copies ran while one was open for 0% -> 0% of each run, Pallas kernels for 7% -> 6%
where the time goes in v8:
time: 113 us
  waiting for transfers between devices  49.4 us (44%)
  starting transfers between devices  47.1 us (42%)
  Pallas kernels  11.5 us (10%)
  other arithmetic  2.31 us (2%)
  local copies, waits for them, and re-layouts  1.27 us (1%)
    ppermute x33, waiting for transfers between devices, send(): return lax.ppermute(value, axis, route)  49.4 us
    ppermute x33, starting transfers between devices, send(): return lax.ppermute(value, axis, route)  47.1 us
    pallas_call x5, Pallas kernels, on_chip(): pl.pallas_call(kernel, out_shape=out_shape, in_specs=specs, out_specs=jax...  11.5 us
  transfers between devices with their start and end apart: 33, of which 16 were waited for; matrix products, arithmetic and copies ran while one was open for 0% of the time, Pallas kernels for 6%

profile of v8, /device:TPU:1, one launch (start us, length us, event | category | flops | bytes accessed | tf_op | source)
XLA Modules:
  0.0 112.5 jit_solution(4183592490653911534)
XLA Ops:
  2.3 3.3 %collective-permute-start.8 = (bf16[128,64]{1,0:T(8,128)(2,1)S(1)}, bf16[128,64]{1,0:T(8,128)(2,1)S(1)}, u32[]{:S(2)}, u32[]{:S(2)}) collective-permute-start(bf16[128,64]{1,0:T(8,128)(2,1)S(1)} %bitcast.43), channel_id=1, source_target_pairs={{0,1},{1,0},{2,3},{3,2},{4,5},{5,4},{6,7},{7,6},{8,9},{9,8},{10,11... | collective-permute-start | bytes 49160 | tf_op jit(solution)/shard_map/ppermute | solution.py:50
  5.6 3.9 %collective-permute-start = (bf16[48,2048]{1,0:T(8,128)(2,1)S(1)}, bf16[48,2048]{1,0:T(8,128)(2,1)S(1)}, u32[]{:S(2)}, u32[]{:S(2)}) collective-permute-start(bf16[48,2048]{1,0:T(8,128)(2,1)S(1)} %bitcast.34), channel_id=1, source_target_pairs={{0,2},{1,15},{2,4},{3,1},{4,6},{5,3},{6,8},{7,5},{8,10},{9,7},{10,... | collective-permute-start | bytes 589832 | tf_op jit(solution)/shard_map/ppermute | solution.py:50
  10.3 1.3 %shard_map.82 = (bf16[128,2048]{1,0:T(8,128)(2,1)S(1)}, bf16[8,2048]{1,0:T(8,128)(2,1)S(1)}) custom-call(s32[6]{0:T(128)S(1)} %stack.35.index, bf16[128,2048]{1,0:T(8,128)(2,1)S(1)} %copy-done, f32[1,2048]{1,0:T(1,128)S(1)} %bitcast.36, f32[1,2048]{1,0:T(1,128)S(1)} %bitcast.37), custom_call_target="tpu_custom_call" | custom-call | flops 2097152 | bytes 4194304 | tf_op jit(solution)/shard_map/pallas_call | solution.py:248
  11.5 1.3 %collective-permute-start.7 = (bf16[8,2048]{1,0:T(8,128)(2,1)S(1)}, bf16[8,2048]{1,0:T(8,128)(2,1)S(1)}, u32[]{:S(2)}, u32[]{:S(2)}) collective-permute-start(bf16[8,2048]{1,0:T(8,128)(2,1)S(1)} %get-tuple-element.35), channel_id=1, source_target_pairs={{0,16},{1,17},{2,18},{3,19},{4,20},{5,21},{6,22},{7,23},{8,24},{9,... | collective-permute-start | bytes 98312 | tf_op jit(solution)/shard_map/ppermute | solution.py:50
  13.3 1.4 %collective-permute-done.7 = bf16[8,2048]{1,0:T(8,128)(2,1)S(1)} collective-permute-done((bf16[8,2048]{1,0:T(8,128)(2,1)S(1)}, bf16[8,2048]{1,0:T(8,128)(2,1)S(1)}, u32[]{:S(2)}, u32[]{:S(2)}) %collective-permute-start.7) | collective-permute-done | bytes 32800 | tf_op jit(solution)/shard_map/ppermute | solution.py:50
  14.7 1.4 %collective-permute-done.9 = bf16[128,128]{1,0:T(8,128)(2,1)S(1)} collective-permute-done((bf16[128,128]{1,0:T(8,128)(2,1)S(1)}, bf16[128,128]{1,0:T(8,128)(2,1)S(1)}, u32[]{:S(2)}, u32[]{:S(2)}) %collective-permute-start.9) | collective-permute-done | bytes 32800 | tf_op jit(solution)/shard_map/ppermute | solution.py:50
  16.4 2.7 %collective-permute-start.10 = (bf16[80,2048]{1,0:T(8,128)(2,1)S(1)}, bf16[80,2048]{1,0:T(8,128)(2,1)S(1)}, u32[]{:S(2)}, u32[]{:S(2)}) collective-permute-start(bf16[80,2048]{1,0:T(8,128)(2,1)S(1)} %pad_maximum_fusion.1.refs_12_), channel_id=1, source_target_pairs={{0,2},{1,15},{2,4},{3,1},{4,6},{5,3},{6,8},{7,5},{8,10},{9,7},{10,... | collective-permute-start | bytes 983048 | tf_op jit(solution)/shard_map/ppermute | solution.py:50
  19.1 4.5 %collective-permute-done.12.refs_14_ = bf16[80,2048]{1,0:T(8,128)(2,1)S(1)} collective-permute-done((bf16[80,2048]{1,0:T(8,128)(2,1)S(1)}, bf16[80,2048]{1,0:T(8,128)(2,1)S(1)}, u32[]{:S(2)}, u32[]{:S(2)}) %collective-permute-start.12) | collective-permute-done | bytes 327712 | tf_op jit(solution)/shard_map/ppermute | solution.py:50
  24.3 3.4 %collective-permute-start.11 = (bf16[80,2048]{1,0:T(8,128)(2,1)S(1)}, bf16[80,2048]{1,0:T(8,128)(2,1)S(1)}, u32[]{:S(2)}, u32[]{:S(2)}) collective-permute-start(bf16[80,2048]{1,0:T(8,128)(2,1)S(1)} %collective-permute-done.10.refs_13_), channel_id=1, source_target_pairs={{0,2},{1,15},{2,4},{3,1},{4,6},{5,3},{6,8},{7,5},{8,10},{9,7},{10,... | collective-permute-start | bytes 983048 | tf_op jit(solution)/shard_map/ppermute | solution.py:50
  28.0 4.2 %collective-permute-done.13.refs_16_ = bf16[80,2048]{1,0:T(8,128)(2,1)S(1)} collective-permute-done((bf16[80,2048]{1,0:T(8,128)(2,1)S(1)}, bf16[80,2048]{1,0:T(8,128)(2,1)S(1)}, u32[]{:S(2)}, u32[]{:S(2)}) %collective-permute-start.13) | collective-permute-done | bytes 327712 | tf_op jit(solution)/shard_map/ppermute | solution.py:50
  32.2 3.2 %collective-permute-start.16 = (bf16[80,2048]{1,0:T(8,128)(2,1)S(1)}, bf16[80,2048]{1,0:T(8,128)(2,1)S(1)}, u32[]{:S(2)}, u32[]{:S(2)}) collective-permute-start(bf16[80,2048]{1,0:T(8,128)(2,1)S(1)} %collective-permute-done.11.refs_15_), channel_id=1, source_target_pairs={{0,2},{1,15},{2,4},{3,1},{4,6},{5,3},{6,8},{7,5},{8,10},{9,7},{10,... | collective-permute-start | bytes 983048 | tf_op jit(solution)/shard_map/ppermute | solution.py:50
  35.5 5.0 %collective-permute-start.2 = (bf16[128,2048]{1,0:T(8,128)(2,1)S(1)}, bf16[128,2048]{1,0:T(8,128)(2,1)S(1)}, u32[]{:S(2)}, u32[]{:S(2)}) collective-permute-start(bf16[128,2048]{1,0:T(8,128)(2,1)S(1)} %get-tuple-element.34.refs_0_), channel_id=1, source_target_pairs={{0,1},{1,0},{2,3},{3,2},{4,5},{5,4},{6,7},{7,6},{8,9},{9,8},{10,11... | collective-permute-start | bytes 1572872 | tf_op jit(solution)/shard_map/ppermute | solution.py:50
  40.5 1.5 %collective-permute-start.3 = (bf16[128,2048]{1,0:T(8,128)(2,1)S(1)}, bf16[128,2048]{1,0:T(8,128)(2,1)S(1)}, u32[]{:S(2)}, u32[]{:S(2)}) collective-permute-start(bf16[128,2048]{1,0:T(8,128)(2,1)S(1)} %collective-permute-done.1.refs_1_), channel_id=1, source_target_pairs={{0,1},{1,0},{2,3},{3,2},{4,5},{5,4},{6,7},{7,6},{8,9},{9,8},{10,11... | collective-permute-start | bytes 1572872 | tf_op jit(solution)/shard_map/ppermute | solution.py:50
  42.1 1.2 %collective-permute-start.17 = (bf16[80,2048]{1,0:T(8,128)(2,1)S(1)}, bf16[80,2048]{1,0:T(8,128)(2,1)S(1)}, u32[]{:S(2)}, u32[]{:S(2)}) collective-permute-start(bf16[80,2048]{1,0:T(8,128)(2,1)S(1)} %collective-permute-done.13.refs_16_), channel_id=1, source_target_pairs={{0,14},{1,3},{2,0},{3,5},{4,2},{5,7},{6,4},{7,9},{8,6},{9,11},{10,... | collective-permute-start | bytes 983048 | tf_op jit(solution)/shard_map/ppermute | solution.py:50
  43.3 2.9 %collective-permute-start.14 = (bf16[48,2048]{1,0:T(8,128)(2,1)S(1)}, bf16[48,2048]{1,0:T(8,128)(2,1)S(1)}, u32[]{:S(2)}, u32[]{:S(2)}) collective-permute-start(bf16[48,2048]{1,0:T(8,128)(2,1)S(1)} %collective-permute-done.5.refs_7_), channel_id=1, source_target_pairs={{0,2},{1,15},{2,4},{3,1},{4,6},{5,3},{6,8},{7,5},{8,10},{9,7},{10,... | collective-permute-start | bytes 589832 | tf_op jit(solution)/shard_map/ppermute | solution.py:50
  46.3 4.6 %collective-permute-done.14.refs_9_ = bf16[48,2048]{1,0:T(8,128)(2,1)S(1)} collective-permute-done((bf16[48,2048]{1,0:T(8,128)(2,1)S(1)}, bf16[48,2048]{1,0:T(8,128)(2,1)S(1)}, u32[]{:S(2)}, u32[]{:S(2)}) %collective-permute-start.14) | collective-permute-done | bytes 196640 | tf_op jit(solution)/shard_map/ppermute | solution.py:50
  50.9 1.9 %collective-permute-start.19 = (bf16[80,2048]{1,0:T(8,128)(2,1)S(1)}, bf16[80,2048]{1,0:T(8,128)(2,1)S(1)}, u32[]{:S(2)}, u32[]{:S(2)}) collective-permute-start(bf16[80,2048]{1,0:T(8,128)(2,1)S(1)} %collective-permute-done.16.refs_17_), channel_id=1, source_target_pairs={{0,2},{1,15},{2,4},{3,1},{4,6},{5,3},{6,8},{7,5},{8,10},{9,7},{10,... | collective-permute-start | bytes 983048 | tf_op jit(solution)/shard_map/ppermute | solution.py:50
  52.7 1.8 %collective-permute-done.15.refs_10_ = bf16[48,2048]{1,0:T(8,128)(2,1)S(1)} collective-permute-done((bf16[48,2048]{1,0:T(8,128)(2,1)S(1)}, bf16[48,2048]{1,0:T(8,128)(2,1)S(1)}, u32[]{:S(2)}, u32[]{:S(2)}) %collective-permute-start.15) | collective-permute-done | bytes 196640 | tf_op jit(solution)/shard_map/ppermute | solution.py:50
  54.5 6.5 %collective-permute-done.18.refs_11_ = bf16[48,2048]{1,0:T(8,128)(2,1)S(1)} collective-permute-done((bf16[48,2048]{1,0:T(8,128)(2,1)S(1)}, bf16[48,2048]{1,0:T(8,128)(2,1)S(1)}, u32[]{:S(2)}, u32[]{:S(2)}) %collective-permute-start.18) | collective-permute-done | bytes 196640 | tf_op jit(solution)/shard_map/ppermute | solution.py:50
  61.1 2.9 %shard_map.83 = (bf16[512,384]{1,0:T(8,128)(2,1)S(1)}, bf16[512,384]{1,0:T(8,128)(2,1)S(1)}, bf16[128,2048]{1,0:T(8,128)(2,1)S(1)}, bf16[512,2048]{1,0:T(8,128)(...) custom-call(s32[6]{0:T(128)S(1)} %stack.35.index, ...), custom_call_target="tpu_custom_call" | custom-call | flops 1610612736 | bytes 4194304 | tf_op jit(solution)/shard_map/pallas_call | solution.py:248
  64.0 9.0 %collective-permute-start.21 = (bf16[128,2048]{1,0:T(8,128)(2,1)S(1)}, bf16[128,2048]{1,0:T(8,128)(2,1)S(1)}, u32[]{:S(2)}, u32[]{:S(2)}) collective-permute-start(bf16[128,2048]{1,0:T(8,128)(2,1)S(1)} %get-tuple-element.46.own_ref), channel_id=1, source_target_pairs={{0,1},{1,0},{2,3},{3,2},{4,5},{5,4},{6,7},{7,6},{8,9},{9,8},{10,11... | collective-permute-start | bytes 1572872 | tf_op jit(solution)/shard_map/ppermute | solution.py:50
  73.0 2.8 %collective-permute-start.29 = (bf16[128,2048]{1,0:T(8,128)(2,1)S(1)}, bf16[128,2048]{1,0:T(8,128)(2,1)S(1)}, u32[]{:S(2)}, u32[]{:S(2)}) collective-permute-start(bf16[128,2048]{1,0:T(8,128)(2,1)S(1)} %get-tuple-element.54.mine), channel_id=1, source_target_pairs={{0,96},{32,0},{64,32},{96,64},{128,224},{160,128},{192,160},{224,1... | collective-permute-start | bytes 1572872 | tf_op jit(solution)/shard_map/ppermute | solution.py:50
  76.1 5.6 %collective-permute-done.23.below_ref = bf16[256,256]{1,0:T(8,128)(2,1)S(1)} collective-permute-done((bf16[256,256]{1,0:T(8,128)(2,1)S(1)}, bf16[256,256]{1,0:T(8,128)(2,1)S(1)}, u32[]{:S(2)}, u32[]{:S(2)}) %collective-permute-start.23) | collective-permute-done | bytes 131104 | tf_op jit(solution)/shard_map/ppermute | solution.py:50
  81.7 6.9 %collective-permute-done.24.below_got = bf16[256,256]{1,0:T(8,128)(2,1)S(1)} collective-permute-done((bf16[256,256]{1,0:T(8,128)(2,1)S(1)}, bf16[256,256]{1,0:T(8,128)(2,1)S(1)}, u32[]{:S(2)}, u32[]{:S(2)}) %collective-permute-start.24) | collective-permute-done | bytes 131104 | tf_op jit(solution)/shard_map/ppermute | solution.py:50
  88.6 2.1 %shard_map.84 = (bf16[256,256]{1,0:T(8,128)(2,1)S(1)}, bf16[256,256]{1,0:T(8,128)(2,1)S(1)}) custom-call(s32[6]{0:T(128)S(1)} %stack.35.index, bf16[128,2048]{1,0:T(8,128)(2,1)S(1)} %get-tuple-element.46.own_ref, bf16[128,2048]{1,0:T(8,128)(2,1)S(1)} %collective-permute-done.21.other_ref, bf16[512,2048]{1,0:T(8,128)(2,1)S(1)} %get-tuple-element.47.table), custom_call_target="tpu_custom_call" | custom-call | flops 536870912 | bytes 4194304 | tf_op jit(solution)/shard_map/pallas_call | solution.py:248
  92.8 3.8 %collective-permute-done.26.above_got = bf16[256,256]{1,0:T(8,128)(2,1)S(1)} collective-permute-done((bf16[256,256]{1,0:T(8,128)(2,1)S(1)}, bf16[256,256]{1,0:T(8,128)(2,1)S(1)}, u32[]{:S(2)}, u32[]{:S(2)}) %collective-permute-start.26) | collective-permute-done | bytes 131104 | tf_op jit(solution)/shard_map/ppermute | solution.py:50
  96.6 2.0 %collective-permute-start.31 = (bf16[64,2048]{1,0:T(8,128)(2,1)S(1)}, bf16[64,2048]{1,0:T(8,128)(2,1)S(1)}, u32[]{:S(2)}, u32[]{:S(2)}) collective-permute-start(bf16[64,2048]{1,0:T(8,128)(2,1)S(1)} %slice.75), channel_id=1, source_target_pairs={{0,96},{32,0},{64,32},{96,64},{128,224},{160,128},{192,160},{224,1... | collective-permute-start | bytes 786440 | tf_op jit(solution)/shard_map/ppermute | solution.py:50
  98.7 4.0 %shard_map.85 = bf16[2,256,256]{2,1,0:T(8,128)(2,1)S(1)} custom-call(s32[6]{0:T(128)S(1)} %stack.35.index, bf16[512,384]{1,0:T(8,128)(2,1)S(1)} %get-tuple-element.44.keep_ref, bf16[512,384]{1,0:T(8,128)(2,1)S(1)} %collective-permute-done.20.got_ref, bf16[256,256]{1,0:T(8,128)(2,1)S(1)} %get-tuple-element.48.g_keep, ...), custom_call_target="tpu_custom_call" | custom-call | flops 1342177280 | bytes 4194304 | tf_op jit(solution)/shard_map/pallas_call | solution.py:248
  103.1 1.7 %collective-permute-done.31.far_b = bf16[64,2048]{1,0:T(8,128)(2,1)S(1)} collective-permute-done((bf16[64,2048]{1,0:T(8,128)(2,1)S(1)}, bf16[64,2048]{1,0:T(8,128)(2,1)S(1)}, u32[]{:S(2)}, u32[]{:S(2)}) %collective-permute-start.31) | collective-permute-done | bytes 262176 | tf_op jit(solution)/shard_map/ppermute | solution.py:50
  104.7 3.4 %collective-permute-done.30.far_a = bf16[64,2048]{1,0:T(8,128)(2,1)S(1)} collective-permute-done((bf16[64,2048]{1,0:T(8,128)(2,1)S(1)}, bf16[64,2048]{1,0:T(8,128)(2,1)S(1)}, u32[]{:S(2)}, u32[]{:S(2)}) %collective-permute-start.30) | collective-permute-done | bytes 262176 | tf_op jit(solution)/shard_map/ppermute | solution.py:50
  108.3 1.3 %shard_map.86 = (f32[128,2048]{1,0:T(8,128)S(1)}, bf16[128,2048]{1,0:T(8,128)(2,1)S(1)}) custom-call(s32[6]{0:T(128)S(1)} %stack.35.index, bf16[256,256]{1,0:T(8,128)(2,1)S(1)} %get-tuple-element.62.own_ref, bf16[256,256]{1,0:T(8,128)(2,1)S(1)} %collective-permute-done.27.there_ref, bf16[128,2048]{1,0:T(8,128)(2,1)S(1)} %get-tuple-element.54.mine, ...), custom_call_target="tpu_custom_call" | custom-call | flops 536870912 | bytes 4194304 | tf_op jit(solution)/shard_map/pallas_call | solution.py:248
  110.1 1.5 %collective-permute-done.32 = bf16[128,2048]{1,0:T(8,128)(2,1)S(1)} collective-permute-done((bf16[128,2048]{1,0:T(8,128)(2,1)S(1)}, bf16[128,2048]{1,0:T(8,128)(2,1)S(1)}, u32[]{:S(2)}, u32[]{:S(2)}) %collective-permute-start.32) | collective-permute-done | bytes 524320 | tf_op jit(solution)/shard_map/ppermute | solution.py:50
  (67 shorter events, 8.7 us)
Async XLA Ops:
  2.3 10.5 %collective-permute-start.8 = (bf16[128,64]{1,0:T(8,128)(2,1)S(1)}, bf16[128,64]{1,0:T(8,128)(2,1)S(1)}, u32[]{:S(2)}, u32[]{:S(2)}) collective-permute-start(bf16[128,64]{1,0:T(8,128)(2,1)S(1)} %bitcast.43), channel_id=1, source_target_pairs={{0,1},{1,0},{2,3},{3,2},{4,5},{5,4},{6,7},{7,6},{8,9},{9,8},{10,11... | collective-permute-start | bytes 49160 | tf_op jit(solution)/shard_map/ppermute | solution.py:50
  5.6 10.7 %collective-permute-start.4 = (bf16[48,2048]{1,0:T(8,128)(2,1)S(1)}, bf16[48,2048]{1,0:T(8,128)(2,1)S(1)}, u32[]{:S(2)}, u32[]{:S(2)}) collective-permute-start(bf16[48,2048]{1,0:T(8,128)(2,1)S(1)} %bitcast.33), channel_id=1, source_target_pairs={{0,14},{1,3},{2,0},{3,5},{4,2},{5,7},{6,4},{7,9},{8,6},{9,11},{10,... | collective-permute-start | bytes 589832 | tf_op jit(solution)/shard_map/ppermute | solution.py:50
  5.6 10.7 %collective-permute-start = (bf16[48,2048]{1,0:T(8,128)(2,1)S(1)}, bf16[48,2048]{1,0:T(8,128)(2,1)S(1)}, u32[]{:S(2)}, u32[]{:S(2)}) collective-permute-start(bf16[48,2048]{1,0:T(8,128)(2,1)S(1)} %bitcast.34), channel_id=1, source_target_pairs={{0,2},{1,15},{2,4},{3,1},{4,6},{5,3},{6,8},{7,5},{8,10},{9,7},{10,... | collective-permute-start | bytes 589832 | tf_op jit(solution)/shard_map/ppermute | solution.py:50
  11.5 3.1 %collective-permute-start.7 = (bf16[8,2048]{1,0:T(8,128)(2,1)S(1)}, bf16[8,2048]{1,0:T(8,128)(2,1)S(1)}, u32[]{:S(2)}, u32[]{:S(2)}) collective-permute-start(bf16[8,2048]{1,0:T(8,128)(2,1)S(1)} %get-tuple-element.35), channel_id=1, source_target_pairs={{0,16},{1,17},{2,18},{3,19},{4,20},{5,21},{6,22},{7,23},{8,24},{9,... | collective-permute-start | bytes 98312 | tf_op jit(solution)/shard_map/ppermute | solution.py:50
  12.9 3.1 %collective-permute-start.9 = (bf16[128,128]{1,0:T(8,128)(2,1)S(1)}, bf16[128,128]{1,0:T(8,128)(2,1)S(1)}, u32[]{:S(2)}, u32[]{:S(2)}) collective-permute-start(bf16[128,128]{1,0:T(8,128)(2,1)S(1)} %pad_maximum_fusion.2), channel_id=1, source_target_pairs={{0,16},{1,17},{2,18},{3,19},{4,20},{5,21},{6,22},{7,23},{8,24},{9,... | collective-permute-start | bytes 98312 | tf_op jit(solution)/shard_map/ppermute | solution.py:50
  16.3 7.2 %collective-permute-start.12 = (bf16[80,2048]{1,0:T(8,128)(2,1)S(1)}, bf16[80,2048]{1,0:T(8,128)(2,1)S(1)}, u32[]{:S(2)}, u32[]{:S(2)}) collective-permute-start(bf16[80,2048]{1,0:T(8,128)(2,1)S(1)} %pad_maximum_fusion.1.refs_12_), channel_id=1, source_target_pairs={{0,14},{1,3},{2,0},{3,5},{4,2},{5,7},{6,4},{7,9},{8,6},{9,11},{10,... | collective-permute-start | bytes 983048 | tf_op jit(solution)/shard_map/ppermute | solution.py:50
  16.4 7.9 %collective-permute-start.10 = (bf16[80,2048]{1,0:T(8,128)(2,1)S(1)}, bf16[80,2048]{1,0:T(8,128)(2,1)S(1)}, u32[]{:S(2)}, u32[]{:S(2)}) collective-permute-start(bf16[80,2048]{1,0:T(8,128)(2,1)S(1)} %pad_maximum_fusion.1.refs_12_), channel_id=1, source_target_pairs={{0,2},{1,15},{2,4},{3,1},{4,6},{5,3},{6,8},{7,5},{8,10},{9,7},{10,... | collective-permute-start | bytes 983048 | tf_op jit(solution)/shard_map/ppermute | solution.py:50
  23.5 8.7 %collective-permute-start.13 = (bf16[80,2048]{1,0:T(8,128)(2,1)S(1)}, bf16[80,2048]{1,0:T(8,128)(2,1)S(1)}, u32[]{:S(2)}, u32[]{:S(2)}) collective-permute-start(bf16[80,2048]{1,0:T(8,128)(2,1)S(1)} %collective-permute-done.12.refs_14_), channel_id=1, source_target_pairs={{0,14},{1,3},{2,0},{3,5},{4,2},{5,7},{6,4},{7,9},{8,6},{9,11},{10,... | collective-permute-start | bytes 983048 | tf_op jit(solution)/shard_map/ppermute | solution.py:50
  24.3 7.9 %collective-permute-start.11 = (bf16[80,2048]{1,0:T(8,128)(2,1)S(1)}, bf16[80,2048]{1,0:T(8,128)(2,1)S(1)}, u32[]{:S(2)}, u32[]{:S(2)}) collective-permute-start(bf16[80,2048]{1,0:T(8,128)(2,1)S(1)} %collective-permute-done.10.refs_13_), channel_id=1, source_target_pairs={{0,2},{1,15},{2,4},{3,1},{4,6},{5,3},{6,8},{7,5},{8,10},{9,7},{10,... | collective-permute-start | bytes 983048 | tf_op jit(solution)/shard_map/ppermute | solution.py:50
  27.7 12.8 %collective-permute-start.1 = (bf16[128,2048]{1,0:T(8,128)(2,1)S(1)}, bf16[128,2048]{1,0:T(8,128)(2,1)S(1)}, u32[]{:S(2)}, u32[]{:S(2)}) collective-permute-start(bf16[128,2048]{1,0:T(8,128)(2,1)S(1)} %get-tuple-element.34.refs_0_), channel_id=1, source_target_pairs={{0,16},{1,17},{2,18},{3,19},{4,20},{5,21},{6,22},{7,23},{8,24},{9,... | collective-permute-start | bytes 1572872 | tf_op jit(solution)/shard_map/ppermute | solution.py:50
  28.0 14.1 %collective-permute-start.6 = (bf16[48,2048]{1,0:T(8,128)(2,1)S(1)}, bf16[48,2048]{1,0:T(8,128)(2,1)S(1)}, u32[]{:S(2)}, u32[]{:S(2)}) collective-permute-start(bf16[48,2048]{1,0:T(8,128)(2,1)S(1)} %collective-permute-done.4.refs_6_), channel_id=1, source_target_pairs={{0,14},{1,3},{2,0},{3,5},{4,2},{5,7},{6,4},{7,9},{8,6},{9,11},{10,... | collective-permute-start | bytes 589832 | tf_op jit(solution)/shard_map/ppermute | solution.py:50
  32.2 14.0 %collective-permute-start.16 = (bf16[80,2048]{1,0:T(8,128)(2,1)S(1)}, bf16[80,2048]{1,0:T(8,128)(2,1)S(1)}, u32[]{:S(2)}, u32[]{:S(2)}) collective-permute-start(bf16[80,2048]{1,0:T(8,128)(2,1)S(1)} %collective-permute-done.11.refs_15_), channel_id=1, source_target_pairs={{0,2},{1,15},{2,4},{3,1},{4,6},{5,3},{6,8},{7,5},{8,10},{9,7},{10,... | collective-permute-start | bytes 983048 | tf_op jit(solution)/shard_map/ppermute | solution.py:50
  35.5 7.8 %collective-permute-start.5 = (bf16[48,2048]{1,0:T(8,128)(2,1)S(1)}, bf16[48,2048]{1,0:T(8,128)(2,1)S(1)}, u32[]{:S(2)}, u32[]{:S(2)}) collective-permute-start(bf16[48,2048]{1,0:T(8,128)(2,1)S(1)} %collective-permute-done.refs_5_), channel_id=1, source_target_pairs={{0,2},{1,15},{2,4},{3,1},{4,6},{5,3},{6,8},{7,5},{8,10},{9,7},{10,... | collective-permute-start | bytes 589832 | tf_op jit(solution)/shard_map/ppermute | solution.py:50
  35.5 19.0 %collective-permute-start.2 = (bf16[128,2048]{1,0:T(8,128)(2,1)S(1)}, bf16[128,2048]{1,0:T(8,128)(2,1)S(1)}, u32[]{:S(2)}, u32[]{:S(2)}) collective-permute-start(bf16[128,2048]{1,0:T(8,128)(2,1)S(1)} %get-tuple-element.34.refs_0_), channel_id=1, source_target_pairs={{0,1},{1,0},{2,3},{3,2},{4,5},{5,4},{6,7},{7,6},{8,9},{9,8},{10,11... | collective-permute-start | bytes 1572872 | tf_op jit(solution)/shard_map/ppermute | solution.py:50
  40.5 14.0 %collective-permute-start.3 = (bf16[128,2048]{1,0:T(8,128)(2,1)S(1)}, bf16[128,2048]{1,0:T(8,128)(2,1)S(1)}, u32[]{:S(2)}, u32[]{:S(2)}) collective-permute-start(bf16[128,2048]{1,0:T(8,128)(2,1)S(1)} %collective-permute-done.1.refs_1_), channel_id=1, source_target_pairs={{0,1},{1,0},{2,3},{3,2},{4,5},{5,4},{6,7},{7,6},{8,9},{9,8},{10,11... | collective-permute-start | bytes 1572872 | tf_op jit(solution)/shard_map/ppermute | solution.py:50
  42.1 12.4 %collective-permute-start.17 = (bf16[80,2048]{1,0:T(8,128)(2,1)S(1)}, bf16[80,2048]{1,0:T(8,128)(2,1)S(1)}, u32[]{:S(2)}, u32[]{:S(2)}) collective-permute-start(bf16[80,2048]{1,0:T(8,128)(2,1)S(1)} %collective-permute-done.13.refs_16_), channel_id=1, source_target_pairs={{0,14},{1,3},{2,0},{3,5},{4,2},{5,7},{6,4},{7,9},{8,6},{9,11},{10,... | collective-permute-start | bytes 983048 | tf_op jit(solution)/shard_map/ppermute | solution.py:50
  43.3 7.6 %collective-permute-start.14 = (bf16[48,2048]{1,0:T(8,128)(2,1)S(1)}, bf16[48,2048]{1,0:T(8,128)(2,1)S(1)}, u32[]{:S(2)}, u32[]{:S(2)}) collective-permute-start(bf16[48,2048]{1,0:T(8,128)(2,1)S(1)} %collective-permute-done.5.refs_7_), channel_id=1, source_target_pairs={{0,2},{1,15},{2,4},{3,1},{4,6},{5,3},{6,8},{7,5},{8,10},{9,7},{10,... | collective-permute-start | bytes 589832 | tf_op jit(solution)/shard_map/ppermute | solution.py:50
  46.2 8.3 %collective-permute-start.15 = (bf16[48,2048]{1,0:T(8,128)(2,1)S(1)}, bf16[48,2048]{1,0:T(8,128)(2,1)S(1)}, u32[]{:S(2)}, u32[]{:S(2)}) collective-permute-start(bf16[48,2048]{1,0:T(8,128)(2,1)S(1)} %collective-permute-done.6.refs_8_), channel_id=1, source_target_pairs={{0,14},{1,3},{2,0},{3,5},{4,2},{5,7},{6,4},{7,9},{8,6},{9,11},{10,... | collective-permute-start | bytes 589832 | tf_op jit(solution)/shard_map/ppermute | solution.py:50
  50.9 10.2 %collective-permute-start.19 = (bf16[80,2048]{1,0:T(8,128)(2,1)S(1)}, bf16[80,2048]{1,0:T(8,128)(2,1)S(1)}, u32[]{:S(2)}, u32[]{:S(2)}) collective-permute-start(bf16[80,2048]{1,0:T(8,128)(2,1)S(1)} %collective-permute-done.16.refs_17_), channel_id=1, source_target_pairs={{0,2},{1,15},{2,4},{3,1},{4,6},{5,3},{6,8},{7,5},{8,10},{9,7},{10,... | collective-permute-start | bytes 983048 | tf_op jit(solution)/shard_map/ppermute | solution.py:50
  54.5 6.5 %collective-permute-start.18 = (bf16[48,2048]{1,0:T(8,128)(2,1)S(1)}, bf16[48,2048]{1,0:T(8,128)(2,1)S(1)}, u32[]{:S(2)}, u32[]{:S(2)}) collective-permute-start(bf16[48,2048]{1,0:T(8,128)(2,1)S(1)} %collective-permute-done.14.refs_9_), channel_id=1, source_target_pairs={{0,2},{1,15},{2,4},{3,1},{4,6},{5,3},{6,8},{7,5},{8,10},{9,7},{10,... | collective-permute-start | bytes 589832 | tf_op jit(solution)/shard_map/ppermute | solution.py:50
  64.0 24.6 %collective-permute-start.21 = (bf16[128,2048]{1,0:T(8,128)(2,1)S(1)}, bf16[128,2048]{1,0:T(8,128)(2,1)S(1)}, u32[]{:S(2)}, u32[]{:S(2)}) collective-permute-start(bf16[128,2048]{1,0:T(8,128)(2,1)S(1)} %get-tuple-element.46.own_ref), channel_id=1, source_target_pairs={{0,1},{1,0},{2,3},{3,2},{4,5},{5,4},{6,7},{7,6},{8,9},{9,8},{10,11... | collective-permute-start | bytes 1572872 | tf_op jit(solution)/shard_map/ppermute | solution.py:50
  73.0 17.6 %collective-permute-start.29 = (bf16[128,2048]{1,0:T(8,128)(2,1)S(1)}, bf16[128,2048]{1,0:T(8,128)(2,1)S(1)}, u32[]{:S(2)}, u32[]{:S(2)}) collective-permute-start(bf16[128,2048]{1,0:T(8,128)(2,1)S(1)} %get-tuple-element.54.mine), channel_id=1, source_target_pairs={{0,96},{32,0},{64,32},{96,64},{128,224},{160,128},{192,160},{224,1... | collective-permute-start | bytes 1572872 | tf_op jit(solution)/shard_map/ppermute | solution.py:50
  75.7 22.8 %collective-permute-start.28 = (bf16[128,2048]{1,0:T(8,128)(2,1)S(1)}, bf16[128,2048]{1,0:T(8,128)(2,1)S(1)}, u32[]{:S(2)}, u32[]{:S(2)}) collective-permute-start(bf16[128,2048]{1,0:T(8,128)(2,1)S(1)} %get-tuple-element.54.mine), channel_id=1, source_target_pairs={{0,32},{32,64},{64,96},{96,0},{128,160},{160,192},{192,224},{224,1... | collective-permute-start | bytes 1572872 | tf_op jit(solution)/shard_map/ppermute | solution.py:50
  75.7 5.9 %collective-permute-start.23 = (bf16[256,256]{1,0:T(8,128)(2,1)S(1)}, bf16[256,256]{1,0:T(8,128)(2,1)S(1)}, u32[]{:S(2)}, u32[]{:S(2)}) collective-permute-start(bf16[256,256]{1,0:T(8,128)(2,1)S(1)} %get-tuple-element.50), channel_id=1, source_target_pairs={{0,2},{1,3},{2,4},{3,5},{4,6},{5,7},{6,8},{7,9},{8,10},{9,11},{10,... | collective-permute-start | bytes 393224 | tf_op jit(solution)/shard_map/ppermute | solution.py:50
  75.8 23.0 %collective-permute-start.20 = (bf16[512,384]{1,0:T(8,128)(2,1)S(1)}, bf16[512,384]{1,0:T(8,128)(2,1)S(1)}, u32[]{:S(2)}, u32[]{:S(2)}) collective-permute-start(bf16[512,384]{1,0:T(8,128)(2,1)S(1)} %get-tuple-element.45), channel_id=1, source_target_pairs={{0,1},{1,0},{2,3},{3,2},{4,5},{5,4},{6,7},{7,6},{8,9},{9,8},{10,11... | collective-permute-start | bytes 1179656 | tf_op jit(solution)/shard_map/ppermute | solution.py:50
  81.7 6.9 %collective-permute-start.24 = (bf16[256,256]{1,0:T(8,128)(2,1)S(1)}, bf16[256,256]{1,0:T(8,128)(2,1)S(1)}, u32[]{:S(2)}, u32[]{:S(2)}) collective-permute-start(bf16[256,256]{1,0:T(8,128)(2,1)S(1)} %get-tuple-element.51), channel_id=1, source_target_pairs={{0,3},{1,2},{2,5},{3,4},{4,7},{5,6},{6,9},{7,8},{8,11},{9,10},{10,... | collective-permute-start | bytes 393224 | tf_op jit(solution)/shard_map/ppermute | solution.py:50
  88.6 4.2 %collective-permute-start.25 = (bf16[256,256]{1,0:T(8,128)(2,1)S(1)}, bf16[256,256]{1,0:T(8,128)(2,1)S(1)}, u32[]{:S(2)}, u32[]{:S(2)}) collective-permute-start(bf16[256,256]{1,0:T(8,128)(2,1)S(1)} %get-tuple-element.52), channel_id=1, source_target_pairs={{0,14},{1,15},{2,0},{3,1},{4,2},{5,3},{6,4},{7,5},{8,6},{9,7},{10,... | collective-permute-start | bytes 393224 | tf_op jit(solution)/shard_map/ppermute | solution.py:50
  88.6 8.0 %collective-permute-start.26 = (bf16[256,256]{1,0:T(8,128)(2,1)S(1)}, bf16[256,256]{1,0:T(8,128)(2,1)S(1)}, u32[]{:S(2)}, u32[]{:S(2)}) collective-permute-start(bf16[256,256]{1,0:T(8,128)(2,1)S(1)} %get-tuple-element.53), channel_id=1, source_target_pairs={{0,15},{1,14},{2,1},{3,0},{4,3},{5,2},{6,5},{7,4},{8,7},{9,6},{10,... | collective-permute-start | bytes 393224 | tf_op jit(solution)/shard_map/ppermute | solution.py:50
  90.6 8.1 %collective-permute-start.22 = (bf16[256,256]{1,0:T(8,128)(2,1)S(1)}, bf16[256,256]{1,0:T(8,128)(2,1)S(1)}, u32[]{:S(2)}, u32[]{:S(2)}) collective-permute-start(bf16[256,256]{1,0:T(8,128)(2,1)S(1)} %get-tuple-element.49), channel_id=1, source_target_pairs={{0,1},{1,0},{2,3},{3,2},{4,5},{5,4},{6,7},{7,6},{8,9},{9,8},{10,11... | collective-permute-start | bytes 393224 | tf_op jit(solution)/shard_map/ppermute | solution.py:50
  96.6 8.2 %collective-permute-start.31 = (bf16[64,2048]{1,0:T(8,128)(2,1)S(1)}, bf16[64,2048]{1,0:T(8,128)(2,1)S(1)}, u32[]{:S(2)}, u32[]{:S(2)}) collective-permute-start(bf16[64,2048]{1,0:T(8,128)(2,1)S(1)} %slice.75), channel_id=1, source_target_pairs={{0,96},{32,0},{64,32},{96,64},{128,224},{160,128},{192,160},{224,1... | collective-permute-start | bytes 786440 | tf_op jit(solution)/shard_map/ppermute | solution.py:50
  98.6 9.6 %collective-permute-start.30 = (bf16[64,2048]{1,0:T(8,128)(2,1)S(1)}, bf16[64,2048]{1,0:T(8,128)(2,1)S(1)}, u32[]{:S(2)}, u32[]{:S(2)}) collective-permute-start(bf16[64,2048]{1,0:T(8,128)(2,1)S(1)} %slice.74), channel_id=1, source_target_pairs={{0,32},{32,64},{64,96},{96,0},{128,160},{160,192},{192,224},{224,1... | collective-permute-start | bytes 786440 | tf_op jit(solution)/shard_map/ppermute | solution.py:50
  102.7 5.6 %collective-permute-start.27 = (bf16[256,256]{1,0:T(8,128)(2,1)S(1)}, bf16[256,256]{1,0:T(8,128)(2,1)S(1)}, u32[]{:S(2)}, u32[]{:S(2)}) collective-permute-start(bf16[256,256]{1,0:T(8,128)(2,1)S(1)} %get-tuple-element.61), channel_id=1, source_target_pairs={{0,16},{1,17},{2,18},{3,19},{4,20},{5,21},{6,22},{7,23},{8,24},{9,... | collective-permute-start | bytes 393224 | tf_op jit(solution)/shard_map/ppermute | solution.py:50
  (4 other events, 32.8 us)

commit v9 on v7

--- a/solution.py
+++ b/solution.py
@@ -316,15 +316,23 @@
     a_one, a_two, b_one, b_two = first, second, first, second
     for step in range(1, 5):
         if step == 2:
+            to_send = after(normed, one[0, 1])
+            across = send(to_send, OTHER_X)
+            beside = send(to_send, OTHER_CORE)
+            beside_across = send(across, OTHER_CORE)
             a_two = b_two = after(second, a_one, b_one)
         if step > 1:
             if step > 2:
                 before = one[0, step - 2], one[1, step - 2]
+                if step == 4:
+                    before = *before, across, beside, beside_across
                 a_two, b_two = lax.optimization_barrier((a_two, b_two, *before))[:2]
             two[0, step - 1] = a_two = send(a_two, AHEAD)
             two[1, step - 1] = b_two = send(b_two, BEHIND)
         if step > 2:
             before = two[0, step - 2], two[1, step - 2]
+            if step == 3:
+                before = *before, across, beside, beside_across
             a_one, b_one = lax.optimization_barrier((a_one, b_one, *before))[:2]
         one[0, step] = a_one = send(a_one, AHEAD)
         if step < 4:
@@ -333,11 +341,6 @@
     two[0, 4] = send(a_two, AHEAD)
     firsts = [one[s] for s in STEPS]
     seconds = [two[s] for s in STEPS]
-
-    to_send = after(normed, one[0, 1])
-    across = send(to_send, OTHER_X)
-    beside = send(to_send, OTHER_CORE)
-    beside_across = send(across, OTHER_CORE)
 
     half = jax.ShapeDtypeStruct((ROWS, 3 * 128), bf16)
     keep, to_swap, g_own, far_table, out_own, *edges = on_chip(
@@ -358,6 +361,7 @@
     )
     got = send(to_swap, OTHER_CORE)
     g_other = send(g_own, OTHER_CORE)
+    g_other, got = lax.optimization_barrier((g_other, got))
 
     below = send(edges[2], UP), send(edges[3], UP_CROSS)
     above = send(edges[0], DOWN), send(edges[1], DOWN_CROSS)

time: 104 us -> 109 us (1.048)
  starting transfers between devices: 42.4 us -> 45.8 us
  waiting for transfers between devices: 45.5 us -> 47.4 us
    ppermute x33, starting transfers between devices: 42.4 us -> 45.8 us  [send(): return lax.ppermute(value, axis, route)]
    ppermute x33, waiting for transfers between devices: 45.5 us -> 47.4 us  [send(): return lax.ppermute(value, axis, route)]
where the time goes in v9:
time: 109 us
  waiting for transfers between devices  47.4 us (43%)
  starting transfers between devices  45.8 us (42%)
  Pallas kernels  11.5 us (11%)
  other arithmetic  2.3 us (2%)
  local copies, waits for them, and re-layouts  1.28 us (1%)
    ppermute x33, waiting for transfers between devices, send(): return lax.ppermute(value, axis, route)  47.4 us
    ppermute x33, starting transfers between devices, send(): return lax.ppermute(value, axis, route)  45.8 us
    pallas_call x5, Pallas kernels, on_chip(): pl.pallas_call(kernel, out_shape=out_shape, in_specs=specs, out_specs=jax...  11.5 us
  transfers between devices with their start and end apart: 33, of which 15 were waited for; matrix products, arithmetic and copies ran while one was open for 0% of the time, Pallas kernels for 7%

profile of v9, /device:TPU:1, one launch (start us, length us, event | category | flops | bytes accessed | tf_op | source)
XLA Modules:
  0.0 109.1 jit_solution(14831504507306286465)
XLA Ops:
  2.3 3.3 %collective-permute-start.8 = (bf16[128,64]{1,0:T(8,128)(2,1)S(1)}, bf16[128,64]{1,0:T(8,128)(2,1)S(1)}, u32[]{:S(2)}, u32[]{:S(2)}) collective-permute-start(bf16[128,64]{1,0:T(8,128)(2,1)S(1)} %bitcast.43), channel_id=1, source_target_pairs={{0,1},{1,0},{2,3},{3,2},{4,5},{5,4},{6,7},{7,6},{8,9},{9,8},{10,11... | collective-permute-start | bytes 49160 | tf_op jit(solution)/shard_map/ppermute | solution.py:50
  5.6 3.9 %collective-permute-start = (bf16[48,2048]{1,0:T(8,128)(2,1)S(1)}, bf16[48,2048]{1,0:T(8,128)(2,1)S(1)}, u32[]{:S(2)}, u32[]{:S(2)}) collective-permute-start(bf16[48,2048]{1,0:T(8,128)(2,1)S(1)} %bitcast.34), channel_id=1, source_target_pairs={{0,2},{1,15},{2,4},{3,1},{4,6},{5,3},{6,8},{7,5},{8,10},{9,7},{10,... | collective-permute-start | bytes 589832 | tf_op jit(solution)/shard_map/ppermute | solution.py:50
  11.5 1.3 %collective-permute-start.7 = (bf16[8,2048]{1,0:T(8,128)(2,1)S(1)}, bf16[8,2048]{1,0:T(8,128)(2,1)S(1)}, u32[]{:S(2)}, u32[]{:S(2)}) collective-permute-start(bf16[8,2048]{1,0:T(8,128)(2,1)S(1)} %get-tuple-element.37), channel_id=1, source_target_pairs={{0,16},{1,17},{2,18},{3,19},{4,20},{5,21},{6,22},{7,23},{8,24},{9,... | collective-permute-start | bytes 98312 | tf_op jit(solution)/shard_map/ppermute | solution.py:50
  13.3 1.4 %collective-permute-done.7 = bf16[8,2048]{1,0:T(8,128)(2,1)S(1)} collective-permute-done((bf16[8,2048]{1,0:T(8,128)(2,1)S(1)}, bf16[8,2048]{1,0:T(8,128)(2,1)S(1)}, u32[]{:S(2)}, u32[]{:S(2)}) %collective-permute-start.7) | collective-permute-done | bytes 32800 | tf_op jit(solution)/shard_map/ppermute | solution.py:50
  14.7 1.4 %collective-permute-done.9 = bf16[128,128]{1,0:T(8,128)(2,1)S(1)} collective-permute-done((bf16[128,128]{1,0:T(8,128)(2,1)S(1)}, bf16[128,128]{1,0:T(8,128)(2,1)S(1)}, u32[]{:S(2)}, u32[]{:S(2)}) %collective-permute-start.9) | collective-permute-done | bytes 32800 | tf_op jit(solution)/shard_map/ppermute | solution.py:50
  16.7 2.7 %collective-permute-start.10 = (bf16[80,2048]{1,0:T(8,128)(2,1)S(1)}, bf16[80,2048]{1,0:T(8,128)(2,1)S(1)}, u32[]{:S(2)}, u32[]{:S(2)}) collective-permute-start(bf16[80,2048]{1,0:T(8,128)(2,1)S(1)} %pad_maximum_fusion.1.refs_12_), channel_id=1, source_target_pairs={{0,2},{1,15},{2,4},{3,1},{4,6},{5,3},{6,8},{7,5},{8,10},{9,7},{10,... | collective-permute-start | bytes 983048 | tf_op jit(solution)/shard_map/ppermute | solution.py:50
  19.4 2.3 %collective-permute-start.2 = (bf16[128,2048]{1,0:T(8,128)(2,1)S(1)}, bf16[128,2048]{1,0:T(8,128)(2,1)S(1)}, u32[]{:S(2)}, u32[]{:S(2)}) collective-permute-start(bf16[128,2048]{1,0:T(8,128)(2,1)S(1)} %get-tuple-element.36.refs_0_), channel_id=1, source_target_pairs={{0,1},{1,0},{2,3},{3,2},{4,5},{5,4},{6,7},{7,6},{8,9},{9,8},{10,11... | collective-permute-start | bytes 1572872 | tf_op jit(solution)/shard_map/ppermute | solution.py:50
  21.7 6.5 %collective-permute-done.1.refs_1_ = bf16[128,2048]{1,0:T(8,128)(2,1)S(1)} collective-permute-done((bf16[128,2048]{1,0:T(8,128)(2,1)S(1)}, bf16[128,2048]{1,0:T(8,128)(2,1)S(1)}, u32[]{:S(2)}, u32[]{:S(2)}) %collective-permute-start.1) | collective-permute-done | bytes 524320 | tf_op jit(solution)/shard_map/ppermute | solution.py:50
  28.3 2.4 %collective-permute-start.3 = (bf16[128,2048]{1,0:T(8,128)(2,1)S(1)}, bf16[128,2048]{1,0:T(8,128)(2,1)S(1)}, u32[]{:S(2)}, u32[]{:S(2)}) collective-permute-start(bf16[128,2048]{1,0:T(8,128)(2,1)S(1)} %collective-permute-done.1.refs_1_), channel_id=1, source_target_pairs={{0,1},{1,0},{2,3},{3,2},{4,5},{5,4},{6,7},{7,6},{8,9},{9,8},{10,11... | collective-permute-start | bytes 1572872 | tf_op jit(solution)/shard_map/ppermute | solution.py:50
  30.7 2.7 %collective-permute-start.14 = (bf16[80,2048]{1,0:T(8,128)(2,1)S(1)}, bf16[80,2048]{1,0:T(8,128)(2,1)S(1)}, u32[]{:S(2)}, u32[]{:S(2)}) collective-permute-start(bf16[80,2048]{1,0:T(8,128)(2,1)S(1)} %collective-permute-done.10.refs_13_), channel_id=1, source_target_pairs={{0,2},{1,15},{2,4},{3,1},{4,6},{5,3},{6,8},{7,5},{8,10},{9,7},{10,... | collective-permute-start | bytes 983048 | tf_op jit(solution)/shard_map/ppermute | solution.py:50
  33.4 3.0 %collective-permute-done.6.refs_8_ = bf16[48,2048]{1,0:T(8,128)(2,1)S(1)} collective-permute-done((bf16[48,2048]{1,0:T(8,128)(2,1)S(1)}, bf16[48,2048]{1,0:T(8,128)(2,1)S(1)}, u32[]{:S(2)}, u32[]{:S(2)}) %collective-permute-start.6) | collective-permute-done | bytes 196640 | tf_op jit(solution)/shard_map/ppermute | solution.py:50
  36.4 1.4 %collective-permute-start.5 = (bf16[48,2048]{1,0:T(8,128)(2,1)S(1)}, bf16[48,2048]{1,0:T(8,128)(2,1)S(1)}, u32[]{:S(2)}, u32[]{:S(2)}) collective-permute-start(bf16[48,2048]{1,0:T(8,128)(2,1)S(1)} %collective-permute-done.refs_5_), channel_id=1, source_target_pairs={{0,2},{1,15},{2,4},{3,1},{4,6},{5,3},{6,8},{7,5},{8,10},{9,7},{10,... | collective-permute-start | bytes 589832 | tf_op jit(solution)/shard_map/ppermute | solution.py:50
  37.8 6.7 %collective-permute-done.5.refs_7_ = bf16[48,2048]{1,0:T(8,128)(2,1)S(1)} collective-permute-done((bf16[48,2048]{1,0:T(8,128)(2,1)S(1)}, bf16[48,2048]{1,0:T(8,128)(2,1)S(1)}, u32[]{:S(2)}, u32[]{:S(2)}) %collective-permute-start.5) | collective-permute-done | bytes 196640 | tf_op jit(solution)/shard_map/ppermute | solution.py:50
  44.5 3.1 %collective-permute-start.17 = (bf16[80,2048]{1,0:T(8,128)(2,1)S(1)}, bf16[80,2048]{1,0:T(8,128)(2,1)S(1)}, u32[]{:S(2)}, u32[]{:S(2)}) collective-permute-start(bf16[80,2048]{1,0:T(8,128)(2,1)S(1)} %collective-permute-done.14.refs_15_), channel_id=1, source_target_pairs={{0,2},{1,15},{2,4},{3,1},{4,6},{5,3},{6,8},{7,5},{8,10},{9,7},{10,... | collective-permute-start | bytes 983048 | tf_op jit(solution)/shard_map/ppermute | solution.py:50
  47.6 1.4 %collective-permute-start.13 = (bf16[48,2048]{1,0:T(8,128)(2,1)S(1)}, bf16[48,2048]{1,0:T(8,128)(2,1)S(1)}, u32[]{:S(2)}, u32[]{:S(2)}) collective-permute-start(bf16[48,2048]{1,0:T(8,128)(2,1)S(1)} %collective-permute-done.6.refs_8_), channel_id=1, source_target_pairs={{0,14},{1,3},{2,0},{3,5},{4,2},{5,7},{6,4},{7,9},{8,6},{9,11},{10,... | collective-permute-start | bytes 589832 | tf_op jit(solution)/shard_map/ppermute | solution.py:50
  49.1 7.8 %collective-permute-done.12.refs_9_ = bf16[48,2048]{1,0:T(8,128)(2,1)S(1)} collective-permute-done((bf16[48,2048]{1,0:T(8,128)(2,1)S(1)}, bf16[48,2048]{1,0:T(8,128)(2,1)S(1)}, u32[]{:S(2)}, u32[]{:S(2)}) %collective-permute-start.12) | collective-permute-done | bytes 196640 | tf_op jit(solution)/shard_map/ppermute | solution.py:50
  56.9 3.4 %collective-permute-start.19 = (bf16[80,2048]{1,0:T(8,128)(2,1)S(1)}, bf16[80,2048]{1,0:T(8,128)(2,1)S(1)}, u32[]{:S(2)}, u32[]{:S(2)}) collective-permute-start(bf16[80,2048]{1,0:T(8,128)(2,1)S(1)} %collective-permute-done.17.refs_17_), channel_id=1, source_target_pairs={{0,2},{1,15},{2,4},{3,1},{4,6},{5,3},{6,8},{7,5},{8,10},{9,7},{10,... | collective-permute-start | bytes 983048 | tf_op jit(solution)/shard_map/ppermute | solution.py:50
  60.4 1.4 %collective-permute-done.18.refs_18_ = bf16[80,2048]{1,0:T(8,128)(2,1)S(1)} collective-permute-done((bf16[80,2048]{1,0:T(8,128)(2,1)S(1)}, bf16[80,2048]{1,0:T(8,128)(2,1)S(1)}, u32[]{:S(2)}, u32[]{:S(2)}) %collective-permute-start.18) | collective-permute-done | bytes 327712 | tf_op jit(solution)/shard_map/ppermute | solution.py:50
  61.7 4.6 %collective-permute-done.16.refs_11_ = bf16[48,2048]{1,0:T(8,128)(2,1)S(1)} collective-permute-done((bf16[48,2048]{1,0:T(8,128)(2,1)S(1)}, bf16[48,2048]{1,0:T(8,128)(2,1)S(1)}, u32[]{:S(2)}, u32[]{:S(2)}) %collective-permute-start.16) | collective-permute-done | bytes 196640 | tf_op jit(solution)/shard_map/ppermute | solution.py:50
  66.4 2.9 %shard_map.83 = (bf16[512,384]{1,0:T(8,128)(2,1)S(1)}, bf16[512,384]{1,0:T(8,128)(2,1)S(1)}, bf16[128,2048]{1,0:T(8,128)(2,1)S(1)}, bf16[512,2048]{1,0:T(8,128)(...) custom-call(s32[6]{0:T(128)S(1)} %stack.35.index, ...), custom_call_target="tpu_custom_call" | custom-call | flops 1610612736 | bytes 4194304 | tf_op jit(solution)/shard_map/pallas_call | solution.py:248
  69.3 5.8 %collective-permute-start.20 = (bf16[128,2048]{1,0:T(8,128)(2,1)S(1)}, bf16[128,2048]{1,0:T(8,128)(2,1)S(1)}, u32[]{:S(2)}, u32[]{:S(2)}) collective-permute-start(bf16[128,2048]{1,0:T(8,128)(2,1)S(1)} %get-tuple-element.49.own_ref), channel_id=1, source_target_pairs={{0,1},{1,0},{2,3},{3,2},{4,5},{5,4},{6,7},{7,6},{8,9},{9,8},{10,11... | collective-permute-start | bytes 1572872 | tf_op jit(solution)/shard_map/ppermute | solution.py:50
  75.1 2.8 %collective-permute-start.29 = (bf16[128,2048]{1,0:T(8,128)(2,1)S(1)}, bf16[128,2048]{1,0:T(8,128)(2,1)S(1)}, u32[]{:S(2)}, u32[]{:S(2)}) collective-permute-start(bf16[128,2048]{1,0:T(8,128)(2,1)S(1)} %get-tuple-element.60.mine), channel_id=1, source_target_pairs={{0,96},{32,0},{64,32},{96,64},{128,224},{160,128},{192,160},{224,1... | collective-permute-start | bytes 1572872 | tf_op jit(solution)/shard_map/ppermute | solution.py:50
  78.3 1.4 %collective-permute-done.21.got_ref = bf16[512,384]{1,0:T(8,128)(2,1)S(1)} collective-permute-done((bf16[512,384]{1,0:T(8,128)(2,1)S(1)}, bf16[512,384]{1,0:T(8,128)(2,1)S(1)}, u32[]{:S(2)}, u32[]{:S(2)}) %collective-permute-start.21) | collective-permute-done | bytes 393248 | tf_op jit(solution)/shard_map/ppermute | solution.py:50
  79.6 2.9 %collective-permute-start.25 = (bf16[256,256]{1,0:T(8,128)(2,1)S(1)}, bf16[256,256]{1,0:T(8,128)(2,1)S(1)}, u32[]{:S(2)}, u32[]{:S(2)}) collective-permute-start(bf16[256,256]{1,0:T(8,128)(2,1)S(1)} %get-tuple-element.58), channel_id=1, source_target_pairs={{0,14},{1,15},{2,0},{3,1},{4,2},{5,3},{6,4},{7,5},{8,6},{9,7},{10,... | collective-permute-start | bytes 393224 | tf_op jit(solution)/shard_map/ppermute | solution.py:50
  82.5 2.1 %shard_map.84 = (bf16[256,256]{1,0:T(8,128)(2,1)S(1)}, bf16[256,256]{1,0:T(8,128)(2,1)S(1)}) custom-call(s32[6]{0:T(128)S(1)} %stack.35.index, bf16[128,2048]{1,0:T(8,128)(2,1)S(1)} %get-tuple-element.49.own_ref, bf16[128,2048]{1,0:T(8,128)(2,1)S(1)} %collective-permute-done.20.other_ref, bf16[512,2048]{1,0:T(8,128)(2,1)S(1)} %get-tuple-element.53.table), custom_call_target="tpu_custom_call" | custom-call | flops 536870912 | bytes 4194304 | tf_op jit(solution)/shard_map/pallas_call | solution.py:248
  84.6 4.6 %collective-permute-done.29.nxt = bf16[128,2048]{1,0:T(8,128)(2,1)S(1)} collective-permute-done((bf16[128,2048]{1,0:T(8,128)(2,1)S(1)}, bf16[128,2048]{1,0:T(8,128)(2,1)S(1)}, u32[]{:S(2)}, u32[]{:S(2)}) %collective-permute-start.29) | collective-permute-done | bytes 524320 | tf_op jit(solution)/shard_map/ppermute | solution.py:50
  89.2 3.1 %collective-permute-done.28.prev = bf16[128,2048]{1,0:T(8,128)(2,1)S(1)} collective-permute-done((bf16[128,2048]{1,0:T(8,128)(2,1)S(1)}, bf16[128,2048]{1,0:T(8,128)(2,1)S(1)}, u32[]{:S(2)}, u32[]{:S(2)}) %collective-permute-start.28) | collective-permute-done | bytes 524320 | tf_op jit(solution)/shard_map/ppermute | solution.py:50
  93.8 1.4 %collective-permute-start.30 = (bf16[64,2048]{1,0:T(8,128)(2,1)S(1)}, bf16[64,2048]{1,0:T(8,128)(2,1)S(1)}, u32[]{:S(2)}, u32[]{:S(2)}) collective-permute-start(bf16[64,2048]{1,0:T(8,128)(2,1)S(1)} %slice.74), channel_id=1, source_target_pairs={{0,32},{32,64},{64,96},{96,0},{128,160},{160,192},{192,224},{224,1... | collective-permute-start | bytes 786440 | tf_op jit(solution)/shard_map/ppermute | solution.py:50
  95.3 4.0 %shard_map.85 = bf16[2,256,256]{2,1,0:T(8,128)(2,1)S(1)} custom-call(s32[6]{0:T(128)S(1)} %stack.35.index, bf16[512,384]{1,0:T(8,128)(2,1)S(1)} %get-tuple-element.48.keep_ref, bf16[512,384]{1,0:T(8,128)(2,1)S(1)} %collective-permute-done.21.got_ref, bf16[256,256]{1,0:T(8,128)(2,1)S(1)} %get-tuple-element.54.g_keep, ...), custom_call_target="tpu_custom_call" | custom-call | flops 1342177280 | bytes 4194304 | tf_op jit(solution)/shard_map/pallas_call | solution.py:248
  99.9 1.8 %collective-permute-done.31.far_b = bf16[64,2048]{1,0:T(8,128)(2,1)S(1)} collective-permute-done((bf16[64,2048]{1,0:T(8,128)(2,1)S(1)}, bf16[64,2048]{1,0:T(8,128)(2,1)S(1)}, u32[]{:S(2)}, u32[]{:S(2)}) %collective-permute-start.31) | collective-permute-done | bytes 262176 | tf_op jit(solution)/shard_map/ppermute | solution.py:50
  105.1 1.5 %collective-permute-start.32 = (bf16[128,2048]{1,0:T(8,128)(2,1)S(1)}, bf16[128,2048]{1,0:T(8,128)(2,1)S(1)}, u32[]{:S(2)}, u32[]{:S(2)}) collective-permute-start(bf16[128,2048]{1,0:T(8,128)(2,1)S(1)} %get-tuple-element.62), channel_id=1, source_target_pairs={{0,1},{1,0},{2,3},{3,2},{4,5},{5,4},{6,7},{7,6},{8,9},{9,8},{10,11... | collective-permute-start | bytes 1572872 | tf_op jit(solution)/shard_map/ppermute | solution.py:50
  106.7 1.5 %collective-permute-done.32 = bf16[128,2048]{1,0:T(8,128)(2,1)S(1)} collective-permute-done((bf16[128,2048]{1,0:T(8,128)(2,1)S(1)}, bf16[128,2048]{1,0:T(8,128)(2,1)S(1)}, u32[]{:S(2)}, u32[]{:S(2)}) %collective-permute-start.32) | collective-permute-done | bytes 524320 | tf_op jit(solution)/shard_map/ppermute | solution.py:50
  (67 shorter events, 11.8 us)
Async XLA Ops:
  2.3 10.5 %collective-permute-start.8 = (bf16[128,64]{1,0:T(8,128)(2,1)S(1)}, bf16[128,64]{1,0:T(8,128)(2,1)S(1)}, u32[]{:S(2)}, u32[]{:S(2)}) collective-permute-start(bf16[128,64]{1,0:T(8,128)(2,1)S(1)} %bitcast.43), channel_id=1, source_target_pairs={{0,1},{1,0},{2,3},{3,2},{4,5},{5,4},{6,7},{7,6},{8,9},{9,8},{10,11... | collective-permute-start | bytes 49160 | tf_op jit(solution)/shard_map/ppermute | solution.py:50
  5.6 11.0 %collective-permute-start.4 = (bf16[48,2048]{1,0:T(8,128)(2,1)S(1)}, bf16[48,2048]{1,0:T(8,128)(2,1)S(1)}, u32[]{:S(2)}, u32[]{:S(2)}) collective-permute-start(bf16[48,2048]{1,0:T(8,128)(2,1)S(1)} %bitcast.33), channel_id=1, source_target_pairs={{0,14},{1,3},{2,0},{3,5},{4,2},{5,7},{6,4},{7,9},{8,6},{9,11},{10,... | collective-permute-start | bytes 589832 | tf_op jit(solution)/shard_map/ppermute | solution.py:50
  5.6 10.6 %collective-permute-start = (bf16[48,2048]{1,0:T(8,128)(2,1)S(1)}, bf16[48,2048]{1,0:T(8,128)(2,1)S(1)}, u32[]{:S(2)}, u32[]{:S(2)}) collective-permute-start(bf16[48,2048]{1,0:T(8,128)(2,1)S(1)} %bitcast.34), channel_id=1, source_target_pairs={{0,2},{1,15},{2,4},{3,1},{4,6},{5,3},{6,8},{7,5},{8,10},{9,7},{10,... | collective-permute-start | bytes 589832 | tf_op jit(solution)/shard_map/ppermute | solution.py:50
  11.5 3.1 %collective-permute-start.7 = (bf16[8,2048]{1,0:T(8,128)(2,1)S(1)}, bf16[8,2048]{1,0:T(8,128)(2,1)S(1)}, u32[]{:S(2)}, u32[]{:S(2)}) collective-permute-start(bf16[8,2048]{1,0:T(8,128)(2,1)S(1)} %get-tuple-element.37), channel_id=1, source_target_pairs={{0,16},{1,17},{2,18},{3,19},{4,20},{5,21},{6,22},{7,23},{8,24},{9,... | collective-permute-start | bytes 98312 | tf_op jit(solution)/shard_map/ppermute | solution.py:50
  12.9 3.1 %collective-permute-start.9 = (bf16[128,128]{1,0:T(8,128)(2,1)S(1)}, bf16[128,128]{1,0:T(8,128)(2,1)S(1)}, u32[]{:S(2)}, u32[]{:S(2)}) collective-permute-start(bf16[128,128]{1,0:T(8,128)(2,1)S(1)} %pad_maximum_fusion.2), channel_id=1, source_target_pairs={{0,16},{1,17},{2,18},{3,19},{4,20},{5,21},{6,22},{7,23},{8,24},{9,... | collective-permute-start | bytes 98312 | tf_op jit(solution)/shard_map/ppermute | solution.py:50
  16.3 12.0 %collective-permute-start.1 = (bf16[128,2048]{1,0:T(8,128)(2,1)S(1)}, bf16[128,2048]{1,0:T(8,128)(2,1)S(1)}, u32[]{:S(2)}, u32[]{:S(2)}) collective-permute-start(bf16[128,2048]{1,0:T(8,128)(2,1)S(1)} %get-tuple-element.36.refs_0_), channel_id=1, source_target_pairs={{0,16},{1,17},{2,18},{3,19},{4,20},{5,21},{6,22},{7,23},{8,24},{9,... | collective-permute-start | bytes 1572872 | tf_op jit(solution)/shard_map/ppermute | solution.py:50
  16.6 14.0 %collective-permute-start.11 = (bf16[80,2048]{1,0:T(8,128)(2,1)S(1)}, bf16[80,2048]{1,0:T(8,128)(2,1)S(1)}, u32[]{:S(2)}, u32[]{:S(2)}) collective-permute-start(bf16[80,2048]{1,0:T(8,128)(2,1)S(1)} %pad_maximum_fusion.1.refs_12_), channel_id=1, source_target_pairs={{0,14},{1,3},{2,0},{3,5},{4,2},{5,7},{6,4},{7,9},{8,6},{9,11},{10,... | collective-permute-start | bytes 983048 | tf_op jit(solution)/shard_map/ppermute | solution.py:50
  16.7 14.0 %collective-permute-start.10 = (bf16[80,2048]{1,0:T(8,128)(2,1)S(1)}, bf16[80,2048]{1,0:T(8,128)(2,1)S(1)}, u32[]{:S(2)}, u32[]{:S(2)}) collective-permute-start(bf16[80,2048]{1,0:T(8,128)(2,1)S(1)} %pad_maximum_fusion.1.refs_12_), channel_id=1, source_target_pairs={{0,2},{1,15},{2,4},{3,1},{4,6},{5,3},{6,8},{7,5},{8,10},{9,7},{10,... | collective-permute-start | bytes 983048 | tf_op jit(solution)/shard_map/ppermute | solution.py:50
  19.4 25.0 %collective-permute-start.2 = (bf16[128,2048]{1,0:T(8,128)(2,1)S(1)}, bf16[128,2048]{1,0:T(8,128)(2,1)S(1)}, u32[]{:S(2)}, u32[]{:S(2)}) collective-permute-start(bf16[128,2048]{1,0:T(8,128)(2,1)S(1)} %get-tuple-element.36.refs_0_), channel_id=1, source_target_pairs={{0,1},{1,0},{2,3},{3,2},{4,5},{5,4},{6,7},{7,6},{8,9},{9,8},{10,11... | collective-permute-start | bytes 1572872 | tf_op jit(solution)/shard_map/ppermute | solution.py:50
  28.3 16.2 %collective-permute-start.3 = (bf16[128,2048]{1,0:T(8,128)(2,1)S(1)}, bf16[128,2048]{1,0:T(8,128)(2,1)S(1)}, u32[]{:S(2)}, u32[]{:S(2)}) collective-permute-start(bf16[128,2048]{1,0:T(8,128)(2,1)S(1)} %collective-permute-done.1.refs_1_), channel_id=1, source_target_pairs={{0,1},{1,0},{2,3},{3,2},{4,5},{5,4},{6,7},{7,6},{8,9},{9,8},{10,11... | collective-permute-start | bytes 1572872 | tf_op jit(solution)/shard_map/ppermute | solution.py:50
  30.7 5.7 %collective-permute-start.6 = (bf16[48,2048]{1,0:T(8,128)(2,1)S(1)}, bf16[48,2048]{1,0:T(8,128)(2,1)S(1)}, u32[]{:S(2)}, u32[]{:S(2)}) collective-permute-start(bf16[48,2048]{1,0:T(8,128)(2,1)S(1)} %collective-permute-done.4.refs_6_), channel_id=1, source_target_pairs={{0,14},{1,3},{2,0},{3,5},{4,2},{5,7},{6,4},{7,9},{8,6},{9,11},{10,... | collective-permute-start | bytes 589832 | tf_op jit(solution)/shard_map/ppermute | solution.py:50
  30.7 13.7 %collective-permute-start.14 = (bf16[80,2048]{1,0:T(8,128)(2,1)S(1)}, bf16[80,2048]{1,0:T(8,128)(2,1)S(1)}, u32[]{:S(2)}, u32[]{:S(2)}) collective-permute-start(bf16[80,2048]{1,0:T(8,128)(2,1)S(1)} %collective-permute-done.10.refs_13_), channel_id=1, source_target_pairs={{0,2},{1,15},{2,4},{3,1},{4,6},{5,3},{6,8},{7,5},{8,10},{9,7},{10,... | collective-permute-start | bytes 983048 | tf_op jit(solution)/shard_map/ppermute | solution.py:50
  33.4 11.1 %collective-permute-start.15 = (bf16[80,2048]{1,0:T(8,128)(2,1)S(1)}, bf16[80,2048]{1,0:T(8,128)(2,1)S(1)}, u32[]{:S(2)}, u32[]{:S(2)}) collective-permute-start(bf16[80,2048]{1,0:T(8,128)(2,1)S(1)} %collective-permute-done.11.refs_14_), channel_id=1, source_target_pairs={{0,14},{1,3},{2,0},{3,5},{4,2},{5,7},{6,4},{7,9},{8,6},{9,11},{10,... | collective-permute-start | bytes 983048 | tf_op jit(solution)/shard_map/ppermute | solution.py:50
  36.4 8.0 %collective-permute-start.5 = (bf16[48,2048]{1,0:T(8,128)(2,1)S(1)}, bf16[48,2048]{1,0:T(8,128)(2,1)S(1)}, u32[]{:S(2)}, u32[]{:S(2)}) collective-permute-start(bf16[48,2048]{1,0:T(8,128)(2,1)S(1)} %collective-permute-done.refs_5_), channel_id=1, source_target_pairs={{0,2},{1,15},{2,4},{3,1},{4,6},{5,3},{6,8},{7,5},{8,10},{9,7},{10,... | collective-permute-start | bytes 589832 | tf_op jit(solution)/shard_map/ppermute | solution.py:50
  44.5 12.4 %collective-permute-start.17 = (bf16[80,2048]{1,0:T(8,128)(2,1)S(1)}, bf16[80,2048]{1,0:T(8,128)(2,1)S(1)}, u32[]{:S(2)}, u32[]{:S(2)}) collective-permute-start(bf16[80,2048]{1,0:T(8,128)(2,1)S(1)} %collective-permute-done.14.refs_15_), channel_id=1, source_target_pairs={{0,2},{1,15},{2,4},{3,1},{4,6},{5,3},{6,8},{7,5},{8,10},{9,7},{10,... | collective-permute-start | bytes 983048 | tf_op jit(solution)/shard_map/ppermute | solution.py:50
  47.6 9.3 %collective-permute-start.12 = (bf16[48,2048]{1,0:T(8,128)(2,1)S(1)}, bf16[48,2048]{1,0:T(8,128)(2,1)S(1)}, u32[]{:S(2)}, u32[]{:S(2)}) collective-permute-start(bf16[48,2048]{1,0:T(8,128)(2,1)S(1)} %collective-permute-done.5.refs_7_), channel_id=1, source_target_pairs={{0,2},{1,15},{2,4},{3,1},{4,6},{5,3},{6,8},{7,5},{8,10},{9,7},{10,... | collective-permute-start | bytes 589832 | tf_op jit(solution)/shard_map/ppermute | solution.py:50
  47.6 9.2 %collective-permute-start.13 = (bf16[48,2048]{1,0:T(8,128)(2,1)S(1)}, bf16[48,2048]{1,0:T(8,128)(2,1)S(1)}, u32[]{:S(2)}, u32[]{:S(2)}) collective-permute-start(bf16[48,2048]{1,0:T(8,128)(2,1)S(1)} %collective-permute-done.6.refs_8_), channel_id=1, source_target_pairs={{0,14},{1,3},{2,0},{3,5},{4,2},{5,7},{6,4},{7,9},{8,6},{9,11},{10,... | collective-permute-start | bytes 589832 | tf_op jit(solution)/shard_map/ppermute | solution.py:50
  49.0 12.7 %collective-permute-start.18 = (bf16[80,2048]{1,0:T(8,128)(2,1)S(1)}, bf16[80,2048]{1,0:T(8,128)(2,1)S(1)}, u32[]{:S(2)}, u32[]{:S(2)}) collective-permute-start(bf16[80,2048]{1,0:T(8,128)(2,1)S(1)} %collective-permute-done.15.refs_16_), channel_id=1, source_target_pairs={{0,14},{1,3},{2,0},{3,5},{4,2},{5,7},{6,4},{7,9},{8,6},{9,11},{10,... | collective-permute-start | bytes 983048 | tf_op jit(solution)/shard_map/ppermute | solution.py:50
  56.9 9.5 %collective-permute-start.19 = (bf16[80,2048]{1,0:T(8,128)(2,1)S(1)}, bf16[80,2048]{1,0:T(8,128)(2,1)S(1)}, u32[]{:S(2)}, u32[]{:S(2)}) collective-permute-start(bf16[80,2048]{1,0:T(8,128)(2,1)S(1)} %collective-permute-done.17.refs_17_), channel_id=1, source_target_pairs={{0,2},{1,15},{2,4},{3,1},{4,6},{5,3},{6,8},{7,5},{8,10},{9,7},{10,... | collective-permute-start | bytes 983048 | tf_op jit(solution)/shard_map/ppermute | solution.py:50
  60.3 6.1 %collective-permute-start.16 = (bf16[48,2048]{1,0:T(8,128)(2,1)S(1)}, bf16[48,2048]{1,0:T(8,128)(2,1)S(1)}, u32[]{:S(2)}, u32[]{:S(2)}) collective-permute-start(bf16[48,2048]{1,0:T(8,128)(2,1)S(1)} %collective-permute-done.12.refs_9_), channel_id=1, source_target_pairs={{0,2},{1,15},{2,4},{3,1},{4,6},{5,3},{6,8},{7,5},{8,10},{9,7},{10,... | collective-permute-start | bytes 589832 | tf_op jit(solution)/shard_map/ppermute | solution.py:50
  69.3 10.3 %collective-permute-start.20 = (bf16[128,2048]{1,0:T(8,128)(2,1)S(1)}, bf16[128,2048]{1,0:T(8,128)(2,1)S(1)}, u32[]{:S(2)}, u32[]{:S(2)}) collective-permute-start(bf16[128,2048]{1,0:T(8,128)(2,1)S(1)} %get-tuple-element.49.own_ref), channel_id=1, source_target_pairs={{0,1},{1,0},{2,3},{3,2},{4,5},{5,4},{6,7},{7,6},{8,9},{9,8},{10,11... | collective-permute-start | bytes 1572872 | tf_op jit(solution)/shard_map/ppermute | solution.py:50
  75.1 14.0 %collective-permute-start.29 = (bf16[128,2048]{1,0:T(8,128)(2,1)S(1)}, bf16[128,2048]{1,0:T(8,128)(2,1)S(1)}, u32[]{:S(2)}, u32[]{:S(2)}) collective-permute-start(bf16[128,2048]{1,0:T(8,128)(2,1)S(1)} %get-tuple-element.60.mine), channel_id=1, source_target_pairs={{0,96},{32,0},{64,32},{96,64},{128,224},{160,128},{192,160},{224,1... | collective-permute-start | bytes 1572872 | tf_op jit(solution)/shard_map/ppermute | solution.py:50
  77.9 14.4 %collective-permute-start.28 = (bf16[128,2048]{1,0:T(8,128)(2,1)S(1)}, bf16[128,2048]{1,0:T(8,128)(2,1)S(1)}, u32[]{:S(2)}, u32[]{:S(2)}) collective-permute-start(bf16[128,2048]{1,0:T(8,128)(2,1)S(1)} %get-tuple-element.60.mine), channel_id=1, source_target_pairs={{0,32},{32,64},{64,96},{96,0},{128,160},{160,192},{192,224},{224,1... | collective-permute-start | bytes 1572872 | tf_op jit(solution)/shard_map/ppermute | solution.py:50
  78.3 15.2 %collective-permute-start.23 = (bf16[256,256]{1,0:T(8,128)(2,1)S(1)}, bf16[256,256]{1,0:T(8,128)(2,1)S(1)}, u32[]{:S(2)}, u32[]{:S(2)}) collective-permute-start(bf16[256,256]{1,0:T(8,128)(2,1)S(1)} %get-tuple-element.56), channel_id=1, source_target_pairs={{0,2},{1,3},{2,4},{3,5},{4,6},{5,7},{6,8},{7,9},{8,10},{9,11},{10,... | collective-permute-start | bytes 393224 | tf_op jit(solution)/shard_map/ppermute | solution.py:50
  79.6 14.2 %collective-permute-start.24 = (bf16[256,256]{1,0:T(8,128)(2,1)S(1)}, bf16[256,256]{1,0:T(8,128)(2,1)S(1)}, u32[]{:S(2)}, u32[]{:S(2)}) collective-permute-start(bf16[256,256]{1,0:T(8,128)(2,1)S(1)} %get-tuple-element.57), channel_id=1, source_target_pairs={{0,3},{1,2},{2,5},{3,4},{4,7},{5,6},{6,9},{7,8},{8,11},{9,10},{10,... | collective-permute-start | bytes 393224 | tf_op jit(solution)/shard_map/ppermute | solution.py:50
  79.6 15.6 %collective-permute-start.25 = (bf16[256,256]{1,0:T(8,128)(2,1)S(1)}, bf16[256,256]{1,0:T(8,128)(2,1)S(1)}, u32[]{:S(2)}, u32[]{:S(2)}) collective-permute-start(bf16[256,256]{1,0:T(8,128)(2,1)S(1)} %get-tuple-element.58), channel_id=1, source_target_pairs={{0,14},{1,15},{2,0},{3,1},{4,2},{5,3},{6,4},{7,5},{8,6},{9,7},{10,... | collective-permute-start | bytes 393224 | tf_op jit(solution)/shard_map/ppermute | solution.py:50
  89.2 6.1 %collective-permute-start.26 = (bf16[256,256]{1,0:T(8,128)(2,1)S(1)}, bf16[256,256]{1,0:T(8,128)(2,1)S(1)}, u32[]{:S(2)}, u32[]{:S(2)}) collective-permute-start(bf16[256,256]{1,0:T(8,128)(2,1)S(1)} %get-tuple-element.59), channel_id=1, source_target_pairs={{0,15},{1,14},{2,1},{3,0},{4,3},{5,2},{6,5},{7,4},{8,7},{9,6},{10,... | collective-permute-start | bytes 393224 | tf_op jit(solution)/shard_map/ppermute | solution.py:50
  92.3 3.0 %collective-permute-start.22 = (bf16[256,256]{1,0:T(8,128)(2,1)S(1)}, bf16[256,256]{1,0:T(8,128)(2,1)S(1)}, u32[]{:S(2)}, u32[]{:S(2)}) collective-permute-start(bf16[256,256]{1,0:T(8,128)(2,1)S(1)} %get-tuple-element.55), channel_id=1, source_target_pairs={{0,1},{1,0},{2,3},{3,2},{4,5},{5,4},{6,7},{7,6},{8,9},{9,8},{10,11... | collective-permute-start | bytes 393224 | tf_op jit(solution)/shard_map/ppermute | solution.py:50
  93.5 8.2 %collective-permute-start.31 = (bf16[64,2048]{1,0:T(8,128)(2,1)S(1)}, bf16[64,2048]{1,0:T(8,128)(2,1)S(1)}, u32[]{:S(2)}, u32[]{:S(2)}) collective-permute-start(bf16[64,2048]{1,0:T(8,128)(2,1)S(1)} %slice.75), channel_id=1, source_target_pairs={{0,96},{32,0},{64,32},{96,64},{128,224},{160,128},{192,160},{224,1... | collective-permute-start | bytes 786440 | tf_op jit(solution)/shard_map/ppermute | solution.py:50
  93.8 9.0 %collective-permute-start.30 = (bf16[64,2048]{1,0:T(8,128)(2,1)S(1)}, bf16[64,2048]{1,0:T(8,128)(2,1)S(1)}, u32[]{:S(2)}, u32[]{:S(2)}) collective-permute-start(bf16[64,2048]{1,0:T(8,128)(2,1)S(1)} %slice.74), channel_id=1, source_target_pairs={{0,32},{32,64},{64,96},{96,0},{128,160},{160,192},{192,224},{224,1... | collective-permute-start | bytes 786440 | tf_op jit(solution)/shard_map/ppermute | solution.py:50
  99.3 4.6 %collective-permute-start.27 = (bf16[256,256]{1,0:T(8,128)(2,1)S(1)}, bf16[256,256]{1,0:T(8,128)(2,1)S(1)}, u32[]{:S(2)}, u32[]{:S(2)}) collective-permute-start(bf16[256,256]{1,0:T(8,128)(2,1)S(1)} %get-tuple-element.65), channel_id=1, source_target_pairs={{0,16},{1,17},{2,18},{3,19},{4,20},{5,21},{6,22},{7,23},{8,24},{9,... | collective-permute-start | bytes 393224 | tf_op jit(solution)/shard_map/ppermute | solution.py:50
  105.1 3.0 %collective-permute-start.32 = (bf16[128,2048]{1,0:T(8,128)(2,1)S(1)}, bf16[128,2048]{1,0:T(8,128)(2,1)S(1)}, u32[]{:S(2)}, u32[]{:S(2)}) collective-permute-start(bf16[128,2048]{1,0:T(8,128)(2,1)S(1)} %get-tuple-element.62), channel_id=1, source_target_pairs={{0,1},{1,0},{2,3},{3,2},{4,5},{5,4},{6,7},{7,6},{8,9},{9,8},{10,11... | collective-permute-start | bytes 1572872 | tf_op jit(solution)/shard_map/ppermute | solution.py:50
  (4 other events, 32.5 us)

commit v10 on v7

--- a/solution.py
+++ b/solution.py
@@ -92,7 +92,7 @@
 
 def project_kernel(index, *refs):
     blocks, firsts, seconds = refs[:4], refs[4 : 4 + SHARDS], refs[4 + SHARDS : 4 + 2 * SHARDS]
-    keep_ref, send_ref, g_rows, far_table, out_rows, *edges, rows, table, sems = refs[4 + 2 * SHARDS :]
+    keep_ref, send_ref, g_rows, far_table, *edges, rows, table, sems = refs[4 + 2 * SHARDS :]
     z, core, x = index[0], index[1], index[2]
     low_core = core == 0
     copies = []
@@ -110,7 +110,6 @@
             there = pl.multiple_of(base + at + 16, 16)
             into[pl.ds(there, 16), :] = seconds[j][kind * 16 : kind * 16 + 16, :]
         g_rows[j * 16 : j * 16 + 16, :] = seconds[j][48:64, :]
-        out_rows[j * 16 : j * 16 + 16, :] = seconds[j][64:80, :]
     for copy in copies:
         copy.wait()
     for kind in range(3):
@@ -127,6 +126,11 @@
                     into = slice(seg * TOK, seg * TOK + TOK)
                     edges[2 * part][into, lanes_out] = keep_ref[at, lanes]
                     edges[2 * part + 1][into, lanes_out] = send_ref[at, lanes]
+
+
+def collect_kernel(*refs):
+    for j, ref in enumerate(refs[1 : 1 + SHARDS]):
+        refs[1 + SHARDS][j * 16 : j * 16 + 16, :] = ref[64:80, :]
 
 
 def far_kernel(index, own_ref, other_ref, table, keep_ref, send_ref):
@@ -334,20 +338,19 @@
     firsts = [one[s] for s in STEPS]
     seconds = [two[s] for s in STEPS]
 
-    to_send = after(normed, one[0, 1])
+    to_send = after(normed, one[0, 2])
     across = send(to_send, OTHER_X)
     beside = send(to_send, OTHER_CORE)
     beside_across = send(across, OTHER_CORE)
 
     half = jax.ShapeDtypeStruct((ROWS, 3 * 128), bf16)
-    keep, to_swap, g_own, far_table, out_own, *edges = on_chip(
+    keep, to_swap, g_own, far_table, *edges = on_chip(
         project_kernel,
         (
             half,
             half,
             jax.ShapeDtypeStruct((G_ROWS, width), bf16),
             jax.ShapeDtypeStruct((2 * Z * HALF, width), bf16),
-            jax.ShapeDtypeStruct((128, width), bf16),
             *[jax.ShapeDtypeStruct((2 * TOK, 256), bf16)] * 4,
         ),
         2 * ROWS * 768 * width,
@@ -367,7 +370,7 @@
     )
     g_got = send(g_swap, OTHER_CORE)
 
-    to_pass = out_own
+    to_pass = out_own = on_chip(collect_kernel, jax.ShapeDtypeStruct((128, width), bf16), 0, 0, (index, *seconds))
     out_prev = send(to_pass, Y_UP, "doc")
     out_next = send(to_pass, Y_DOWN, "doc")
     out_far_a = send(out_prev[:64], Y_UP, "doc")

time: 104 us -> 108 us (1.038)
  waiting for transfers between devices: 45.5 us -> 56.4 us
  starting transfers between devices: 42.4 us -> 34.6 us
    ppermute x33, waiting for transfers between devices: 45.5 us -> 56.4 us  [send(): return lax.ppermute(value, axis, route)]
    ppermute x33, starting transfers between devices: 42.4 us -> 34.6 us  [send(): return lax.ppermute(value, axis, route)]
    pallas_call x5 -> x6, Pallas kernels: 11.5 us -> 12 us  [on_chip(): pl.pallas_call(kernel, out_shape=out_shape, in_specs=specs, out_specs=jax...]
  transfers between devices with their start and end apart: 33 -> 33, of which waited for: 15 -> 12; matrix products, arithmetic and copies ran while one was open for 0% -> 0% of each run, Pallas kernels for 7% -> 7%
where the time goes in v10:
time: 108 us
  waiting for transfers between devices  56.4 us (52%)
  starting transfers between devices  34.6 us (32%)
  Pallas kernels  12 us (11%)
  other arithmetic  2.31 us (2%)
  local copies, waits for them, and re-layouts  1.28 us (1%)
    ppermute x33, waiting for transfers between devices, send(): return lax.ppermute(value, axis, route)  56.4 us
    ppermute x33, starting transfers between devices, send(): return lax.ppermute(value, axis, route)  34.6 us
    pallas_call x6, Pallas kernels, on_chip(): pl.pallas_call(kernel, out_shape=out_shape, in_specs=specs, out_specs=jax...  12 us
  transfers between devices with their start and end apart: 33, of which 12 were waited for; matrix products, arithmetic and copies ran while one was open for 0% of the time, Pallas kernels for 7%

profile of v10, /device:TPU:1, one launch (start us, length us, event | category | flops | bytes accessed | tf_op | source)
XLA Modules:
  0.0 107.5 jit_solution(1055541417015669576)
XLA Ops:
  0.0 1.1 %pad_maximum_fusion = bf16[3,2,16,2048]{3,2,0,1:T(8,128)(2,1)S(1)} fusion(bf16[1,2,16,2048]{3,2,0,1:T(8,128)(2,1)} %bitcast.40, bf16[1,2,16,2048]{3,2,0,1:T(8,128)(2,1)} %bitcast.41, bf16[1,2,16,2048]{3,2,0,1:T(8,128)(2,1)} %bitcast.42), kind=kLoop, calls=%fused_computation.1 | loop fusion | flops 393216 | bytes 786432 | tf_op jit(solution)/shard_map/stack | solution.py:278
  2.3 3.3 %collective-permute-start.8 = (bf16[128,64]{1,0:T(8,128)(2,1)S(1)}, bf16[128,64]{1,0:T(8,128)(2,1)S(1)}, u32[]{:S(2)}, u32[]{:S(2)}) collective-permute-start(bf16[128,64]{1,0:T(8,128)(2,1)S(1)} %bitcast.43), channel_id=1, source_target_pairs={{0,1},{1,0},{2,3},{3,2},{4,5},{5,4},{6,7},{7,6},{8,9},{9,8},{10,11... | collective-permute-start | bytes 49160 | tf_op jit(solution)/shard_map/ppermute | solution.py:50
  5.6 3.9 %collective-permute-start = (bf16[48,2048]{1,0:T(8,128)(2,1)S(1)}, bf16[48,2048]{1,0:T(8,128)(2,1)S(1)}, u32[]{:S(2)}, u32[]{:S(2)}) collective-permute-start(bf16[48,2048]{1,0:T(8,128)(2,1)S(1)} %bitcast.33), channel_id=1, source_target_pairs={{0,2},{1,15},{2,4},{3,1},{4,6},{5,3},{6,8},{7,5},{8,10},{9,7},{10,... | collective-permute-start | bytes 589832 | tf_op jit(solution)/shard_map/ppermute | solution.py:50
  10.2 1.3 %shard_map.82 = (bf16[128,2048]{1,0:T(8,128)(2,1)S(1)}, bf16[8,2048]{1,0:T(8,128)(2,1)S(1)}) custom-call(s32[6]{0:T(128)S(1)} %stack.35.index.refs_0_, bf16[128,2048]{1,0:T(8,128)(2,1)S(1)} %copy-done, f32[1,2048]{1,0:T(1,128)S(1)} %bitcast.36, f32[1,2048]{1,0:T(1,128)S(1)} %bitcast.37), custom_call_target="tpu_custom_call" | custom-call | flops 2097152 | bytes 4194304 | tf_op jit(solution)/shard_map/pallas_call | solution.py:252
  11.5 1.3 %collective-permute-start.7 = (bf16[8,2048]{1,0:T(8,128)(2,1)S(1)}, bf16[8,2048]{1,0:T(8,128)(2,1)S(1)}, u32[]{:S(2)}, u32[]{:S(2)}) collective-permute-start(bf16[8,2048]{1,0:T(8,128)(2,1)S(1)} %get-tuple-element.34), channel_id=1, source_target_pairs={{0,16},{1,17},{2,18},{3,19},{4,20},{5,21},{6,22},{7,23},{8,24},{9,... | collective-permute-start | bytes 98312 | tf_op jit(solution)/shard_map/ppermute | solution.py:50
  14.4 1.4 %collective-permute-done.9 = bf16[128,128]{1,0:T(8,128)(2,1)S(1)} collective-permute-done((bf16[128,128]{1,0:T(8,128)(2,1)S(1)}, bf16[128,128]{1,0:T(8,128)(2,1)S(1)}, u32[]{:S(2)}, u32[]{:S(2)}) %collective-permute-start.9) | collective-permute-done | bytes 32800 | tf_op jit(solution)/shard_map/ppermute | solution.py:50
  16.0 3.2 %collective-permute-start.10 = (bf16[80,2048]{1,0:T(8,128)(2,1)S(1)}, bf16[80,2048]{1,0:T(8,128)(2,1)S(1)}, u32[]{:S(2)}, u32[]{:S(2)}) collective-permute-start(bf16[80,2048]{1,0:T(8,128)(2,1)S(1)} %pad_maximum_fusion.1.refs_12_.refs_1_), channel_id=1, source_target_pairs={{0,2},{1,15},{2,4},{3,1},{4,6},{5,3},{6,8},{7,5},{8,10},{9,7},{10,... | collective-permute-start | bytes 983048 | tf_op jit(solution)/shard_map/ppermute | solution.py:50
  19.2 2.7 %collective-permute-start.1 = (bf16[48,2048]{1,0:T(8,128)(2,1)S(1)}, bf16[48,2048]{1,0:T(8,128)(2,1)S(1)}, u32[]{:S(2)}, u32[]{:S(2)}) collective-permute-start(bf16[48,2048]{1,0:T(8,128)(2,1)S(1)} %collective-permute-done.refs_5_), channel_id=1, source_target_pairs={{0,2},{1,15},{2,4},{3,1},{4,6},{5,3},{6,8},{7,5},{8,10},{9,7},{10,... | collective-permute-start | bytes 589832 | tf_op jit(solution)/shard_map/ppermute | solution.py:50
  21.9 6.8 %collective-permute-done.1.refs_7_ = bf16[48,2048]{1,0:T(8,128)(2,1)S(1)} collective-permute-done((bf16[48,2048]{1,0:T(8,128)(2,1)S(1)}, bf16[48,2048]{1,0:T(8,128)(2,1)S(1)}, u32[]{:S(2)}, u32[]{:S(2)}) %collective-permute-start.1) | collective-permute-done | bytes 196640 | tf_op jit(solution)/shard_map/ppermute | solution.py:50
  30.1 2.5 %collective-permute-start.14 = (bf16[80,2048]{1,0:T(8,128)(2,1)S(1)}, bf16[80,2048]{1,0:T(8,128)(2,1)S(1)}, u32[]{:S(2)}, u32[]{:S(2)}) collective-permute-start(bf16[80,2048]{1,0:T(8,128)(2,1)S(1)} %collective-permute-done.10.refs_13_.refs_2_), channel_id=1, source_target_pairs={{0,2},{1,15},{2,4},{3,1},{4,6},{5,3},{6,8},{7,5},{8,10},{9,7},{10,... | collective-permute-start | bytes 983048 | tf_op jit(solution)/shard_map/ppermute | solution.py:50
  32.7 12.7 %collective-permute-done.6.refs_8_ = bf16[48,2048]{1,0:T(8,128)(2,1)S(1)} collective-permute-done((bf16[48,2048]{1,0:T(8,128)(2,1)S(1)}, bf16[48,2048]{1,0:T(8,128)(2,1)S(1)}, u32[]{:S(2)}, u32[]{:S(2)}) %collective-permute-start.6) | collective-permute-done | bytes 196640 | tf_op jit(solution)/shard_map/ppermute | solution.py:50
  45.5 1.5 %collective-permute-start.13 = (bf16[48,2048]{1,0:T(8,128)(2,1)S(1)}, bf16[48,2048]{1,0:T(8,128)(2,1)S(1)}, u32[]{:S(2)}, u32[]{:S(2)}) collective-permute-start(bf16[48,2048]{1,0:T(8,128)(2,1)S(1)} %collective-permute-done.6.refs_8_), channel_id=1, source_target_pairs={{0,14},{1,3},{2,0},{3,5},{4,2},{5,7},{6,4},{7,9},{8,6},{9,11},{10,... | collective-permute-start | bytes 589832 | tf_op jit(solution)/shard_map/ppermute | solution.py:50
  47.5 8.1 %collective-permute-done.12.refs_9_ = bf16[48,2048]{1,0:T(8,128)(2,1)S(1)} collective-permute-done((bf16[48,2048]{1,0:T(8,128)(2,1)S(1)}, bf16[48,2048]{1,0:T(8,128)(2,1)S(1)}, u32[]{:S(2)}, u32[]{:S(2)}) %collective-permute-start.12) | collective-permute-done | bytes 196640 | tf_op jit(solution)/shard_map/ppermute | solution.py:50
  55.7 2.7 %collective-permute-start.19 = (bf16[80,2048]{1,0:T(8,128)(2,1)S(1)}, bf16[80,2048]{1,0:T(8,128)(2,1)S(1)}, u32[]{:S(2)}, u32[]{:S(2)}) collective-permute-start(bf16[80,2048]{1,0:T(8,128)(2,1)S(1)} %collective-permute-done.17.refs_17_.refs_6_), channel_id=1, source_target_pairs={{0,2},{1,15},{2,4},{3,1},{4,6},{5,3},{6,8},{7,5},{8,10},{9,7},{10,... | collective-permute-start | bytes 983048 | tf_op jit(solution)/shard_map/ppermute | solution.py:50
  58.4 9.2 %collective-permute-done.16.refs_11_ = bf16[48,2048]{1,0:T(8,128)(2,1)S(1)} collective-permute-done((bf16[48,2048]{1,0:T(8,128)(2,1)S(1)}, bf16[48,2048]{1,0:T(8,128)(2,1)S(1)}, u32[]{:S(2)}, u32[]{:S(2)}) %collective-permute-start.16) | collective-permute-done | bytes 196640 | tf_op jit(solution)/shard_map/ppermute | solution.py:50
  67.6 2.9 %shard_map.83 = (bf16[512,384]{1,0:T(8,128)(2,1)S(1)}, bf16[512,384]{1,0:T(8,128)(2,1)S(1)}, bf16[128,2048]{1,0:T(8,128)(2,1)S(1)}, bf16[512,2048]{1,0:T(8,128)(...) custom-call(s32[6]{0:T(128)S(1)} %stack.35.index.refs_0_, ...), custom_call_target="tpu_custom_call" | custom-call | flops 1610612736 | bytes 4194304 | tf_op jit(solution)/shard_map/pallas_call | solution.py:252
  70.5 1.6 %collective-permute-start.21 = (bf16[128,2048]{1,0:T(8,128)(2,1)S(1)}, bf16[128,2048]{1,0:T(8,128)(2,1)S(1)}, u32[]{:S(2)}, u32[]{:S(2)}) collective-permute-start(bf16[128,2048]{1,0:T(8,128)(2,1)S(1)} %get-tuple-element.47.own_ref), channel_id=1, source_target_pairs={{0,1},{1,0},{2,3},{3,2},{4,5},{5,4},{6,7},{7,6},{8,9},{9,8},{10,11... | collective-permute-start | bytes 1572872 | tf_op jit(solution)/shard_map/ppermute | solution.py:50
  72.7 1.4 %collective-permute-start.28 = (bf16[128,2048]{1,0:T(8,128)(2,1)S(1)}, bf16[128,2048]{1,0:T(8,128)(2,1)S(1)}, u32[]{:S(2)}, u32[]{:S(2)}) collective-permute-start(bf16[128,2048]{1,0:T(8,128)(2,1)S(1)} %shard_map.86.mine), channel_id=1, source_target_pairs={{0,32},{32,64},{64,96},{96,0},{128,160},{160,192},{192,224},{224,1... | collective-permute-start | bytes 1572872 | tf_op jit(solution)/shard_map/ppermute | solution.py:50
  74.1 1.5 %collective-permute-start.29 = (bf16[128,2048]{1,0:T(8,128)(2,1)S(1)}, bf16[128,2048]{1,0:T(8,128)(2,1)S(1)}, u32[]{:S(2)}, u32[]{:S(2)}) collective-permute-start(bf16[128,2048]{1,0:T(8,128)(2,1)S(1)} %shard_map.86.mine), channel_id=1, source_target_pairs={{0,96},{32,0},{64,32},{96,64},{128,224},{160,128},{192,160},{224,1... | collective-permute-start | bytes 1572872 | tf_op jit(solution)/shard_map/ppermute | solution.py:50
  76.1 2.1 %shard_map.84 = (bf16[256,256]{1,0:T(8,128)(2,1)S(1)}, bf16[256,256]{1,0:T(8,128)(2,1)S(1)}) custom-call(s32[6]{0:T(128)S(1)} %stack.35.index.refs_0_, bf16[128,2048]{1,0:T(8,128)(2,1)S(1)} %get-tuple-element.47.own_ref, bf16[128,2048]{1,0:T(8,128)(2,1)S(1)} %collective-permute-done.21.other_ref, bf16[512,2048]{1,0:T(8,128)(2,1)S(1)} %get-tuple-element.48.table), custom_call_target="tpu_custom_call" | custom-call | flops 536870912 | bytes 4194304 | tf_op jit(solution)/shard_map/pallas_call | solution.py:252
  78.1 4.2 %collective-permute-done.23.below_ref = bf16[256,256]{1,0:T(8,128)(2,1)S(1)} collective-permute-done((bf16[256,256]{1,0:T(8,128)(2,1)S(1)}, bf16[256,256]{1,0:T(8,128)(2,1)S(1)}, u32[]{:S(2)}, u32[]{:S(2)}) %collective-permute-start.23) | collective-permute-done | bytes 131104 | tf_op jit(solution)/shard_map/ppermute | solution.py:50
  82.4 5.3 %collective-permute-done.28.prev = bf16[128,2048]{1,0:T(8,128)(2,1)S(1)} collective-permute-done((bf16[128,2048]{1,0:T(8,128)(2,1)S(1)}, bf16[128,2048]{1,0:T(8,128)(2,1)S(1)}, u32[]{:S(2)}, u32[]{:S(2)}) %collective-permute-start.28) | collective-permute-done | bytes 524320 | tf_op jit(solution)/shard_map/ppermute | solution.py:50
  87.6 1.2 %collective-permute-start.26 = (bf16[256,256]{1,0:T(8,128)(2,1)S(1)}, bf16[256,256]{1,0:T(8,128)(2,1)S(1)}, u32[]{:S(2)}, u32[]{:S(2)}) collective-permute-start(bf16[256,256]{1,0:T(8,128)(2,1)S(1)} %get-tuple-element.54), channel_id=1, source_target_pairs={{0,15},{1,14},{2,1},{3,0},{4,3},{5,2},{6,5},{7,4},{8,7},{9,6},{10,... | collective-permute-start | bytes 393224 | tf_op jit(solution)/shard_map/ppermute | solution.py:50
  88.9 1.1 %collective-permute-start.30 = (bf16[64,2048]{1,0:T(8,128)(2,1)S(1)}, bf16[64,2048]{1,0:T(8,128)(2,1)S(1)}, u32[]{:S(2)}, u32[]{:S(2)}) collective-permute-start(bf16[64,2048]{1,0:T(8,128)(2,1)S(1)} %slice.74), channel_id=1, source_target_pairs={{0,32},{32,64},{64,96},{96,0},{128,160},{160,192},{192,224},{224,1... | collective-permute-start | bytes 786440 | tf_op jit(solution)/shard_map/ppermute | solution.py:50
  90.1 1.8 %collective-permute-start.31 = (bf16[64,2048]{1,0:T(8,128)(2,1)S(1)}, bf16[64,2048]{1,0:T(8,128)(2,1)S(1)}, u32[]{:S(2)}, u32[]{:S(2)}) collective-permute-start(bf16[64,2048]{1,0:T(8,128)(2,1)S(1)} %slice.75), channel_id=1, source_target_pairs={{0,96},{32,0},{64,32},{96,64},{128,224},{160,128},{192,160},{224,1... | collective-permute-start | bytes 786440 | tf_op jit(solution)/shard_map/ppermute | solution.py:50
  91.9 1.8 %collective-permute-done.26.above_got = bf16[256,256]{1,0:T(8,128)(2,1)S(1)} collective-permute-done((bf16[256,256]{1,0:T(8,128)(2,1)S(1)}, bf16[256,256]{1,0:T(8,128)(2,1)S(1)}, u32[]{:S(2)}, u32[]{:S(2)}) %collective-permute-start.26) | collective-permute-done | bytes 131104 | tf_op jit(solution)/shard_map/ppermute | solution.py:50
  93.7 4.0 %shard_map.85 = bf16[2,256,256]{2,1,0:T(8,128)(2,1)S(1)} custom-call(s32[6]{0:T(128)S(1)} %stack.35.index.refs_0_, bf16[512,384]{1,0:T(8,128)(2,1)S(1)} %get-tuple-element.45.keep_ref, bf16[512,384]{1,0:T(8,128)(2,1)S(1)} %collective-permute-done.20.got_ref, bf16[256,256]{1,0:T(8,128)(2,1)S(1)} %get-tuple-element.49.g_keep, ...), custom_call_target="tpu_custom_call" | custom-call | flops 1342177280 | bytes 4194304 | tf_op jit(solution)/shard_map/pallas_call | solution.py:252
  97.7 1.3 %collective-permute-start.27 = (bf16[256,256]{1,0:T(8,128)(2,1)S(1)}, bf16[256,256]{1,0:T(8,128)(2,1)S(1)}, u32[]{:S(2)}, u32[]{:S(2)}) collective-permute-start(bf16[256,256]{1,0:T(8,128)(2,1)S(1)} %get-tuple-element.59), channel_id=1, source_target_pairs={{0,16},{1,17},{2,18},{3,19},{4,20},{5,21},{6,22},{7,23},{8,24},{9,... | collective-permute-start | bytes 393224 | tf_op jit(solution)/shard_map/ppermute | solution.py:50
  99.0 3.4 %collective-permute-done.27.there_ref = bf16[256,256]{1,0:T(8,128)(2,1)S(1)} collective-permute-done((bf16[256,256]{1,0:T(8,128)(2,1)S(1)}, bf16[256,256]{1,0:T(8,128)(2,1)S(1)}, u32[]{:S(2)}, u32[]{:S(2)}) %collective-permute-start.27) | collective-permute-done | bytes 131104 | tf_op jit(solution)/shard_map/ppermute | solution.py:50
  102.4 1.3 %shard_map.87 = (f32[128,2048]{1,0:T(8,128)S(1)}, bf16[128,2048]{1,0:T(8,128)(2,1)S(1)}) custom-call(s32[6]{0:T(128)S(1)} %stack.35.index.refs_0_, bf16[256,256]{1,0:T(8,128)(2,1)S(1)} %get-tuple-element.60.own_ref, bf16[256,256]{1,0:T(8,128)(2,1)S(1)} %collective-permute-done.27.there_ref, bf16[128,2048]{1,0:T(8,128)(2,1)S(1)} %shard_map.86.mine, ...), custom_call_target="tpu_custom_call" | custom-call | flops 536870912 | bytes 4194304 | tf_op jit(solution)/shard_map/pallas_call | solution.py:252
  103.7 1.4 %collective-permute-start.32 = (bf16[128,2048]{1,0:T(8,128)(2,1)S(1)}, bf16[128,2048]{1,0:T(8,128)(2,1)S(1)}, u32[]{:S(2)}, u32[]{:S(2)}) collective-permute-start(bf16[128,2048]{1,0:T(8,128)(2,1)S(1)} %get-tuple-element.56), channel_id=1, source_target_pairs={{0,1},{1,0},{2,3},{3,2},{4,5},{5,4},{6,7},{7,6},{8,9},{9,8},{10,11... | collective-permute-start | bytes 1572872 | tf_op jit(solution)/shard_map/ppermute | solution.py:50
  105.1 1.5 %collective-permute-done.32 = bf16[128,2048]{1,0:T(8,128)(2,1)S(1)} collective-permute-done((bf16[128,2048]{1,0:T(8,128)(2,1)S(1)}, bf16[128,2048]{1,0:T(8,128)(2,1)S(1)}, u32[]{:S(2)}, u32[]{:S(2)}) %collective-permute-start.32) | collective-permute-done | bytes 524320 | tf_op jit(solution)/shard_map/ppermute | solution.py:50
  (68 shorter events, 7.1 us)
Async XLA Ops:
  2.3 10.5 %collective-permute-start.8 = (bf16[128,64]{1,0:T(8,128)(2,1)S(1)}, bf16[128,64]{1,0:T(8,128)(2,1)S(1)}, u32[]{:S(2)}, u32[]{:S(2)}) collective-permute-start(bf16[128,64]{1,0:T(8,128)(2,1)S(1)} %bitcast.43), channel_id=1, source_target_pairs={{0,1},{1,0},{2,3},{3,2},{4,5},{5,4},{6,7},{7,6},{8,9},{9,8},{10,11... | collective-permute-start | bytes 49160 | tf_op jit(solution)/shard_map/ppermute | solution.py:50
  5.6 10.4 %collective-permute-start = (bf16[48,2048]{1,0:T(8,128)(2,1)S(1)}, bf16[48,2048]{1,0:T(8,128)(2,1)S(1)}, u32[]{:S(2)}, u32[]{:S(2)}) collective-permute-start(bf16[48,2048]{1,0:T(8,128)(2,1)S(1)} %bitcast.33), channel_id=1, source_target_pairs={{0,2},{1,15},{2,4},{3,1},{4,6},{5,3},{6,8},{7,5},{8,10},{9,7},{10,... | collective-permute-start | bytes 589832 | tf_op jit(solution)/shard_map/ppermute | solution.py:50
  9.5 6.5 %collective-permute-start.5 = (bf16[48,2048]{1,0:T(8,128)(2,1)S(1)}, bf16[48,2048]{1,0:T(8,128)(2,1)S(1)}, u32[]{:S(2)}, u32[]{:S(2)}) collective-permute-start(bf16[48,2048]{1,0:T(8,128)(2,1)S(1)} %bitcast.34), channel_id=1, source_target_pairs={{0,14},{1,3},{2,0},{3,5},{4,2},{5,7},{6,4},{7,9},{8,6},{9,11},{10,... | collective-permute-start | bytes 589832 | tf_op jit(solution)/shard_map/ppermute | solution.py:50
  11.5 2.9 %collective-permute-start.7 = (bf16[8,2048]{1,0:T(8,128)(2,1)S(1)}, bf16[8,2048]{1,0:T(8,128)(2,1)S(1)}, u32[]{:S(2)}, u32[]{:S(2)}) collective-permute-start(bf16[8,2048]{1,0:T(8,128)(2,1)S(1)} %get-tuple-element.34), channel_id=1, source_target_pairs={{0,16},{1,17},{2,18},{3,19},{4,20},{5,21},{6,22},{7,23},{8,24},{9,... | collective-permute-start | bytes 98312 | tf_op jit(solution)/shard_map/ppermute | solution.py:50
  16.0 13.4 %collective-permute-start.10 = (bf16[80,2048]{1,0:T(8,128)(2,1)S(1)}, bf16[80,2048]{1,0:T(8,128)(2,1)S(1)}, u32[]{:S(2)}, u32[]{:S(2)}) collective-permute-start(bf16[80,2048]{1,0:T(8,128)(2,1)S(1)} %pad_maximum_fusion.1.refs_12_.refs_1_), channel_id=1, source_target_pairs={{0,2},{1,15},{2,4},{3,1},{4,6},{5,3},{6,8},{7,5},{8,10},{9,7},{10,... | collective-permute-start | bytes 983048 | tf_op jit(solution)/shard_map/ppermute | solution.py:50
  19.2 10.9 %collective-permute-start.11 = (bf16[80,2048]{1,0:T(8,128)(2,1)S(1)}, bf16[80,2048]{1,0:T(8,128)(2,1)S(1)}, u32[]{:S(2)}, u32[]{:S(2)}) collective-permute-start(bf16[80,2048]{1,0:T(8,128)(2,1)S(1)} %pad_maximum_fusion.1.refs_12_.refs_1_), channel_id=1, source_target_pairs={{0,14},{1,3},{2,0},{3,5},{4,2},{5,7},{6,4},{7,9},{8,6},{9,11},{10,... | collective-permute-start | bytes 983048 | tf_op jit(solution)/shard_map/ppermute | solution.py:50
  19.2 9.5 %collective-permute-start.1 = (bf16[48,2048]{1,0:T(8,128)(2,1)S(1)}, bf16[48,2048]{1,0:T(8,128)(2,1)S(1)}, u32[]{:S(2)}, u32[]{:S(2)}) collective-permute-start(bf16[48,2048]{1,0:T(8,128)(2,1)S(1)} %collective-permute-done.refs_5_), channel_id=1, source_target_pairs={{0,2},{1,15},{2,4},{3,1},{4,6},{5,3},{6,8},{7,5},{8,10},{9,7},{10,... | collective-permute-start | bytes 589832 | tf_op jit(solution)/shard_map/ppermute | solution.py:50
  28.7 18.8 %collective-permute-start.2 = (bf16[128,2048]{1,0:T(8,128)(2,1)S(1)}, bf16[128,2048]{1,0:T(8,128)(2,1)S(1)}, u32[]{:S(2)}, u32[]{:S(2)}) collective-permute-start(bf16[128,2048]{1,0:T(8,128)(2,1)S(1)} %get-tuple-element.33.refs_0_), channel_id=1, source_target_pairs={{0,16},{1,17},{2,18},{3,19},{4,20},{5,21},{6,22},{7,23},{8,24},{9,... | collective-permute-start | bytes 1572872 | tf_op jit(solution)/shard_map/ppermute | solution.py:50
  30.1 15.3 %collective-permute-start.14 = (bf16[80,2048]{1,0:T(8,128)(2,1)S(1)}, bf16[80,2048]{1,0:T(8,128)(2,1)S(1)}, u32[]{:S(2)}, u32[]{:S(2)}) collective-permute-start(bf16[80,2048]{1,0:T(8,128)(2,1)S(1)} %collective-permute-done.10.refs_13_.refs_2_), channel_id=1, source_target_pairs={{0,2},{1,15},{2,4},{3,1},{4,6},{5,3},{6,8},{7,5},{8,10},{9,7},{10,... | collective-permute-start | bytes 983048 | tf_op jit(solution)/shard_map/ppermute | solution.py:50
  32.7 12.8 %collective-permute-start.15 = (bf16[80,2048]{1,0:T(8,128)(2,1)S(1)}, bf16[80,2048]{1,0:T(8,128)(2,1)S(1)}, u32[]{:S(2)}, u32[]{:S(2)}) collective-permute-start(bf16[80,2048]{1,0:T(8,128)(2,1)S(1)} %collective-permute-done.11.refs_14_.refs_3_), channel_id=1, source_target_pairs={{0,14},{1,3},{2,0},{3,5},{4,2},{5,7},{6,4},{7,9},{8,6},{9,11},{10,... | collective-permute-start | bytes 983048 | tf_op jit(solution)/shard_map/ppermute | solution.py:50
  32.7 12.8 %collective-permute-start.6 = (bf16[48,2048]{1,0:T(8,128)(2,1)S(1)}, bf16[48,2048]{1,0:T(8,128)(2,1)S(1)}, u32[]{:S(2)}, u32[]{:S(2)}) collective-permute-start(bf16[48,2048]{1,0:T(8,128)(2,1)S(1)} %collective-permute-done.5.refs_6_), channel_id=1, source_target_pairs={{0,14},{1,3},{2,0},{3,5},{4,2},{5,7},{6,4},{7,9},{8,6},{9,11},{10,... | collective-permute-start | bytes 589832 | tf_op jit(solution)/shard_map/ppermute | solution.py:50
  45.4 10.2 %collective-permute-start.17 = (bf16[80,2048]{1,0:T(8,128)(2,1)S(1)}, bf16[80,2048]{1,0:T(8,128)(2,1)S(1)}, u32[]{:S(2)}, u32[]{:S(2)}) collective-permute-start(bf16[80,2048]{1,0:T(8,128)(2,1)S(1)} %collective-permute-done.14.refs_15_.refs_4_), channel_id=1, source_target_pairs={{0,2},{1,15},{2,4},{3,1},{4,6},{5,3},{6,8},{7,5},{8,10},{9,7},{10,... | collective-permute-start | bytes 983048 | tf_op jit(solution)/shard_map/ppermute | solution.py:50
  45.4 10.2 %collective-permute-start.12 = (bf16[48,2048]{1,0:T(8,128)(2,1)S(1)}, bf16[48,2048]{1,0:T(8,128)(2,1)S(1)}, u32[]{:S(2)}, u32[]{:S(2)}) collective-permute-start(bf16[48,2048]{1,0:T(8,128)(2,1)S(1)} %collective-permute-done.1.refs_7_), channel_id=1, source_target_pairs={{0,2},{1,15},{2,4},{3,1},{4,6},{5,3},{6,8},{7,5},{8,10},{9,7},{10,... | collective-permute-start | bytes 589832 | tf_op jit(solution)/shard_map/ppermute | solution.py:50
  45.5 10.1 %collective-permute-start.13 = (bf16[48,2048]{1,0:T(8,128)(2,1)S(1)}, bf16[48,2048]{1,0:T(8,128)(2,1)S(1)}, u32[]{:S(2)}, u32[]{:S(2)}) collective-permute-start(bf16[48,2048]{1,0:T(8,128)(2,1)S(1)} %collective-permute-done.6.refs_8_), channel_id=1, source_target_pairs={{0,14},{1,3},{2,0},{3,5},{4,2},{5,7},{6,4},{7,9},{8,6},{9,11},{10,... | collective-permute-start | bytes 589832 | tf_op jit(solution)/shard_map/ppermute | solution.py:50
  47.0 11.4 %collective-permute-start.3 = (bf16[128,2048]{1,0:T(8,128)(2,1)S(1)}, bf16[128,2048]{1,0:T(8,128)(2,1)S(1)}, u32[]{:S(2)}, u32[]{:S(2)}) collective-permute-start(bf16[128,2048]{1,0:T(8,128)(2,1)S(1)} %get-tuple-element.33.refs_0_), channel_id=1, source_target_pairs={{0,1},{1,0},{2,3},{3,2},{4,5},{5,4},{6,7},{7,6},{8,9},{9,8},{10,11... | collective-permute-start | bytes 1572872 | tf_op jit(solution)/shard_map/ppermute | solution.py:50
  47.5 20.1 %collective-permute-start.4 = (bf16[128,2048]{1,0:T(8,128)(2,1)S(1)}, bf16[128,2048]{1,0:T(8,128)(2,1)S(1)}, u32[]{:S(2)}, u32[]{:S(2)}) collective-permute-start(bf16[128,2048]{1,0:T(8,128)(2,1)S(1)} %collective-permute-done.2.refs_1_), channel_id=1, source_target_pairs={{0,1},{1,0},{2,3},{3,2},{4,5},{5,4},{6,7},{7,6},{8,9},{9,8},{10,11... | collective-permute-start | bytes 1572872 | tf_op jit(solution)/shard_map/ppermute | solution.py:50
  55.6 11.9 %collective-permute-start.18 = (bf16[80,2048]{1,0:T(8,128)(2,1)S(1)}, bf16[80,2048]{1,0:T(8,128)(2,1)S(1)}, u32[]{:S(2)}, u32[]{:S(2)}) collective-permute-start(bf16[80,2048]{1,0:T(8,128)(2,1)S(1)} %collective-permute-done.15.refs_16_.refs_5_), channel_id=1, source_target_pairs={{0,14},{1,3},{2,0},{3,5},{4,2},{5,7},{6,4},{7,9},{8,6},{9,11},{10,... | collective-permute-start | bytes 983048 | tf_op jit(solution)/shard_map/ppermute | solution.py:50
  55.7 11.9 %collective-permute-start.19 = (bf16[80,2048]{1,0:T(8,128)(2,1)S(1)}, bf16[80,2048]{1,0:T(8,128)(2,1)S(1)}, u32[]{:S(2)}, u32[]{:S(2)}) collective-permute-start(bf16[80,2048]{1,0:T(8,128)(2,1)S(1)} %collective-permute-done.17.refs_17_.refs_6_), channel_id=1, source_target_pairs={{0,2},{1,15},{2,4},{3,1},{4,6},{5,3},{6,8},{7,5},{8,10},{9,7},{10,... | collective-permute-start | bytes 983048 | tf_op jit(solution)/shard_map/ppermute | solution.py:50
  58.3 9.2 %collective-permute-start.16 = (bf16[48,2048]{1,0:T(8,128)(2,1)S(1)}, bf16[48,2048]{1,0:T(8,128)(2,1)S(1)}, u32[]{:S(2)}, u32[]{:S(2)}) collective-permute-start(bf16[48,2048]{1,0:T(8,128)(2,1)S(1)} %collective-permute-done.12.refs_9_), channel_id=1, source_target_pairs={{0,2},{1,15},{2,4},{3,1},{4,6},{5,3},{6,8},{7,5},{8,10},{9,7},{10,... | collective-permute-start | bytes 589832 | tf_op jit(solution)/shard_map/ppermute | solution.py:50
  70.5 5.5 %collective-permute-start.21 = (bf16[128,2048]{1,0:T(8,128)(2,1)S(1)}, bf16[128,2048]{1,0:T(8,128)(2,1)S(1)}, u32[]{:S(2)}, u32[]{:S(2)}) collective-permute-start(bf16[128,2048]{1,0:T(8,128)(2,1)S(1)} %get-tuple-element.47.own_ref), channel_id=1, source_target_pairs={{0,1},{1,0},{2,3},{3,2},{4,5},{5,4},{6,7},{7,6},{8,9},{9,8},{10,11... | collective-permute-start | bytes 1572872 | tf_op jit(solution)/shard_map/ppermute | solution.py:50
  72.7 15.0 %collective-permute-start.28 = (bf16[128,2048]{1,0:T(8,128)(2,1)S(1)}, bf16[128,2048]{1,0:T(8,128)(2,1)S(1)}, u32[]{:S(2)}, u32[]{:S(2)}) collective-permute-start(bf16[128,2048]{1,0:T(8,128)(2,1)S(1)} %shard_map.86.mine), channel_id=1, source_target_pairs={{0,32},{32,64},{64,96},{96,0},{128,160},{160,192},{192,224},{224,1... | collective-permute-start | bytes 1572872 | tf_op jit(solution)/shard_map/ppermute | solution.py:50
  74.1 14.8 %collective-permute-start.29 = (bf16[128,2048]{1,0:T(8,128)(2,1)S(1)}, bf16[128,2048]{1,0:T(8,128)(2,1)S(1)}, u32[]{:S(2)}, u32[]{:S(2)}) collective-permute-start(bf16[128,2048]{1,0:T(8,128)(2,1)S(1)} %shard_map.86.mine), channel_id=1, source_target_pairs={{0,96},{32,0},{64,32},{96,64},{128,224},{160,128},{192,160},{224,1... | collective-permute-start | bytes 1572872 | tf_op jit(solution)/shard_map/ppermute | solution.py:50
  75.6 18.1 %collective-permute-start.20 = (bf16[512,384]{1,0:T(8,128)(2,1)S(1)}, bf16[512,384]{1,0:T(8,128)(2,1)S(1)}, u32[]{:S(2)}, u32[]{:S(2)}) collective-permute-start(bf16[512,384]{1,0:T(8,128)(2,1)S(1)} %get-tuple-element.46), channel_id=1, source_target_pairs={{0,1},{1,0},{2,3},{3,2},{4,5},{5,4},{6,7},{7,6},{8,9},{9,8},{10,11... | collective-permute-start | bytes 1179656 | tf_op jit(solution)/shard_map/ppermute | solution.py:50
  76.0 6.3 %collective-permute-start.23 = (bf16[256,256]{1,0:T(8,128)(2,1)S(1)}, bf16[256,256]{1,0:T(8,128)(2,1)S(1)}, u32[]{:S(2)}, u32[]{:S(2)}) collective-permute-start(bf16[256,256]{1,0:T(8,128)(2,1)S(1)} %get-tuple-element.51), channel_id=1, source_target_pairs={{0,2},{1,3},{2,4},{3,5},{4,6},{5,7},{6,8},{7,9},{8,10},{9,11},{10,... | collective-permute-start | bytes 393224 | tf_op jit(solution)/shard_map/ppermute | solution.py:50
  76.0 12.9 %collective-permute-start.24 = (bf16[256,256]{1,0:T(8,128)(2,1)S(1)}, bf16[256,256]{1,0:T(8,128)(2,1)S(1)}, u32[]{:S(2)}, u32[]{:S(2)}) collective-permute-start(bf16[256,256]{1,0:T(8,128)(2,1)S(1)} %get-tuple-element.52), channel_id=1, source_target_pairs={{0,3},{1,2},{2,5},{3,4},{4,7},{5,6},{6,9},{7,8},{8,11},{9,10},{10,... | collective-permute-start | bytes 393224 | tf_op jit(solution)/shard_map/ppermute | solution.py:50
  82.4 7.7 %collective-permute-start.25 = (bf16[256,256]{1,0:T(8,128)(2,1)S(1)}, bf16[256,256]{1,0:T(8,128)(2,1)S(1)}, u32[]{:S(2)}, u32[]{:S(2)}) collective-permute-start(bf16[256,256]{1,0:T(8,128)(2,1)S(1)} %get-tuple-element.53), channel_id=1, source_target_pairs={{0,14},{1,15},{2,0},{3,1},{4,2},{5,3},{6,4},{7,5},{8,6},{9,7},{10,... | collective-permute-start | bytes 393224 | tf_op jit(solution)/shard_map/ppermute | solution.py:50
  87.6 6.0 %collective-permute-start.26 = (bf16[256,256]{1,0:T(8,128)(2,1)S(1)}, bf16[256,256]{1,0:T(8,128)(2,1)S(1)}, u32[]{:S(2)}, u32[]{:S(2)}) collective-permute-start(bf16[256,256]{1,0:T(8,128)(2,1)S(1)} %get-tuple-element.54), channel_id=1, source_target_pairs={{0,15},{1,14},{2,1},{3,0},{4,3},{5,2},{6,5},{7,4},{8,7},{9,6},{10,... | collective-permute-start | bytes 393224 | tf_op jit(solution)/shard_map/ppermute | solution.py:50
  88.9 4.8 %collective-permute-start.22 = (bf16[256,256]{1,0:T(8,128)(2,1)S(1)}, bf16[256,256]{1,0:T(8,128)(2,1)S(1)}, u32[]{:S(2)}, u32[]{:S(2)}) collective-permute-start(bf16[256,256]{1,0:T(8,128)(2,1)S(1)} %get-tuple-element.50), channel_id=1, source_target_pairs={{0,1},{1,0},{2,3},{3,2},{4,5},{5,4},{6,7},{7,6},{8,9},{9,8},{10,11... | collective-permute-start | bytes 393224 | tf_op jit(solution)/shard_map/ppermute | solution.py:50
  88.9 10.1 %collective-permute-start.30 = (bf16[64,2048]{1,0:T(8,128)(2,1)S(1)}, bf16[64,2048]{1,0:T(8,128)(2,1)S(1)}, u32[]{:S(2)}, u32[]{:S(2)}) collective-permute-start(bf16[64,2048]{1,0:T(8,128)(2,1)S(1)} %slice.74), channel_id=1, source_target_pairs={{0,32},{32,64},{64,96},{96,0},{128,160},{160,192},{192,224},{224,1... | collective-permute-start | bytes 786440 | tf_op jit(solution)/shard_map/ppermute | solution.py:50
  90.1 8.9 %collective-permute-start.31 = (bf16[64,2048]{1,0:T(8,128)(2,1)S(1)}, bf16[64,2048]{1,0:T(8,128)(2,1)S(1)}, u32[]{:S(2)}, u32[]{:S(2)}) collective-permute-start(bf16[64,2048]{1,0:T(8,128)(2,1)S(1)} %slice.75), channel_id=1, source_target_pairs={{0,96},{32,0},{64,32},{96,64},{128,224},{160,128},{192,160},{224,1... | collective-permute-start | bytes 786440 | tf_op jit(solution)/shard_map/ppermute | solution.py:50
  97.7 4.7 %collective-permute-start.27 = (bf16[256,256]{1,0:T(8,128)(2,1)S(1)}, bf16[256,256]{1,0:T(8,128)(2,1)S(1)}, u32[]{:S(2)}, u32[]{:S(2)}) collective-permute-start(bf16[256,256]{1,0:T(8,128)(2,1)S(1)} %get-tuple-element.59), channel_id=1, source_target_pairs={{0,16},{1,17},{2,18},{3,19},{4,20},{5,21},{6,22},{7,23},{8,24},{9,... | collective-permute-start | bytes 393224 | tf_op jit(solution)/shard_map/ppermute | solution.py:50
  103.7 2.9 %collective-permute-start.32 = (bf16[128,2048]{1,0:T(8,128)(2,1)S(1)}, bf16[128,2048]{1,0:T(8,128)(2,1)S(1)}, u32[]{:S(2)}, u32[]{:S(2)}) collective-permute-start(bf16[128,2048]{1,0:T(8,128)(2,1)S(1)} %get-tuple-element.56), channel_id=1, source_target_pairs={{0,1},{1,0},{2,3},{3,2},{4,5},{5,4},{6,7},{7,6},{8,9},{9,8},{10,11... | collective-permute-start | bytes 1572872 | tf_op jit(solution)/shard_map/ppermute | solution.py:50
  (4 other events, 33.5 us)

commit v11 on v7

--- a/solution.py
+++ b/solution.py
@@ -40,10 +40,6 @@
 Y = 4
 Y_UP = [(d, (d & 4) | ((d + 1) & 3)) for d in range(2 * Y)]
 Y_DOWN = [(d, (d & 4) | ((d - 1) & 3)) for d in range(2 * Y)]
-
-
-UP_CROSS = pairs(lambda x, z, c: (x, (z + 1) % Z, 1 - c))
-DOWN_CROSS = pairs(lambda x, z, c: (x, (z - 1) % Z, 1 - c))
 
 
 def send(value, route, axis="seq"):
@@ -125,8 +121,9 @@
                 for seg in range(2):
                     at = slice((seg * 2 + part) * TOK, (seg * 2 + part + 1) * TOK)
                     into = slice(seg * TOK, seg * TOK + TOK)
-                    edges[2 * part][into, lanes_out] = keep_ref[at, lanes]
-                    edges[2 * part + 1][into, lanes_out] = send_ref[at, lanes]
+                    edges[part][into, lanes_out] = keep_ref[at, lanes]
+                    into = slice(2 * TOK + seg * TOK, 2 * TOK + seg * TOK + TOK)
+                    edges[part][into, lanes_out] = send_ref[at, lanes]
 
 
 def far_kernel(index, own_ref, other_ref, table, keep_ref, send_ref):
@@ -348,7 +345,7 @@
             jax.ShapeDtypeStruct((G_ROWS, width), bf16),
             jax.ShapeDtypeStruct((2 * Z * HALF, width), bf16),
             jax.ShapeDtypeStruct((128, width), bf16),
-            *[jax.ShapeDtypeStruct((2 * TOK, 256), bf16)] * 4,
+            *[jax.ShapeDtypeStruct((4 * TOK, 256), bf16)] * 2,
         ),
         2 * ROWS * 768 * width,
         0,
@@ -359,8 +356,9 @@
     got = send(to_swap, OTHER_CORE)
     g_other = send(g_own, OTHER_CORE)
 
-    below = send(edges[2], UP), send(edges[3], UP_CROSS)
-    above = send(edges[0], DOWN), send(edges[1], DOWN_CROSS)
+    below, above = send(edges[1], UP), send(edges[0], DOWN)
+    below = below, send(below[2 * TOK :], OTHER_CORE)
+    above = above, send(above[2 * TOK :], OTHER_CORE)
     far_half = jax.ShapeDtypeStruct((2 * G_ROWS, 256), bf16)
     g_keep, g_swap = on_chip(
         far_kernel, (far_half, far_half), 2 * 256 * 512 * width, 0, (index, g_own, g_other, far_table)

time: 104 us -> 104 us (level)
  waiting for transfers between devices: 45.5 us -> 41.6 us
  starting transfers between devices: 42.4 us -> 46 us
    ppermute x33, waiting for transfers between devices: 45.5 us -> 41.6 us  [send(): return lax.ppermute(value, axis, route)]
    ppermute x33, starting transfers between devices: 42.4 us -> 46 us  [send(): return lax.ppermute(value, axis, route)]
  transfers between devices with their start and end apart: 33 -> 33, of which waited for: 15 -> 14; matrix products, arithmetic and copies ran while one was open for 0% -> 0% of each run, Pallas kernels for 7% -> 7%
where the time goes in v11:
time: 104 us
  starting transfers between devices  46 us (44%)
  waiting for transfers between devices  41.6 us (40%)
  Pallas kernels  11.5 us (11%)
  other arithmetic  2.31 us (2%)
  local copies, waits for them, and re-layouts  1.29 us (1%)
    ppermute x33, starting transfers between devices, send(): return lax.ppermute(value, axis, route)  46 us
    ppermute x33, waiting for transfers between devices, send(): return lax.ppermute(value, axis, route)  41.6 us
    pallas_call x5, Pallas kernels, on_chip(): pl.pallas_call(kernel, out_shape=out_shape, in_specs=specs, out_specs=jax...  11.5 us
  transfers between devices with their start and end apart: 33, of which 14 were waited for; matrix products, arithmetic and copies ran while one was open for 0% of the time, Pallas kernels for 7%

profile of v11, /device:TPU:1, one launch (start us, length us, event | category | flops | bytes accessed | tf_op | source)
XLA Modules:
  0.0 103.7 jit_solution(11435075647846419131)
XLA Ops:
  2.3 3.3 %collective-permute-start.8 = (bf16[128,64]{1,0:T(8,128)(2,1)S(1)}, bf16[128,64]{1,0:T(8,128)(2,1)S(1)}, u32[]{:S(2)}, u32[]{:S(2)}) collective-permute-start(bf16[128,64]{1,0:T(8,128)(2,1)S(1)} %bitcast.43), channel_id=1, source_target_pairs={{0,1},{1,0},{2,3},{3,2},{4,5},{5,4},{6,7},{7,6},{8,9},{9,8},{10,11... | collective-permute-start | bytes 49160 | tf_op jit(solution)/shard_map/ppermute | solution.py:46
  5.6 3.9 %collective-permute-start = (bf16[48,2048]{1,0:T(8,128)(2,1)S(1)}, bf16[48,2048]{1,0:T(8,128)(2,1)S(1)}, u32[]{:S(2)}, u32[]{:S(2)}) collective-permute-start(bf16[48,2048]{1,0:T(8,128)(2,1)S(1)} %bitcast.34), channel_id=1, source_target_pairs={{0,2},{1,15},{2,4},{3,1},{4,6},{5,3},{6,8},{7,5},{8,10},{9,7},{10,... | collective-permute-start | bytes 589832 | tf_op jit(solution)/shard_map/ppermute | solution.py:46
  10.3 1.3 %shard_map.82 = (bf16[128,2048]{1,0:T(8,128)(2,1)S(1)}, bf16[8,2048]{1,0:T(8,128)(2,1)S(1)}) custom-call(s32[6]{0:T(128)S(1)} %stack.35.index, bf16[128,2048]{1,0:T(8,128)(2,1)S(1)} %copy-done, f32[1,2048]{1,0:T(1,128)S(1)} %bitcast.36, f32[1,2048]{1,0:T(1,128)S(1)} %bitcast.37), custom_call_target="tpu_custom_call" | custom-call | flops 2097152 | bytes 4194304 | tf_op jit(solution)/shard_map/pallas_call | solution.py:245
  11.5 1.3 %collective-permute-start.7 = (bf16[8,2048]{1,0:T(8,128)(2,1)S(1)}, bf16[8,2048]{1,0:T(8,128)(2,1)S(1)}, u32[]{:S(2)}, u32[]{:S(2)}) collective-permute-start(bf16[8,2048]{1,0:T(8,128)(2,1)S(1)} %get-tuple-element.33), channel_id=1, source_target_pairs={{0,16},{1,17},{2,18},{3,19},{4,20},{5,21},{6,22},{7,23},{8,24},{9,... | collective-permute-start | bytes 98312 | tf_op jit(solution)/shard_map/ppermute | solution.py:46
  13.3 1.4 %collective-permute-done.7 = bf16[8,2048]{1,0:T(8,128)(2,1)S(1)} collective-permute-done((bf16[8,2048]{1,0:T(8,128)(2,1)S(1)}, bf16[8,2048]{1,0:T(8,128)(2,1)S(1)}, u32[]{:S(2)}, u32[]{:S(2)}) %collective-permute-start.7) | collective-permute-done | bytes 32800 | tf_op jit(solution)/shard_map/ppermute | solution.py:46
  14.7 1.4 %collective-permute-done.9 = bf16[128,128]{1,0:T(8,128)(2,1)S(1)} collective-permute-done((bf16[128,128]{1,0:T(8,128)(2,1)S(1)}, bf16[128,128]{1,0:T(8,128)(2,1)S(1)}, u32[]{:S(2)}, u32[]{:S(2)}) %collective-permute-start.9) | collective-permute-done | bytes 32800 | tf_op jit(solution)/shard_map/ppermute | solution.py:46
  16.4 2.7 %collective-permute-start.10 = (bf16[80,2048]{1,0:T(8,128)(2,1)S(1)}, bf16[80,2048]{1,0:T(8,128)(2,1)S(1)}, u32[]{:S(2)}, u32[]{:S(2)}) collective-permute-start(bf16[80,2048]{1,0:T(8,128)(2,1)S(1)} %pad_maximum_fusion.1.refs_12_), channel_id=1, source_target_pairs={{0,2},{1,15},{2,4},{3,1},{4,6},{5,3},{6,8},{7,5},{8,10},{9,7},{10,... | collective-permute-start | bytes 983048 | tf_op jit(solution)/shard_map/ppermute | solution.py:46
  19.3 4.2 %collective-permute-done.11.refs_14_ = bf16[80,2048]{1,0:T(8,128)(2,1)S(1)} collective-permute-done((bf16[80,2048]{1,0:T(8,128)(2,1)S(1)}, bf16[80,2048]{1,0:T(8,128)(2,1)S(1)}, u32[]{:S(2)}, u32[]{:S(2)}) %collective-permute-start.11) | collective-permute-done | bytes 327712 | tf_op jit(solution)/shard_map/ppermute | solution.py:46
  24.3 3.4 %collective-permute-start.14 = (bf16[80,2048]{1,0:T(8,128)(2,1)S(1)}, bf16[80,2048]{1,0:T(8,128)(2,1)S(1)}, u32[]{:S(2)}, u32[]{:S(2)}) collective-permute-start(bf16[80,2048]{1,0:T(8,128)(2,1)S(1)} %collective-permute-done.10.refs_13_), channel_id=1, source_target_pairs={{0,2},{1,15},{2,4},{3,1},{4,6},{5,3},{6,8},{7,5},{8,10},{9,7},{10,... | collective-permute-start | bytes 983048 | tf_op jit(solution)/shard_map/ppermute | solution.py:46
  28.6 1.8 %collective-permute-start.5 = (bf16[48,2048]{1,0:T(8,128)(2,1)S(1)}, bf16[48,2048]{1,0:T(8,128)(2,1)S(1)}, u32[]{:S(2)}, u32[]{:S(2)}) collective-permute-start(bf16[48,2048]{1,0:T(8,128)(2,1)S(1)} %collective-permute-done.refs_5_), channel_id=1, source_target_pairs={{0,2},{1,15},{2,4},{3,1},{4,6},{5,3},{6,8},{7,5},{8,10},{9,7},{10,... | collective-permute-start | bytes 589832 | tf_op jit(solution)/shard_map/ppermute | solution.py:46
  30.4 10.2 %collective-permute-done.6.refs_8_ = bf16[48,2048]{1,0:T(8,128)(2,1)S(1)} collective-permute-done((bf16[48,2048]{1,0:T(8,128)(2,1)S(1)}, bf16[48,2048]{1,0:T(8,128)(2,1)S(1)}, u32[]{:S(2)}, u32[]{:S(2)}) %collective-permute-start.6) | collective-permute-done | bytes 196640 | tf_op jit(solution)/shard_map/ppermute | solution.py:46
  40.8 2.2 %collective-permute-start.12 = (bf16[48,2048]{1,0:T(8,128)(2,1)S(1)}, bf16[48,2048]{1,0:T(8,128)(2,1)S(1)}, u32[]{:S(2)}, u32[]{:S(2)}) collective-permute-start(bf16[48,2048]{1,0:T(8,128)(2,1)S(1)} %collective-permute-done.5.refs_7_), channel_id=1, source_target_pairs={{0,2},{1,15},{2,4},{3,1},{4,6},{5,3},{6,8},{7,5},{8,10},{9,7},{10,... | collective-permute-start | bytes 589832 | tf_op jit(solution)/shard_map/ppermute | solution.py:46
  43.0 3.6 %collective-permute-start.2 = (bf16[128,2048]{1,0:T(8,128)(2,1)S(1)}, bf16[128,2048]{1,0:T(8,128)(2,1)S(1)}, u32[]{:S(2)}, u32[]{:S(2)}) collective-permute-start(bf16[128,2048]{1,0:T(8,128)(2,1)S(1)} %get-tuple-element.32.refs_0_), channel_id=1, source_target_pairs={{0,1},{1,0},{2,3},{3,2},{4,5},{5,4},{6,7},{7,6},{8,9},{9,8},{10,11... | collective-permute-start | bytes 1572872 | tf_op jit(solution)/shard_map/ppermute | solution.py:46
  46.6 2.6 %collective-permute-done.12.refs_9_ = bf16[48,2048]{1,0:T(8,128)(2,1)S(1)} collective-permute-done((bf16[48,2048]{1,0:T(8,128)(2,1)S(1)}, bf16[48,2048]{1,0:T(8,128)(2,1)S(1)}, u32[]{:S(2)}, u32[]{:S(2)}) %collective-permute-start.12) | collective-permute-done | bytes 196640 | tf_op jit(solution)/shard_map/ppermute | solution.py:46
  50.3 3.3 %collective-permute-start.19 = (bf16[80,2048]{1,0:T(8,128)(2,1)S(1)}, bf16[80,2048]{1,0:T(8,128)(2,1)S(1)}, u32[]{:S(2)}, u32[]{:S(2)}) collective-permute-start(bf16[80,2048]{1,0:T(8,128)(2,1)S(1)} %collective-permute-done.17.refs_17_), channel_id=1, source_target_pairs={{0,2},{1,15},{2,4},{3,1},{4,6},{5,3},{6,8},{7,5},{8,10},{9,7},{10,... | collective-permute-start | bytes 983048 | tf_op jit(solution)/shard_map/ppermute | solution.py:46
  54.3 8.1 %collective-permute-done.16.refs_11_ = bf16[48,2048]{1,0:T(8,128)(2,1)S(1)} collective-permute-done((bf16[48,2048]{1,0:T(8,128)(2,1)S(1)}, bf16[48,2048]{1,0:T(8,128)(2,1)S(1)}, u32[]{:S(2)}, u32[]{:S(2)}) %collective-permute-start.16) | collective-permute-done | bytes 196640 | tf_op jit(solution)/shard_map/ppermute | solution.py:46
  62.5 2.9 %shard_map.83 = (bf16[512,384]{1,0:T(8,128)(2,1)S(1)}, bf16[512,384]{1,0:T(8,128)(2,1)S(1)}, bf16[128,2048]{1,0:T(8,128)(2,1)S(1)}, bf16[512,2048]{1,0:T(8,128)(...) custom-call(s32[6]{0:T(128)S(1)} %stack.35.index, ...), custom_call_target="tpu_custom_call" | custom-call | flops 1610612736 | bytes 4194304 | tf_op jit(solution)/shard_map/pallas_call | solution.py:245
  65.4 4.5 %collective-permute-start.21 = (bf16[128,2048]{1,0:T(8,128)(2,1)S(1)}, bf16[128,2048]{1,0:T(8,128)(2,1)S(1)}, u32[]{:S(2)}, u32[]{:S(2)}) collective-permute-start(bf16[128,2048]{1,0:T(8,128)(2,1)S(1)} %get-tuple-element.46.own_ref), channel_id=1, source_target_pairs={{0,1},{1,0},{2,3},{3,2},{4,5},{5,4},{6,7},{7,6},{8,9},{9,8},{10,11... | collective-permute-start | bytes 1572872 | tf_op jit(solution)/shard_map/ppermute | solution.py:46
  70.4 2.7 %collective-permute-start.29 = (bf16[128,2048]{1,0:T(8,128)(2,1)S(1)}, bf16[128,2048]{1,0:T(8,128)(2,1)S(1)}, u32[]{:S(2)}, u32[]{:S(2)}) collective-permute-start(bf16[128,2048]{1,0:T(8,128)(2,1)S(1)} %get-tuple-element.52.mine), channel_id=1, source_target_pairs={{0,96},{32,0},{64,32},{96,64},{128,224},{160,128},{192,160},{224,1... | collective-permute-start | bytes 1572872 | tf_op jit(solution)/shard_map/ppermute | solution.py:46
  73.1 2.2 %collective-permute-start.25 = (bf16[512,256]{1,0:T(8,128)(2,1)S(1)}, bf16[512,256]{1,0:T(8,128)(2,1)S(1)}, u32[]{:S(2)}, u32[]{:S(2)}) collective-permute-start(bf16[512,256]{1,0:T(8,128)(2,1)S(1)} %get-tuple-element.51), channel_id=1, source_target_pairs={{0,14},{1,15},{2,0},{3,1},{4,2},{5,3},{6,4},{7,5},{8,6},{9,7},{10,... | collective-permute-start | bytes 786440 | tf_op jit(solution)/shard_map/ppermute | solution.py:46
  75.4 3.7 %collective-permute-done.23.below_ref = bf16[512,256]{1,0:T(8,128)(2,1)S(1)} collective-permute-done((bf16[512,256]{1,0:T(8,128)(2,1)S(1)}, bf16[512,256]{1,0:T(8,128)(2,1)S(1)}, u32[]{:S(2)}, u32[]{:S(2)}) %collective-permute-start.23) | collective-permute-done | bytes 262176 | tf_op jit(solution)/shard_map/ppermute | solution.py:46
  80.4 1.5 %collective-permute-start.24 = (bf16[256,256]{1,0:T(8,128)(2,1)S(1)}, bf16[256,256]{1,0:T(8,128)(2,1)S(1)}, u32[]{:S(2)}, u32[]{:S(2)}) collective-permute-start(bf16[256,256]{1,0:T(8,128)(2,1)S(1)} %slice.80), channel_id=1, source_target_pairs={{0,1},{1,0},{2,3},{3,2},{4,5},{5,4},{6,7},{7,6},{8,9},{9,8},{10,11... | collective-permute-start | bytes 393224 | tf_op jit(solution)/shard_map/ppermute | solution.py:46
  82.0 2.1 %shard_map.84 = (bf16[256,256]{1,0:T(8,128)(2,1)S(1)}, bf16[256,256]{1,0:T(8,128)(2,1)S(1)}) custom-call(s32[6]{0:T(128)S(1)} %stack.35.index, bf16[128,2048]{1,0:T(8,128)(2,1)S(1)} %get-tuple-element.46.own_ref, bf16[128,2048]{1,0:T(8,128)(2,1)S(1)} %collective-permute-done.21.other_ref, bf16[512,2048]{1,0:T(8,128)(2,1)S(1)} %get-tuple-element.47.table), custom_call_target="tpu_custom_call" | custom-call | flops 536870912 | bytes 4194304 | tf_op jit(solution)/shard_map/pallas_call | solution.py:245
  84.1 1.2 %collective-permute-start.22 = (bf16[256,256]{1,0:T(8,128)(2,1)S(1)}, bf16[256,256]{1,0:T(8,128)(2,1)S(1)}, u32[]{:S(2)}, u32[]{:S(2)}) collective-permute-start(bf16[256,256]{1,0:T(8,128)(2,1)S(1)} %get-tuple-element.49), channel_id=1, source_target_pairs={{0,1},{1,0},{2,3},{3,2},{4,5},{5,4},{6,7},{7,6},{8,9},{9,8},{10,11... | collective-permute-start | bytes 393224 | tf_op jit(solution)/shard_map/ppermute | solution.py:46
  85.3 1.8 %collective-permute-done.28.prev = bf16[128,2048]{1,0:T(8,128)(2,1)S(1)} collective-permute-done((bf16[128,2048]{1,0:T(8,128)(2,1)S(1)}, bf16[128,2048]{1,0:T(8,128)(2,1)S(1)}, u32[]{:S(2)}, u32[]{:S(2)}) %collective-permute-start.28) | collective-permute-done | bytes 524320 | tf_op jit(solution)/shard_map/ppermute | solution.py:46
  87.1 1.9 %collective-permute-start.31 = (bf16[64,2048]{1,0:T(8,128)(2,1)S(1)}, bf16[64,2048]{1,0:T(8,128)(2,1)S(1)}, u32[]{:S(2)}, u32[]{:S(2)}) collective-permute-start(bf16[64,2048]{1,0:T(8,128)(2,1)S(1)} %slice.85), channel_id=1, source_target_pairs={{0,96},{32,0},{64,32},{96,64},{128,224},{160,128},{192,160},{224,1... | collective-permute-start | bytes 786440 | tf_op jit(solution)/shard_map/ppermute | solution.py:46
  89.2 4.0 %shard_map.85 = bf16[2,256,256]{2,1,0:T(8,128)(2,1)S(1)} custom-call(s32[6]{0:T(128)S(1)} %stack.35.index, bf16[512,384]{1,0:T(8,128)(2,1)S(1)} %get-tuple-element.44.keep_ref, bf16[512,384]{1,0:T(8,128)(2,1)S(1)} %collective-permute-done.20.got_ref, bf16[256,256]{1,0:T(8,128)(2,1)S(1)} %get-tuple-element.48.g_keep, ...), custom_call_target="tpu_custom_call" | custom-call | flops 1342177280 | bytes 4194304 | tf_op jit(solution)/shard_map/pallas_call | solution.py:245
  93.3 1.5 %collective-permute-done.31.far_b = bf16[64,2048]{1,0:T(8,128)(2,1)S(1)} collective-permute-done((bf16[64,2048]{1,0:T(8,128)(2,1)S(1)}, bf16[64,2048]{1,0:T(8,128)(2,1)S(1)}, u32[]{:S(2)}, u32[]{:S(2)}) %collective-permute-start.31) | collective-permute-done | bytes 262176 | tf_op jit(solution)/shard_map/ppermute | solution.py:46
  94.8 3.2 %collective-permute-done.30.far_a = bf16[64,2048]{1,0:T(8,128)(2,1)S(1)} collective-permute-done((bf16[64,2048]{1,0:T(8,128)(2,1)S(1)}, bf16[64,2048]{1,0:T(8,128)(2,1)S(1)}, u32[]{:S(2)}, u32[]{:S(2)}) %collective-permute-start.30) | collective-permute-done | bytes 262176 | tf_op jit(solution)/shard_map/ppermute | solution.py:46
  98.0 1.3 %shard_map.86 = (f32[128,2048]{1,0:T(8,128)S(1)}, bf16[128,2048]{1,0:T(8,128)(2,1)S(1)}) custom-call(s32[6]{0:T(128)S(1)} %stack.35.index, bf16[256,256]{1,0:T(8,128)(2,1)S(1)} %get-tuple-element.58.own_ref, bf16[256,256]{1,0:T(8,128)(2,1)S(1)} %collective-permute-done.27.there_ref, bf16[128,2048]{1,0:T(8,128)(2,1)S(1)} %get-tuple-element.52.mine, ...), custom_call_target="tpu_custom_call" | custom-call | flops 536870912 | bytes 4194304 | tf_op jit(solution)/shard_map/pallas_call | solution.py:245
  99.3 2.0 %collective-permute-start.32 = (bf16[128,2048]{1,0:T(8,128)(2,1)S(1)}, bf16[128,2048]{1,0:T(8,128)(2,1)S(1)}, u32[]{:S(2)}, u32[]{:S(2)}) collective-permute-start(bf16[128,2048]{1,0:T(8,128)(2,1)S(1)} %get-tuple-element.54), channel_id=1, source_target_pairs={{0,1},{1,0},{2,3},{3,2},{4,5},{5,4},{6,7},{7,6},{8,9},{9,8},{10,11... | collective-permute-start | bytes 1572872 | tf_op jit(solution)/shard_map/ppermute | solution.py:46
  101.3 1.5 %collective-permute-done.32 = bf16[128,2048]{1,0:T(8,128)(2,1)S(1)} collective-permute-done((bf16[128,2048]{1,0:T(8,128)(2,1)S(1)}, bf16[128,2048]{1,0:T(8,128)(2,1)S(1)}, u32[]{:S(2)}, u32[]{:S(2)}) %collective-permute-start.32) | collective-permute-done | bytes 524320 | tf_op jit(solution)/shard_map/ppermute | solution.py:46
  (69 shorter events, 10.0 us)
Async XLA Ops:
  2.3 10.5 %collective-permute-start.8 = (bf16[128,64]{1,0:T(8,128)(2,1)S(1)}, bf16[128,64]{1,0:T(8,128)(2,1)S(1)}, u32[]{:S(2)}, u32[]{:S(2)}) collective-permute-start(bf16[128,64]{1,0:T(8,128)(2,1)S(1)} %bitcast.43), channel_id=1, source_target_pairs={{0,1},{1,0},{2,3},{3,2},{4,5},{5,4},{6,7},{7,6},{8,9},{9,8},{10,11... | collective-permute-start | bytes 49160 | tf_op jit(solution)/shard_map/ppermute | solution.py:46
  5.6 10.7 %collective-permute-start.4 = (bf16[48,2048]{1,0:T(8,128)(2,1)S(1)}, bf16[48,2048]{1,0:T(8,128)(2,1)S(1)}, u32[]{:S(2)}, u32[]{:S(2)}) collective-permute-start(bf16[48,2048]{1,0:T(8,128)(2,1)S(1)} %bitcast.33), channel_id=1, source_target_pairs={{0,14},{1,3},{2,0},{3,5},{4,2},{5,7},{6,4},{7,9},{8,6},{9,11},{10,... | collective-permute-start | bytes 589832 | tf_op jit(solution)/shard_map/ppermute | solution.py:46
  5.6 10.7 %collective-permute-start = (bf16[48,2048]{1,0:T(8,128)(2,1)S(1)}, bf16[48,2048]{1,0:T(8,128)(2,1)S(1)}, u32[]{:S(2)}, u32[]{:S(2)}) collective-permute-start(bf16[48,2048]{1,0:T(8,128)(2,1)S(1)} %bitcast.34), channel_id=1, source_target_pairs={{0,2},{1,15},{2,4},{3,1},{4,6},{5,3},{6,8},{7,5},{8,10},{9,7},{10,... | collective-permute-start | bytes 589832 | tf_op jit(solution)/shard_map/ppermute | solution.py:46
  11.5 3.1 %collective-permute-start.7 = (bf16[8,2048]{1,0:T(8,128)(2,1)S(1)}, bf16[8,2048]{1,0:T(8,128)(2,1)S(1)}, u32[]{:S(2)}, u32[]{:S(2)}) collective-permute-start(bf16[8,2048]{1,0:T(8,128)(2,1)S(1)} %get-tuple-element.33), channel_id=1, source_target_pairs={{0,16},{1,17},{2,18},{3,19},{4,20},{5,21},{6,22},{7,23},{8,24},{9,... | collective-permute-start | bytes 98312 | tf_op jit(solution)/shard_map/ppermute | solution.py:46
  16.3 7.2 %collective-permute-start.11 = (bf16[80,2048]{1,0:T(8,128)(2,1)S(1)}, bf16[80,2048]{1,0:T(8,128)(2,1)S(1)}, u32[]{:S(2)}, u32[]{:S(2)}) collective-permute-start(bf16[80,2048]{1,0:T(8,128)(2,1)S(1)} %pad_maximum_fusion.1.refs_12_), channel_id=1, source_target_pairs={{0,14},{1,3},{2,0},{3,5},{4,2},{5,7},{6,4},{7,9},{8,6},{9,11},{10,... | collective-permute-start | bytes 983048 | tf_op jit(solution)/shard_map/ppermute | solution.py:46
  16.4 7.9 %collective-permute-start.10 = (bf16[80,2048]{1,0:T(8,128)(2,1)S(1)}, bf16[80,2048]{1,0:T(8,128)(2,1)S(1)}, u32[]{:S(2)}, u32[]{:S(2)}) collective-permute-start(bf16[80,2048]{1,0:T(8,128)(2,1)S(1)} %pad_maximum_fusion.1.refs_12_), channel_id=1, source_target_pairs={{0,2},{1,15},{2,4},{3,1},{4,6},{5,3},{6,8},{7,5},{8,10},{9,7},{10,... | collective-permute-start | bytes 983048 | tf_op jit(solution)/shard_map/ppermute | solution.py:46
  19.1 27.5 %collective-permute-start.1 = (bf16[128,2048]{1,0:T(8,128)(2,1)S(1)}, bf16[128,2048]{1,0:T(8,128)(2,1)S(1)}, u32[]{:S(2)}, u32[]{:S(2)}) collective-permute-start(bf16[128,2048]{1,0:T(8,128)(2,1)S(1)} %get-tuple-element.32.refs_0_), channel_id=1, source_target_pairs={{0,16},{1,17},{2,18},{3,19},{4,20},{5,21},{6,22},{7,23},{8,24},{9,... | collective-permute-start | bytes 1572872 | tf_op jit(solution)/shard_map/ppermute | solution.py:46
  24.3 16.4 %collective-permute-start.14 = (bf16[80,2048]{1,0:T(8,128)(2,1)S(1)}, bf16[80,2048]{1,0:T(8,128)(2,1)S(1)}, u32[]{:S(2)}, u32[]{:S(2)}) collective-permute-start(bf16[80,2048]{1,0:T(8,128)(2,1)S(1)} %collective-permute-done.10.refs_13_), channel_id=1, source_target_pairs={{0,2},{1,15},{2,4},{3,1},{4,6},{5,3},{6,8},{7,5},{8,10},{9,7},{10,... | collective-permute-start | bytes 983048 | tf_op jit(solution)/shard_map/ppermute | solution.py:46
  27.7 13.0 %collective-permute-start.15 = (bf16[80,2048]{1,0:T(8,128)(2,1)S(1)}, bf16[80,2048]{1,0:T(8,128)(2,1)S(1)}, u32[]{:S(2)}, u32[]{:S(2)}) collective-permute-start(bf16[80,2048]{1,0:T(8,128)(2,1)S(1)} %collective-permute-done.11.refs_14_), channel_id=1, source_target_pairs={{0,14},{1,3},{2,0},{3,5},{4,2},{5,7},{6,4},{7,9},{8,6},{9,11},{10,... | collective-permute-start | bytes 983048 | tf_op jit(solution)/shard_map/ppermute | solution.py:46
  27.7 12.9 %collective-permute-start.6 = (bf16[48,2048]{1,0:T(8,128)(2,1)S(1)}, bf16[48,2048]{1,0:T(8,128)(2,1)S(1)}, u32[]{:S(2)}, u32[]{:S(2)}) collective-permute-start(bf16[48,2048]{1,0:T(8,128)(2,1)S(1)} %collective-permute-done.4.refs_6_), channel_id=1, source_target_pairs={{0,14},{1,3},{2,0},{3,5},{4,2},{5,7},{6,4},{7,9},{8,6},{9,11},{10,... | collective-permute-start | bytes 589832 | tf_op jit(solution)/shard_map/ppermute | solution.py:46
  28.6 12.0 %collective-permute-start.5 = (bf16[48,2048]{1,0:T(8,128)(2,1)S(1)}, bf16[48,2048]{1,0:T(8,128)(2,1)S(1)}, u32[]{:S(2)}, u32[]{:S(2)}) collective-permute-start(bf16[48,2048]{1,0:T(8,128)(2,1)S(1)} %collective-permute-done.refs_5_), channel_id=1, source_target_pairs={{0,2},{1,15},{2,4},{3,1},{4,6},{5,3},{6,8},{7,5},{8,10},{9,7},{10,... | collective-permute-start | bytes 589832 | tf_op jit(solution)/shard_map/ppermute | solution.py:46
  40.7 9.7 %collective-permute-start.17 = (bf16[80,2048]{1,0:T(8,128)(2,1)S(1)}, bf16[80,2048]{1,0:T(8,128)(2,1)S(1)}, u32[]{:S(2)}, u32[]{:S(2)}) collective-permute-start(bf16[80,2048]{1,0:T(8,128)(2,1)S(1)} %collective-permute-done.14.refs_15_), channel_id=1, source_target_pairs={{0,2},{1,15},{2,4},{3,1},{4,6},{5,3},{6,8},{7,5},{8,10},{9,7},{10,... | collective-permute-start | bytes 983048 | tf_op jit(solution)/shard_map/ppermute | solution.py:46
  40.8 8.4 %collective-permute-start.12 = (bf16[48,2048]{1,0:T(8,128)(2,1)S(1)}, bf16[48,2048]{1,0:T(8,128)(2,1)S(1)}, u32[]{:S(2)}, u32[]{:S(2)}) collective-permute-start(bf16[48,2048]{1,0:T(8,128)(2,1)S(1)} %collective-permute-done.5.refs_7_), channel_id=1, source_target_pairs={{0,2},{1,15},{2,4},{3,1},{4,6},{5,3},{6,8},{7,5},{8,10},{9,7},{10,... | collective-permute-start | bytes 589832 | tf_op jit(solution)/shard_map/ppermute | solution.py:46
  43.0 7.4 %collective-permute-start.13 = (bf16[48,2048]{1,0:T(8,128)(2,1)S(1)}, bf16[48,2048]{1,0:T(8,128)(2,1)S(1)}, u32[]{:S(2)}, u32[]{:S(2)}) collective-permute-start(bf16[48,2048]{1,0:T(8,128)(2,1)S(1)} %collective-permute-done.6.refs_8_), channel_id=1, source_target_pairs={{0,14},{1,3},{2,0},{3,5},{4,2},{5,7},{6,4},{7,9},{8,6},{9,11},{10,... | collective-permute-start | bytes 589832 | tf_op jit(solution)/shard_map/ppermute | solution.py:46
  43.0 11.4 %collective-permute-start.2 = (bf16[128,2048]{1,0:T(8,128)(2,1)S(1)}, bf16[128,2048]{1,0:T(8,128)(2,1)S(1)}, u32[]{:S(2)}, u32[]{:S(2)}) collective-permute-start(bf16[128,2048]{1,0:T(8,128)(2,1)S(1)} %get-tuple-element.32.refs_0_), channel_id=1, source_target_pairs={{0,1},{1,0},{2,3},{3,2},{4,5},{5,4},{6,7},{7,6},{8,9},{9,8},{10,11... | collective-permute-start | bytes 1572872 | tf_op jit(solution)/shard_map/ppermute | solution.py:46
  46.6 15.9 %collective-permute-start.3 = (bf16[128,2048]{1,0:T(8,128)(2,1)S(1)}, bf16[128,2048]{1,0:T(8,128)(2,1)S(1)}, u32[]{:S(2)}, u32[]{:S(2)}) collective-permute-start(bf16[128,2048]{1,0:T(8,128)(2,1)S(1)} %collective-permute-done.1.refs_1_), channel_id=1, source_target_pairs={{0,1},{1,0},{2,3},{3,2},{4,5},{5,4},{6,7},{7,6},{8,9},{9,8},{10,11... | collective-permute-start | bytes 1572872 | tf_op jit(solution)/shard_map/ppermute | solution.py:46
  49.2 13.3 %collective-permute-start.18 = (bf16[80,2048]{1,0:T(8,128)(2,1)S(1)}, bf16[80,2048]{1,0:T(8,128)(2,1)S(1)}, u32[]{:S(2)}, u32[]{:S(2)}) collective-permute-start(bf16[80,2048]{1,0:T(8,128)(2,1)S(1)} %collective-permute-done.15.refs_16_), channel_id=1, source_target_pairs={{0,14},{1,3},{2,0},{3,5},{4,2},{5,7},{6,4},{7,9},{8,6},{9,11},{10,... | collective-permute-start | bytes 983048 | tf_op jit(solution)/shard_map/ppermute | solution.py:46
  50.3 12.1 %collective-permute-start.19 = (bf16[80,2048]{1,0:T(8,128)(2,1)S(1)}, bf16[80,2048]{1,0:T(8,128)(2,1)S(1)}, u32[]{:S(2)}, u32[]{:S(2)}) collective-permute-start(bf16[80,2048]{1,0:T(8,128)(2,1)S(1)} %collective-permute-done.17.refs_17_), channel_id=1, source_target_pairs={{0,2},{1,15},{2,4},{3,1},{4,6},{5,3},{6,8},{7,5},{8,10},{9,7},{10,... | collective-permute-start | bytes 983048 | tf_op jit(solution)/shard_map/ppermute | solution.py:46
  53.7 8.8 %collective-permute-start.16 = (bf16[48,2048]{1,0:T(8,128)(2,1)S(1)}, bf16[48,2048]{1,0:T(8,128)(2,1)S(1)}, u32[]{:S(2)}, u32[]{:S(2)}) collective-permute-start(bf16[48,2048]{1,0:T(8,128)(2,1)S(1)} %collective-permute-done.12.refs_9_), channel_id=1, source_target_pairs={{0,2},{1,15},{2,4},{3,1},{4,6},{5,3},{6,8},{7,5},{8,10},{9,7},{10,... | collective-permute-start | bytes 589832 | tf_op jit(solution)/shard_map/ppermute | solution.py:46
  65.4 16.5 %collective-permute-start.21 = (bf16[128,2048]{1,0:T(8,128)(2,1)S(1)}, bf16[128,2048]{1,0:T(8,128)(2,1)S(1)}, u32[]{:S(2)}, u32[]{:S(2)}) collective-permute-start(bf16[128,2048]{1,0:T(8,128)(2,1)S(1)} %get-tuple-element.46.own_ref), channel_id=1, source_target_pairs={{0,1},{1,0},{2,3},{3,2},{4,5},{5,4},{6,7},{7,6},{8,9},{9,8},{10,11... | collective-permute-start | bytes 1572872 | tf_op jit(solution)/shard_map/ppermute | solution.py:46
  70.0 9.1 %collective-permute-start.23 = (bf16[512,256]{1,0:T(8,128)(2,1)S(1)}, bf16[512,256]{1,0:T(8,128)(2,1)S(1)}, u32[]{:S(2)}, u32[]{:S(2)}) collective-permute-start(bf16[512,256]{1,0:T(8,128)(2,1)S(1)} %get-tuple-element.50), channel_id=1, source_target_pairs={{0,2},{1,3},{2,4},{3,5},{4,6},{5,7},{6,8},{7,9},{8,10},{9,11},{10,... | collective-permute-start | bytes 786440 | tf_op jit(solution)/shard_map/ppermute | solution.py:46
  70.4 13.7 %collective-permute-start.29 = (bf16[128,2048]{1,0:T(8,128)(2,1)S(1)}, bf16[128,2048]{1,0:T(8,128)(2,1)S(1)}, u32[]{:S(2)}, u32[]{:S(2)}) collective-permute-start(bf16[128,2048]{1,0:T(8,128)(2,1)S(1)} %get-tuple-element.52.mine), channel_id=1, source_target_pairs={{0,96},{32,0},{64,32},{96,64},{128,224},{160,128},{192,160},{224,1... | collective-permute-start | bytes 1572872 | tf_op jit(solution)/shard_map/ppermute | solution.py:46
  73.1 14.0 %collective-permute-start.28 = (bf16[128,2048]{1,0:T(8,128)(2,1)S(1)}, bf16[128,2048]{1,0:T(8,128)(2,1)S(1)}, u32[]{:S(2)}, u32[]{:S(2)}) collective-permute-start(bf16[128,2048]{1,0:T(8,128)(2,1)S(1)} %get-tuple-element.52.mine), channel_id=1, source_target_pairs={{0,32},{32,64},{64,96},{96,0},{128,160},{160,192},{192,224},{224,1... | collective-permute-start | bytes 1572872 | tf_op jit(solution)/shard_map/ppermute | solution.py:46
  73.1 7.3 %collective-permute-start.25 = (bf16[512,256]{1,0:T(8,128)(2,1)S(1)}, bf16[512,256]{1,0:T(8,128)(2,1)S(1)}, u32[]{:S(2)}, u32[]{:S(2)}) collective-permute-start(bf16[512,256]{1,0:T(8,128)(2,1)S(1)} %get-tuple-element.51), channel_id=1, source_target_pairs={{0,14},{1,15},{2,0},{3,1},{4,2},{5,3},{6,4},{7,5},{8,6},{9,7},{10,... | collective-permute-start | bytes 786440 | tf_op jit(solution)/shard_map/ppermute | solution.py:46
  79.0 10.1 %collective-permute-start.20 = (bf16[512,384]{1,0:T(8,128)(2,1)S(1)}, bf16[512,384]{1,0:T(8,128)(2,1)S(1)}, u32[]{:S(2)}, u32[]{:S(2)}) collective-permute-start(bf16[512,384]{1,0:T(8,128)(2,1)S(1)} %get-tuple-element.45), channel_id=1, source_target_pairs={{0,1},{1,0},{2,3},{3,2},{4,5},{5,4},{6,7},{7,6},{8,9},{9,8},{10,11... | collective-permute-start | bytes 1179656 | tf_op jit(solution)/shard_map/ppermute | solution.py:46
  80.4 8.6 %collective-permute-start.24 = (bf16[256,256]{1,0:T(8,128)(2,1)S(1)}, bf16[256,256]{1,0:T(8,128)(2,1)S(1)}, u32[]{:S(2)}, u32[]{:S(2)}) collective-permute-start(bf16[256,256]{1,0:T(8,128)(2,1)S(1)} %slice.80), channel_id=1, source_target_pairs={{0,1},{1,0},{2,3},{3,2},{4,5},{5,4},{6,7},{7,6},{8,9},{9,8},{10,11... | collective-permute-start | bytes 393224 | tf_op jit(solution)/shard_map/ppermute | solution.py:46
  81.9 7.2 %collective-permute-start.26 = (bf16[256,256]{1,0:T(8,128)(2,1)S(1)}, bf16[256,256]{1,0:T(8,128)(2,1)S(1)}, u32[]{:S(2)}, u32[]{:S(2)}) collective-permute-start(bf16[256,256]{1,0:T(8,128)(2,1)S(1)} %slice.81), channel_id=1, source_target_pairs={{0,1},{1,0},{2,3},{3,2},{4,5},{5,4},{6,7},{7,6},{8,9},{9,8},{10,11... | collective-permute-start | bytes 393224 | tf_op jit(solution)/shard_map/ppermute | solution.py:46
  84.1 5.1 %collective-permute-start.22 = (bf16[256,256]{1,0:T(8,128)(2,1)S(1)}, bf16[256,256]{1,0:T(8,128)(2,1)S(1)}, u32[]{:S(2)}, u32[]{:S(2)}) collective-permute-start(bf16[256,256]{1,0:T(8,128)(2,1)S(1)} %get-tuple-element.49), channel_id=1, source_target_pairs={{0,1},{1,0},{2,3},{3,2},{4,5},{5,4},{6,7},{7,6},{8,9},{9,8},{10,11... | collective-permute-start | bytes 393224 | tf_op jit(solution)/shard_map/ppermute | solution.py:46
  87.1 7.7 %collective-permute-start.31 = (bf16[64,2048]{1,0:T(8,128)(2,1)S(1)}, bf16[64,2048]{1,0:T(8,128)(2,1)S(1)}, u32[]{:S(2)}, u32[]{:S(2)}) collective-permute-start(bf16[64,2048]{1,0:T(8,128)(2,1)S(1)} %slice.85), channel_id=1, source_target_pairs={{0,96},{32,0},{64,32},{96,64},{128,224},{160,128},{192,160},{224,1... | collective-permute-start | bytes 786440 | tf_op jit(solution)/shard_map/ppermute | solution.py:46
  89.1 8.9 %collective-permute-start.30 = (bf16[64,2048]{1,0:T(8,128)(2,1)S(1)}, bf16[64,2048]{1,0:T(8,128)(2,1)S(1)}, u32[]{:S(2)}, u32[]{:S(2)}) collective-permute-start(bf16[64,2048]{1,0:T(8,128)(2,1)S(1)} %slice.84), channel_id=1, source_target_pairs={{0,32},{32,64},{64,96},{96,0},{128,160},{160,192},{192,224},{224,1... | collective-permute-start | bytes 786440 | tf_op jit(solution)/shard_map/ppermute | solution.py:46
  93.2 4.8 %collective-permute-start.27 = (bf16[256,256]{1,0:T(8,128)(2,1)S(1)}, bf16[256,256]{1,0:T(8,128)(2,1)S(1)}, u32[]{:S(2)}, u32[]{:S(2)}) collective-permute-start(bf16[256,256]{1,0:T(8,128)(2,1)S(1)} %get-tuple-element.57), channel_id=1, source_target_pairs={{0,16},{1,17},{2,18},{3,19},{4,20},{5,21},{6,22},{7,23},{8,24},{9,... | collective-permute-start | bytes 393224 | tf_op jit(solution)/shard_map/ppermute | solution.py:46
  99.3 3.5 %collective-permute-start.32 = (bf16[128,2048]{1,0:T(8,128)(2,1)S(1)}, bf16[128,2048]{1,0:T(8,128)(2,1)S(1)}, u32[]{:S(2)}, u32[]{:S(2)}) collective-permute-start(bf16[128,2048]{1,0:T(8,128)(2,1)S(1)} %get-tuple-element.54), channel_id=1, source_target_pairs={{0,1},{1,0},{2,3},{3,2},{4,5},{5,4},{6,7},{7,6},{8,9},{9,8},{10,11... | collective-permute-start | bytes 1572872 | tf_op jit(solution)/shard_map/ppermute | solution.py:46
  (4 other events, 33.9 us)

commit v12 on v11

--- a/solution.py
+++ b/solution.py
@@ -313,12 +313,18 @@
     a_one, a_two, b_one, b_two = first, second, first, second
     for step in range(1, 5):
         if step == 2:
+            to_send = after(normed, one[0, 1])
+            across = send(to_send, OTHER_X)
+            beside = send(to_send, OTHER_CORE)
+            beside_across = send(across, OTHER_CORE)
             a_two = b_two = after(second, a_one, b_one)
         if step > 1:
             if step > 2:
                 before = one[0, step - 2], one[1, step - 2]
                 a_two, b_two = lax.optimization_barrier((a_two, b_two, *before))[:2]
             two[0, step - 1] = a_two = send(a_two, AHEAD)
+            if step == 4:
+                b_two = after(b_two, across, beside, beside_across)
             two[1, step - 1] = b_two = send(b_two, BEHIND)
         if step > 2:
             before = two[0, step - 2], two[1, step - 2]
@@ -330,11 +336,6 @@
     two[0, 4] = send(a_two, AHEAD)
     firsts = [one[s] for s in STEPS]
     seconds = [two[s] for s in STEPS]
-
-    to_send = after(normed, one[0, 1])
-    across = send(to_send, OTHER_X)
-    beside = send(to_send, OTHER_CORE)
-    beside_across = send(across, OTHER_CORE)
 
     half = jax.ShapeDtypeStruct((ROWS, 3 * 128), bf16)
     keep, to_swap, g_own, far_table, out_own, *edges = on_chip(

time: 104 us -> 102 us (0.981)
  waiting for transfers between devices: 41.6 us -> 35.9 us
  starting transfers between devices: 46 us -> 49.9 us
    ppermute x33, waiting for transfers between devices: 41.6 us -> 35.9 us  [send(): return lax.ppermute(value, axis, route)]
    ppermute x33, starting transfers between devices: 46 us -> 49.9 us  [send(): return lax.ppermute(value, axis, route)]
  transfers between devices with their start and end apart: 33 -> 33, of which waited for: 14 -> 16; matrix products, arithmetic and copies ran while one was open for 0% -> 0% of each run, Pallas kernels for 7% -> 7%
where the time goes in v12:
time: 102 us
  starting transfers between devices  49.9 us (49%)
  waiting for transfers between devices  35.9 us (35%)
  Pallas kernels  11.5 us (11%)
  other arithmetic  2.31 us (2%)
  local copies, waits for them, and re-layouts  1.29 us (1%)
    ppermute x33, starting transfers between devices, send(): return lax.ppermute(value, axis, route)  49.9 us
    ppermute x33, waiting for transfers between devices, send(): return lax.ppermute(value, axis, route)  35.9 us
    pallas_call x5, Pallas kernels, on_chip(): pl.pallas_call(kernel, out_shape=out_shape, in_specs=specs, out_specs=jax...  11.5 us
  transfers between devices with their start and end apart: 33, of which 16 were waited for; matrix products, arithmetic and copies ran while one was open for 0% of the time, Pallas kernels for 7%

profile of v12, /device:TPU:1, one launch (start us, length us, event | category | flops | bytes accessed | tf_op | source)
XLA Modules:
  0.0 101.8 jit_solution(1958617306801772188)
XLA Ops:
  2.3 3.3 %collective-permute-start.8 = (bf16[128,64]{1,0:T(8,128)(2,1)S(1)}, bf16[128,64]{1,0:T(8,128)(2,1)S(1)}, u32[]{:S(2)}, u32[]{:S(2)}) collective-permute-start(bf16[128,64]{1,0:T(8,128)(2,1)S(1)} %bitcast.43), channel_id=1, source_target_pairs={{0,1},{1,0},{2,3},{3,2},{4,5},{5,4},{6,7},{7,6},{8,9},{9,8},{10,11... | collective-permute-start | bytes 49160 | tf_op jit(solution)/shard_map/ppermute | solution.py:46
  5.6 3.9 %collective-permute-start = (bf16[48,2048]{1,0:T(8,128)(2,1)S(1)}, bf16[48,2048]{1,0:T(8,128)(2,1)S(1)}, u32[]{:S(2)}, u32[]{:S(2)}) collective-permute-start(bf16[48,2048]{1,0:T(8,128)(2,1)S(1)} %bitcast.34), channel_id=1, source_target_pairs={{0,2},{1,15},{2,4},{3,1},{4,6},{5,3},{6,8},{7,5},{8,10},{9,7},{10,... | collective-permute-start | bytes 589832 | tf_op jit(solution)/shard_map/ppermute | solution.py:46
  11.5 1.3 %collective-permute-start.7 = (bf16[8,2048]{1,0:T(8,128)(2,1)S(1)}, bf16[8,2048]{1,0:T(8,128)(2,1)S(1)}, u32[]{:S(2)}, u32[]{:S(2)}) collective-permute-start(bf16[8,2048]{1,0:T(8,128)(2,1)S(1)} %get-tuple-element.34), channel_id=1, source_target_pairs={{0,16},{1,17},{2,18},{3,19},{4,20},{5,21},{6,22},{7,23},{8,24},{9,... | collective-permute-start | bytes 98312 | tf_op jit(solution)/shard_map/ppermute | solution.py:46
  13.3 1.4 %collective-permute-done.7 = bf16[8,2048]{1,0:T(8,128)(2,1)S(1)} collective-permute-done((bf16[8,2048]{1,0:T(8,128)(2,1)S(1)}, bf16[8,2048]{1,0:T(8,128)(2,1)S(1)}, u32[]{:S(2)}, u32[]{:S(2)}) %collective-permute-start.7) | collective-permute-done | bytes 32800 | tf_op jit(solution)/shard_map/ppermute | solution.py:46
  14.7 1.4 %collective-permute-done.9 = bf16[128,128]{1,0:T(8,128)(2,1)S(1)} collective-permute-done((bf16[128,128]{1,0:T(8,128)(2,1)S(1)}, bf16[128,128]{1,0:T(8,128)(2,1)S(1)}, u32[]{:S(2)}, u32[]{:S(2)}) %collective-permute-start.9) | collective-permute-done | bytes 32800 | tf_op jit(solution)/shard_map/ppermute | solution.py:46
  16.8 2.7 %collective-permute-start.10 = (bf16[80,2048]{1,0:T(8,128)(2,1)S(1)}, bf16[80,2048]{1,0:T(8,128)(2,1)S(1)}, u32[]{:S(2)}, u32[]{:S(2)}) collective-permute-start(bf16[80,2048]{1,0:T(8,128)(2,1)S(1)} %pad_maximum_fusion.1.refs_12_), channel_id=1, source_target_pairs={{0,2},{1,15},{2,4},{3,1},{4,6},{5,3},{6,8},{7,5},{8,10},{9,7},{10,... | collective-permute-start | bytes 983048 | tf_op jit(solution)/shard_map/ppermute | solution.py:46
  19.4 4.5 %collective-permute-done.11.refs_14_ = bf16[80,2048]{1,0:T(8,128)(2,1)S(1)} collective-permute-done((bf16[80,2048]{1,0:T(8,128)(2,1)S(1)}, bf16[80,2048]{1,0:T(8,128)(2,1)S(1)}, u32[]{:S(2)}, u32[]{:S(2)}) %collective-permute-start.11) | collective-permute-done | bytes 327712 | tf_op jit(solution)/shard_map/ppermute | solution.py:46
  24.4 3.4 %collective-permute-start.14 = (bf16[80,2048]{1,0:T(8,128)(2,1)S(1)}, bf16[80,2048]{1,0:T(8,128)(2,1)S(1)}, u32[]{:S(2)}, u32[]{:S(2)}) collective-permute-start(bf16[80,2048]{1,0:T(8,128)(2,1)S(1)} %collective-permute-done.10.refs_13_), channel_id=1, source_target_pairs={{0,2},{1,15},{2,4},{3,1},{4,6},{5,3},{6,8},{7,5},{8,10},{9,7},{10,... | collective-permute-start | bytes 983048 | tf_op jit(solution)/shard_map/ppermute | solution.py:46
  27.8 2.7 %collective-permute-start.5 = (bf16[48,2048]{1,0:T(8,128)(2,1)S(1)}, bf16[48,2048]{1,0:T(8,128)(2,1)S(1)}, u32[]{:S(2)}, u32[]{:S(2)}) collective-permute-start(bf16[48,2048]{1,0:T(8,128)(2,1)S(1)} %collective-permute-done.refs_5_), channel_id=1, source_target_pairs={{0,2},{1,15},{2,4},{3,1},{4,6},{5,3},{6,8},{7,5},{8,10},{9,7},{10,... | collective-permute-start | bytes 589832 | tf_op jit(solution)/shard_map/ppermute | solution.py:46
  30.5 3.0 %collective-permute-start.2 = (bf16[128,2048]{1,0:T(8,128)(2,1)S(1)}, bf16[128,2048]{1,0:T(8,128)(2,1)S(1)}, u32[]{:S(2)}, u32[]{:S(2)}) collective-permute-start(bf16[128,2048]{1,0:T(8,128)(2,1)S(1)} %get-tuple-element.33.refs_0_), channel_id=1, source_target_pairs={{0,1},{1,0},{2,3},{3,2},{4,5},{5,4},{6,7},{7,6},{8,9},{9,8},{10,11... | collective-permute-start | bytes 1572872 | tf_op jit(solution)/shard_map/ppermute | solution.py:46
  33.5 1.6 %collective-permute-done.5.refs_7_ = bf16[48,2048]{1,0:T(8,128)(2,1)S(1)} collective-permute-done((bf16[48,2048]{1,0:T(8,128)(2,1)S(1)}, bf16[48,2048]{1,0:T(8,128)(2,1)S(1)}, u32[]{:S(2)}, u32[]{:S(2)}) %collective-permute-start.5) | collective-permute-done | bytes 196640 | tf_op jit(solution)/shard_map/ppermute | solution.py:46
  35.8 2.8 %collective-permute-start.17 = (bf16[80,2048]{1,0:T(8,128)(2,1)S(1)}, bf16[80,2048]{1,0:T(8,128)(2,1)S(1)}, u32[]{:S(2)}, u32[]{:S(2)}) collective-permute-start(bf16[80,2048]{1,0:T(8,128)(2,1)S(1)} %collective-permute-done.14.refs_15_), channel_id=1, source_target_pairs={{0,2},{1,15},{2,4},{3,1},{4,6},{5,3},{6,8},{7,5},{8,10},{9,7},{10,... | collective-permute-start | bytes 983048 | tf_op jit(solution)/shard_map/ppermute | solution.py:46
  39.6 1.3 %collective-permute-start.13 = (bf16[48,2048]{1,0:T(8,128)(2,1)S(1)}, bf16[48,2048]{1,0:T(8,128)(2,1)S(1)}, u32[]{:S(2)}, u32[]{:S(2)}) collective-permute-start(bf16[48,2048]{1,0:T(8,128)(2,1)S(1)} %collective-permute-done.6.refs_8_), channel_id=1, source_target_pairs={{0,14},{1,3},{2,0},{3,5},{4,2},{5,7},{6,4},{7,9},{8,6},{9,11},{10,... | collective-permute-start | bytes 589832 | tf_op jit(solution)/shard_map/ppermute | solution.py:46
  40.9 6.5 %collective-permute-done.12.refs_9_ = bf16[48,2048]{1,0:T(8,128)(2,1)S(1)} collective-permute-done((bf16[48,2048]{1,0:T(8,128)(2,1)S(1)}, bf16[48,2048]{1,0:T(8,128)(2,1)S(1)}, u32[]{:S(2)}, u32[]{:S(2)}) %collective-permute-start.12) | collective-permute-done | bytes 196640 | tf_op jit(solution)/shard_map/ppermute | solution.py:46
  47.4 1.5 %collective-permute-done.13.refs_10_ = bf16[48,2048]{1,0:T(8,128)(2,1)S(1)} collective-permute-done((bf16[48,2048]{1,0:T(8,128)(2,1)S(1)}, bf16[48,2048]{1,0:T(8,128)(2,1)S(1)}, u32[]{:S(2)}, u32[]{:S(2)}) %collective-permute-start.13) | collective-permute-done | bytes 196640 | tf_op jit(solution)/shard_map/ppermute | solution.py:46
  48.9 2.9 %collective-permute-start.19 = (bf16[80,2048]{1,0:T(8,128)(2,1)S(1)}, bf16[80,2048]{1,0:T(8,128)(2,1)S(1)}, u32[]{:S(2)}, u32[]{:S(2)}) collective-permute-start(bf16[80,2048]{1,0:T(8,128)(2,1)S(1)} %collective-permute-done.17.refs_17_), channel_id=1, source_target_pairs={{0,2},{1,15},{2,4},{3,1},{4,6},{5,3},{6,8},{7,5},{8,10},{9,7},{10,... | collective-permute-start | bytes 983048 | tf_op jit(solution)/shard_map/ppermute | solution.py:46
  51.8 2.7 %collective-permute-start.16 = (bf16[48,2048]{1,0:T(8,128)(2,1)S(1)}, bf16[48,2048]{1,0:T(8,128)(2,1)S(1)}, u32[]{:S(2)}, u32[]{:S(2)}) collective-permute-start(bf16[48,2048]{1,0:T(8,128)(2,1)S(1)} %collective-permute-done.12.refs_9_), channel_id=1, source_target_pairs={{0,2},{1,15},{2,4},{3,1},{4,6},{5,3},{6,8},{7,5},{8,10},{9,7},{10,... | collective-permute-start | bytes 589832 | tf_op jit(solution)/shard_map/ppermute | solution.py:46
  54.5 4.1 %collective-permute-done.16.refs_11_ = bf16[48,2048]{1,0:T(8,128)(2,1)S(1)} collective-permute-done((bf16[48,2048]{1,0:T(8,128)(2,1)S(1)}, bf16[48,2048]{1,0:T(8,128)(2,1)S(1)}, u32[]{:S(2)}, u32[]{:S(2)}) %collective-permute-start.16) | collective-permute-done | bytes 196640 | tf_op jit(solution)/shard_map/ppermute | solution.py:46
  58.6 2.2 %collective-permute-done.18.refs_18_ = bf16[80,2048]{1,0:T(8,128)(2,1)S(1)} collective-permute-done((bf16[80,2048]{1,0:T(8,128)(2,1)S(1)}, bf16[80,2048]{1,0:T(8,128)(2,1)S(1)}, u32[]{:S(2)}, u32[]{:S(2)}) %collective-permute-start.18) | collective-permute-done | bytes 327712 | tf_op jit(solution)/shard_map/ppermute | solution.py:46
  60.8 2.9 %shard_map.83 = (bf16[512,384]{1,0:T(8,128)(2,1)S(1)}, bf16[512,384]{1,0:T(8,128)(2,1)S(1)}, bf16[128,2048]{1,0:T(8,128)(2,1)S(1)}, bf16[512,2048]{1,0:T(8,128)(...) custom-call(s32[6]{0:T(128)S(1)} %stack.35.index, ...), custom_call_target="tpu_custom_call" | custom-call | flops 1610612736 | bytes 4194304 | tf_op jit(solution)/shard_map/pallas_call | solution.py:245
  63.7 4.6 %collective-permute-start.21 = (bf16[128,2048]{1,0:T(8,128)(2,1)S(1)}, bf16[128,2048]{1,0:T(8,128)(2,1)S(1)}, u32[]{:S(2)}, u32[]{:S(2)}) collective-permute-start(bf16[128,2048]{1,0:T(8,128)(2,1)S(1)} %get-tuple-element.48.own_ref), channel_id=1, source_target_pairs={{0,1},{1,0},{2,3},{3,2},{4,5},{5,4},{6,7},{7,6},{8,9},{9,8},{10,11... | collective-permute-start | bytes 1572872 | tf_op jit(solution)/shard_map/ppermute | solution.py:46
  68.3 2.7 %collective-permute-start.29 = (bf16[128,2048]{1,0:T(8,128)(2,1)S(1)}, bf16[128,2048]{1,0:T(8,128)(2,1)S(1)}, u32[]{:S(2)}, u32[]{:S(2)}) collective-permute-start(bf16[128,2048]{1,0:T(8,128)(2,1)S(1)} %get-tuple-element.54.mine), channel_id=1, source_target_pairs={{0,96},{32,0},{64,32},{96,64},{128,224},{160,128},{192,160},{224,1... | collective-permute-start | bytes 1572872 | tf_op jit(solution)/shard_map/ppermute | solution.py:46
  71.0 2.7 %collective-permute-start.25 = (bf16[512,256]{1,0:T(8,128)(2,1)S(1)}, bf16[512,256]{1,0:T(8,128)(2,1)S(1)}, u32[]{:S(2)}, u32[]{:S(2)}) collective-permute-start(bf16[512,256]{1,0:T(8,128)(2,1)S(1)} %get-tuple-element.53), channel_id=1, source_target_pairs={{0,14},{1,15},{2,0},{3,1},{4,2},{5,3},{6,4},{7,5},{8,6},{9,7},{10,... | collective-permute-start | bytes 786440 | tf_op jit(solution)/shard_map/ppermute | solution.py:46
  73.7 3.6 %collective-permute-done.23.below_ref = bf16[512,256]{1,0:T(8,128)(2,1)S(1)} collective-permute-done((bf16[512,256]{1,0:T(8,128)(2,1)S(1)}, bf16[512,256]{1,0:T(8,128)(2,1)S(1)}, u32[]{:S(2)}, u32[]{:S(2)}) %collective-permute-start.23) | collective-permute-done | bytes 262176 | tf_op jit(solution)/shard_map/ppermute | solution.py:46
  78.7 1.5 %collective-permute-start.24 = (bf16[256,256]{1,0:T(8,128)(2,1)S(1)}, bf16[256,256]{1,0:T(8,128)(2,1)S(1)}, u32[]{:S(2)}, u32[]{:S(2)}) collective-permute-start(bf16[256,256]{1,0:T(8,128)(2,1)S(1)} %slice.80), channel_id=1, source_target_pairs={{0,1},{1,0},{2,3},{3,2},{4,5},{5,4},{6,7},{7,6},{8,9},{9,8},{10,11... | collective-permute-start | bytes 393224 | tf_op jit(solution)/shard_map/ppermute | solution.py:46
  80.3 2.1 %shard_map.84 = (bf16[256,256]{1,0:T(8,128)(2,1)S(1)}, bf16[256,256]{1,0:T(8,128)(2,1)S(1)}) custom-call(s32[6]{0:T(128)S(1)} %stack.35.index, bf16[128,2048]{1,0:T(8,128)(2,1)S(1)} %get-tuple-element.48.own_ref, bf16[128,2048]{1,0:T(8,128)(2,1)S(1)} %collective-permute-done.21.other_ref, bf16[512,2048]{1,0:T(8,128)(2,1)S(1)} %get-tuple-element.49.table), custom_call_target="tpu_custom_call" | custom-call | flops 536870912 | bytes 4194304 | tf_op jit(solution)/shard_map/pallas_call | solution.py:245
  83.2 2.1 %collective-permute-done.28.prev = bf16[128,2048]{1,0:T(8,128)(2,1)S(1)} collective-permute-done((bf16[128,2048]{1,0:T(8,128)(2,1)S(1)}, bf16[128,2048]{1,0:T(8,128)(2,1)S(1)}, u32[]{:S(2)}, u32[]{:S(2)}) %collective-permute-start.28) | collective-permute-done | bytes 524320 | tf_op jit(solution)/shard_map/ppermute | solution.py:46
  85.3 1.4 %collective-permute-start.31 = (bf16[64,2048]{1,0:T(8,128)(2,1)S(1)}, bf16[64,2048]{1,0:T(8,128)(2,1)S(1)}, u32[]{:S(2)}, u32[]{:S(2)}) collective-permute-start(bf16[64,2048]{1,0:T(8,128)(2,1)S(1)} %slice.85), channel_id=1, source_target_pairs={{0,96},{32,0},{64,32},{96,64},{128,224},{160,128},{192,160},{224,1... | collective-permute-start | bytes 786440 | tf_op jit(solution)/shard_map/ppermute | solution.py:46
  87.1 4.0 %shard_map.85 = bf16[2,256,256]{2,1,0:T(8,128)(2,1)S(1)} custom-call(s32[6]{0:T(128)S(1)} %stack.35.index, bf16[512,384]{1,0:T(8,128)(2,1)S(1)} %get-tuple-element.46.keep_ref, bf16[512,384]{1,0:T(8,128)(2,1)S(1)} %collective-permute-done.20.got_ref, bf16[256,256]{1,0:T(8,128)(2,1)S(1)} %get-tuple-element.50.g_keep, ...), custom_call_target="tpu_custom_call" | custom-call | flops 1342177280 | bytes 4194304 | tf_op jit(solution)/shard_map/pallas_call | solution.py:245
  92.4 3.4 %collective-permute-done.30.far_a = bf16[64,2048]{1,0:T(8,128)(2,1)S(1)} collective-permute-done((bf16[64,2048]{1,0:T(8,128)(2,1)S(1)}, bf16[64,2048]{1,0:T(8,128)(2,1)S(1)}, u32[]{:S(2)}, u32[]{:S(2)}) %collective-permute-start.30) | collective-permute-done | bytes 262176 | tf_op jit(solution)/shard_map/ppermute | solution.py:46
  97.1 2.2 %collective-permute-start.32 = (bf16[128,2048]{1,0:T(8,128)(2,1)S(1)}, bf16[128,2048]{1,0:T(8,128)(2,1)S(1)}, u32[]{:S(2)}, u32[]{:S(2)}) collective-permute-start(bf16[128,2048]{1,0:T(8,128)(2,1)S(1)} %get-tuple-element.56), channel_id=1, source_target_pairs={{0,1},{1,0},{2,3},{3,2},{4,5},{5,4},{6,7},{7,6},{8,9},{9,8},{10,11... | collective-permute-start | bytes 1572872 | tf_op jit(solution)/shard_map/ppermute | solution.py:46
  99.4 1.5 %collective-permute-done.32 = bf16[128,2048]{1,0:T(8,128)(2,1)S(1)} collective-permute-done((bf16[128,2048]{1,0:T(8,128)(2,1)S(1)}, bf16[128,2048]{1,0:T(8,128)(2,1)S(1)}, u32[]{:S(2)}, u32[]{:S(2)}) %collective-permute-start.32) | collective-permute-done | bytes 524320 | tf_op jit(solution)/shard_map/ppermute | solution.py:46
  (69 shorter events, 13.1 us)
Async XLA Ops:
  2.3 10.5 %collective-permute-start.8 = (bf16[128,64]{1,0:T(8,128)(2,1)S(1)}, bf16[128,64]{1,0:T(8,128)(2,1)S(1)}, u32[]{:S(2)}, u32[]{:S(2)}) collective-permute-start(bf16[128,64]{1,0:T(8,128)(2,1)S(1)} %bitcast.43), channel_id=1, source_target_pairs={{0,1},{1,0},{2,3},{3,2},{4,5},{5,4},{6,7},{7,6},{8,9},{9,8},{10,11... | collective-permute-start | bytes 49160 | tf_op jit(solution)/shard_map/ppermute | solution.py:46
  5.6 11.0 %collective-permute-start.4 = (bf16[48,2048]{1,0:T(8,128)(2,1)S(1)}, bf16[48,2048]{1,0:T(8,128)(2,1)S(1)}, u32[]{:S(2)}, u32[]{:S(2)}) collective-permute-start(bf16[48,2048]{1,0:T(8,128)(2,1)S(1)} %bitcast.33), channel_id=1, source_target_pairs={{0,14},{1,3},{2,0},{3,5},{4,2},{5,7},{6,4},{7,9},{8,6},{9,11},{10,... | collective-permute-start | bytes 589832 | tf_op jit(solution)/shard_map/ppermute | solution.py:46
  5.6 10.6 %collective-permute-start = (bf16[48,2048]{1,0:T(8,128)(2,1)S(1)}, bf16[48,2048]{1,0:T(8,128)(2,1)S(1)}, u32[]{:S(2)}, u32[]{:S(2)}) collective-permute-start(bf16[48,2048]{1,0:T(8,128)(2,1)S(1)} %bitcast.34), channel_id=1, source_target_pairs={{0,2},{1,15},{2,4},{3,1},{4,6},{5,3},{6,8},{7,5},{8,10},{9,7},{10,... | collective-permute-start | bytes 589832 | tf_op jit(solution)/shard_map/ppermute | solution.py:46
  11.5 3.1 %collective-permute-start.7 = (bf16[8,2048]{1,0:T(8,128)(2,1)S(1)}, bf16[8,2048]{1,0:T(8,128)(2,1)S(1)}, u32[]{:S(2)}, u32[]{:S(2)}) collective-permute-start(bf16[8,2048]{1,0:T(8,128)(2,1)S(1)} %get-tuple-element.34), channel_id=1, source_target_pairs={{0,16},{1,17},{2,18},{3,19},{4,20},{5,21},{6,22},{7,23},{8,24},{9,... | collective-permute-start | bytes 98312 | tf_op jit(solution)/shard_map/ppermute | solution.py:46
  16.3 17.1 %collective-permute-start.1 = (bf16[128,2048]{1,0:T(8,128)(2,1)S(1)}, bf16[128,2048]{1,0:T(8,128)(2,1)S(1)}, u32[]{:S(2)}, u32[]{:S(2)}) collective-permute-start(bf16[128,2048]{1,0:T(8,128)(2,1)S(1)} %get-tuple-element.33.refs_0_), channel_id=1, source_target_pairs={{0,16},{1,17},{2,18},{3,19},{4,20},{5,21},{6,22},{7,23},{8,24},{9,... | collective-permute-start | bytes 1572872 | tf_op jit(solution)/shard_map/ppermute | solution.py:46
  16.7 7.2 %collective-permute-start.11 = (bf16[80,2048]{1,0:T(8,128)(2,1)S(1)}, bf16[80,2048]{1,0:T(8,128)(2,1)S(1)}, u32[]{:S(2)}, u32[]{:S(2)}) collective-permute-start(bf16[80,2048]{1,0:T(8,128)(2,1)S(1)} %pad_maximum_fusion.1.refs_12_), channel_id=1, source_target_pairs={{0,14},{1,3},{2,0},{3,5},{4,2},{5,7},{6,4},{7,9},{8,6},{9,11},{10,... | collective-permute-start | bytes 983048 | tf_op jit(solution)/shard_map/ppermute | solution.py:46
  16.8 7.6 %collective-permute-start.10 = (bf16[80,2048]{1,0:T(8,128)(2,1)S(1)}, bf16[80,2048]{1,0:T(8,128)(2,1)S(1)}, u32[]{:S(2)}, u32[]{:S(2)}) collective-permute-start(bf16[80,2048]{1,0:T(8,128)(2,1)S(1)} %pad_maximum_fusion.1.refs_12_), channel_id=1, source_target_pairs={{0,2},{1,15},{2,4},{3,1},{4,6},{5,3},{6,8},{7,5},{8,10},{9,7},{10,... | collective-permute-start | bytes 983048 | tf_op jit(solution)/shard_map/ppermute | solution.py:46
  19.4 11.0 %collective-permute-start.6 = (bf16[48,2048]{1,0:T(8,128)(2,1)S(1)}, bf16[48,2048]{1,0:T(8,128)(2,1)S(1)}, u32[]{:S(2)}, u32[]{:S(2)}) collective-permute-start(bf16[48,2048]{1,0:T(8,128)(2,1)S(1)} %collective-permute-done.4.refs_6_), channel_id=1, source_target_pairs={{0,14},{1,3},{2,0},{3,5},{4,2},{5,7},{6,4},{7,9},{8,6},{9,11},{10,... | collective-permute-start | bytes 589832 | tf_op jit(solution)/shard_map/ppermute | solution.py:46
  24.4 10.8 %collective-permute-start.14 = (bf16[80,2048]{1,0:T(8,128)(2,1)S(1)}, bf16[80,2048]{1,0:T(8,128)(2,1)S(1)}, u32[]{:S(2)}, u32[]{:S(2)}) collective-permute-start(bf16[80,2048]{1,0:T(8,128)(2,1)S(1)} %collective-permute-done.10.refs_13_), channel_id=1, source_target_pairs={{0,2},{1,15},{2,4},{3,1},{4,6},{5,3},{6,8},{7,5},{8,10},{9,7},{10,... | collective-permute-start | bytes 983048 | tf_op jit(solution)/shard_map/ppermute | solution.py:46
  27.8 8.0 %collective-permute-start.15 = (bf16[80,2048]{1,0:T(8,128)(2,1)S(1)}, bf16[80,2048]{1,0:T(8,128)(2,1)S(1)}, u32[]{:S(2)}, u32[]{:S(2)}) collective-permute-start(bf16[80,2048]{1,0:T(8,128)(2,1)S(1)} %collective-permute-done.11.refs_14_), channel_id=1, source_target_pairs={{0,14},{1,3},{2,0},{3,5},{4,2},{5,7},{6,4},{7,9},{8,6},{9,11},{10,... | collective-permute-start | bytes 983048 | tf_op jit(solution)/shard_map/ppermute | solution.py:46
  27.8 7.4 %collective-permute-start.5 = (bf16[48,2048]{1,0:T(8,128)(2,1)S(1)}, bf16[48,2048]{1,0:T(8,128)(2,1)S(1)}, u32[]{:S(2)}, u32[]{:S(2)}) collective-permute-start(bf16[48,2048]{1,0:T(8,128)(2,1)S(1)} %collective-permute-done.refs_5_), channel_id=1, source_target_pairs={{0,2},{1,15},{2,4},{3,1},{4,6},{5,3},{6,8},{7,5},{8,10},{9,7},{10,... | collective-permute-start | bytes 589832 | tf_op jit(solution)/shard_map/ppermute | solution.py:46
  30.5 21.3 %collective-permute-start.2 = (bf16[128,2048]{1,0:T(8,128)(2,1)S(1)}, bf16[128,2048]{1,0:T(8,128)(2,1)S(1)}, u32[]{:S(2)}, u32[]{:S(2)}) collective-permute-start(bf16[128,2048]{1,0:T(8,128)(2,1)S(1)} %get-tuple-element.33.refs_0_), channel_id=1, source_target_pairs={{0,1},{1,0},{2,3},{3,2},{4,5},{5,4},{6,7},{7,6},{8,9},{9,8},{10,11... | collective-permute-start | bytes 1572872 | tf_op jit(solution)/shard_map/ppermute | solution.py:46
  33.4 18.4 %collective-permute-start.3 = (bf16[128,2048]{1,0:T(8,128)(2,1)S(1)}, bf16[128,2048]{1,0:T(8,128)(2,1)S(1)}, u32[]{:S(2)}, u32[]{:S(2)}) collective-permute-start(bf16[128,2048]{1,0:T(8,128)(2,1)S(1)} %collective-permute-done.1.refs_1_), channel_id=1, source_target_pairs={{0,1},{1,0},{2,3},{3,2},{4,5},{5,4},{6,7},{7,6},{8,9},{9,8},{10,11... | collective-permute-start | bytes 1572872 | tf_op jit(solution)/shard_map/ppermute | solution.py:46
  35.8 13.1 %collective-permute-start.17 = (bf16[80,2048]{1,0:T(8,128)(2,1)S(1)}, bf16[80,2048]{1,0:T(8,128)(2,1)S(1)}, u32[]{:S(2)}, u32[]{:S(2)}) collective-permute-start(bf16[80,2048]{1,0:T(8,128)(2,1)S(1)} %collective-permute-done.14.refs_15_), channel_id=1, source_target_pairs={{0,2},{1,15},{2,4},{3,1},{4,6},{5,3},{6,8},{7,5},{8,10},{9,7},{10,... | collective-permute-start | bytes 983048 | tf_op jit(solution)/shard_map/ppermute | solution.py:46
  38.6 8.8 %collective-permute-start.12 = (bf16[48,2048]{1,0:T(8,128)(2,1)S(1)}, bf16[48,2048]{1,0:T(8,128)(2,1)S(1)}, u32[]{:S(2)}, u32[]{:S(2)}) collective-permute-start(bf16[48,2048]{1,0:T(8,128)(2,1)S(1)} %collective-permute-done.5.refs_7_), channel_id=1, source_target_pairs={{0,2},{1,15},{2,4},{3,1},{4,6},{5,3},{6,8},{7,5},{8,10},{9,7},{10,... | collective-permute-start | bytes 589832 | tf_op jit(solution)/shard_map/ppermute | solution.py:46
  39.6 9.3 %collective-permute-start.13 = (bf16[48,2048]{1,0:T(8,128)(2,1)S(1)}, bf16[48,2048]{1,0:T(8,128)(2,1)S(1)}, u32[]{:S(2)}, u32[]{:S(2)}) collective-permute-start(bf16[48,2048]{1,0:T(8,128)(2,1)S(1)} %collective-permute-done.6.refs_8_), channel_id=1, source_target_pairs={{0,14},{1,3},{2,0},{3,5},{4,2},{5,7},{6,4},{7,9},{8,6},{9,11},{10,... | collective-permute-start | bytes 589832 | tf_op jit(solution)/shard_map/ppermute | solution.py:46
  48.9 9.7 %collective-permute-start.19 = (bf16[80,2048]{1,0:T(8,128)(2,1)S(1)}, bf16[80,2048]{1,0:T(8,128)(2,1)S(1)}, u32[]{:S(2)}, u32[]{:S(2)}) collective-permute-start(bf16[80,2048]{1,0:T(8,128)(2,1)S(1)} %collective-permute-done.17.refs_17_), channel_id=1, source_target_pairs={{0,2},{1,15},{2,4},{3,1},{4,6},{5,3},{6,8},{7,5},{8,10},{9,7},{10,... | collective-permute-start | bytes 983048 | tf_op jit(solution)/shard_map/ppermute | solution.py:46
  51.8 9.0 %collective-permute-start.18 = (bf16[80,2048]{1,0:T(8,128)(2,1)S(1)}, bf16[80,2048]{1,0:T(8,128)(2,1)S(1)}, u32[]{:S(2)}, u32[]{:S(2)}) collective-permute-start(bf16[80,2048]{1,0:T(8,128)(2,1)S(1)} %collective-permute-done.15.refs_16_), channel_id=1, source_target_pairs={{0,14},{1,3},{2,0},{3,5},{4,2},{5,7},{6,4},{7,9},{8,6},{9,11},{10,... | collective-permute-start | bytes 983048 | tf_op jit(solution)/shard_map/ppermute | solution.py:46
  51.8 6.8 %collective-permute-start.16 = (bf16[48,2048]{1,0:T(8,128)(2,1)S(1)}, bf16[48,2048]{1,0:T(8,128)(2,1)S(1)}, u32[]{:S(2)}, u32[]{:S(2)}) collective-permute-start(bf16[48,2048]{1,0:T(8,128)(2,1)S(1)} %collective-permute-done.12.refs_9_), channel_id=1, source_target_pairs={{0,2},{1,15},{2,4},{3,1},{4,6},{5,3},{6,8},{7,5},{8,10},{9,7},{10,... | collective-permute-start | bytes 589832 | tf_op jit(solution)/shard_map/ppermute | solution.py:46
  63.7 16.5 %collective-permute-start.21 = (bf16[128,2048]{1,0:T(8,128)(2,1)S(1)}, bf16[128,2048]{1,0:T(8,128)(2,1)S(1)}, u32[]{:S(2)}, u32[]{:S(2)}) collective-permute-start(bf16[128,2048]{1,0:T(8,128)(2,1)S(1)} %get-tuple-element.48.own_ref), channel_id=1, source_target_pairs={{0,1},{1,0},{2,3},{3,2},{4,5},{5,4},{6,7},{7,6},{8,9},{9,8},{10,11... | collective-permute-start | bytes 1572872 | tf_op jit(solution)/shard_map/ppermute | solution.py:46
  68.3 9.1 %collective-permute-start.23 = (bf16[512,256]{1,0:T(8,128)(2,1)S(1)}, bf16[512,256]{1,0:T(8,128)(2,1)S(1)}, u32[]{:S(2)}, u32[]{:S(2)}) collective-permute-start(bf16[512,256]{1,0:T(8,128)(2,1)S(1)} %get-tuple-element.52), channel_id=1, source_target_pairs={{0,2},{1,3},{2,4},{3,5},{4,6},{5,7},{6,8},{7,9},{8,10},{9,11},{10,... | collective-permute-start | bytes 786440 | tf_op jit(solution)/shard_map/ppermute | solution.py:46
  68.3 14.1 %collective-permute-start.29 = (bf16[128,2048]{1,0:T(8,128)(2,1)S(1)}, bf16[128,2048]{1,0:T(8,128)(2,1)S(1)}, u32[]{:S(2)}, u32[]{:S(2)}) collective-permute-start(bf16[128,2048]{1,0:T(8,128)(2,1)S(1)} %get-tuple-element.54.mine), channel_id=1, source_target_pairs={{0,96},{32,0},{64,32},{96,64},{128,224},{160,128},{192,160},{224,1... | collective-permute-start | bytes 1572872 | tf_op jit(solution)/shard_map/ppermute | solution.py:46
  71.0 14.2 %collective-permute-start.28 = (bf16[128,2048]{1,0:T(8,128)(2,1)S(1)}, bf16[128,2048]{1,0:T(8,128)(2,1)S(1)}, u32[]{:S(2)}, u32[]{:S(2)}) collective-permute-start(bf16[128,2048]{1,0:T(8,128)(2,1)S(1)} %get-tuple-element.54.mine), channel_id=1, source_target_pairs={{0,32},{32,64},{64,96},{96,0},{128,160},{160,192},{192,224},{224,1... | collective-permute-start | bytes 1572872 | tf_op jit(solution)/shard_map/ppermute | solution.py:46
  71.0 7.7 %collective-permute-start.25 = (bf16[512,256]{1,0:T(8,128)(2,1)S(1)}, bf16[512,256]{1,0:T(8,128)(2,1)S(1)}, u32[]{:S(2)}, u32[]{:S(2)}) collective-permute-start(bf16[512,256]{1,0:T(8,128)(2,1)S(1)} %get-tuple-element.53), channel_id=1, source_target_pairs={{0,14},{1,15},{2,0},{3,1},{4,2},{5,3},{6,4},{7,5},{8,6},{9,7},{10,... | collective-permute-start | bytes 786440 | tf_op jit(solution)/shard_map/ppermute | solution.py:46
  77.4 9.7 %collective-permute-start.20 = (bf16[512,384]{1,0:T(8,128)(2,1)S(1)}, bf16[512,384]{1,0:T(8,128)(2,1)S(1)}, u32[]{:S(2)}, u32[]{:S(2)}) collective-permute-start(bf16[512,384]{1,0:T(8,128)(2,1)S(1)} %get-tuple-element.47), channel_id=1, source_target_pairs={{0,1},{1,0},{2,3},{3,2},{4,5},{5,4},{6,7},{7,6},{8,9},{9,8},{10,11... | collective-permute-start | bytes 1179656 | tf_op jit(solution)/shard_map/ppermute | solution.py:46
  78.7 8.0 %collective-permute-start.24 = (bf16[256,256]{1,0:T(8,128)(2,1)S(1)}, bf16[256,256]{1,0:T(8,128)(2,1)S(1)}, u32[]{:S(2)}, u32[]{:S(2)}) collective-permute-start(bf16[256,256]{1,0:T(8,128)(2,1)S(1)} %slice.80), channel_id=1, source_target_pairs={{0,1},{1,0},{2,3},{3,2},{4,5},{5,4},{6,7},{7,6},{8,9},{9,8},{10,11... | collective-permute-start | bytes 393224 | tf_op jit(solution)/shard_map/ppermute | solution.py:46
  80.2 6.8 %collective-permute-start.26 = (bf16[256,256]{1,0:T(8,128)(2,1)S(1)}, bf16[256,256]{1,0:T(8,128)(2,1)S(1)}, u32[]{:S(2)}, u32[]{:S(2)}) collective-permute-start(bf16[256,256]{1,0:T(8,128)(2,1)S(1)} %slice.81), channel_id=1, source_target_pairs={{0,1},{1,0},{2,3},{3,2},{4,5},{5,4},{6,7},{7,6},{8,9},{9,8},{10,11... | collective-permute-start | bytes 393224 | tf_op jit(solution)/shard_map/ppermute | solution.py:46
  82.4 4.6 %collective-permute-start.22 = (bf16[256,256]{1,0:T(8,128)(2,1)S(1)}, bf16[256,256]{1,0:T(8,128)(2,1)S(1)}, u32[]{:S(2)}, u32[]{:S(2)}) collective-permute-start(bf16[256,256]{1,0:T(8,128)(2,1)S(1)} %get-tuple-element.51), channel_id=1, source_target_pairs={{0,1},{1,0},{2,3},{3,2},{4,5},{5,4},{6,7},{7,6},{8,9},{9,8},{10,11... | collective-permute-start | bytes 393224 | tf_op jit(solution)/shard_map/ppermute | solution.py:46
  85.3 7.2 %collective-permute-start.31 = (bf16[64,2048]{1,0:T(8,128)(2,1)S(1)}, bf16[64,2048]{1,0:T(8,128)(2,1)S(1)}, u32[]{:S(2)}, u32[]{:S(2)}) collective-permute-start(bf16[64,2048]{1,0:T(8,128)(2,1)S(1)} %slice.85), channel_id=1, source_target_pairs={{0,96},{32,0},{64,32},{96,64},{128,224},{160,128},{192,160},{224,1... | collective-permute-start | bytes 786440 | tf_op jit(solution)/shard_map/ppermute | solution.py:46
  86.7 9.1 %collective-permute-start.30 = (bf16[64,2048]{1,0:T(8,128)(2,1)S(1)}, bf16[64,2048]{1,0:T(8,128)(2,1)S(1)}, u32[]{:S(2)}, u32[]{:S(2)}) collective-permute-start(bf16[64,2048]{1,0:T(8,128)(2,1)S(1)} %slice.84), channel_id=1, source_target_pairs={{0,32},{32,64},{64,96},{96,0},{128,160},{160,192},{192,224},{224,1... | collective-permute-start | bytes 786440 | tf_op jit(solution)/shard_map/ppermute | solution.py:46
  91.1 4.8 %collective-permute-start.27 = (bf16[256,256]{1,0:T(8,128)(2,1)S(1)}, bf16[256,256]{1,0:T(8,128)(2,1)S(1)}, u32[]{:S(2)}, u32[]{:S(2)}) collective-permute-start(bf16[256,256]{1,0:T(8,128)(2,1)S(1)} %get-tuple-element.59), channel_id=1, source_target_pairs={{0,16},{1,17},{2,18},{3,19},{4,20},{5,21},{6,22},{7,23},{8,24},{9,... | collective-permute-start | bytes 393224 | tf_op jit(solution)/shard_map/ppermute | solution.py:46
  97.1 3.8 %collective-permute-start.32 = (bf16[128,2048]{1,0:T(8,128)(2,1)S(1)}, bf16[128,2048]{1,0:T(8,128)(2,1)S(1)}, u32[]{:S(2)}, u32[]{:S(2)}) collective-permute-start(bf16[128,2048]{1,0:T(8,128)(2,1)S(1)} %get-tuple-element.56), channel_id=1, source_target_pairs={{0,1},{1,0},{2,3},{3,2},{4,5},{5,4},{6,7},{7,6},{8,9},{9,8},{10,11... | collective-permute-start | bytes 1572872 | tf_op jit(solution)/shard_map/ppermute | solution.py:46
  (4 other events, 33.9 us)

commit v13 on v12

--- a/solution.py
+++ b/solution.py
@@ -322,9 +322,9 @@
             if step > 2:
                 before = one[0, step - 2], one[1, step - 2]
                 a_two, b_two = lax.optimization_barrier((a_two, b_two, *before))[:2]
+            if step == 4:
+                a_two, b_two = lax.optimization_barrier((a_two, b_two, across, beside, beside_across))[:2]
             two[0, step - 1] = a_two = send(a_two, AHEAD)
-            if step == 4:
-                b_two = after(b_two, across, beside, beside_across)
             two[1, step - 1] = b_two = send(b_two, BEHIND)
         if step > 2:
             before = two[0, step - 2], two[1, step - 2]

time: 102 us -> 109 us (1.069)
  waiting for transfers between devices: 35.9 us -> 44.8 us
  starting transfers between devices: 49.9 us -> 47.9 us
    ppermute x33, waiting for transfers between devices: 35.9 us -> 44.8 us  [send(): return lax.ppermute(value, axis, route)]
    ppermute x33, starting transfers between devices: 49.9 us -> 47.9 us  [send(): return lax.ppermute(value, axis, route)]
  transfers between devices with their start and end apart: 33 -> 33, of which waited for: 16 -> 13; matrix products, arithmetic and copies ran while one was open for 0% -> 0% of each run, Pallas kernels for 7% -> 7%
where the time goes in v13:
time: 109 us
  starting transfers between devices  47.9 us (44%)
  waiting for transfers between devices  44.8 us (41%)
  Pallas kernels  11.5 us (11%)
  other arithmetic  2.3 us (2%)
  local copies, waits for them, and re-layouts  1.29 us (1%)
    ppermute x33, starting transfers between devices, send(): return lax.ppermute(value, axis, route)  47.9 us
    ppermute x33, waiting for transfers between devices, send(): return lax.ppermute(value, axis, route)  44.8 us
    pallas_call x5, Pallas kernels, on_chip(): pl.pallas_call(kernel, out_shape=out_shape, in_specs=specs, out_specs=jax...  11.5 us
  transfers between devices with their start and end apart: 33, of which 13 were waited for; matrix products, arithmetic and copies ran while one was open for 0% of the time, Pallas kernels for 7%

profile of v13, /device:TPU:1, one launch (start us, length us, event | category | flops | bytes accessed | tf_op | source)
XLA Modules:
  0.0 108.7 jit_solution(4053536767934890841)
XLA Ops:
  2.3 3.3 %collective-permute-start.8 = (bf16[128,64]{1,0:T(8,128)(2,1)S(1)}, bf16[128,64]{1,0:T(8,128)(2,1)S(1)}, u32[]{:S(2)}, u32[]{:S(2)}) collective-permute-start(bf16[128,64]{1,0:T(8,128)(2,1)S(1)} %bitcast.43), channel_id=1, source_target_pairs={{0,1},{1,0},{2,3},{3,2},{4,5},{5,4},{6,7},{7,6},{8,9},{9,8},{10,11... | collective-permute-start | bytes 49160 | tf_op jit(solution)/shard_map/ppermute | solution.py:46
  5.6 3.9 %collective-permute-start = (bf16[48,2048]{1,0:T(8,128)(2,1)S(1)}, bf16[48,2048]{1,0:T(8,128)(2,1)S(1)}, u32[]{:S(2)}, u32[]{:S(2)}) collective-permute-start(bf16[48,2048]{1,0:T(8,128)(2,1)S(1)} %bitcast.34), channel_id=1, source_target_pairs={{0,2},{1,15},{2,4},{3,1},{4,6},{5,3},{6,8},{7,5},{8,10},{9,7},{10,... | collective-permute-start | bytes 589832 | tf_op jit(solution)/shard_map/ppermute | solution.py:46
  11.5 1.3 %collective-permute-start.7 = (bf16[8,2048]{1,0:T(8,128)(2,1)S(1)}, bf16[8,2048]{1,0:T(8,128)(2,1)S(1)}, u32[]{:S(2)}, u32[]{:S(2)}) collective-permute-start(bf16[8,2048]{1,0:T(8,128)(2,1)S(1)} %get-tuple-element.35), channel_id=1, source_target_pairs={{0,16},{1,17},{2,18},{3,19},{4,20},{5,21},{6,22},{7,23},{8,24},{9,... | collective-permute-start | bytes 98312 | tf_op jit(solution)/shard_map/ppermute | solution.py:46
  13.3 1.4 %collective-permute-done.7 = bf16[8,2048]{1,0:T(8,128)(2,1)S(1)} collective-permute-done((bf16[8,2048]{1,0:T(8,128)(2,1)S(1)}, bf16[8,2048]{1,0:T(8,128)(2,1)S(1)}, u32[]{:S(2)}, u32[]{:S(2)}) %collective-permute-start.7) | collective-permute-done | bytes 32800 | tf_op jit(solution)/shard_map/ppermute | solution.py:46
  14.7 1.4 %collective-permute-done.9 = bf16[128,128]{1,0:T(8,128)(2,1)S(1)} collective-permute-done((bf16[128,128]{1,0:T(8,128)(2,1)S(1)}, bf16[128,128]{1,0:T(8,128)(2,1)S(1)}, u32[]{:S(2)}, u32[]{:S(2)}) %collective-permute-start.9) | collective-permute-done | bytes 32800 | tf_op jit(solution)/shard_map/ppermute | solution.py:46
  16.7 2.7 %collective-permute-start.10 = (bf16[80,2048]{1,0:T(8,128)(2,1)S(1)}, bf16[80,2048]{1,0:T(8,128)(2,1)S(1)}, u32[]{:S(2)}, u32[]{:S(2)}) collective-permute-start(bf16[80,2048]{1,0:T(8,128)(2,1)S(1)} %pad_maximum_fusion.1.refs_12_), channel_id=1, source_target_pairs={{0,2},{1,15},{2,4},{3,1},{4,6},{5,3},{6,8},{7,5},{8,10},{9,7},{10,... | collective-permute-start | bytes 983048 | tf_op jit(solution)/shard_map/ppermute | solution.py:46
  19.4 2.3 %collective-permute-start.2 = (bf16[128,2048]{1,0:T(8,128)(2,1)S(1)}, bf16[128,2048]{1,0:T(8,128)(2,1)S(1)}, u32[]{:S(2)}, u32[]{:S(2)}) collective-permute-start(bf16[128,2048]{1,0:T(8,128)(2,1)S(1)} %get-tuple-element.34.refs_0_), channel_id=1, source_target_pairs={{0,1},{1,0},{2,3},{3,2},{4,5},{5,4},{6,7},{7,6},{8,9},{9,8},{10,11... | collective-permute-start | bytes 1572872 | tf_op jit(solution)/shard_map/ppermute | solution.py:46
  21.7 6.5 %collective-permute-done.1.refs_1_ = bf16[128,2048]{1,0:T(8,128)(2,1)S(1)} collective-permute-done((bf16[128,2048]{1,0:T(8,128)(2,1)S(1)}, bf16[128,2048]{1,0:T(8,128)(2,1)S(1)}, u32[]{:S(2)}, u32[]{:S(2)}) %collective-permute-start.1) | collective-permute-done | bytes 524320 | tf_op jit(solution)/shard_map/ppermute | solution.py:46
  28.3 2.4 %collective-permute-start.3 = (bf16[128,2048]{1,0:T(8,128)(2,1)S(1)}, bf16[128,2048]{1,0:T(8,128)(2,1)S(1)}, u32[]{:S(2)}, u32[]{:S(2)}) collective-permute-start(bf16[128,2048]{1,0:T(8,128)(2,1)S(1)} %collective-permute-done.1.refs_1_), channel_id=1, source_target_pairs={{0,1},{1,0},{2,3},{3,2},{4,5},{5,4},{6,7},{7,6},{8,9},{9,8},{10,11... | collective-permute-start | bytes 1572872 | tf_op jit(solution)/shard_map/ppermute | solution.py:46
  30.7 2.7 %collective-permute-start.14 = (bf16[80,2048]{1,0:T(8,128)(2,1)S(1)}, bf16[80,2048]{1,0:T(8,128)(2,1)S(1)}, u32[]{:S(2)}, u32[]{:S(2)}) collective-permute-start(bf16[80,2048]{1,0:T(8,128)(2,1)S(1)} %collective-permute-done.10.refs_13_), channel_id=1, source_target_pairs={{0,2},{1,15},{2,4},{3,1},{4,6},{5,3},{6,8},{7,5},{8,10},{9,7},{10,... | collective-permute-start | bytes 983048 | tf_op jit(solution)/shard_map/ppermute | solution.py:46
  33.4 3.0 %collective-permute-done.6.refs_8_ = bf16[48,2048]{1,0:T(8,128)(2,1)S(1)} collective-permute-done((bf16[48,2048]{1,0:T(8,128)(2,1)S(1)}, bf16[48,2048]{1,0:T(8,128)(2,1)S(1)}, u32[]{:S(2)}, u32[]{:S(2)}) %collective-permute-start.6) | collective-permute-done | bytes 196640 | tf_op jit(solution)/shard_map/ppermute | solution.py:46
  36.4 1.4 %collective-permute-start.5 = (bf16[48,2048]{1,0:T(8,128)(2,1)S(1)}, bf16[48,2048]{1,0:T(8,128)(2,1)S(1)}, u32[]{:S(2)}, u32[]{:S(2)}) collective-permute-start(bf16[48,2048]{1,0:T(8,128)(2,1)S(1)} %collective-permute-done.refs_5_), channel_id=1, source_target_pairs={{0,2},{1,15},{2,4},{3,1},{4,6},{5,3},{6,8},{7,5},{8,10},{9,7},{10,... | collective-permute-start | bytes 589832 | tf_op jit(solution)/shard_map/ppermute | solution.py:46
  37.8 6.7 %collective-permute-done.5.refs_7_ = bf16[48,2048]{1,0:T(8,128)(2,1)S(1)} collective-permute-done((bf16[48,2048]{1,0:T(8,128)(2,1)S(1)}, bf16[48,2048]{1,0:T(8,128)(2,1)S(1)}, u32[]{:S(2)}, u32[]{:S(2)}) %collective-permute-start.5) | collective-permute-done | bytes 196640 | tf_op jit(solution)/shard_map/ppermute | solution.py:46
  44.5 3.1 %collective-permute-start.17 = (bf16[80,2048]{1,0:T(8,128)(2,1)S(1)}, bf16[80,2048]{1,0:T(8,128)(2,1)S(1)}, u32[]{:S(2)}, u32[]{:S(2)}) collective-permute-start(bf16[80,2048]{1,0:T(8,128)(2,1)S(1)} %collective-permute-done.14.refs_15_), channel_id=1, source_target_pairs={{0,2},{1,15},{2,4},{3,1},{4,6},{5,3},{6,8},{7,5},{8,10},{9,7},{10,... | collective-permute-start | bytes 983048 | tf_op jit(solution)/shard_map/ppermute | solution.py:46
  47.6 1.4 %collective-permute-start.13 = (bf16[48,2048]{1,0:T(8,128)(2,1)S(1)}, bf16[48,2048]{1,0:T(8,128)(2,1)S(1)}, u32[]{:S(2)}, u32[]{:S(2)}) collective-permute-start(bf16[48,2048]{1,0:T(8,128)(2,1)S(1)} %collective-permute-done.6.refs_8_), channel_id=1, source_target_pairs={{0,14},{1,3},{2,0},{3,5},{4,2},{5,7},{6,4},{7,9},{8,6},{9,11},{10,... | collective-permute-start | bytes 589832 | tf_op jit(solution)/shard_map/ppermute | solution.py:46
  49.1 7.8 %collective-permute-done.12.refs_9_ = bf16[48,2048]{1,0:T(8,128)(2,1)S(1)} collective-permute-done((bf16[48,2048]{1,0:T(8,128)(2,1)S(1)}, bf16[48,2048]{1,0:T(8,128)(2,1)S(1)}, u32[]{:S(2)}, u32[]{:S(2)}) %collective-permute-start.12) | collective-permute-done | bytes 196640 | tf_op jit(solution)/shard_map/ppermute | solution.py:46
  56.9 3.4 %collective-permute-start.19 = (bf16[80,2048]{1,0:T(8,128)(2,1)S(1)}, bf16[80,2048]{1,0:T(8,128)(2,1)S(1)}, u32[]{:S(2)}, u32[]{:S(2)}) collective-permute-start(bf16[80,2048]{1,0:T(8,128)(2,1)S(1)} %collective-permute-done.17.refs_17_), channel_id=1, source_target_pairs={{0,2},{1,15},{2,4},{3,1},{4,6},{5,3},{6,8},{7,5},{8,10},{9,7},{10,... | collective-permute-start | bytes 983048 | tf_op jit(solution)/shard_map/ppermute | solution.py:46
  60.4 6.0 %collective-permute-done.16.refs_11_ = bf16[48,2048]{1,0:T(8,128)(2,1)S(1)} collective-permute-done((bf16[48,2048]{1,0:T(8,128)(2,1)S(1)}, bf16[48,2048]{1,0:T(8,128)(2,1)S(1)}, u32[]{:S(2)}, u32[]{:S(2)}) %collective-permute-start.16) | collective-permute-done | bytes 196640 | tf_op jit(solution)/shard_map/ppermute | solution.py:46
  66.4 2.9 %shard_map.83 = (bf16[512,384]{1,0:T(8,128)(2,1)S(1)}, bf16[512,384]{1,0:T(8,128)(2,1)S(1)}, bf16[128,2048]{1,0:T(8,128)(2,1)S(1)}, bf16[512,2048]{1,0:T(8,128)(...) custom-call(s32[6]{0:T(128)S(1)} %stack.35.index, ...), custom_call_target="tpu_custom_call" | custom-call | flops 1610612736 | bytes 4194304 | tf_op jit(solution)/shard_map/pallas_call | solution.py:245
  69.3 5.8 %collective-permute-start.21 = (bf16[128,2048]{1,0:T(8,128)(2,1)S(1)}, bf16[128,2048]{1,0:T(8,128)(2,1)S(1)}, u32[]{:S(2)}, u32[]{:S(2)}) collective-permute-start(bf16[128,2048]{1,0:T(8,128)(2,1)S(1)} %get-tuple-element.50.own_ref), channel_id=1, source_target_pairs={{0,1},{1,0},{2,3},{3,2},{4,5},{5,4},{6,7},{7,6},{8,9},{9,8},{10,11... | collective-permute-start | bytes 1572872 | tf_op jit(solution)/shard_map/ppermute | solution.py:46
  75.1 2.7 %collective-permute-start.29 = (bf16[128,2048]{1,0:T(8,128)(2,1)S(1)}, bf16[128,2048]{1,0:T(8,128)(2,1)S(1)}, u32[]{:S(2)}, u32[]{:S(2)}) collective-permute-start(bf16[128,2048]{1,0:T(8,128)(2,1)S(1)} %get-tuple-element.56.mine), channel_id=1, source_target_pairs={{0,96},{32,0},{64,32},{96,64},{128,224},{160,128},{192,160},{224,1... | collective-permute-start | bytes 1572872 | tf_op jit(solution)/shard_map/ppermute | solution.py:46
  77.9 2.7 %collective-permute-start.25 = (bf16[512,256]{1,0:T(8,128)(2,1)S(1)}, bf16[512,256]{1,0:T(8,128)(2,1)S(1)}, u32[]{:S(2)}, u32[]{:S(2)}) collective-permute-start(bf16[512,256]{1,0:T(8,128)(2,1)S(1)} %get-tuple-element.55), channel_id=1, source_target_pairs={{0,14},{1,15},{2,0},{3,1},{4,2},{5,3},{6,4},{7,5},{8,6},{9,7},{10,... | collective-permute-start | bytes 786440 | tf_op jit(solution)/shard_map/ppermute | solution.py:46
  80.6 3.6 %collective-permute-done.23.below_ref = bf16[512,256]{1,0:T(8,128)(2,1)S(1)} collective-permute-done((bf16[512,256]{1,0:T(8,128)(2,1)S(1)}, bf16[512,256]{1,0:T(8,128)(2,1)S(1)}, u32[]{:S(2)}, u32[]{:S(2)}) %collective-permute-start.23) | collective-permute-done | bytes 262176 | tf_op jit(solution)/shard_map/ppermute | solution.py:46
  85.6 1.5 %collective-permute-start.24 = (bf16[256,256]{1,0:T(8,128)(2,1)S(1)}, bf16[256,256]{1,0:T(8,128)(2,1)S(1)}, u32[]{:S(2)}, u32[]{:S(2)}) collective-permute-start(bf16[256,256]{1,0:T(8,128)(2,1)S(1)} %slice.80), channel_id=1, source_target_pairs={{0,1},{1,0},{2,3},{3,2},{4,5},{5,4},{6,7},{7,6},{8,9},{9,8},{10,11... | collective-permute-start | bytes 393224 | tf_op jit(solution)/shard_map/ppermute | solution.py:46
  87.2 2.1 %shard_map.84 = (bf16[256,256]{1,0:T(8,128)(2,1)S(1)}, bf16[256,256]{1,0:T(8,128)(2,1)S(1)}) custom-call(s32[6]{0:T(128)S(1)} %stack.35.index, bf16[128,2048]{1,0:T(8,128)(2,1)S(1)} %get-tuple-element.50.own_ref, bf16[128,2048]{1,0:T(8,128)(2,1)S(1)} %collective-permute-done.21.other_ref, bf16[512,2048]{1,0:T(8,128)(2,1)S(1)} %get-tuple-element.51.table), custom_call_target="tpu_custom_call" | custom-call | flops 536870912 | bytes 4194304 | tf_op jit(solution)/shard_map/pallas_call | solution.py:245
  90.0 2.1 %collective-permute-done.28.prev = bf16[128,2048]{1,0:T(8,128)(2,1)S(1)} collective-permute-done((bf16[128,2048]{1,0:T(8,128)(2,1)S(1)}, bf16[128,2048]{1,0:T(8,128)(2,1)S(1)}, u32[]{:S(2)}, u32[]{:S(2)}) %collective-permute-start.28) | collective-permute-done | bytes 524320 | tf_op jit(solution)/shard_map/ppermute | solution.py:46
  92.1 1.4 %collective-permute-start.31 = (bf16[64,2048]{1,0:T(8,128)(2,1)S(1)}, bf16[64,2048]{1,0:T(8,128)(2,1)S(1)}, u32[]{:S(2)}, u32[]{:S(2)}) collective-permute-start(bf16[64,2048]{1,0:T(8,128)(2,1)S(1)} %slice.85), channel_id=1, source_target_pairs={{0,96},{32,0},{64,32},{96,64},{128,224},{160,128},{192,160},{224,1... | collective-permute-start | bytes 786440 | tf_op jit(solution)/shard_map/ppermute | solution.py:46
  93.9 4.0 %shard_map.85 = bf16[2,256,256]{2,1,0:T(8,128)(2,1)S(1)} custom-call(s32[6]{0:T(128)S(1)} %stack.35.index, bf16[512,384]{1,0:T(8,128)(2,1)S(1)} %get-tuple-element.48.keep_ref, bf16[512,384]{1,0:T(8,128)(2,1)S(1)} %collective-permute-done.20.got_ref, bf16[256,256]{1,0:T(8,128)(2,1)S(1)} %get-tuple-element.52.g_keep, ...), custom_call_target="tpu_custom_call" | custom-call | flops 1342177280 | bytes 4194304 | tf_op jit(solution)/shard_map/pallas_call | solution.py:245
  99.3 3.4 %collective-permute-done.30.far_a = bf16[64,2048]{1,0:T(8,128)(2,1)S(1)} collective-permute-done((bf16[64,2048]{1,0:T(8,128)(2,1)S(1)}, bf16[64,2048]{1,0:T(8,128)(2,1)S(1)}, u32[]{:S(2)}, u32[]{:S(2)}) %collective-permute-start.30) | collective-permute-done | bytes 262176 | tf_op jit(solution)/shard_map/ppermute | solution.py:46
  102.7 1.3 %shard_map.86 = (f32[128,2048]{1,0:T(8,128)S(1)}, bf16[128,2048]{1,0:T(8,128)(2,1)S(1)}) custom-call(s32[6]{0:T(128)S(1)} %stack.35.index, bf16[256,256]{1,0:T(8,128)(2,1)S(1)} %get-tuple-element.62.own_ref, bf16[256,256]{1,0:T(8,128)(2,1)S(1)} %collective-permute-done.27.there_ref, bf16[128,2048]{1,0:T(8,128)(2,1)S(1)} %get-tuple-element.56.mine, ...), custom_call_target="tpu_custom_call" | custom-call | flops 536870912 | bytes 4194304 | tf_op jit(solution)/shard_map/pallas_call | solution.py:245
  104.0 2.2 %collective-permute-start.32 = (bf16[128,2048]{1,0:T(8,128)(2,1)S(1)}, bf16[128,2048]{1,0:T(8,128)(2,1)S(1)}, u32[]{:S(2)}, u32[]{:S(2)}) collective-permute-start(bf16[128,2048]{1,0:T(8,128)(2,1)S(1)} %get-tuple-element.58), channel_id=1, source_target_pairs={{0,1},{1,0},{2,3},{3,2},{4,5},{5,4},{6,7},{7,6},{8,9},{9,8},{10,11... | collective-permute-start | bytes 1572872 | tf_op jit(solution)/shard_map/ppermute | solution.py:46
  106.2 1.5 %collective-permute-done.32 = bf16[128,2048]{1,0:T(8,128)(2,1)S(1)} collective-permute-done((bf16[128,2048]{1,0:T(8,128)(2,1)S(1)}, bf16[128,2048]{1,0:T(8,128)(2,1)S(1)}, u32[]{:S(2)}, u32[]{:S(2)}) %collective-permute-start.32) | collective-permute-done | bytes 524320 | tf_op jit(solution)/shard_map/ppermute | solution.py:46
  (69 shorter events, 9.8 us)
Async XLA Ops:
  2.3 10.5 %collective-permute-start.8 = (bf16[128,64]{1,0:T(8,128)(2,1)S(1)}, bf16[128,64]{1,0:T(8,128)(2,1)S(1)}, u32[]{:S(2)}, u32[]{:S(2)}) collective-permute-start(bf16[128,64]{1,0:T(8,128)(2,1)S(1)} %bitcast.43), channel_id=1, source_target_pairs={{0,1},{1,0},{2,3},{3,2},{4,5},{5,4},{6,7},{7,6},{8,9},{9,8},{10,11... | collective-permute-start | bytes 49160 | tf_op jit(solution)/shard_map/ppermute | solution.py:46
  5.6 11.0 %collective-permute-start.4 = (bf16[48,2048]{1,0:T(8,128)(2,1)S(1)}, bf16[48,2048]{1,0:T(8,128)(2,1)S(1)}, u32[]{:S(2)}, u32[]{:S(2)}) collective-permute-start(bf16[48,2048]{1,0:T(8,128)(2,1)S(1)} %bitcast.33), channel_id=1, source_target_pairs={{0,14},{1,3},{2,0},{3,5},{4,2},{5,7},{6,4},{7,9},{8,6},{9,11},{10,... | collective-permute-start | bytes 589832 | tf_op jit(solution)/shard_map/ppermute | solution.py:46
  5.6 10.6 %collective-permute-start = (bf16[48,2048]{1,0:T(8,128)(2,1)S(1)}, bf16[48,2048]{1,0:T(8,128)(2,1)S(1)}, u32[]{:S(2)}, u32[]{:S(2)}) collective-permute-start(bf16[48,2048]{1,0:T(8,128)(2,1)S(1)} %bitcast.34), channel_id=1, source_target_pairs={{0,2},{1,15},{2,4},{3,1},{4,6},{5,3},{6,8},{7,5},{8,10},{9,7},{10,... | collective-permute-start | bytes 589832 | tf_op jit(solution)/shard_map/ppermute | solution.py:46
  12.9 3.1 %collective-permute-start.9 = (bf16[128,128]{1,0:T(8,128)(2,1)S(1)}, bf16[128,128]{1,0:T(8,128)(2,1)S(1)}, u32[]{:S(2)}, u32[]{:S(2)}) collective-permute-start(bf16[128,128]{1,0:T(8,128)(2,1)S(1)} %pad_maximum_fusion.2), channel_id=1, source_target_pairs={{0,16},{1,17},{2,18},{3,19},{4,20},{5,21},{6,22},{7,23},{8,24},{9,... | collective-permute-start | bytes 98312 | tf_op jit(solution)/shard_map/ppermute | solution.py:46
  16.3 12.0 %collective-permute-start.1 = (bf16[128,2048]{1,0:T(8,128)(2,1)S(1)}, bf16[128,2048]{1,0:T(8,128)(2,1)S(1)}, u32[]{:S(2)}, u32[]{:S(2)}) collective-permute-start(bf16[128,2048]{1,0:T(8,128)(2,1)S(1)} %get-tuple-element.34.refs_0_), channel_id=1, source_target_pairs={{0,16},{1,17},{2,18},{3,19},{4,20},{5,21},{6,22},{7,23},{8,24},{9,... | collective-permute-start | bytes 1572872 | tf_op jit(solution)/shard_map/ppermute | solution.py:46
  16.6 14.0 %collective-permute-start.11 = (bf16[80,2048]{1,0:T(8,128)(2,1)S(1)}, bf16[80,2048]{1,0:T(8,128)(2,1)S(1)}, u32[]{:S(2)}, u32[]{:S(2)}) collective-permute-start(bf16[80,2048]{1,0:T(8,128)(2,1)S(1)} %pad_maximum_fusion.1.refs_12_), channel_id=1, source_target_pairs={{0,14},{1,3},{2,0},{3,5},{4,2},{5,7},{6,4},{7,9},{8,6},{9,11},{10,... | collective-permute-start | bytes 983048 | tf_op jit(solution)/shard_map/ppermute | solution.py:46
  16.7 14.0 %collective-permute-start.10 = (bf16[80,2048]{1,0:T(8,128)(2,1)S(1)}, bf16[80,2048]{1,0:T(8,128)(2,1)S(1)}, u32[]{:S(2)}, u32[]{:S(2)}) collective-permute-start(bf16[80,2048]{1,0:T(8,128)(2,1)S(1)} %pad_maximum_fusion.1.refs_12_), channel_id=1, source_target_pairs={{0,2},{1,15},{2,4},{3,1},{4,6},{5,3},{6,8},{7,5},{8,10},{9,7},{10,... | collective-permute-start | bytes 983048 | tf_op jit(solution)/shard_map/ppermute | solution.py:46
  19.4 25.0 %collective-permute-start.2 = (bf16[128,2048]{1,0:T(8,128)(2,1)S(1)}, bf16[128,2048]{1,0:T(8,128)(2,1)S(1)}, u32[]{:S(2)}, u32[]{:S(2)}) collective-permute-start(bf16[128,2048]{1,0:T(8,128)(2,1)S(1)} %get-tuple-element.34.refs_0_), channel_id=1, source_target_pairs={{0,1},{1,0},{2,3},{3,2},{4,5},{5,4},{6,7},{7,6},{8,9},{9,8},{10,11... | collective-permute-start | bytes 1572872 | tf_op jit(solution)/shard_map/ppermute | solution.py:46
  28.3 16.2 %collective-permute-start.3 = (bf16[128,2048]{1,0:T(8,128)(2,1)S(1)}, bf16[128,2048]{1,0:T(8,128)(2,1)S(1)}, u32[]{:S(2)}, u32[]{:S(2)}) collective-permute-start(bf16[128,2048]{1,0:T(8,128)(2,1)S(1)} %collective-permute-done.1.refs_1_), channel_id=1, source_target_pairs={{0,1},{1,0},{2,3},{3,2},{4,5},{5,4},{6,7},{7,6},{8,9},{9,8},{10,11... | collective-permute-start | bytes 1572872 | tf_op jit(solution)/shard_map/ppermute | solution.py:46
  30.7 5.7 %collective-permute-start.6 = (bf16[48,2048]{1,0:T(8,128)(2,1)S(1)}, bf16[48,2048]{1,0:T(8,128)(2,1)S(1)}, u32[]{:S(2)}, u32[]{:S(2)}) collective-permute-start(bf16[48,2048]{1,0:T(8,128)(2,1)S(1)} %collective-permute-done.4.refs_6_), channel_id=1, source_target_pairs={{0,14},{1,3},{2,0},{3,5},{4,2},{5,7},{6,4},{7,9},{8,6},{9,11},{10,... | collective-permute-start | bytes 589832 | tf_op jit(solution)/shard_map/ppermute | solution.py:46
  30.7 13.7 %collective-permute-start.14 = (bf16[80,2048]{1,0:T(8,128)(2,1)S(1)}, bf16[80,2048]{1,0:T(8,128)(2,1)S(1)}, u32[]{:S(2)}, u32[]{:S(2)}) collective-permute-start(bf16[80,2048]{1,0:T(8,128)(2,1)S(1)} %collective-permute-done.10.refs_13_), channel_id=1, source_target_pairs={{0,2},{1,15},{2,4},{3,1},{4,6},{5,3},{6,8},{7,5},{8,10},{9,7},{10,... | collective-permute-start | bytes 983048 | tf_op jit(solution)/shard_map/ppermute | solution.py:46
  33.4 11.1 %collective-permute-start.15 = (bf16[80,2048]{1,0:T(8,128)(2,1)S(1)}, bf16[80,2048]{1,0:T(8,128)(2,1)S(1)}, u32[]{:S(2)}, u32[]{:S(2)}) collective-permute-start(bf16[80,2048]{1,0:T(8,128)(2,1)S(1)} %collective-permute-done.11.refs_14_), channel_id=1, source_target_pairs={{0,14},{1,3},{2,0},{3,5},{4,2},{5,7},{6,4},{7,9},{8,6},{9,11},{10,... | collective-permute-start | bytes 983048 | tf_op jit(solution)/shard_map/ppermute | solution.py:46
  36.4 8.0 %collective-permute-start.5 = (bf16[48,2048]{1,0:T(8,128)(2,1)S(1)}, bf16[48,2048]{1,0:T(8,128)(2,1)S(1)}, u32[]{:S(2)}, u32[]{:S(2)}) collective-permute-start(bf16[48,2048]{1,0:T(8,128)(2,1)S(1)} %collective-permute-done.refs_5_), channel_id=1, source_target_pairs={{0,2},{1,15},{2,4},{3,1},{4,6},{5,3},{6,8},{7,5},{8,10},{9,7},{10,... | collective-permute-start | bytes 589832 | tf_op jit(solution)/shard_map/ppermute | solution.py:46
  44.5 12.4 %collective-permute-start.17 = (bf16[80,2048]{1,0:T(8,128)(2,1)S(1)}, bf16[80,2048]{1,0:T(8,128)(2,1)S(1)}, u32[]{:S(2)}, u32[]{:S(2)}) collective-permute-start(bf16[80,2048]{1,0:T(8,128)(2,1)S(1)} %collective-permute-done.14.refs_15_), channel_id=1, source_target_pairs={{0,2},{1,15},{2,4},{3,1},{4,6},{5,3},{6,8},{7,5},{8,10},{9,7},{10,... | collective-permute-start | bytes 983048 | tf_op jit(solution)/shard_map/ppermute | solution.py:46
  47.6 9.3 %collective-permute-start.12 = (bf16[48,2048]{1,0:T(8,128)(2,1)S(1)}, bf16[48,2048]{1,0:T(8,128)(2,1)S(1)}, u32[]{:S(2)}, u32[]{:S(2)}) collective-permute-start(bf16[48,2048]{1,0:T(8,128)(2,1)S(1)} %collective-permute-done.5.refs_7_), channel_id=1, source_target_pairs={{0,2},{1,15},{2,4},{3,1},{4,6},{5,3},{6,8},{7,5},{8,10},{9,7},{10,... | collective-permute-start | bytes 589832 | tf_op jit(solution)/shard_map/ppermute | solution.py:46
  47.6 9.2 %collective-permute-start.13 = (bf16[48,2048]{1,0:T(8,128)(2,1)S(1)}, bf16[48,2048]{1,0:T(8,128)(2,1)S(1)}, u32[]{:S(2)}, u32[]{:S(2)}) collective-permute-start(bf16[48,2048]{1,0:T(8,128)(2,1)S(1)} %collective-permute-done.6.refs_8_), channel_id=1, source_target_pairs={{0,14},{1,3},{2,0},{3,5},{4,2},{5,7},{6,4},{7,9},{8,6},{9,11},{10,... | collective-permute-start | bytes 589832 | tf_op jit(solution)/shard_map/ppermute | solution.py:46
  49.0 17.4 %collective-permute-start.18 = (bf16[80,2048]{1,0:T(8,128)(2,1)S(1)}, bf16[80,2048]{1,0:T(8,128)(2,1)S(1)}, u32[]{:S(2)}, u32[]{:S(2)}) collective-permute-start(bf16[80,2048]{1,0:T(8,128)(2,1)S(1)} %collective-permute-done.15.refs_16_), channel_id=1, source_target_pairs={{0,14},{1,3},{2,0},{3,5},{4,2},{5,7},{6,4},{7,9},{8,6},{9,11},{10,... | collective-permute-start | bytes 983048 | tf_op jit(solution)/shard_map/ppermute | solution.py:46
  56.9 9.5 %collective-permute-start.19 = (bf16[80,2048]{1,0:T(8,128)(2,1)S(1)}, bf16[80,2048]{1,0:T(8,128)(2,1)S(1)}, u32[]{:S(2)}, u32[]{:S(2)}) collective-permute-start(bf16[80,2048]{1,0:T(8,128)(2,1)S(1)} %collective-permute-done.17.refs_17_), channel_id=1, source_target_pairs={{0,2},{1,15},{2,4},{3,1},{4,6},{5,3},{6,8},{7,5},{8,10},{9,7},{10,... | collective-permute-start | bytes 983048 | tf_op jit(solution)/shard_map/ppermute | solution.py:46
  60.3 6.1 %collective-permute-start.16 = (bf16[48,2048]{1,0:T(8,128)(2,1)S(1)}, bf16[48,2048]{1,0:T(8,128)(2,1)S(1)}, u32[]{:S(2)}, u32[]{:S(2)}) collective-permute-start(bf16[48,2048]{1,0:T(8,128)(2,1)S(1)} %collective-permute-done.12.refs_9_), channel_id=1, source_target_pairs={{0,2},{1,15},{2,4},{3,1},{4,6},{5,3},{6,8},{7,5},{8,10},{9,7},{10,... | collective-permute-start | bytes 589832 | tf_op jit(solution)/shard_map/ppermute | solution.py:46
  69.3 17.8 %collective-permute-start.21 = (bf16[128,2048]{1,0:T(8,128)(2,1)S(1)}, bf16[128,2048]{1,0:T(8,128)(2,1)S(1)}, u32[]{:S(2)}, u32[]{:S(2)}) collective-permute-start(bf16[128,2048]{1,0:T(8,128)(2,1)S(1)} %get-tuple-element.50.own_ref), channel_id=1, source_target_pairs={{0,1},{1,0},{2,3},{3,2},{4,5},{5,4},{6,7},{7,6},{8,9},{9,8},{10,11... | collective-permute-start | bytes 1572872 | tf_op jit(solution)/shard_map/ppermute | solution.py:46
  75.1 9.1 %collective-permute-start.23 = (bf16[512,256]{1,0:T(8,128)(2,1)S(1)}, bf16[512,256]{1,0:T(8,128)(2,1)S(1)}, u32[]{:S(2)}, u32[]{:S(2)}) collective-permute-start(bf16[512,256]{1,0:T(8,128)(2,1)S(1)} %get-tuple-element.54), channel_id=1, source_target_pairs={{0,2},{1,3},{2,4},{3,5},{4,6},{5,7},{6,8},{7,9},{8,10},{9,11},{10,... | collective-permute-start | bytes 786440 | tf_op jit(solution)/shard_map/ppermute | solution.py:46
  75.1 14.1 %collective-permute-start.29 = (bf16[128,2048]{1,0:T(8,128)(2,1)S(1)}, bf16[128,2048]{1,0:T(8,128)(2,1)S(1)}, u32[]{:S(2)}, u32[]{:S(2)}) collective-permute-start(bf16[128,2048]{1,0:T(8,128)(2,1)S(1)} %get-tuple-element.56.mine), channel_id=1, source_target_pairs={{0,96},{32,0},{64,32},{96,64},{128,224},{160,128},{192,160},{224,1... | collective-permute-start | bytes 1572872 | tf_op jit(solution)/shard_map/ppermute | solution.py:46
  77.9 14.2 %collective-permute-start.28 = (bf16[128,2048]{1,0:T(8,128)(2,1)S(1)}, bf16[128,2048]{1,0:T(8,128)(2,1)S(1)}, u32[]{:S(2)}, u32[]{:S(2)}) collective-permute-start(bf16[128,2048]{1,0:T(8,128)(2,1)S(1)} %get-tuple-element.56.mine), channel_id=1, source_target_pairs={{0,32},{32,64},{64,96},{96,0},{128,160},{160,192},{192,224},{224,1... | collective-permute-start | bytes 1572872 | tf_op jit(solution)/shard_map/ppermute | solution.py:46
  77.9 7.7 %collective-permute-start.25 = (bf16[512,256]{1,0:T(8,128)(2,1)S(1)}, bf16[512,256]{1,0:T(8,128)(2,1)S(1)}, u32[]{:S(2)}, u32[]{:S(2)}) collective-permute-start(bf16[512,256]{1,0:T(8,128)(2,1)S(1)} %get-tuple-element.55), channel_id=1, source_target_pairs={{0,14},{1,15},{2,0},{3,1},{4,2},{5,3},{6,4},{7,5},{8,6},{9,7},{10,... | collective-permute-start | bytes 786440 | tf_op jit(solution)/shard_map/ppermute | solution.py:46
  84.2 9.7 %collective-permute-start.20 = (bf16[512,384]{1,0:T(8,128)(2,1)S(1)}, bf16[512,384]{1,0:T(8,128)(2,1)S(1)}, u32[]{:S(2)}, u32[]{:S(2)}) collective-permute-start(bf16[512,384]{1,0:T(8,128)(2,1)S(1)} %get-tuple-element.49), channel_id=1, source_target_pairs={{0,1},{1,0},{2,3},{3,2},{4,5},{5,4},{6,7},{7,6},{8,9},{9,8},{10,11... | collective-permute-start | bytes 1179656 | tf_op jit(solution)/shard_map/ppermute | solution.py:46
  85.6 8.0 %collective-permute-start.24 = (bf16[256,256]{1,0:T(8,128)(2,1)S(1)}, bf16[256,256]{1,0:T(8,128)(2,1)S(1)}, u32[]{:S(2)}, u32[]{:S(2)}) collective-permute-start(bf16[256,256]{1,0:T(8,128)(2,1)S(1)} %slice.80), channel_id=1, source_target_pairs={{0,1},{1,0},{2,3},{3,2},{4,5},{5,4},{6,7},{7,6},{8,9},{9,8},{10,11... | collective-permute-start | bytes 393224 | tf_op jit(solution)/shard_map/ppermute | solution.py:46
  87.1 6.8 %collective-permute-start.26 = (bf16[256,256]{1,0:T(8,128)(2,1)S(1)}, bf16[256,256]{1,0:T(8,128)(2,1)S(1)}, u32[]{:S(2)}, u32[]{:S(2)}) collective-permute-start(bf16[256,256]{1,0:T(8,128)(2,1)S(1)} %slice.81), channel_id=1, source_target_pairs={{0,1},{1,0},{2,3},{3,2},{4,5},{5,4},{6,7},{7,6},{8,9},{9,8},{10,11... | collective-permute-start | bytes 393224 | tf_op jit(solution)/shard_map/ppermute | solution.py:46
  89.3 4.6 %collective-permute-start.22 = (bf16[256,256]{1,0:T(8,128)(2,1)S(1)}, bf16[256,256]{1,0:T(8,128)(2,1)S(1)}, u32[]{:S(2)}, u32[]{:S(2)}) collective-permute-start(bf16[256,256]{1,0:T(8,128)(2,1)S(1)} %get-tuple-element.53), channel_id=1, source_target_pairs={{0,1},{1,0},{2,3},{3,2},{4,5},{5,4},{6,7},{7,6},{8,9},{9,8},{10,11... | collective-permute-start | bytes 393224 | tf_op jit(solution)/shard_map/ppermute | solution.py:46
  92.1 7.2 %collective-permute-start.31 = (bf16[64,2048]{1,0:T(8,128)(2,1)S(1)}, bf16[64,2048]{1,0:T(8,128)(2,1)S(1)}, u32[]{:S(2)}, u32[]{:S(2)}) collective-permute-start(bf16[64,2048]{1,0:T(8,128)(2,1)S(1)} %slice.85), channel_id=1, source_target_pairs={{0,96},{32,0},{64,32},{96,64},{128,224},{160,128},{192,160},{224,1... | collective-permute-start | bytes 786440 | tf_op jit(solution)/shard_map/ppermute | solution.py:46
  93.6 9.1 %collective-permute-start.30 = (bf16[64,2048]{1,0:T(8,128)(2,1)S(1)}, bf16[64,2048]{1,0:T(8,128)(2,1)S(1)}, u32[]{:S(2)}, u32[]{:S(2)}) collective-permute-start(bf16[64,2048]{1,0:T(8,128)(2,1)S(1)} %slice.84), channel_id=1, source_target_pairs={{0,32},{32,64},{64,96},{96,0},{128,160},{160,192},{192,224},{224,1... | collective-permute-start | bytes 786440 | tf_op jit(solution)/shard_map/ppermute | solution.py:46
  97.9 4.8 %collective-permute-start.27 = (bf16[256,256]{1,0:T(8,128)(2,1)S(1)}, bf16[256,256]{1,0:T(8,128)(2,1)S(1)}, u32[]{:S(2)}, u32[]{:S(2)}) collective-permute-start(bf16[256,256]{1,0:T(8,128)(2,1)S(1)} %get-tuple-element.61), channel_id=1, source_target_pairs={{0,16},{1,17},{2,18},{3,19},{4,20},{5,21},{6,22},{7,23},{8,24},{9,... | collective-permute-start | bytes 393224 | tf_op jit(solution)/shard_map/ppermute | solution.py:46
  104.0 3.8 %collective-permute-start.32 = (bf16[128,2048]{1,0:T(8,128)(2,1)S(1)}, bf16[128,2048]{1,0:T(8,128)(2,1)S(1)}, u32[]{:S(2)}, u32[]{:S(2)}) collective-permute-start(bf16[128,2048]{1,0:T(8,128)(2,1)S(1)} %get-tuple-element.58), channel_id=1, source_target_pairs={{0,1},{1,0},{2,3},{3,2},{4,5},{5,4},{6,7},{7,6},{8,9},{9,8},{10,11... | collective-permute-start | bytes 1572872 | tf_op jit(solution)/shard_map/ppermute | solution.py:46
  (4 other events, 33.9 us)

commit v14 on v12

--- a/solution.py
+++ b/solution.py
@@ -366,7 +366,7 @@
     )
     g_got = send(g_swap, OTHER_CORE)
 
-    to_pass = out_own
+    to_pass = after(out_own, g_other)
     out_prev = send(to_pass, Y_UP, "doc")
     out_next = send(to_pass, Y_DOWN, "doc")
     out_far_a = send(out_prev[:64], Y_UP, "doc")

time: 102 us -> 103 us (level)
  waiting for transfers between devices: 35.9 us -> 37 us
    ppermute x33, waiting for transfers between devices: 35.9 us -> 37 us  [send(): return lax.ppermute(value, axis, route)]
where the time goes in v14:
time: 103 us
  starting transfers between devices  50 us (49%)
  waiting for transfers between devices  37 us (36%)
  Pallas kernels  11.5 us (11%)
  other arithmetic  2.31 us (2%)
  local copies, waits for them, and re-layouts  1.29 us (1%)
    ppermute x33, starting transfers between devices, send(): return lax.ppermute(value, axis, route)  50 us
    ppermute x33, waiting for transfers between devices, send(): return lax.ppermute(value, axis, route)  37 us
    pallas_call x5, Pallas kernels, on_chip(): pl.pallas_call(kernel, out_shape=out_shape, in_specs=specs, out_specs=jax...  11.5 us
  transfers between devices with their start and end apart: 33, of which 16 were waited for; matrix products, arithmetic and copies ran while one was open for 0% of the time, Pallas kernels for 7%

profile of v14, /device:TPU:1, one launch (start us, length us, event | category | flops | bytes accessed | tf_op | source)
XLA Modules:
  0.0 103.0 jit_solution(15487431188426923648)
XLA Ops:
  2.3 3.3 %collective-permute-start.8 = (bf16[128,64]{1,0:T(8,128)(2,1)S(1)}, bf16[128,64]{1,0:T(8,128)(2,1)S(1)}, u32[]{:S(2)}, u32[]{:S(2)}) collective-permute-start(bf16[128,64]{1,0:T(8,128)(2,1)S(1)} %bitcast.43), channel_id=1, source_target_pairs={{0,1},{1,0},{2,3},{3,2},{4,5},{5,4},{6,7},{7,6},{8,9},{9,8},{10,11... | collective-permute-start | bytes 49160 | tf_op jit(solution)/shard_map/ppermute | solution.py:46
  5.6 3.9 %collective-permute-start = (bf16[48,2048]{1,0:T(8,128)(2,1)S(1)}, bf16[48,2048]{1,0:T(8,128)(2,1)S(1)}, u32[]{:S(2)}, u32[]{:S(2)}) collective-permute-start(bf16[48,2048]{1,0:T(8,128)(2,1)S(1)} %bitcast.34), channel_id=1, source_target_pairs={{0,2},{1,15},{2,4},{3,1},{4,6},{5,3},{6,8},{7,5},{8,10},{9,7},{10,... | collective-permute-start | bytes 589832 | tf_op jit(solution)/shard_map/ppermute | solution.py:46
  11.5 1.3 %collective-permute-start.7 = (bf16[8,2048]{1,0:T(8,128)(2,1)S(1)}, bf16[8,2048]{1,0:T(8,128)(2,1)S(1)}, u32[]{:S(2)}, u32[]{:S(2)}) collective-permute-start(bf16[8,2048]{1,0:T(8,128)(2,1)S(1)} %get-tuple-element.35), channel_id=1, source_target_pairs={{0,16},{1,17},{2,18},{3,19},{4,20},{5,21},{6,22},{7,23},{8,24},{9,... | collective-permute-start | bytes 98312 | tf_op jit(solution)/shard_map/ppermute | solution.py:46
  13.3 1.4 %collective-permute-done.7 = bf16[8,2048]{1,0:T(8,128)(2,1)S(1)} collective-permute-done((bf16[8,2048]{1,0:T(8,128)(2,1)S(1)}, bf16[8,2048]{1,0:T(8,128)(2,1)S(1)}, u32[]{:S(2)}, u32[]{:S(2)}) %collective-permute-start.7) | collective-permute-done | bytes 32800 | tf_op jit(solution)/shard_map/ppermute | solution.py:46
  14.7 1.4 %collective-permute-done.9 = bf16[128,128]{1,0:T(8,128)(2,1)S(1)} collective-permute-done((bf16[128,128]{1,0:T(8,128)(2,1)S(1)}, bf16[128,128]{1,0:T(8,128)(2,1)S(1)}, u32[]{:S(2)}, u32[]{:S(2)}) %collective-permute-start.9) | collective-permute-done | bytes 32800 | tf_op jit(solution)/shard_map/ppermute | solution.py:46
  16.8 2.7 %collective-permute-start.10 = (bf16[80,2048]{1,0:T(8,128)(2,1)S(1)}, bf16[80,2048]{1,0:T(8,128)(2,1)S(1)}, u32[]{:S(2)}, u32[]{:S(2)}) collective-permute-start(bf16[80,2048]{1,0:T(8,128)(2,1)S(1)} %pad_maximum_fusion.1.refs_12_), channel_id=1, source_target_pairs={{0,2},{1,15},{2,4},{3,1},{4,6},{5,3},{6,8},{7,5},{8,10},{9,7},{10,... | collective-permute-start | bytes 983048 | tf_op jit(solution)/shard_map/ppermute | solution.py:46
  19.4 4.5 %collective-permute-done.11.refs_14_ = bf16[80,2048]{1,0:T(8,128)(2,1)S(1)} collective-permute-done((bf16[80,2048]{1,0:T(8,128)(2,1)S(1)}, bf16[80,2048]{1,0:T(8,128)(2,1)S(1)}, u32[]{:S(2)}, u32[]{:S(2)}) %collective-permute-start.11) | collective-permute-done | bytes 327712 | tf_op jit(solution)/shard_map/ppermute | solution.py:46
  24.4 3.4 %collective-permute-start.14 = (bf16[80,2048]{1,0:T(8,128)(2,1)S(1)}, bf16[80,2048]{1,0:T(8,128)(2,1)S(1)}, u32[]{:S(2)}, u32[]{:S(2)}) collective-permute-start(bf16[80,2048]{1,0:T(8,128)(2,1)S(1)} %collective-permute-done.10.refs_13_), channel_id=1, source_target_pairs={{0,2},{1,15},{2,4},{3,1},{4,6},{5,3},{6,8},{7,5},{8,10},{9,7},{10,... | collective-permute-start | bytes 983048 | tf_op jit(solution)/shard_map/ppermute | solution.py:46
  27.8 2.7 %collective-permute-start.5 = (bf16[48,2048]{1,0:T(8,128)(2,1)S(1)}, bf16[48,2048]{1,0:T(8,128)(2,1)S(1)}, u32[]{:S(2)}, u32[]{:S(2)}) collective-permute-start(bf16[48,2048]{1,0:T(8,128)(2,1)S(1)} %collective-permute-done.refs_5_), channel_id=1, source_target_pairs={{0,2},{1,15},{2,4},{3,1},{4,6},{5,3},{6,8},{7,5},{8,10},{9,7},{10,... | collective-permute-start | bytes 589832 | tf_op jit(solution)/shard_map/ppermute | solution.py:46
  30.5 3.0 %collective-permute-start.2 = (bf16[128,2048]{1,0:T(8,128)(2,1)S(1)}, bf16[128,2048]{1,0:T(8,128)(2,1)S(1)}, u32[]{:S(2)}, u32[]{:S(2)}) collective-permute-start(bf16[128,2048]{1,0:T(8,128)(2,1)S(1)} %get-tuple-element.34.refs_0_), channel_id=1, source_target_pairs={{0,1},{1,0},{2,3},{3,2},{4,5},{5,4},{6,7},{7,6},{8,9},{9,8},{10,11... | collective-permute-start | bytes 1572872 | tf_op jit(solution)/shard_map/ppermute | solution.py:46
  33.5 1.6 %collective-permute-done.5.refs_7_ = bf16[48,2048]{1,0:T(8,128)(2,1)S(1)} collective-permute-done((bf16[48,2048]{1,0:T(8,128)(2,1)S(1)}, bf16[48,2048]{1,0:T(8,128)(2,1)S(1)}, u32[]{:S(2)}, u32[]{:S(2)}) %collective-permute-start.5) | collective-permute-done | bytes 196640 | tf_op jit(solution)/shard_map/ppermute | solution.py:46
  35.8 2.8 %collective-permute-start.17 = (bf16[80,2048]{1,0:T(8,128)(2,1)S(1)}, bf16[80,2048]{1,0:T(8,128)(2,1)S(1)}, u32[]{:S(2)}, u32[]{:S(2)}) collective-permute-start(bf16[80,2048]{1,0:T(8,128)(2,1)S(1)} %collective-permute-done.14.refs_15_), channel_id=1, source_target_pairs={{0,2},{1,15},{2,4},{3,1},{4,6},{5,3},{6,8},{7,5},{8,10},{9,7},{10,... | collective-permute-start | bytes 983048 | tf_op jit(solution)/shard_map/ppermute | solution.py:46
  39.6 1.3 %collective-permute-start.13 = (bf16[48,2048]{1,0:T(8,128)(2,1)S(1)}, bf16[48,2048]{1,0:T(8,128)(2,1)S(1)}, u32[]{:S(2)}, u32[]{:S(2)}) collective-permute-start(bf16[48,2048]{1,0:T(8,128)(2,1)S(1)} %collective-permute-done.6.refs_8_), channel_id=1, source_target_pairs={{0,14},{1,3},{2,0},{3,5},{4,2},{5,7},{6,4},{7,9},{8,6},{9,11},{10,... | collective-permute-start | bytes 589832 | tf_op jit(solution)/shard_map/ppermute | solution.py:46
  40.9 6.5 %collective-permute-done.12.refs_9_ = bf16[48,2048]{1,0:T(8,128)(2,1)S(1)} collective-permute-done((bf16[48,2048]{1,0:T(8,128)(2,1)S(1)}, bf16[48,2048]{1,0:T(8,128)(2,1)S(1)}, u32[]{:S(2)}, u32[]{:S(2)}) %collective-permute-start.12) | collective-permute-done | bytes 196640 | tf_op jit(solution)/shard_map/ppermute | solution.py:46
  47.4 1.5 %collective-permute-done.13.refs_10_ = bf16[48,2048]{1,0:T(8,128)(2,1)S(1)} collective-permute-done((bf16[48,2048]{1,0:T(8,128)(2,1)S(1)}, bf16[48,2048]{1,0:T(8,128)(2,1)S(1)}, u32[]{:S(2)}, u32[]{:S(2)}) %collective-permute-start.13) | collective-permute-done | bytes 196640 | tf_op jit(solution)/shard_map/ppermute | solution.py:46
  48.9 2.9 %collective-permute-start.19 = (bf16[80,2048]{1,0:T(8,128)(2,1)S(1)}, bf16[80,2048]{1,0:T(8,128)(2,1)S(1)}, u32[]{:S(2)}, u32[]{:S(2)}) collective-permute-start(bf16[80,2048]{1,0:T(8,128)(2,1)S(1)} %collective-permute-done.17.refs_17_), channel_id=1, source_target_pairs={{0,2},{1,15},{2,4},{3,1},{4,6},{5,3},{6,8},{7,5},{8,10},{9,7},{10,... | collective-permute-start | bytes 983048 | tf_op jit(solution)/shard_map/ppermute | solution.py:46
  51.8 2.7 %collective-permute-start.16 = (bf16[48,2048]{1,0:T(8,128)(2,1)S(1)}, bf16[48,2048]{1,0:T(8,128)(2,1)S(1)}, u32[]{:S(2)}, u32[]{:S(2)}) collective-permute-start(bf16[48,2048]{1,0:T(8,128)(2,1)S(1)} %collective-permute-done.12.refs_9_), channel_id=1, source_target_pairs={{0,2},{1,15},{2,4},{3,1},{4,6},{5,3},{6,8},{7,5},{8,10},{9,7},{10,... | collective-permute-start | bytes 589832 | tf_op jit(solution)/shard_map/ppermute | solution.py:46
  54.5 4.1 %collective-permute-done.16.refs_11_ = bf16[48,2048]{1,0:T(8,128)(2,1)S(1)} collective-permute-done((bf16[48,2048]{1,0:T(8,128)(2,1)S(1)}, bf16[48,2048]{1,0:T(8,128)(2,1)S(1)}, u32[]{:S(2)}, u32[]{:S(2)}) %collective-permute-start.16) | collective-permute-done | bytes 196640 | tf_op jit(solution)/shard_map/ppermute | solution.py:46
  58.6 2.2 %collective-permute-done.18.refs_18_ = bf16[80,2048]{1,0:T(8,128)(2,1)S(1)} collective-permute-done((bf16[80,2048]{1,0:T(8,128)(2,1)S(1)}, bf16[80,2048]{1,0:T(8,128)(2,1)S(1)}, u32[]{:S(2)}, u32[]{:S(2)}) %collective-permute-start.18) | collective-permute-done | bytes 327712 | tf_op jit(solution)/shard_map/ppermute | solution.py:46
  60.8 2.9 %shard_map.83 = (bf16[512,384]{1,0:T(8,128)(2,1)S(1)}, bf16[512,384]{1,0:T(8,128)(2,1)S(1)}, bf16[128,2048]{1,0:T(8,128)(2,1)S(1)}, bf16[512,2048]{1,0:T(8,128)(...) custom-call(s32[6]{0:T(128)S(1)} %stack.35.index, ...), custom_call_target="tpu_custom_call" | custom-call | flops 1610612736 | bytes 4194304 | tf_op jit(solution)/shard_map/pallas_call | solution.py:245
  63.7 4.6 %collective-permute-start.21 = (bf16[128,2048]{1,0:T(8,128)(2,1)S(1)}, bf16[128,2048]{1,0:T(8,128)(2,1)S(1)}, u32[]{:S(2)}, u32[]{:S(2)}) collective-permute-start(bf16[128,2048]{1,0:T(8,128)(2,1)S(1)} %get-tuple-element.49.own_ref), channel_id=1, source_target_pairs={{0,1},{1,0},{2,3},{3,2},{4,5},{5,4},{6,7},{7,6},{8,9},{9,8},{10,11... | collective-permute-start | bytes 1572872 | tf_op jit(solution)/shard_map/ppermute | solution.py:46
  68.3 2.7 %collective-permute-start.25 = (bf16[512,256]{1,0:T(8,128)(2,1)S(1)}, bf16[512,256]{1,0:T(8,128)(2,1)S(1)}, u32[]{:S(2)}, u32[]{:S(2)}) collective-permute-start(bf16[512,256]{1,0:T(8,128)(2,1)S(1)} %get-tuple-element.54), channel_id=1, source_target_pairs={{0,14},{1,15},{2,0},{3,1},{4,2},{5,3},{6,4},{7,5},{8,6},{9,7},{10,... | collective-permute-start | bytes 786440 | tf_op jit(solution)/shard_map/ppermute | solution.py:46
  71.0 2.7 %collective-permute-start.29 = (bf16[128,2048]{1,0:T(8,128)(2,1)S(1)}, bf16[128,2048]{1,0:T(8,128)(2,1)S(1)}, u32[]{:S(2)}, u32[]{:S(2)}) collective-permute-start(bf16[128,2048]{1,0:T(8,128)(2,1)S(1)} %get-tuple-element.56.mine), channel_id=1, source_target_pairs={{0,96},{32,0},{64,32},{96,64},{128,224},{160,128},{192,160},{224,1... | collective-permute-start | bytes 1572872 | tf_op jit(solution)/shard_map/ppermute | solution.py:46
  74.6 2.7 %collective-permute-done.23.below_ref = bf16[512,256]{1,0:T(8,128)(2,1)S(1)} collective-permute-done((bf16[512,256]{1,0:T(8,128)(2,1)S(1)}, bf16[512,256]{1,0:T(8,128)(2,1)S(1)}, u32[]{:S(2)}, u32[]{:S(2)}) %collective-permute-start.23) | collective-permute-done | bytes 262176 | tf_op jit(solution)/shard_map/ppermute | solution.py:46
  78.4 2.1 %shard_map.84 = (bf16[256,256]{1,0:T(8,128)(2,1)S(1)}, bf16[256,256]{1,0:T(8,128)(2,1)S(1)}) custom-call(s32[6]{0:T(128)S(1)} %stack.35.index, bf16[128,2048]{1,0:T(8,128)(2,1)S(1)} %get-tuple-element.49.own_ref, bf16[128,2048]{1,0:T(8,128)(2,1)S(1)} %collective-permute-done.21.other_ref, bf16[512,2048]{1,0:T(8,128)(2,1)S(1)} %get-tuple-element.50.table), custom_call_target="tpu_custom_call" | custom-call | flops 536870912 | bytes 4194304 | tf_op jit(solution)/shard_map/pallas_call | solution.py:245
  82.3 4.0 %shard_map.85 = bf16[2,256,256]{2,1,0:T(8,128)(2,1)S(1)} custom-call(s32[6]{0:T(128)S(1)} %stack.35.index, bf16[512,384]{1,0:T(8,128)(2,1)S(1)} %get-tuple-element.47.keep_ref, bf16[512,384]{1,0:T(8,128)(2,1)S(1)} %collective-permute-done.20.got_ref, bf16[256,256]{1,0:T(8,128)(2,1)S(1)} %get-tuple-element.51.g_keep, ...), custom_call_target="tpu_custom_call" | custom-call | flops 1342177280 | bytes 4194304 | tf_op jit(solution)/shard_map/pallas_call | solution.py:245
  86.3 2.8 %collective-permute-start.31 = (bf16[64,2048]{1,0:T(8,128)(2,1)S(1)}, bf16[64,2048]{1,0:T(8,128)(2,1)S(1)}, u32[]{:S(2)}, u32[]{:S(2)}) collective-permute-start(bf16[64,2048]{1,0:T(8,128)(2,1)S(1)} %slice.85), channel_id=1, source_target_pairs={{0,96},{32,0},{64,32},{96,64},{128,224},{160,128},{192,160},{224,1... | collective-permute-start | bytes 786440 | tf_op jit(solution)/shard_map/ppermute | solution.py:46
  90.3 3.5 %collective-permute-done.27.there_ref = bf16[256,256]{1,0:T(8,128)(2,1)S(1)} collective-permute-done((bf16[256,256]{1,0:T(8,128)(2,1)S(1)}, bf16[256,256]{1,0:T(8,128)(2,1)S(1)}, u32[]{:S(2)}, u32[]{:S(2)}) %collective-permute-start.27) | collective-permute-done | bytes 131104 | tf_op jit(solution)/shard_map/ppermute | solution.py:46
  94.4 3.2 %collective-permute-done.30.far_a = bf16[64,2048]{1,0:T(8,128)(2,1)S(1)} collective-permute-done((bf16[64,2048]{1,0:T(8,128)(2,1)S(1)}, bf16[64,2048]{1,0:T(8,128)(2,1)S(1)}, u32[]{:S(2)}, u32[]{:S(2)}) %collective-permute-start.30) | collective-permute-done | bytes 262176 | tf_op jit(solution)/shard_map/ppermute | solution.py:46
  97.6 1.3 %shard_map.86 = (f32[128,2048]{1,0:T(8,128)S(1)}, bf16[128,2048]{1,0:T(8,128)(2,1)S(1)}) custom-call(s32[6]{0:T(128)S(1)} %stack.35.index, bf16[256,256]{1,0:T(8,128)(2,1)S(1)} %get-tuple-element.62.own_ref, bf16[256,256]{1,0:T(8,128)(2,1)S(1)} %collective-permute-done.27.there_ref, bf16[128,2048]{1,0:T(8,128)(2,1)S(1)} %get-tuple-element.56.mine, ...), custom_call_target="tpu_custom_call" | custom-call | flops 536870912 | bytes 4194304 | tf_op jit(solution)/shard_map/pallas_call | solution.py:245
  98.9 1.6 %collective-permute-start.32 = (bf16[128,2048]{1,0:T(8,128)(2,1)S(1)}, bf16[128,2048]{1,0:T(8,128)(2,1)S(1)}, u32[]{:S(2)}, u32[]{:S(2)}) collective-permute-start(bf16[128,2048]{1,0:T(8,128)(2,1)S(1)} %get-tuple-element.58), channel_id=1, source_target_pairs={{0,1},{1,0},{2,3},{3,2},{4,5},{5,4},{6,7},{7,6},{8,9},{9,8},{10,11... | collective-permute-start | bytes 1572872 | tf_op jit(solution)/shard_map/ppermute | solution.py:46
  100.5 1.5 %collective-permute-done.32 = bf16[128,2048]{1,0:T(8,128)(2,1)S(1)} collective-permute-done((bf16[128,2048]{1,0:T(8,128)(2,1)S(1)}, bf16[128,2048]{1,0:T(8,128)(2,1)S(1)}, u32[]{:S(2)}, u32[]{:S(2)}) %collective-permute-start.32) | collective-permute-done | bytes 524320 | tf_op jit(solution)/shard_map/ppermute | solution.py:46
  (69 shorter events, 13.5 us)
Async XLA Ops:
  2.3 10.5 %collective-permute-start.8 = (bf16[128,64]{1,0:T(8,128)(2,1)S(1)}, bf16[128,64]{1,0:T(8,128)(2,1)S(1)}, u32[]{:S(2)}, u32[]{:S(2)}) collective-permute-start(bf16[128,64]{1,0:T(8,128)(2,1)S(1)} %bitcast.43), channel_id=1, source_target_pairs={{0,1},{1,0},{2,3},{3,2},{4,5},{5,4},{6,7},{7,6},{8,9},{9,8},{10,11... | collective-permute-start | bytes 49160 | tf_op jit(solution)/shard_map/ppermute | solution.py:46
  5.6 11.0 %collective-permute-start.4 = (bf16[48,2048]{1,0:T(8,128)(2,1)S(1)}, bf16[48,2048]{1,0:T(8,128)(2,1)S(1)}, u32[]{:S(2)}, u32[]{:S(2)}) collective-permute-start(bf16[48,2048]{1,0:T(8,128)(2,1)S(1)} %bitcast.33), channel_id=1, source_target_pairs={{0,14},{1,3},{2,0},{3,5},{4,2},{5,7},{6,4},{7,9},{8,6},{9,11},{10,... | collective-permute-start | bytes 589832 | tf_op jit(solution)/shard_map/ppermute | solution.py:46
  5.6 10.6 %collective-permute-start = (bf16[48,2048]{1,0:T(8,128)(2,1)S(1)}, bf16[48,2048]{1,0:T(8,128)(2,1)S(1)}, u32[]{:S(2)}, u32[]{:S(2)}) collective-permute-start(bf16[48,2048]{1,0:T(8,128)(2,1)S(1)} %bitcast.34), channel_id=1, source_target_pairs={{0,2},{1,15},{2,4},{3,1},{4,6},{5,3},{6,8},{7,5},{8,10},{9,7},{10,... | collective-permute-start | bytes 589832 | tf_op jit(solution)/shard_map/ppermute | solution.py:46
  11.5 3.1 %collective-permute-start.7 = (bf16[8,2048]{1,0:T(8,128)(2,1)S(1)}, bf16[8,2048]{1,0:T(8,128)(2,1)S(1)}, u32[]{:S(2)}, u32[]{:S(2)}) collective-permute-start(bf16[8,2048]{1,0:T(8,128)(2,1)S(1)} %get-tuple-element.35), channel_id=1, source_target_pairs={{0,16},{1,17},{2,18},{3,19},{4,20},{5,21},{6,22},{7,23},{8,24},{9,... | collective-permute-start | bytes 98312 | tf_op jit(solution)/shard_map/ppermute | solution.py:46
  12.9 3.1 %collective-permute-start.9 = (bf16[128,128]{1,0:T(8,128)(2,1)S(1)}, bf16[128,128]{1,0:T(8,128)(2,1)S(1)}, u32[]{:S(2)}, u32[]{:S(2)}) collective-permute-start(bf16[128,128]{1,0:T(8,128)(2,1)S(1)} %pad_maximum_fusion.2), channel_id=1, source_target_pairs={{0,16},{1,17},{2,18},{3,19},{4,20},{5,21},{6,22},{7,23},{8,24},{9,... | collective-permute-start | bytes 98312 | tf_op jit(solution)/shard_map/ppermute | solution.py:46
  16.3 17.1 %collective-permute-start.1 = (bf16[128,2048]{1,0:T(8,128)(2,1)S(1)}, bf16[128,2048]{1,0:T(8,128)(2,1)S(1)}, u32[]{:S(2)}, u32[]{:S(2)}) collective-permute-start(bf16[128,2048]{1,0:T(8,128)(2,1)S(1)} %get-tuple-element.34.refs_0_), channel_id=1, source_target_pairs={{0,16},{1,17},{2,18},{3,19},{4,20},{5,21},{6,22},{7,23},{8,24},{9,... | collective-permute-start | bytes 1572872 | tf_op jit(solution)/shard_map/ppermute | solution.py:46
  16.7 7.2 %collective-permute-start.11 = (bf16[80,2048]{1,0:T(8,128)(2,1)S(1)}, bf16[80,2048]{1,0:T(8,128)(2,1)S(1)}, u32[]{:S(2)}, u32[]{:S(2)}) collective-permute-start(bf16[80,2048]{1,0:T(8,128)(2,1)S(1)} %pad_maximum_fusion.1.refs_12_), channel_id=1, source_target_pairs={{0,14},{1,3},{2,0},{3,5},{4,2},{5,7},{6,4},{7,9},{8,6},{9,11},{10,... | collective-permute-start | bytes 983048 | tf_op jit(solution)/shard_map/ppermute | solution.py:46
  16.8 7.6 %collective-permute-start.10 = (bf16[80,2048]{1,0:T(8,128)(2,1)S(1)}, bf16[80,2048]{1,0:T(8,128)(2,1)S(1)}, u32[]{:S(2)}, u32[]{:S(2)}) collective-permute-start(bf16[80,2048]{1,0:T(8,128)(2,1)S(1)} %pad_maximum_fusion.1.refs_12_), channel_id=1, source_target_pairs={{0,2},{1,15},{2,4},{3,1},{4,6},{5,3},{6,8},{7,5},{8,10},{9,7},{10,... | collective-permute-start | bytes 983048 | tf_op jit(solution)/shard_map/ppermute | solution.py:46
  19.4 11.0 %collective-permute-start.6 = (bf16[48,2048]{1,0:T(8,128)(2,1)S(1)}, bf16[48,2048]{1,0:T(8,128)(2,1)S(1)}, u32[]{:S(2)}, u32[]{:S(2)}) collective-permute-start(bf16[48,2048]{1,0:T(8,128)(2,1)S(1)} %collective-permute-done.4.refs_6_), channel_id=1, source_target_pairs={{0,14},{1,3},{2,0},{3,5},{4,2},{5,7},{6,4},{7,9},{8,6},{9,11},{10,... | collective-permute-start | bytes 589832 | tf_op jit(solution)/shard_map/ppermute | solution.py:46
  24.4 10.8 %collective-permute-start.14 = (bf16[80,2048]{1,0:T(8,128)(2,1)S(1)}, bf16[80,2048]{1,0:T(8,128)(2,1)S(1)}, u32[]{:S(2)}, u32[]{:S(2)}) collective-permute-start(bf16[80,2048]{1,0:T(8,128)(2,1)S(1)} %collective-permute-done.10.refs_13_), channel_id=1, source_target_pairs={{0,2},{1,15},{2,4},{3,1},{4,6},{5,3},{6,8},{7,5},{8,10},{9,7},{10,... | collective-permute-start | bytes 983048 | tf_op jit(solution)/shard_map/ppermute | solution.py:46
  27.8 8.0 %collective-permute-start.15 = (bf16[80,2048]{1,0:T(8,128)(2,1)S(1)}, bf16[80,2048]{1,0:T(8,128)(2,1)S(1)}, u32[]{:S(2)}, u32[]{:S(2)}) collective-permute-start(bf16[80,2048]{1,0:T(8,128)(2,1)S(1)} %collective-permute-done.11.refs_14_), channel_id=1, source_target_pairs={{0,14},{1,3},{2,0},{3,5},{4,2},{5,7},{6,4},{7,9},{8,6},{9,11},{10,... | collective-permute-start | bytes 983048 | tf_op jit(solution)/shard_map/ppermute | solution.py:46
  27.8 7.4 %collective-permute-start.5 = (bf16[48,2048]{1,0:T(8,128)(2,1)S(1)}, bf16[48,2048]{1,0:T(8,128)(2,1)S(1)}, u32[]{:S(2)}, u32[]{:S(2)}) collective-permute-start(bf16[48,2048]{1,0:T(8,128)(2,1)S(1)} %collective-permute-done.refs_5_), channel_id=1, source_target_pairs={{0,2},{1,15},{2,4},{3,1},{4,6},{5,3},{6,8},{7,5},{8,10},{9,7},{10,... | collective-permute-start | bytes 589832 | tf_op jit(solution)/shard_map/ppermute | solution.py:46
  30.5 21.3 %collective-permute-start.2 = (bf16[128,2048]{1,0:T(8,128)(2,1)S(1)}, bf16[128,2048]{1,0:T(8,128)(2,1)S(1)}, u32[]{:S(2)}, u32[]{:S(2)}) collective-permute-start(bf16[128,2048]{1,0:T(8,128)(2,1)S(1)} %get-tuple-element.34.refs_0_), channel_id=1, source_target_pairs={{0,1},{1,0},{2,3},{3,2},{4,5},{5,4},{6,7},{7,6},{8,9},{9,8},{10,11... | collective-permute-start | bytes 1572872 | tf_op jit(solution)/shard_map/ppermute | solution.py:46
  33.4 18.4 %collective-permute-start.3 = (bf16[128,2048]{1,0:T(8,128)(2,1)S(1)}, bf16[128,2048]{1,0:T(8,128)(2,1)S(1)}, u32[]{:S(2)}, u32[]{:S(2)}) collective-permute-start(bf16[128,2048]{1,0:T(8,128)(2,1)S(1)} %collective-permute-done.1.refs_1_), channel_id=1, source_target_pairs={{0,1},{1,0},{2,3},{3,2},{4,5},{5,4},{6,7},{7,6},{8,9},{9,8},{10,11... | collective-permute-start | bytes 1572872 | tf_op jit(solution)/shard_map/ppermute | solution.py:46
  35.8 13.1 %collective-permute-start.17 = (bf16[80,2048]{1,0:T(8,128)(2,1)S(1)}, bf16[80,2048]{1,0:T(8,128)(2,1)S(1)}, u32[]{:S(2)}, u32[]{:S(2)}) collective-permute-start(bf16[80,2048]{1,0:T(8,128)(2,1)S(1)} %collective-permute-done.14.refs_15_), channel_id=1, source_target_pairs={{0,2},{1,15},{2,4},{3,1},{4,6},{5,3},{6,8},{7,5},{8,10},{9,7},{10,... | collective-permute-start | bytes 983048 | tf_op jit(solution)/shard_map/ppermute | solution.py:46
  38.6 8.8 %collective-permute-start.12 = (bf16[48,2048]{1,0:T(8,128)(2,1)S(1)}, bf16[48,2048]{1,0:T(8,128)(2,1)S(1)}, u32[]{:S(2)}, u32[]{:S(2)}) collective-permute-start(bf16[48,2048]{1,0:T(8,128)(2,1)S(1)} %collective-permute-done.5.refs_7_), channel_id=1, source_target_pairs={{0,2},{1,15},{2,4},{3,1},{4,6},{5,3},{6,8},{7,5},{8,10},{9,7},{10,... | collective-permute-start | bytes 589832 | tf_op jit(solution)/shard_map/ppermute | solution.py:46
  39.6 9.3 %collective-permute-start.13 = (bf16[48,2048]{1,0:T(8,128)(2,1)S(1)}, bf16[48,2048]{1,0:T(8,128)(2,1)S(1)}, u32[]{:S(2)}, u32[]{:S(2)}) collective-permute-start(bf16[48,2048]{1,0:T(8,128)(2,1)S(1)} %collective-permute-done.6.refs_8_), channel_id=1, source_target_pairs={{0,14},{1,3},{2,0},{3,5},{4,2},{5,7},{6,4},{7,9},{8,6},{9,11},{10,... | collective-permute-start | bytes 589832 | tf_op jit(solution)/shard_map/ppermute | solution.py:46
  48.9 9.7 %collective-permute-start.19 = (bf16[80,2048]{1,0:T(8,128)(2,1)S(1)}, bf16[80,2048]{1,0:T(8,128)(2,1)S(1)}, u32[]{:S(2)}, u32[]{:S(2)}) collective-permute-start(bf16[80,2048]{1,0:T(8,128)(2,1)S(1)} %collective-permute-done.17.refs_17_), channel_id=1, source_target_pairs={{0,2},{1,15},{2,4},{3,1},{4,6},{5,3},{6,8},{7,5},{8,10},{9,7},{10,... | collective-permute-start | bytes 983048 | tf_op jit(solution)/shard_map/ppermute | solution.py:46
  51.8 9.0 %collective-permute-start.18 = (bf16[80,2048]{1,0:T(8,128)(2,1)S(1)}, bf16[80,2048]{1,0:T(8,128)(2,1)S(1)}, u32[]{:S(2)}, u32[]{:S(2)}) collective-permute-start(bf16[80,2048]{1,0:T(8,128)(2,1)S(1)} %collective-permute-done.15.refs_16_), channel_id=1, source_target_pairs={{0,14},{1,3},{2,0},{3,5},{4,2},{5,7},{6,4},{7,9},{8,6},{9,11},{10,... | collective-permute-start | bytes 983048 | tf_op jit(solution)/shard_map/ppermute | solution.py:46
  51.8 6.8 %collective-permute-start.16 = (bf16[48,2048]{1,0:T(8,128)(2,1)S(1)}, bf16[48,2048]{1,0:T(8,128)(2,1)S(1)}, u32[]{:S(2)}, u32[]{:S(2)}) collective-permute-start(bf16[48,2048]{1,0:T(8,128)(2,1)S(1)} %collective-permute-done.12.refs_9_), channel_id=1, source_target_pairs={{0,2},{1,15},{2,4},{3,1},{4,6},{5,3},{6,8},{7,5},{8,10},{9,7},{10,... | collective-permute-start | bytes 589832 | tf_op jit(solution)/shard_map/ppermute | solution.py:46
  63.7 7.3 %collective-permute-start.21 = (bf16[128,2048]{1,0:T(8,128)(2,1)S(1)}, bf16[128,2048]{1,0:T(8,128)(2,1)S(1)}, u32[]{:S(2)}, u32[]{:S(2)}) collective-permute-start(bf16[128,2048]{1,0:T(8,128)(2,1)S(1)} %get-tuple-element.49.own_ref), channel_id=1, source_target_pairs={{0,1},{1,0},{2,3},{3,2},{4,5},{5,4},{6,7},{7,6},{8,9},{9,8},{10,11... | collective-permute-start | bytes 1572872 | tf_op jit(solution)/shard_map/ppermute | solution.py:46
  68.3 9.1 %collective-permute-start.23 = (bf16[512,256]{1,0:T(8,128)(2,1)S(1)}, bf16[512,256]{1,0:T(8,128)(2,1)S(1)}, u32[]{:S(2)}, u32[]{:S(2)}) collective-permute-start(bf16[512,256]{1,0:T(8,128)(2,1)S(1)} %get-tuple-element.53), channel_id=1, source_target_pairs={{0,2},{1,3},{2,4},{3,5},{4,6},{5,7},{6,8},{7,9},{8,10},{9,11},{10,... | collective-permute-start | bytes 786440 | tf_op jit(solution)/shard_map/ppermute | solution.py:46
  68.3 10.0 %collective-permute-start.25 = (bf16[512,256]{1,0:T(8,128)(2,1)S(1)}, bf16[512,256]{1,0:T(8,128)(2,1)S(1)}, u32[]{:S(2)}, u32[]{:S(2)}) collective-permute-start(bf16[512,256]{1,0:T(8,128)(2,1)S(1)} %get-tuple-element.54), channel_id=1, source_target_pairs={{0,14},{1,15},{2,0},{3,1},{4,2},{5,3},{6,4},{7,5},{8,6},{9,7},{10,... | collective-permute-start | bytes 786440 | tf_op jit(solution)/shard_map/ppermute | solution.py:46
  71.0 15.3 %collective-permute-start.29 = (bf16[128,2048]{1,0:T(8,128)(2,1)S(1)}, bf16[128,2048]{1,0:T(8,128)(2,1)S(1)}, u32[]{:S(2)}, u32[]{:S(2)}) collective-permute-start(bf16[128,2048]{1,0:T(8,128)(2,1)S(1)} %get-tuple-element.56.mine), channel_id=1, source_target_pairs={{0,96},{32,0},{64,32},{96,64},{128,224},{160,128},{192,160},{224,1... | collective-permute-start | bytes 1572872 | tf_op jit(solution)/shard_map/ppermute | solution.py:46
  73.7 15.4 %collective-permute-start.28 = (bf16[128,2048]{1,0:T(8,128)(2,1)S(1)}, bf16[128,2048]{1,0:T(8,128)(2,1)S(1)}, u32[]{:S(2)}, u32[]{:S(2)}) collective-permute-start(bf16[128,2048]{1,0:T(8,128)(2,1)S(1)} %get-tuple-element.56.mine), channel_id=1, source_target_pairs={{0,32},{32,64},{64,96},{96,0},{128,160},{160,192},{192,224},{224,1... | collective-permute-start | bytes 1572872 | tf_op jit(solution)/shard_map/ppermute | solution.py:46
  73.7 7.6 %collective-permute-start.20 = (bf16[512,384]{1,0:T(8,128)(2,1)S(1)}, bf16[512,384]{1,0:T(8,128)(2,1)S(1)}, u32[]{:S(2)}, u32[]{:S(2)}) collective-permute-start(bf16[512,384]{1,0:T(8,128)(2,1)S(1)} %get-tuple-element.48), channel_id=1, source_target_pairs={{0,1},{1,0},{2,3},{3,2},{4,5},{5,4},{6,7},{7,6},{8,9},{9,8},{10,11... | collective-permute-start | bytes 1179656 | tf_op jit(solution)/shard_map/ppermute | solution.py:46
  77.4 3.1 %collective-permute-start.24 = (bf16[256,256]{1,0:T(8,128)(2,1)S(1)}, bf16[256,256]{1,0:T(8,128)(2,1)S(1)}, u32[]{:S(2)}, u32[]{:S(2)}) collective-permute-start(bf16[256,256]{1,0:T(8,128)(2,1)S(1)} %slice.80), channel_id=1, source_target_pairs={{0,1},{1,0},{2,3},{3,2},{4,5},{5,4},{6,7},{7,6},{8,9},{9,8},{10,11... | collective-permute-start | bytes 393224 | tf_op jit(solution)/shard_map/ppermute | solution.py:46
  78.3 3.0 %collective-permute-start.26 = (bf16[256,256]{1,0:T(8,128)(2,1)S(1)}, bf16[256,256]{1,0:T(8,128)(2,1)S(1)}, u32[]{:S(2)}, u32[]{:S(2)}) collective-permute-start(bf16[256,256]{1,0:T(8,128)(2,1)S(1)} %slice.81), channel_id=1, source_target_pairs={{0,1},{1,0},{2,3},{3,2},{4,5},{5,4},{6,7},{7,6},{8,9},{9,8},{10,11... | collective-permute-start | bytes 393224 | tf_op jit(solution)/shard_map/ppermute | solution.py:46
  86.3 8.1 %collective-permute-start.31 = (bf16[64,2048]{1,0:T(8,128)(2,1)S(1)}, bf16[64,2048]{1,0:T(8,128)(2,1)S(1)}, u32[]{:S(2)}, u32[]{:S(2)}) collective-permute-start(bf16[64,2048]{1,0:T(8,128)(2,1)S(1)} %slice.85), channel_id=1, source_target_pairs={{0,96},{32,0},{64,32},{96,64},{128,224},{160,128},{192,160},{224,1... | collective-permute-start | bytes 786440 | tf_op jit(solution)/shard_map/ppermute | solution.py:46
  89.1 8.5 %collective-permute-start.30 = (bf16[64,2048]{1,0:T(8,128)(2,1)S(1)}, bf16[64,2048]{1,0:T(8,128)(2,1)S(1)}, u32[]{:S(2)}, u32[]{:S(2)}) collective-permute-start(bf16[64,2048]{1,0:T(8,128)(2,1)S(1)} %slice.84), channel_id=1, source_target_pairs={{0,32},{32,64},{64,96},{96,0},{128,160},{160,192},{192,224},{224,1... | collective-permute-start | bytes 786440 | tf_op jit(solution)/shard_map/ppermute | solution.py:46
  89.3 4.5 %collective-permute-start.27 = (bf16[256,256]{1,0:T(8,128)(2,1)S(1)}, bf16[256,256]{1,0:T(8,128)(2,1)S(1)}, u32[]{:S(2)}, u32[]{:S(2)}) collective-permute-start(bf16[256,256]{1,0:T(8,128)(2,1)S(1)} %get-tuple-element.61), channel_id=1, source_target_pairs={{0,16},{1,17},{2,18},{3,19},{4,20},{5,21},{6,22},{7,23},{8,24},{9,... | collective-permute-start | bytes 393224 | tf_op jit(solution)/shard_map/ppermute | solution.py:46
  98.9 3.1 %collective-permute-start.32 = (bf16[128,2048]{1,0:T(8,128)(2,1)S(1)}, bf16[128,2048]{1,0:T(8,128)(2,1)S(1)}, u32[]{:S(2)}, u32[]{:S(2)}) collective-permute-start(bf16[128,2048]{1,0:T(8,128)(2,1)S(1)} %get-tuple-element.58), channel_id=1, source_target_pairs={{0,1},{1,0},{2,3},{3,2},{4,5},{5,4},{6,7},{7,6},{8,9},{9,8},{10,11... | collective-permute-start | bytes 1572872 | tf_op jit(solution)/shard_map/ppermute | solution.py:46
  (4 other events, 32.5 us)
